TPU v7x, 32 devices: a whole 2x2x4 slice. The times are simulated.
32 devices in a mesh: dp: 8 (over z, core), tensor: 4 (over y, x).
Axes of the slice: x: 2, y: 2, z: 4, core: 2. Of those that a mesh axis runs over, the one named last changes fastest.
Arguments:
- tokens: bfloat16 [16384, 1024], P(('dp', 'tensor')), may hold values from -6 to 6
- cotangent: bfloat16 [16384, 1024], P(('dp', 'tensor')), may hold values from -6 to 6
- routes: int32 [1, 16384, 8], P(None, 'dp'), may hold values from 0 to 31, all different within a row; in each aligned block of 2048 rows (0 to 2047, 2048 to 4095, ..., all dimensions but the last counted through in order) at most 1024 rows name the same one
- gate_weights: float32 [1, 16384, 8], P(None, 'dp'), may hold values from 0.05 to 0.25
- norm_gains: float32 [1, 2, 1024], P(None, None, ('dp', 'tensor')), may hold values from 0.5 to 1.5
- norm_gains_first: float32 [1, 2, 1024], P(None, None, ('dp', 'tensor')), may hold values from -128 to 128
- norm_gains_second: float32 [1, 2, 1024], P(None, None, ('dp', 'tensor')), may hold values from 1619.0862 to 6476.3447
- query_weight: float32 [1, 1024, 1024], P(None, 'dp', 'tensor'), may hold values from -0.1875 to 0.1875
- query_first: float32 [1, 1024, 1024], P(None, 'dp', 'tensor'), may hold values from -96 to 96
- query_second: float32 [1, 1024, 1024], P(None, 'dp', 'tensor'), may hold values from 1152 to 4608
- keyval_weight: float32 [1, 1024, 1024], P(None, 'dp', 'tensor'), may hold values from -0.1875 to 0.1875
- keyval_first: float32 [1, 1024, 1024], P(None, 'dp', 'tensor'), may hold values from -96 to 96
- keyval_second: float32 [1, 1024, 1024], P(None, 'dp', 'tensor'), may hold values from 1152 to 4608
- output_weight: float32 [1, 1024, 1024], P(None, 'tensor', 'dp'), may hold values from -1.5 to 1.5
- output_first: float32 [1, 1024, 1024], P(None, 'tensor', 'dp'), may hold values from -12 to 12
- output_second: float32 [1, 1024, 1024], P(None, 'tensor', 'dp'), may hold values from 17.92 to 72
- expert_in: float32 [1, 32, 1024, 1024], P(None, 'tensor', 'dp'), may hold values from -0.1875 to 0.1875
- expert_in_first: float32 [1, 32, 1024, 1024], P(None, 'tensor', 'dp'), may hold values from -20 to 20
- expert_in_second: float32 [1, 32, 1024, 1024], P(None, 'tensor', 'dp'), may hold values from 49.152 to 204.8
- expert_down: float32 [1, 32, 512, 1024], P(None, 'tensor', 'dp'), may hold values from -1 to 1
- expert_down_first: float32 [1, 32, 512, 1024], P(None, 'tensor', 'dp'), may hold values from -4 to 4
- expert_down_second: float32 [1, 32, 512, 1024], P(None, 'tensor', 'dp'), may hold values from 1.6384 to 6.5536
Outputs:
- block_out: float32 [16384, 1024], P(('dp', 'tensor'))
- input_grad: float32 [16384, 1024], P(('dp', 'tensor'))
- gains_step: float32 [1, 2, 1024], P(None, None, ('dp', 'tensor'))
- new_gains_first: float32 [1, 2, 1024], P(None, None, ('dp', 'tensor'))
- new_gains_second: float32 [1, 2, 1024], P(None, None, ('dp', 'tensor'))
- new_query: float32 [1, 1024, 1024], P(None, 'dp', 'tensor')
- new_query_first: float32 [1, 1024, 1024], P(None, 'dp', 'tensor')
- new_query_second: float32 [1, 1024, 1024], P(None, 'dp', 'tensor')
- new_keyval: float32 [1, 1024, 1024], P(None, 'dp', 'tensor')
- new_keyval_first: float32 [1, 1024, 1024], P(None, 'dp', 'tensor')
- new_keyval_second: float32 [1, 1024, 1024], P(None, 'dp', 'tensor')
- new_output: float32 [1, 1024, 1024], P(None, 'tensor', 'dp')
- new_output_first: float32 [1, 1024, 1024], P(None, 'tensor', 'dp')
- new_output_second: float32 [1, 1024, 1024], P(None, 'tensor', 'dp')
- new_expert_in: float32 [1, 32, 1024, 1024], P(None, 'tensor', 'dp')
- new_expert_in_first: float32 [1, 32, 1024, 1024], P(None, 'tensor', 'dp')
- new_expert_in_second: float32 [1, 32, 1024, 1024], P(None, 'tensor', 'dp')
- new_expert_down: float32 [1, 32, 512, 1024], P(None, 'tensor', 'dp')
- new_expert_down_first: float32 [1, 32, 512, 1024], P(None, 'tensor', 'dp')
- new_expert_down_second: float32 [1, 32, 512, 1024], P(None, 'tensor', 'dp')
Inputs may be any that keep to these rules, and one draw needn't show every extreme that they name: `routes`: in every block of 2048 consecutive tokens of a layer, each row names 8 different experts and no expert is named by more than 1024 rows; some expert is named by exactly 1024 rows.
All inputs are finite; a program needn't handle non-finite values.
Results may differ from a plain program's by a relative error of at most 0.012.
Values may be sent and summed in bfloat16 or wider, within the bound.
No kernel may reach another device: no remote copies, remote signals or barrier semaphores. Data moves between devices by JAX's collectives and lax.ppermute only.
A program may use at most 320 MiB of HBM per device.

v0:
```python
import math

import jax
import jax.numpy as jnp
from jax import lax
from jax.sharding import PartitionSpec as P

D = 1024
HEADS = 16
KV = 8
HD = 64
FFE = 512
SEQ_LEN = 512
LAYERS = 1
STEP = 10
CAP = 1024


NORM_EPS = 1e-05
ROPE_BASE = 10000.0
BETA_ONE = 0.9
BETA_TWO = 0.95
ADAM_EPS = 1e-08
LEARN_RATE = 0.1
WEIGHT_DECAY = 0.1
MASK_FILL = -1e30


def rope_tables(length, width):
    half_width = width // 2
    position = jnp.arange(length, dtype=jnp.int32).astype(jnp.float32)
    exponent = jnp.arange(half_width, dtype=jnp.int32).astype(jnp.float32) * (-2.0 / width)
    frequency = jnp.exp(exponent * math.log(ROPE_BASE))
    angle = position[:, None] * frequency[None, :]
    return (jnp.cos(angle), jnp.sin(angle))


def rotate(values, cosine, sine_table):
    half_width = values.shape[-1] // 2
    first_half = values[..., :half_width]
    second_half = values[..., half_width:]
    cos_wide = cosine[None, :, None, :]
    sin_wide = sine_table[None, :, None, :]
    return jnp.concatenate(
        [
            first_half * cos_wide - second_half * sin_wide,
            second_half * cos_wide + first_half * sin_wide,
        ],
        axis=-1,
    )


def rotate_back(grads, cosine, sine_table):
    half_width = grads.shape[-1] // 2
    first_half = grads[..., :half_width]
    second_half = grads[..., half_width:]
    cos_wide = cosine[None, :, None, :]
    sin_wide = sine_table[None, :, None, :]
    return jnp.concatenate(
        [
            first_half * cos_wide + second_half * sin_wide,
            second_half * cos_wide - first_half * sin_wide,
        ],
        axis=-1,
    )


def rms_scale(values):
    return lax.rsqrt(jnp.mean(values * values, axis=-1, keepdims=True) + NORM_EPS)


def adam_update(master, first_moment, second_moment, gradient, decay_rate):
    first_new = BETA_ONE * first_moment + (1.0 - BETA_ONE) * gradient
    second_new = BETA_TWO * second_moment + (1.0 - BETA_TWO) * gradient * gradient
    first_fixed = first_new / (1.0 - BETA_ONE**STEP)
    second_fixed = second_new / (1.0 - BETA_TWO**STEP)
    master_new = master - LEARN_RATE * (
        first_fixed / (jnp.sqrt(second_fixed) + ADAM_EPS) + decay_rate * master
    )
    return (master_new, first_new, second_new)


def adam_change(first_moment, second_moment, gradient):
    first_new = BETA_ONE * first_moment + (1.0 - BETA_ONE) * gradient
    second_new = BETA_TWO * second_moment + (1.0 - BETA_TWO) * gradient * gradient
    first_fixed = first_new / (1.0 - BETA_ONE**STEP)
    second_fixed = second_new / (1.0 - BETA_TWO**STEP)
    change = -LEARN_RATE * (first_fixed / (jnp.sqrt(second_fixed) + ADAM_EPS))
    return (change, first_new, second_new)


def spread_rows(values):
    return lax.all_gather(values, "tensor", axis=0, tiled=True)


def spread_grads(values):
    return lax.all_gather(values, "tensor", axis=0, tiled=True)


def collect_rows(values):
    return lax.psum_scatter(values, "tensor", scatter_dimension=0, tiled=True)


def gather_layer(query_low, keyval_low, output_low, in_low, down_low):
    return (
        lax.all_gather(query_low, "dp", axis=0, tiled=True),
        lax.all_gather(keyval_low, "dp", axis=0, tiled=True),
        lax.all_gather(output_low, "dp", axis=1, tiled=True),
        lax.all_gather(in_low, "dp", axis=1, tiled=True),
        lax.all_gather(down_low, "dp", axis=1, tiled=True),
    )


def gather_again(query_low, keyval_low, output_low, in_low, down_low):
    return (
        lax.all_gather(query_low, "dp", axis=0, tiled=True),
        lax.all_gather(keyval_low, "dp", axis=0, tiled=True),
        lax.all_gather(output_low, "dp", axis=1, tiled=True),
        lax.all_gather(in_low, "dp", axis=1, tiled=True),
        lax.all_gather(down_low, "dp", axis=1, tiled=True),
    )


def score_block(queries, keys):
    scale_factor = 1.0 / math.sqrt(queries.shape[-1])
    scores = (
        jnp.einsum("stkgd,sukd->skgtu", queries, keys, preferred_element_type=jnp.float32)
        * scale_factor
    )
    length = queries.shape[1]
    row_index = lax.broadcasted_iota(jnp.int32, (length, length), 0)
    column_index = lax.broadcasted_iota(jnp.int32, (length, length), 1)
    return (jnp.where(column_index <= row_index, scores, MASK_FILL), scale_factor)


def attend_forward(normed_all, query_w, keyval_w, cosine, sine_table):
    row_count = normed_all.shape[0]
    seq_count = row_count // SEQ_LEN
    keyval_heads = keyval_w.shape[1] // (2 * HD)
    group_size = HEADS // KV
    query_lin = jnp.dot(normed_all, query_w, preferred_element_type=jnp.float32)
    keyval_lin = jnp.dot(normed_all, keyval_w, preferred_element_type=jnp.float32)
    query_rot = rotate(
        query_lin.reshape(seq_count, SEQ_LEN, keyval_heads * group_size, HD), cosine, sine_table
    )
    queries = query_rot.astype(jnp.bfloat16).reshape(
        seq_count, SEQ_LEN, keyval_heads, group_size, HD
    )
    keyval_split = keyval_lin.reshape(seq_count, SEQ_LEN, keyval_heads, 2, HD)
    keys = rotate(keyval_split[:, :, :, 0], cosine, sine_table).astype(jnp.bfloat16)
    values = keyval_split[:, :, :, 1].astype(jnp.bfloat16)
    scores, scale_factor = score_block(queries, keys)
    total = jax.nn.logsumexp(scores, axis=-1, keepdims=True)
    probability = jnp.exp(scores - total).astype(jnp.bfloat16)
    heads = jnp.einsum("skgtu,sukd->stkgd", probability, values, preferred_element_type=jnp.float32)
    heads = heads.reshape(row_count, -1).astype(jnp.bfloat16)
    return (queries, keys, values, total, heads)


def expert_plan(route_rows, gate_rows, first_expert, experts_local):
    row_count = route_rows.shape[0]
    expert_ids = first_expert + jnp.arange(experts_local, dtype=jnp.int32)
    match = route_rows[:, :, None] == expert_ids[None, None, :]
    chosen = jnp.any(match, axis=1)
    weight = jnp.sum(jnp.where(match, gate_rows[:, :, None], 0.0), axis=1)
    slot = jnp.cumsum(chosen.astype(jnp.int32), axis=0) - 1
    target = jnp.where(chosen, slot, CAP)
    token_ids = lax.broadcasted_iota(jnp.int32, (row_count, experts_local), 0)
    expert_column = lax.broadcasted_iota(jnp.int32, (row_count, experts_local), 1)
    index = (
        jnp.zeros((experts_local, CAP), jnp.int32)
        .at[expert_column, target]
        .set(token_ids, mode="drop")
    )
    slot_weight = (
        jnp.zeros((experts_local, CAP), jnp.float32)
        .at[expert_column, target]
        .set(weight, mode="drop")
    )
    return (index, slot_weight)


def layer_low(query_weight, keyval_weight, output_weight, expert_in, expert_down, layer_index):
    return (
        query_weight[layer_index].astype(jnp.bfloat16),
        keyval_weight[layer_index].astype(jnp.bfloat16),
        output_weight[layer_index].astype(jnp.bfloat16),
        expert_in[layer_index].astype(jnp.bfloat16),
        expert_down[layer_index].astype(jnp.bfloat16),
    )


def on_device(
    tokens,
    cotangent,
    routes,
    gate_weights,
    norm_gains,
    norm_gains_first,
    norm_gains_second,
    query_weight,
    query_first,
    query_second,
    keyval_weight,
    keyval_first,
    keyval_second,
    output_weight,
    output_first,
    output_second,
    expert_in,
    expert_in_first,
    expert_in_second,
    expert_down,
    expert_down_first,
    expert_down_second,
):
    cosine, sine_table = rope_tables(SEQ_LEN, HD)
    experts_local = expert_in.shape[1]
    first_expert = lax.axis_index("tensor") * experts_local
    all_gains = lax.all_gather(norm_gains, ("dp", "tensor"), axis=2, tiled=True)
    stream = tokens.astype(jnp.float32)
    layer_index = 0
    lows = layer_low(
        query_weight, keyval_weight, output_weight, expert_in, expert_down, layer_index
    )
    layer_weights = gather_layer(lows[0], lows[1], lows[2], lows[3], lows[4])
    query_w, keyval_w, output_w, in_w, down_w = layer_weights
    inverse_one = rms_scale(stream)
    unit_one = stream * inverse_one
    normed_all = spread_rows((unit_one * all_gains[layer_index, 0]).astype(jnp.bfloat16))
    queries, keys, values, total, heads = attend_forward(
        normed_all, query_w, keyval_w, cosine, sine_table
    )
    block = heads
    stream_mid = stream + lax.psum_scatter(
        jnp.dot(block, output_w, preferred_element_type=jnp.float32),
        "tensor",
        scatter_dimension=0,
        tiled=True,
    )
    inverse_two = rms_scale(stream_mid)
    unit_two = stream_mid * inverse_two
    normed_two_all = spread_rows((unit_two * all_gains[layer_index, 1]).astype(jnp.bfloat16))
    index, slot_weight = expert_plan(
        routes[layer_index], gate_weights[layer_index], first_expert, experts_local
    )
    slot_rows = normed_two_all[index]
    hidden_lin = jnp.einsum("ecd,edf->ecf", slot_rows, in_w, preferred_element_type=jnp.float32)
    gate_lin = hidden_lin[..., :FFE]
    up_lin = hidden_lin[..., FFE:]
    active = (gate_lin * jax.nn.sigmoid(gate_lin) * up_lin).astype(jnp.bfloat16)
    expert_out = jnp.einsum("ecf,efd->ecd", active, down_w, preferred_element_type=jnp.float32)
    weighted = slot_weight[:, :, None] * expert_out
    partial_sum = (
        jnp.zeros((normed_two_all.shape[0], D), jnp.float32)
        .at[index.reshape(-1)]
        .add(weighted.reshape(-1, D))
    )
    stream_next = stream_mid + collect_rows(partial_sum)
    held = None
    saved = [
        (
            inverse_one,
            unit_one,
            normed_all,
            queries,
            keys,
            values,
            total,
            heads,
            inverse_two,
            unit_two,
            slot_rows,
            index,
            slot_weight,
            hidden_lin,
            active,
            held,
        )
    ]
    grad_stream = cotangent.astype(jnp.float32)
    gain_grads = [None] * LAYERS
    weight_grads = [None] * LAYERS
    for layer_index in reversed(range(LAYERS)):
        (
            inverse_one,
            unit_one,
            normed_all,
            queries,
            keys,
            values,
            total,
            heads,
            inverse_two,
            unit_two,
            slot_rows,
            index,
            slot_weight,
            hidden_lin,
            active,
            held,
        ) = saved[layer_index]
        lows = layer_low(
            query_weight, keyval_weight, output_weight, expert_in, expert_down, layer_index
        )
        query_w, keyval_w, output_w, in_w, down_w = gather_again(
            lows[0], lows[1], lows[2], lows[3], lows[4]
        )
        row_count = normed_all.shape[0]
        mixed_grad = spread_grads(grad_stream.astype(jnp.bfloat16))
        slot_grad = (slot_weight[:, :, None] * mixed_grad[index]).astype(jnp.bfloat16)
        down_grad = jnp.einsum(
            "ecf,ecd->efd", active, slot_grad, preferred_element_type=jnp.float32
        )
        active_grad = jnp.einsum(
            "ecd,efd->ecf", slot_grad, down_w, preferred_element_type=jnp.float32
        )
        gate_lin = hidden_lin[..., :FFE]
        up_lin = hidden_lin[..., FFE:]
        sigma = jax.nn.sigmoid(gate_lin)
        gate_side = active_grad * up_lin
        gate_grad = gate_side * sigma + gate_side * gate_lin * (sigma * (1.0 - sigma))
        up_grad = active_grad * (gate_lin * sigma)
        hidden_grad = jnp.concatenate([gate_grad, up_grad], axis=-1).astype(jnp.bfloat16)
        in_grad = jnp.einsum(
            "ecd,ecf->edf", slot_rows, hidden_grad, preferred_element_type=jnp.float32
        )
        slot_back = jnp.einsum(
            "ecf,edf->ecd", hidden_grad, in_w, preferred_element_type=jnp.float32
        )
        partial_grad = (
            jnp.zeros((row_count, D), jnp.float32)
            .at[index.reshape(-1)]
            .add(slot_back.reshape(-1, D))
        )
        normed_two_grad = collect_rows(partial_grad)
        gain_two = jnp.sum(normed_two_grad * unit_two, axis=0)
        scaled_two = normed_two_grad * all_gains[layer_index, 1]
        mid_grad = grad_stream + inverse_two * (
            scaled_two - unit_two * jnp.mean(scaled_two * unit_two, axis=-1, keepdims=True)
        )
        branch_grad = spread_grads(mid_grad.astype(jnp.bfloat16))
        out_grad = jnp.einsum("rq,rd->qd", heads, branch_grad, preferred_element_type=jnp.float32)
        heads_grad = jnp.einsum(
            "rd,qd->rq", branch_grad, output_w, preferred_element_type=jnp.float32
        ).astype(jnp.bfloat16)
        shaped_grad = heads_grad.reshape(queries.shape)
        scores, scale_factor = score_block(queries, keys)
        probability = jnp.exp(scores - total)
        prob_grad = jnp.einsum(
            "stkgd,sukd->skgtu", shaped_grad, values, preferred_element_type=jnp.float32
        )
        score_grad = (
            probability * (prob_grad - jnp.sum(probability * prob_grad, axis=-1, keepdims=True))
        ).astype(jnp.bfloat16)
        query_grad = (
            jnp.einsum("skgtu,sukd->stkgd", score_grad, keys, preferred_element_type=jnp.float32)
            * scale_factor
        )
        key_grad = (
            jnp.einsum("skgtu,stkgd->sukd", score_grad, queries, preferred_element_type=jnp.float32)
            * scale_factor
        )
        value_grad = jnp.einsum(
            "skgtu,stkgd->sukd",
            probability.astype(jnp.bfloat16),
            shaped_grad,
            preferred_element_type=jnp.float32,
        )
        seq_count = queries.shape[0]
        query_lin_grad = (
            rotate_back(query_grad.reshape(seq_count, SEQ_LEN, -1, HD), cosine, sine_table)
            .reshape(row_count, -1)
            .astype(jnp.bfloat16)
        )
        key_lin_grad = rotate_back(key_grad, cosine, sine_table)
        keyval_grad = (
            jnp.stack([key_lin_grad, value_grad], axis=3)
            .reshape(row_count, -1)
            .astype(jnp.bfloat16)
        )
        query_w_grad = jnp.einsum(
            "rd,rq->dq", normed_all, query_lin_grad, preferred_element_type=jnp.float32
        )
        keyval_w_grad = jnp.einsum(
            "rd,rq->dq", normed_all, keyval_grad, preferred_element_type=jnp.float32
        )
        normed_part = jnp.einsum(
            "rq,dq->rd", query_lin_grad, query_w, preferred_element_type=jnp.float32
        ) + jnp.einsum("rq,dq->rd", keyval_grad, keyval_w, preferred_element_type=jnp.float32)
        normed_grad = collect_rows(normed_part)
        gain_one = jnp.sum(normed_grad * unit_one, axis=0)
        scaled_one = normed_grad * all_gains[layer_index, 0]
        grad_stream = mid_grad + inverse_one * (
            scaled_one - unit_one * jnp.mean(scaled_one * unit_one, axis=-1, keepdims=True)
        )
        gain_grads[layer_index] = jnp.stack([gain_one, gain_two])
        weight_grads[layer_index] = (
            lax.psum_scatter(query_w_grad, "dp", scatter_dimension=0, tiled=True),
            lax.psum_scatter(keyval_w_grad, "dp", scatter_dimension=0, tiled=True),
            lax.psum_scatter(out_grad, "dp", scatter_dimension=1, tiled=True),
            lax.psum_scatter(in_grad, "dp", scatter_dimension=1, tiled=True),
            lax.psum_scatter(down_grad, "dp", scatter_dimension=1, tiled=True),
        )
    gain_shards = lax.psum_scatter(
        jnp.stack(gain_grads), ("dp", "tensor"), scatter_dimension=2, tiled=True
    )
    stacked = [jnp.stack([weight_grads[0][member]]) for member in range(5)]
    gains_new = adam_change(norm_gains_first, norm_gains_second, gain_shards)
    query_new = adam_update(query_weight, query_first, query_second, stacked[0], WEIGHT_DECAY)
    keyval_new = adam_update(keyval_weight, keyval_first, keyval_second, stacked[1], WEIGHT_DECAY)
    output_new = adam_update(output_weight, output_first, output_second, stacked[2], WEIGHT_DECAY)
    in_new = adam_update(expert_in, expert_in_first, expert_in_second, stacked[3], WEIGHT_DECAY)
    down_new = adam_update(
        expert_down, expert_down_first, expert_down_second, stacked[4], WEIGHT_DECAY
    )
    return (
        stream_next,
        grad_stream,
        gains_new[0],
        gains_new[1],
        gains_new[2],
        query_new[0],
        query_new[1],
        query_new[2],
        keyval_new[0],
        keyval_new[1],
        keyval_new[2],
        output_new[0],
        output_new[1],
        output_new[2],
        in_new[0],
        in_new[1],
        in_new[2],
        down_new[0],
        down_new[1],
        down_new[2],
    )


def solution(mesh):
    placed = (
        P(("dp", "tensor"), None),
        P(("dp", "tensor"), None),
        P(None, "dp", None),
        P(None, "dp", None),
        P(None, None, ("dp", "tensor")),
        P(None, None, ("dp", "tensor")),
        P(None, None, ("dp", "tensor")),
        P(None, "dp", "tensor"),
        P(None, "dp", "tensor"),
        P(None, "dp", "tensor"),
        P(None, "dp", "tensor"),
        P(None, "dp", "tensor"),
        P(None, "dp", "tensor"),
        P(None, "tensor", "dp"),
        P(None, "tensor", "dp"),
        P(None, "tensor", "dp"),
        P(None, "tensor", "dp", None),
        P(None, "tensor", "dp", None),
        P(None, "tensor", "dp", None),
        P(None, "tensor", "dp", None),
        P(None, "tensor", "dp", None),
        P(None, "tensor", "dp", None),
    )
    return jax.shard_map(
        on_device,
        mesh=mesh,
        in_specs=placed,
        out_specs=(
            P(("dp", "tensor"), None),
            P(("dp", "tensor"), None),
            P(None, None, ("dp", "tensor")),
            P(None, None, ("dp", "tensor")),
            P(None, None, ("dp", "tensor")),
            P(None, "dp", "tensor"),
            P(None, "dp", "tensor"),
            P(None, "dp", "tensor"),
            P(None, "dp", "tensor"),
            P(None, "dp", "tensor"),
            P(None, "dp", "tensor"),
            P(None, "tensor", "dp"),
            P(None, "tensor", "dp"),
            P(None, "tensor", "dp"),
            P(None, "tensor", "dp", None),
            P(None, "tensor", "dp", None),
            P(None, "tensor", "dp", None),
            P(None, "tensor", "dp", None),
            P(None, "tensor", "dp", None),
            P(None, "tensor", "dp", None),
        ),
        check_vma=False,
    )
```

profile of v0, /device:TPU:0, one launch (start us, length us, event | category | flops | bytes accessed | tf_op | source)
XLA Modules:
  0.0 1893.3 jit_solution(17440433741583437900)
XLA Ops:
  7.3 1.6 fusion.40
  9.7 72.5 %all_gather.35 = f32[1,2,1024]{1,0,2:T(1,128)S(1)} all-gather(f32[1,2,32]{1,0,2:T(1,128)S(1)} %copy.145), channel_id=1, replica_groups=mesh['dp'=8,'tensor'=4] {'dp','tensor'}, dimensions={2}, use_global_device_ids=true | all-gather | bytes 8448 | tf_op jit(solution)/shard_map/all_gather | solution.py:220
  82.2 6.2 slice_reduce_fusion
  88.4 2.5 fusion.34
  91.5 14.6 all-gather.2
  106.1 15.0 all-gather
  121.1 15.4 all-gather.1
  136.6 3.1 all-gather.12.cloned.1.call-done
  139.7 4.8 fusion.70
  144.5 2.7 reshape.258
  148.6 4.8 fusion.67
  153.4 2.8 reshape.259
  157.6 7.4 fusion.103
  165.1 8.3 exponential_reduce_fusion
  173.5 8.4 fusion.46
  184.0 4.5 fusion.63
  189.3 85.8 %reduce-scatter.13.cloned.1.call-done = f32[512,1024]{1,0:T(8,128)} async-done(((f32[2048,1024]{1,0:T(8,128)}), f32[512,1024]{1,0:T(8,128)}) %reduce-scatter.13.cloned.1.call-update) | async-done | bytes 2097168 | tf_op jit(solution)/shard_map/reduce_scatter | solution.py:235
  275.1 1.9 multiply_reduce_fusion.2
  279.7 4.7 copy.157
  285.9 2.3 reduce-window.6
  290.9 60.6 %scatter_custom_fusion.3 = f32[8192]{0:T(1024)S(1)} fusion(s32[16384]{0:T(1024)S(1)} %reshape.309, f32[16384]{0:T(1024)S(1)} %reshape.317, f32[]{:T(128)} %constant.23.clone.1), kind=kCustom, calls=%fused_computation.149 | custom fusion | bytes 32772
  352.0 60.3 %scatter_custom_fusion.2 = s32[8192]{0:T(1024)S(1)} fusion(s32[16384]{0:T(1024)S(1)} %reshape.309, s32[16384]{0:T(1024)S(1)} %reshape.311, s32[]{:T(128)} %constant.30.clone.1), kind=kCustom, calls=%fused_computation.151 | custom fusion | bytes 32772
  413.1 43.4 %gather_fusion.1 = bf16[8192,1024]{1,0:T(8,128)(2,1)} fusion(bf16[2048,1024]{1,0:T(8,128)(2,1)} %all-gather.16.cloned.1.call-done, s32[8192]{0:T(1024)S(1)} %bitcast_clamp_fusion), kind=kCustom, calls=%fused_computation.1 | custom fusion | bytes 33587200 | tf_op jit(solution)/shard_map/gather | solution.py:311
  456.4 43.5 %gather_fusion = bf16[8192,1024]{1,0:T(8,128)(2,1)} fusion(bf16[2048,1024]{1,0:T(8,128)(2,1)} %all-gather.14.cloned.1.call-done, s32[8192]{0:T(1024)S(1)} %bitcast_clamp_fusion), kind=kCustom, calls=%fused_computation | custom fusion | bytes 33587200 | tf_op jit(solution)/shard_map/gather | solution.py:247
  500.0 39.0 %all-gather.20.cloned.1.call-done = bf16[1,8,1024,1024]{2,3,1,0:T(8,128)(2,1)} async-done(((bf16[1,8,128,1024]{2,3,1,0:T(8,128)(2,1)}), bf16[1,8,1024,1024]{2,3,1,0:T(8,128)(2,1)}) %all-gather.20.cloned.1.call-update) | async-done | bytes 16777232 | tf_op jit(solution)/shard_map/all_gather | solution.py:109
  539.0 29.5 %fusion.9 = f32[8,1024,1024]{1,2,0:T(8,128)} fusion(bf16[8,1024,1024]{2,1,0:T(8,128)(2,1)} %bitcast.215, bf16[1,8,1024,1024]{2,3,1,0:T(8,128)(2,1)} %all-gather.20.cloned.1.call-done), kind=kOutput, calls=%fused_computation.20 | convolution fusion | flops 17179869184 | bytes 67108864 | tf_op jit(solution)/shard_map/ecd,edf->ecf/dot_general | solution.py:248
  568.5 52.9 %all-gather.22.cloned.1.call-done = bf16[1,8,512,1024]{3,2,1,0:T(8,128)(2,1)} async-done(((bf16[1,8,64,1024]{3,2,1,0:T(8,128)(2,1)}), bf16[1,8,512,1024]{3,2,1,0:T(8,128)(2,1)}) %all-gather.22.cloned.1.call-update) | async-done | bytes 8388624 | tf_op jit(solution)/shard_map/all_gather | solution.py:110
  621.4 31.7 %fusion.3 = (bf16[8,1024,512]{1,2,0:T(8,128)(2,1)}, bf16[8,1024,512]{1,2,0:T(8,128)(2,1)}, bf16[8,1024,512]{1,2,0:T(8,128)(2,1)}) fusion(f32[8,1024,1024]{1,2,0:T(8,128)} %fusion.9, bf16[1,8,512,1024]{3,2,1,0:T(8,128)(2,1)} %all-gather.22.cloned.1.call-done, bf16[8,1024,1024]{2,1,0:T(8,128)(2,1)} %bitcast.217, f32[8,1024]{1,0:T(8,128)S(1)} %reshape.274), kind=kOutput, calls=%fused_computation.11 | convolution fusion | flops 8682209280 | bytes 83918848 | tf_op jit(solution)/shard_map/ecd,efd->ecf/dot_general | solution.py:315
  653.0 29.9 %fusion.7 = f32[8,1024,1024]{2,1,0:T(8,128)} fusion(bf16[1,8,1024,1024]{2,3,1,0:T(8,128)(2,1)} %all-gather.20.cloned.1.call-done, bf16[8,1024,512]{1,2,0:T(8,128)(2,1)} %get-tuple-element.47, bf16[8,1024,512]{1,2,0:T(8,128)(2,1)} %get-tuple-element.46), kind=kOutput, calls=%fused_computation.18 | convolution fusion | flops 17213423616 | bytes 67108864 | tf_op jit(solution)/shard_map/ecf,edf->ecd/dot_general | solution.py:328
  683.0 74.8 %scatter_custom_fusion.1 = f32[2048,1024]{1,0:T(8,128)} fusion(s32[8192]{0:T(1024)} %bitcast.239, f32[8192,1024]{1,0:T(8,128)} %bitcast.245, f32[]{:T(128)} %constant.23.clone.1), kind=kCustom, calls=%fused_computation.42 | custom fusion | flops 8388608 | bytes 8389120 | tf_op jit(solution)/shard_map/scatter-add | solution.py:334
  757.8 85.0 %reduce-scatter.17.cloned.1.call-done = f32[512,1024]{1,0:T(8,128)} async-done(((f32[2048,1024]{1,0:T(8,128)}), f32[512,1024]{1,0:T(8,128)}) %reduce-scatter.17.cloned.1.call-update) | async-done | bytes 2097168 | tf_op jit(solution)/shard_map/reduce_scatter | solution.py:101
  842.9 2.4 multiply_reduce_fusion
  845.3 2.9 fusion.95
  848.3 52.8 %all-gather.18.cloned.1.call-done = bf16[2048,1024]{1,0:T(8,128)(2,1)} async-done(((bf16[512,1024]{1,0:T(8,128)(2,1)}), bf16[2048,1024]{1,0:T(8,128)(2,1)}) %all-gather.18.cloned.1.call-update) | async-done | bytes 4194320 | tf_op jit(solution)/shard_map/all_gather | solution.py:97
  901.1 4.4 convolution_convert_fusion
  905.6 5.2 reshape.337
  910.8 5.9 copy.162
  916.7 9.7 fusion.57
  926.4 13.9 fusion.4
  940.3 11.1 fusion.6
  951.4 6.3 fusion.53
  957.8 1.5 convolution_multiply_fusion
  961.1 1.4 add_convert_fusion
  963.4 1.3 fusion.65
  964.9 4.7 convolution_add_fusion
  969.6 4.7 fusion.106
  974.4 5.5 fusion.104
  980.4 4.8 fusion.105
  985.3 17.6 fusion.12
  1003.0 20.9 %broadcast_multiply_fusion = f32[8,1024,1024]{2,1,0:T(8,128)} fusion(f32[8,1024]{1,0:T(8,128)S(1)} %copy-done.31, bf16[8,1024,512]{1,2,0:T(8,128)(2,1)} %get-tuple-element.48, bf16[1,8,512,1024]{3,2,1,0:T(8,128)(2,1)} %all-gather.22.cloned.1.call-done), kind=kOutput, calls=%fused_computation.27 | convolution fusion | flops 8598323200 | bytes 50364416 | tf_op jit(solution)/shard_map/ecf,efd->ecd/dot_general | solution.py:252
  1023.8 74.8 %scatter_custom_fusion = f32[2048,1024]{1,0:T(8,128)} fusion(s32[8192]{0:T(1024)} %bitcast.240, f32[8192,1024]{1,0:T(8,128)} %bitcast.214, f32[]{:T(128)} %constant.23.clone.1), kind=kCustom, calls=%fused_computation.44 | custom fusion | flops 8388608 | bytes 8389120 | tf_op jit(solution)/shard_map/scatter-add | solution.py:257
  1099.3 2.5 fusion.39
  1103.1 29.7 %fusion.17 = f32[8,1024,1024]{2,1,0:T(8,128)} fusion(bf16[8,1024,1024]{2,1,0:T(8,128)(2,1)} %bitcast.216, bf16[8,1024,512]{1,2,0:T(8,128)(2,1)} %get-tuple-element.47, bf16[8,1024,512]{1,2,0:T(8,128)(2,1)} %get-tuple-element.46), kind=kOutput, calls=%fused_computation.33 | convolution fusion | flops 17213423616 | bytes 67108864 | tf_op jit(solution)/shard_map/ecd,ecf->edf/dot_general | solution.py:325
  1133.9 1.7 multiply_subtract_fusion.2
  1135.6 1.7 multiply_subtract_fusion.4
  1137.3 20.9 %reduce-scatter.23.cloned.1.call-done = f32[128,256]{1,0:T(8,128)} async-done(((f32[1024,256]{1,0:T(8,128)}), f32[128,256]{1,0:T(8,128)}) %reduce-scatter.23.cloned.1.call-update) | async-done | bytes 131088 | tf_op jit(solution)/shard_map/reduce_scatter | solution.py:400
  1158.2 1.7 multiply_subtract_fusion.3
  1159.9 167.4 %reduce-scatter.29.cloned.1.call-done = f32[8,64,1024]{2,1,0:T(8,128)} async-done(((f32[8,512,1024]{2,1,0:T(8,128)}), f32[8,64,1024]{2,1,0:T(8,128)}) %reduce-scatter.29.cloned.1.call-update) | async-done | bytes 2097168 | tf_op jit(solution)/shard_map/reduce_scatter | solution.py:403
  1327.3 7.6 multiply_subtract_fusion.1
  1334.9 80.4 %reduce-scatter.15.cloned.1.call-done = f32[512,1024]{1,0:T(8,128)} async-done(((f32[2048,1024]{1,0:T(8,128)}), f32[512,1024]{1,0:T(8,128)}) %reduce-scatter.15.cloned.1.call-update) | async-done | bytes 2097168 | tf_op jit(solution)/shard_map/reduce_scatter | solution.py:101
  1415.3 5.3 fusion.38
  1420.6 131.1 %reduce-scatter.31.cloned.1.call-done = f32[32,2]{1,0:T(8,128)} async-done(((f32[1024,2]{1,0:T(8,128)}), f32[32,2]{1,0:T(8,128)}) %reduce-scatter.31.cloned.1.call-update) | async-done | bytes 272
  1553.2 322.6 %reduce-scatter.27.cloned.1.call-done = f32[8,128,1024]{2,1,0:T(8,128)} async-done(((f32[8,1024,1024]{2,1,0:T(8,128)}), f32[8,128,1024]{2,1,0:T(8,128)}) %reduce-scatter.27.cloned.1.call-update) | async-done | bytes 4194320 | tf_op jit(solution)/shard_map/reduce_scatter | solution.py:402
  1875.8 10.8 multiply_subtract_fusion
  (228 shorter events, 22.7 us)
Async XLA Ops:
  7.2 83.8 %copy-start.36 = (f32[1,128,256]{2,1,0:T(8,128)S(1)}, f32[1,128,256]{2,1,0:T(8,128)}, u32[]{:S(2)}) copy-start(f32[1,128,256]{2,1,0:T(8,128)} %param.29) | copy-start | bytes 393220
  7.2 83.8 %copy-start.38 = (f32[1,128,256]{2,1,0:T(8,128)S(1)}, f32[1,128,256]{2,1,0:T(8,128)}, u32[]{:S(2)}) copy-start(f32[1,128,256]{2,1,0:T(8,128)} %param.32) | copy-start | bytes 393220
  7.2 83.8 %copy-start.34 = (f32[1,256,128]{2,1,0:T(8,128)S(1)}, f32[1,256,128]{2,1,0:T(8,128)}, u32[]{:S(2)}) copy-start(f32[1,256,128]{2,1,0:T(8,128)} %param.35) | copy-start | bytes 393220
  7.2 132.4 %all-gather.12.cloned.1.call-start = ((), (), s32[]{:S(2)}) async-start(), calls=%async_computation.10 | async-start | bytes 5242880 | tf_op jit(solution)/shard_map/all_gather | solution.py:93
  8.9 82.6 %copy-start.54 = (f32[512]{0:T(512)}, f32[512]{0:T(512)S(1)}, u32[]{:S(2)}) copy-start(f32[512]{0:T(512)S(1)} %add_rsqrt_fusion.1) | copy-start | bytes 6148
  88.4 3.1 copy-start.49
  88.4 188.7 %copy-start.47 = (f32[1024]{0:T(1024)}, f32[1024]{0:T(1024)S(1)}, u32[]{:S(2)}) copy-start(f32[1024]{0:T(1024)S(1)} %get-tuple-element.24) | copy-start | bytes 12292
  90.9 184.2 %reduce-scatter.13.cloned.1.call-start = ((), (), s32[]{:S(2)}) async-start(), calls=%async_computation.11 | async-start | bytes 10485760 | tf_op jit(solution)/shard_map/reduce_scatter | solution.py:235
  91.5 65.8 %copy-start.22 = (f32[512,32]{0,1:T(8,128)}, f32[512,32]{0,1:T(8,128)S(1)}, u32[]{:S(2)}) copy-start(f32[512,32]{0,1:T(8,128)S(1)} %get-tuple-element.61) | copy-start | bytes 196612
  91.5 65.8 %copy-start.24 = (f32[512,32]{0,1:T(8,128)}, f32[512,32]{0,1:T(8,128)S(1)}, u32[]{:S(2)}) copy-start(f32[512,32]{0,1:T(8,128)S(1)} %get-tuple-element.62) | copy-start | bytes 196612
  121.1 18.5 copy-start.12
  136.6 11.8 copy-start.14
  153.4 3.5 slice-start.4
  156.9 8.1 copy-start.18
  157.0 8.0 copy-start.20
  157.5 7.5 copy-start.26
  157.5 7.5 copy-start.28
  165.1 8.4 copy-start.9
  173.5 8.4 copy-start.32
  188.5 86.6 %copy-start.3 = (bf16[512,1024]{1,0:T(8,128)(2,1)S(1)}, bf16[512,1024]{1,0:T(8,128)(2,1)}, u32[]{:S(2)}) copy-start(bf16[512,1024]{1,0:T(8,128)(2,1)} %param.22) | copy-start | bytes 3145732
  188.5 224.5 %all-gather.16.cloned.1.call-start = ((), (), s32[]{:S(2)}) async-start(), calls=%async_computation.14 | async-start | bytes 5242880 | tf_op jit(solution)/shard_map/all_gather | solution.py:97
  189.3 267.2 %all-gather.14.cloned.1.call-start = ((), (), s32[]{:S(2)}) async-start(), calls=%async_computation.12 | async-start | bytes 5242880 | tf_op jit(solution)/shard_map/all_gather | solution.py:93
  279.6 4.9 copy-start.5
  279.6 259.3 %all-gather.20.cloned.1.call-start = ((), (), s32[]{:S(2)}) async-start(), calls=%async_computation.23 | async-start | bytes 18874368 | tf_op jit(solution)/shard_map/all_gather | solution.py:109
  284.4 4.4 copy-start.59
  284.4 4.5 copy-start.58
  284.5 5.4 copy-start.51
  284.5 336.9 %all-gather.22.cloned.1.call-start = ((), (), s32[]{:S(2)}) async-start(), calls=%async_computation.24 | async-start | bytes 9437184 | tf_op jit(solution)/shard_map/all_gather | solution.py:110
  285.7 557.2 %reduce-scatter.17.cloned.1.call-start = ((), (), s32[]{:S(2)}) async-start(), calls=%async_computation.15 | async-start | bytes 10485760 | tf_op jit(solution)/shard_map/reduce_scatter | solution.py:101
  351.4 269.9 %copy-start.30 = (f32[8,1024]{1,0:T(8,128)}, f32[8,1024]{1,0:T(8,128)S(1)}, u32[]{:S(2)}) copy-start(f32[8,1024]{1,0:T(8,128)S(1)} %reshape.274) | copy-start | bytes 98308
  757.8 85.1 %copy-start.2 = (f32[512,1024]{1,0:T(8,128)S(1)}, f32[512,1024]{1,0:T(8,128)}, u32[]{:S(2)}) copy-start(f32[512,1024]{1,0:T(8,128)} %copy-done.1) | copy-start | bytes 6291460
  757.8 85.1 %copy-start.48 = (f32[1024]{0:T(1024)S(1)}, f32[1024]{0:T(1024)}, u32[]{:S(2)}) copy-start(f32[1024]{0:T(1024)} %copy-done.47) | copy-start | bytes 12292
  757.8 85.1 %copy-start.53 = (f32[512]{0:T(512)S(1)}, f32[512]{0:T(512)}, u32[]{:S(2)}) copy-start(f32[512]{0:T(512)} %copy-done.52) | copy-start | bytes 6148
  757.8 143.3 %all-gather.18.cloned.1.call-start = ((), (), s32[]{:S(2)}) async-start(), calls=%async_computation.16 | async-start | bytes 5242880 | tf_op jit(solution)/shard_map/all_gather | solution.py:97
  842.9 2.4 copy-start.4
  845.3 55.8 %copy-start.17 = (bf16[1,256,1024]{2,1,0:T(8,128)(2,1)S(1)}, bf16[1,256,1024]{2,1,0:T(8,128)(2,1)}, u32[]{:S(2)}) copy-start(bf16[1,256,1024]{2,1,0:T(8,128)(2,1)} %all-gather.2) | copy-start | bytes 1572868
  848.2 250.5 %reduce-scatter.19.cloned.1.call-start = ((), (), s32[]{:S(2)}) async-start(), calls=%async_computation.17 | async-start | bytes 10485760 | tf_op jit(solution)/shard_map/reduce_scatter | solution.py:101
  905.6 11.1 copy-start.33
  916.6 9.7 copy-start.10
  916.6 23.6 %slice-start = ((s8[16777216]{0:T(1024)(128)(4,1)}), s8[4194304]{0:T(1024)(128)(4,1)S(1)}, s32[]{:S(2)}) async-start(s8[16777216]{0:T(1024)(128)(4,1)} %bitcast.212), calls=%async_computation.26 | async-start | bytes 8388608
  916.6 23.6 %slice-start.1 = ((s8[16777216]{0:T(1024)(128)(4,1)}), s8[4194304]{0:T(1024)(128)(4,1)S(1)}, s32[]{:S(2)}) async-start(s8[16777216]{0:T(1024)(128)(4,1)} %bitcast.212), calls=%async_computation.27 | async-start | bytes 8388608
  926.4 13.9 slice-start.2
  926.4 13.9 slice-start.3
  940.3 11.1 copy-start.19
  951.4 6.3 copy-start
  951.4 6.3 copy-start.27
  951.4 6.3 copy-start.29
  960.8 4.0 copy-start.11
  969.5 163.4 %reduce-scatter.25.cloned.1.call-start = ((), (), s32[]{:S(2)}) async-start(), calls=%async_computation.20 | async-start | bytes 1179648 | tf_op jit(solution)/shard_map/reduce_scatter | solution.py:401
  974.3 161.2 %reduce-scatter.21.cloned.1.call-start = ((), (), s32[]{:S(2)}) async-start(), calls=%async_computation.18 | async-start | bytes 1179648 | tf_op jit(solution)/shard_map/reduce_scatter | solution.py:399
  979.9 5.4 copy-start.31
  979.9 178.3 %reduce-scatter.23.cloned.1.call-start = ((), (), s32[]{:S(2)}) async-start(), calls=%async_computation.19 | async-start | bytes 1179648 | tf_op jit(solution)/shard_map/reduce_scatter | solution.py:400
  985.2 342.1 %reduce-scatter.29.cloned.1.call-start = ((), (), s32[]{:S(2)}) async-start(), calls=%async_computation.22 | async-start | bytes 18874368 | tf_op jit(solution)/shard_map/reduce_scatter | solution.py:403
  1002.9 412.4 %reduce-scatter.15.cloned.1.call-start = ((), (), s32[]{:S(2)}) async-start(), calls=%async_computation.13 | async-start | bytes 10485760 | tf_op jit(solution)/shard_map/reduce_scatter | solution.py:101
  1098.7 453.1 %reduce-scatter.31.cloned.1.call-start = ((), (), s32[]{:S(2)}) async-start(), calls=%async_computation.25 | async-start | bytes 540672
  1102.9 772.9 %reduce-scatter.27.cloned.1.call-start = ((), (), s32[]{:S(2)}) async-start(), calls=%async_computation.21 | async-start | bytes 37748736 | tf_op jit(solution)/shard_map/reduce_scatter | solution.py:402
  1132.8 2.7 copy-start.37
  1132.8 2.7 copy-start.43
  1132.9 2.7 copy-start.44
  1132.9 25.3 %copy-start.39 = (f32[1,128,256]{2,1,0:T(8,128)S(1)}, f32[1,128,256]{2,1,0:T(8,128)}, u32[]{:S(2)}) copy-start(f32[1,128,256]{2,1,0:T(8,128)} %param.32) | copy-start | bytes 393220
  1132.9 25.3 %copy-start.45 = (f32[1,128,256]{2,1,0:T(8,128)S(1)}, f32[1,128,256]{2,1,0:T(8,128)}, u32[]{:S(2)}) copy-start(f32[1,128,256]{2,1,0:T(8,128)} %param.33) | copy-start | bytes 393220
  1132.9 25.3 %copy-start.46 = (f32[1,128,256]{2,1,0:T(8,128)S(1)}, f32[1,128,256]{2,1,0:T(8,128)}, u32[]{:S(2)}) copy-start(f32[1,128,256]{2,1,0:T(8,128)} %param.34) | copy-start | bytes 393220
  1334.9 217.7 %copy-start.56 = (f32[1,2,32]{2,1,0:T(2,128)S(1)}, f32[1,2,32]{2,1,0:T(2,128)}, u32[]{:S(2)}) copy-start(f32[1,2,32]{2,1,0:T(2,128)} %param.27) | copy-start | bytes 772
  1334.9 217.7 %copy-start.57 = (f32[1,2,32]{2,1,0:T(2,128)S(1)}, f32[1,2,32]{2,1,0:T(2,128)}, u32[]{:S(2)}) copy-start(f32[1,2,32]{2,1,0:T(2,128)} %param.28) | copy-start | bytes 772
  (17 other events, 22.8 us)
Sparse Core Ops, SparseCore 0:
  91.1 48.5 all-gather.11
  188.7 86.4 reduce-scatter.12
  277.1 52.6 all-gather.15
  332.3 52.6 all-gather.13
  387.1 151.8 all-gather.19
  541.1 80.2 all-gather.21
  757.9 84.9 reduce-scatter.16
  848.4 52.7 all-gather.17
  969.7 86.3 reduce-scatter.18
  1058.9 32.2 reduce-scatter.24
  1094.1 30.6 reduce-scatter.20
  1127.5 30.5 reduce-scatter.22
  1160.6 166.6 reduce-scatter.28
  1330.5 84.7 reduce-scatter.14
  1418.0 133.7 reduce-scatter.30
  1554.1 321.6 reduce-scatter.26
where the time goes:
time: 1900 us; the launch traced here: 1890 us
  waiting for transfers between devices  1040 us (55%)
  local copies, waits for them, and re-layouts  249 us (13%)
  matrix products  246 us (13%)
  other arithmetic  222 us (12%)
  blocking collectives  118 us (6%)
    reduce_scatter x1, waiting for transfers between devices, on_device(): lax.psum_scatter(in_grad, 'dp', scatter_dimension=1, tiled=True)  323 us
    reduce_scatter x1, waiting for transfers between devices, on_device(): lax.psum_scatter(down_grad, 'dp', scatter_dimension=1, tiled=True)  167 us
    reduce_scatter x3, waiting for transfers between devices, collect_rows(): return lax.psum_scatter(values, 'tensor', scatter_dimension=0, tiled=True)  165 us
    unnamed x140, local copies, waits for them, and re-layouts  135 us
    unnamed x17, waiting for transfers between devices  132 us
    reduce_scatter x1, waiting for transfers between devices, on_device(): lax.psum_scatter(jnp.dot(block, output_w, preferred_element_type=jnp.floa...  85.8 us
    scatter-add x1, other arithmetic, on_device(): partial_sum = jnp.zeros((normed_two_all.shape[0], D), jnp.float32).at[ind...  74.8 us
    scatter-add x1, other arithmetic, on_device(): partial_grad = jnp.zeros((row_count, D), jnp.float32).at[index.reshape(-1...  74.8 us
  transfers between devices with their start and end apart: 16, of which 11 were waited for; matrix products, arithmetic and copies ran while one was open for 23% of the time, Pallas kernels for 0%

commit v1 on v0

v1 whole, which is shorter than its diff:
```python
import functools
import math

import jax
import jax.numpy as jnp
import numpy as np
from jax import lax
from jax.experimental import pallas as pl
from jax.experimental.pallas import tpu as pltpu
from jax.sharding import PartitionSpec as P

D = 1024
HEADS = 16
KV = 8
HD = 64
FFE = 512
SEQ_LEN = 512
STEP = 10
PIECES = 2
QBLK = 256

NORM_EPS = 1e-05
ROPE_BASE = 10000.0
BETA_ONE = 0.9
BETA_TWO = 0.95
ADAM_EPS = 1e-08
LEARN_RATE = 0.1
WEIGHT_DECAY = 0.1
MASK_FILL = -1e30
SCALE = 1.0 / math.sqrt(HD)

bf16 = jnp.bfloat16
f32 = jnp.float32
ANY = pl.BlockSpec(memory_space=pl.ANY)
SMEM = pl.BlockSpec(memory_space=pltpu.SMEM)
VMEM = pl.BlockSpec(memory_space=pltpu.VMEM)


def dot(a, b):
    return jnp.dot(a, b, preferred_element_type=f32)


def dot_t(a, b):
    return lax.dot_general(a, b, (((1,), (1,)), ((), ())), preferred_element_type=f32)


def t_dot(a, b):
    return lax.dot_general(a, b, (((0,), (0,)), ((), ())), preferred_element_type=f32)


def rope_tables():
    half = HD // 2
    position = np.arange(SEQ_LEN, dtype=np.float32)
    exponent = np.arange(half, dtype=np.float32) * np.float32(-2.0 / HD)
    frequency = np.exp(exponent * np.float32(math.log(ROPE_BASE))).astype(np.float32)
    angle = (position[:, None] * frequency[None, :]).astype(np.float32)
    cosine = np.cos(angle).astype(np.float32)
    sine = np.sin(angle).astype(np.float32)
    return np.tile(cosine, (1, 4)), np.concatenate([-sine, sine, -sine, sine], axis=1)


def adam_update(master, first_moment, second_moment, gradient, decay_rate):
    first_new = BETA_ONE * first_moment + (1.0 - BETA_ONE) * gradient
    second_new = BETA_TWO * second_moment + (1.0 - BETA_TWO) * gradient * gradient
    first_fixed = first_new / (1.0 - BETA_ONE**STEP)
    second_fixed = second_new / (1.0 - BETA_TWO**STEP)
    master_new = master - LEARN_RATE * (
        first_fixed / (jnp.sqrt(second_fixed) + ADAM_EPS) + decay_rate * master
    )
    return (master_new, first_new, second_new)


def adam_change(first_moment, second_moment, gradient):
    first_new = BETA_ONE * first_moment + (1.0 - BETA_ONE) * gradient
    second_new = BETA_TWO * second_moment + (1.0 - BETA_TWO) * gradient * gradient
    first_fixed = first_new / (1.0 - BETA_ONE**STEP)
    second_fixed = second_new / (1.0 - BETA_TWO**STEP)
    change = -LEARN_RATE * (first_fixed / (jnp.sqrt(second_fixed) + ADAM_EPS))
    return (change, first_new, second_new)


def rms_scale(values):
    return lax.rsqrt(jnp.mean(values * values, axis=-1, keepdims=True) + NORM_EPS)


def weight_copies(place_ref, pieces, w_ref, sems, nz, nt, outward):
    rows, cols = D // (2 * nz), D // nt
    z, core, t = place_ref[0], place_ref[1], place_ref[2]
    copies = []
    for c in range(2):
        for k in range(nt):
            for j in range(nz):
                row = pl.multiple_of(((z ^ j) * 2 + (core ^ c)) * rows, rows)
                col = pl.multiple_of((t ^ k) * cols, cols)
                whole = w_ref.at[:, pl.ds(row, rows), pl.ds(col, cols)]
                part = pieces[c * nt + k].at[j]
                sem = sems.at[(c * nt + k) * nz + j]
                src, dst = (whole, part) if outward else (part, whole)
                copies.append(pltpu.make_async_copy(src, dst, sem))
    return copies


def rotate(x, cosine, sine, first_half):
    width = x.shape[-1]
    swapped = jnp.where(
        first_half, pltpu.roll(x, width - HD // 2, 1), pltpu.roll(x, HD // 2, 1)
    )
    return x * cosine + swapped * sine


def attend_forward_kernel(nz, nt, place_ref, tokens_ref, gains_ref, cos_ref, sin_ref, *rest):
    pieces = rest[: 2 * nt]
    s1_ref, n2_ref, q_ref, kv_ref, o_ref, lse_ref = rest[2 * nt : 2 * nt + 6]
    w_ref, qlin_ref, kvlin_ref, sems = rest[2 * nt + 6 :]
    length = tokens_ref.shape[0]
    copies = weight_copies(place_ref, pieces, w_ref, sems, nz, nt, False)
    for copy in copies:
        copy.start()
    stream = tokens_ref[...].astype(f32)
    n1 = (stream * rms_scale(stream) * gains_ref[0:1, :]).astype(bf16)
    for copy in copies:
        copy.wait()
    qlin_ref[...] = dot(n1, w_ref[0])
    kvlin_ref[...] = dot(n1, w_ref[1])
    lse_ref[...] = jnp.zeros_like(lse_ref)

    def group(g, carry):
        part = pl.ds(pl.multiple_of(g * 128, 128), 128)
        lane = lax.broadcasted_iota(jnp.int32, (length, 128), 1)
        low = lane < HD
        first_half = (lane & (HD // 2)) == 0
        cosine, sine = cos_ref[...], sin_ref[...]
        q = rotate(qlin_ref[:, part], cosine, sine, first_half)
        kv = kvlin_ref[:, part]
        kv = jnp.where(low, rotate(kv, cosine, sine, first_half), kv)
        q_ref[:, part] = q.astype(bf16)
        kv_ref[:, part] = kv.astype(bf16)
        vk = pltpu.roll(kv, HD, 1).astype(bf16)
        kv = kv.astype(bf16)
        heads = (
            (jnp.where(low, q, 0.0).astype(bf16), kv, vk),
            (jnp.where(low, 0.0, q).astype(bf16), vk, kv),
        )
        for b in range(length // QBLK):
            rows = slice(b * QBLK, (b + 1) * QBLK)
            keys = (b + 1) * QBLK
            row = lax.broadcasted_iota(jnp.int32, (QBLK, keys), 0) + b * QBLK
            column = lax.broadcasted_iota(jnp.int32, (QBLK, keys), 1)
            seen = column <= row
            outs = []
            lses = lse_ref[rows, :]
            lane_b = lax.broadcasted_iota(jnp.int32, (QBLK, 128), 1)
            for h, (qh, key_side, value_side) in enumerate(heads):
                scores = dot_t(qh[rows], key_side[:keys]) * SCALE
                scores = jnp.where(seen, scores, MASK_FILL)
                top = jnp.max(scores, axis=-1, keepdims=True)
                e = jnp.exp(scores - top)
                total = jnp.sum(e, axis=-1, keepdims=True)
                p = (e * (1.0 / total)).astype(bf16)
                outs.append(dot(p, value_side[:keys]))
                lses = jnp.where(lane_b == 2 * g + h, top + jnp.log(total), lses)
            lse_ref[rows, :] = lses
            o_ref[rows, part] = jnp.where(lane_b < HD, outs[0], outs[1]).astype(bf16)
        return carry

    lax.fori_loop(0, D // 128, group, 0)
    s1 = tokens_ref[...].astype(f32) + dot_t(o_ref[...], w_ref[2])
    s1_ref[...] = s1
    n2_ref[...] = (s1 * rms_scale(s1) * gains_ref[1:2, :]).astype(bf16)


def attend_forward(mesh_sizes, place, tokens, gains, pieces):
    nz, nt = mesh_sizes
    length = tokens.shape[0]
    cosine, sine = rope_tables()
    return pl.pallas_call(
        functools.partial(attend_forward_kernel, nz, nt),
        out_shape=(
            jax.ShapeDtypeStruct((length, D), f32),
            jax.ShapeDtypeStruct((length, D), bf16),
            jax.ShapeDtypeStruct((length, D), bf16),
            jax.ShapeDtypeStruct((length, D), bf16),
            jax.ShapeDtypeStruct((length, D), bf16),
            jax.ShapeDtypeStruct((length, 128), f32),
        ),
        in_specs=[SMEM] + [VMEM] * 4 + [ANY] * len(pieces),
        out_specs=[VMEM] * 6,
        scratch_shapes=[
            pltpu.VMEM((3, D, D), bf16),
            pltpu.VMEM((length, D), f32),
            pltpu.VMEM((length, D), f32),
            pltpu.SemaphoreType.DMA((2 * nt * nz,)),
        ],
        compiler_params=pltpu.CompilerParams(vmem_limit_bytes=48 * 2**20),
        cost_estimate=pl.CostEstimate(flops=12 * 10**9, bytes_accessed=16 * 2**20, transcendentals=4 * 2**20),
        name="attend_forward",
    )(place, tokens, gains, jnp.asarray(cosine), jnp.asarray(sine), *pieces)


def attend_backward_kernel(
    nz, nt, place_ref, tokens_ref, da_ref, gains_ref, cos_ref, sin_ref, q_ref, kv_ref, o_ref, lse_ref, *rest
):
    pieces = rest[: 2 * nt]
    dn1_ref = rest[2 * nt]
    grads = rest[2 * nt + 1 : 4 * nt + 1]
    w_ref, gw_ref, do_ref, dq_ref, dkv_ref, lse_t_ref, sems = rest[4 * nt + 1 :]
    length = tokens_ref.shape[0]
    copies = weight_copies(place_ref, pieces, w_ref, sems, nz, nt, False)
    for copy in copies:
        copy.start()
    da = da_ref[...]
    gw_ref[2] = t_dot(da, o_ref[...]).astype(bf16)
    lse_t_ref[...] = lse_ref[...].T
    for copy in copies:
        copy.wait()
    do_ref[...] = dot(da, w_ref[2]).astype(bf16)

    def group(g, carry):
        part = pl.ds(pl.multiple_of(g * 128, 128), 128)
        lane = lax.broadcasted_iota(jnp.int32, (length, 128), 1)
        low = lane < HD
        first_half = (lane & (HD // 2)) == 0
        cosine, sine = cos_ref[...], sin_ref[...]
        q = q_ref[:, part].astype(f32)
        kv = kv_ref[:, part].astype(f32)
        do = do_ref[:, part].astype(f32)
        vk = pltpu.roll(kv, HD, 1).astype(bf16)
        kv = kv.astype(bf16)
        q_low = jnp.where(low, q, 0.0).astype(bf16)
        q_high = jnp.where(low, 0.0, q).astype(bf16)
        q_moved = jnp.where(low, pltpu.roll(q, HD, 1), 0.0).astype(bf16)
        do_low = jnp.where(low, do, 0.0).astype(bf16)
        do_high = jnp.where(low, 0.0, do).astype(bf16)
        do_moved = jnp.where(low, 0.0, pltpu.roll(do, HD, 1)).astype(bf16)
        heads = (
            (q_low, kv, vk, do_low, q_low, do_moved),
            (q_high, vk, kv, do_high, q_moved, do_high),
        )
        blocks = length // QBLK
        dkv = [jnp.zeros((QBLK, 128), f32) for _ in range(blocks)]
        dqs = []
        for b in range(blocks):
            rows = slice(b * QBLK, (b + 1) * QBLK)
            keys = (b + 1) * QBLK
            row = lax.broadcasted_iota(jnp.int32, (keys, QBLK), 0)
            column = lax.broadcasted_iota(jnp.int32, (keys, QBLK), 1) + b * QBLK
            seen = row <= column
            both = []
            for h, (qh, key_side, value_side, doh, q_for_k, do_for_v) in enumerate(heads):
                scores = dot_t(key_side[:keys], qh[rows]) * SCALE
                scores = jnp.where(seen, scores, MASK_FILL)
                e = jnp.exp(scores - lse_t_ref[pl.ds(2 * g + h, 1), rows])
                dp = dot_t(value_side[:keys], doh[rows])
                mean = jnp.sum(e * dp, axis=0, keepdims=True)
                dz = (e * (dp - mean)).astype(bf16)
                both.append(t_dot(dz, key_side[:keys]))
                add = dot(dz, q_for_k[rows]) + dot(e.astype(bf16), do_for_v[rows])
                for i in range(b + 1):
                    dkv[i] = dkv[i] + add[i * QBLK : (i + 1) * QBLK]
            lane_b = lax.broadcasted_iota(jnp.int32, (QBLK, 128), 1)
            dqs.append(jnp.where(lane_b < HD, both[0], both[1]))
        dq = jnp.concatenate(dqs, axis=0) * SCALE
        dkv_all = jnp.concatenate(dkv, axis=0)
        dq_ref[:, part] = rotate(dq, cosine, -sine, first_half).astype(bf16)
        dk = rotate(dkv_all * SCALE, cosine, -sine, first_half)
        dkv_ref[:, part] = jnp.where(low, dk, dkv_all).astype(bf16)
        return carry

    lax.fori_loop(0, D // 128, group, 0)
    stream = tokens_ref[...].astype(f32)
    n1 = (stream * rms_scale(stream) * gains_ref[0:1, :]).astype(bf16)
    gw_ref[0] = t_dot(n1, dq_ref[...]).astype(bf16)
    gw_ref[1] = t_dot(n1, dkv_ref[...]).astype(bf16)
    outward = weight_copies(place_ref, grads, gw_ref, sems, nz, nt, True)
    for copy in outward:
        copy.start()
    dn1_ref[...] = dot_t(dq_ref[...], w_ref[0]) + dot_t(dkv_ref[...], w_ref[1])
    for copy in outward:
        copy.wait()


def attend_backward(mesh_sizes, place, tokens, da, gains, q, kv, o, lse, pieces):
    nz, nt = mesh_sizes
    length = tokens.shape[0]
    cosine, sine = rope_tables()
    rows, cols = D // (2 * nz), D // nt
    part = jax.ShapeDtypeStruct((nz, 3, rows, cols), bf16)
    out = pl.pallas_call(
        functools.partial(attend_backward_kernel, nz, nt),
        out_shape=(jax.ShapeDtypeStruct((length, D), f32),) + (part,) * (2 * nt),
        in_specs=[SMEM] + [VMEM] * 9 + [ANY] * len(pieces),
        out_specs=[VMEM] + [ANY] * (2 * nt),
        scratch_shapes=[
            pltpu.VMEM((3, D, D), bf16),
            pltpu.VMEM((3, D, D), bf16),
            pltpu.VMEM((length, D), bf16),
            pltpu.VMEM((length, D), bf16),
            pltpu.VMEM((length, D), bf16),
            pltpu.VMEM((128, length), f32),
            pltpu.SemaphoreType.DMA((2 * nt * nz,)),
        ],
        compiler_params=pltpu.CompilerParams(vmem_limit_bytes=52 * 2**20),
        cost_estimate=pl.CostEstimate(flops=20 * 10**9, bytes_accessed=24 * 2**20, transcendentals=4 * 2**20),
        name="attend_backward",
    )(place, tokens, da, gains, jnp.asarray(cosine), jnp.asarray(sine), q, kv, o, lse, *pieces)
    return out[0], out[1:]


def experts_kernel(first, last, count, n2_parts, dm_parts, *rest):
    tiles = count
    n2_parts, rest = rest[:tiles], rest[tiles:]
    dm_parts, rest = rest[:tiles], rest[tiles:]
    c_ref, win_ref, wdown_ref = rest[:3]
    rest = rest[3:]
    if not first:
        m_before, d_before = rest[:2]
        rest = rest[2:]
    m_ref, d_ref, gw_ref = rest[:3]
    n2_buf, dm_buf, n2_t, dm_t, m_acc, d_acc, gin, gdown, sems = rest[3:]
    i, e = pl.program_id(0), pl.program_id(1)
    slot = lax.rem(i, 2)
    experts = win_ref.shape[1]

    def start(tile):
        for j in range(tiles):

            @pl.when(tile == j)
            def _():
                pltpu.make_async_copy(n2_parts[j], n2_buf.at[j % 2], sems.at[0, j % 2]).start()
                pltpu.make_async_copy(dm_parts[j], dm_buf.at[j % 2], sems.at[1, j % 2]).start()

    @pl.when(e == 0)
    def _():
        @pl.when(i == 0)
        def _():
            start(0)

        for s in range(2):

            @pl.when(slot == s)
            def _():
                pltpu.make_async_copy(n2_parts[s], n2_buf.at[s], sems.at[0, s]).wait()
                pltpu.make_async_copy(dm_parts[s], dm_buf.at[s], sems.at[1, s]).wait()

        start(i + 1)
        n2_t[...] = n2_buf[slot].T
        dm_t[...] = dm_buf[slot].T
        if first:
            m_acc[...] = jnp.zeros_like(m_acc)
            d_acc[...] = jnp.zeros_like(d_acc)
        else:
            m_acc[...] = m_before[...]
            d_acc[...] = d_before[...]

    @pl.when(i == 0)
    def _():
        gin[e] = jnp.zeros(gin.shape[1:], f32)
        gdown[e] = jnp.zeros(gdown.shape[1:], f32)

    win = win_ref[:, e].reshape(D, D)
    wdown = wdown_ref[:, e].reshape(FFE, D)
    lane = lax.broadcasted_iota(jnp.int32, c_ref.shape, 1)
    c = jnp.sum(jnp.where(lane == e, c_ref[...], 0.0), axis=1, keepdims=True)
    hidden = dot(n2_buf[slot], win)
    gate, up = hidden[:, :FFE], hidden[:, FFE:]
    sigma = jax.nn.sigmoid(gate)
    silu = gate * sigma
    active = (c * silu * up).astype(bf16)
    m_acc[...] += dot(active, wdown)
    gdown[e] += dot(dm_t[...], active)
    da = c * dot_t(dm_buf[slot], wdown)
    dgate = da * up * (sigma + silu * (1.0 - sigma))
    dup = da * silu
    dh = jnp.concatenate([dgate.astype(bf16), dup.astype(bf16)], axis=1)
    gin[e] += dot(n2_t[...], dh)
    d_acc[...] += dot_t(dh, win)

    @pl.when(e == experts - 1)
    def _():
        m_ref[...] = m_acc[...].astype(m_ref.dtype)
        d_ref[...] = d_acc[...].astype(d_ref.dtype)

    @pl.when(i == tiles - 1)
    def _():
        nz, _, cores, rows, _ = gw_ref.shape
        rin = D // (nz * cores)
        gw_ref[:, 0, :, :rin, :] = gin[e].astype(bf16).reshape(nz, cores, rin, D)
        gw_ref[:, 0, :, rin:, :] = gdown[e].T.astype(bf16).reshape(nz, cores, rows - rin, D)


def experts_step(n2_parts, dm_parts, c, weights, before, last):
    tiles, rows = len(n2_parts), n2_parts[0].shape[0]
    nz, experts, cores, wrows, _ = weights.shape
    rin, rdown = D // (nz * cores), FFE // (nz * cores)
    first = before is None
    out_type = bf16 if last else f32
    tile_spec = pl.BlockSpec((rows, D), lambda i, e: (i, 0))
    once = pl.Buffered(1)
    in_specs = (
        [ANY] * (2 * tiles)
        + [
            pl.BlockSpec((rows, experts), lambda i, e: (i, 0)),
            pl.BlockSpec((nz, experts, cores, rin, D), lambda i, e: (0, 0, 0, 0, 0), pipeline_mode=once),
            pl.BlockSpec(
                (nz, experts, cores, rdown, D), lambda i, e: (0, 0, 0, rin // rdown, 0), pipeline_mode=once
            ),
        ]
        + ([] if first else [tile_spec, tile_spec])
    )
    out_specs = (
        tile_spec,
        tile_spec,
        pl.BlockSpec(
            (nz, 1, cores, wrows, D), lambda i, e: (0, jnp.where(i == tiles - 1, e, 0), 0, 0, 0)
        ),
    )
    return pl.pallas_call(
        functools.partial(experts_kernel, first, last, tiles, None, None),
        grid=(tiles, experts),
        out_shape=(
            jax.ShapeDtypeStruct((tiles * rows, D), out_type),
            jax.ShapeDtypeStruct((tiles * rows, D), out_type),
            jax.ShapeDtypeStruct(weights.shape, bf16),
        ),
        in_specs=in_specs,
        out_specs=out_specs,
        scratch_shapes=[
            pltpu.VMEM((2, rows, D), bf16),
            pltpu.VMEM((2, rows, D), bf16),
            pltpu.VMEM((D, rows), bf16),
            pltpu.VMEM((D, rows), bf16),
            pltpu.VMEM((rows, D), f32),
            pltpu.VMEM((rows, D), f32),
            pltpu.VMEM((experts, D, D), f32),
            pltpu.VMEM((experts, D, FFE), f32),
            pltpu.SemaphoreType.DMA((2, 2)),
        ],
        compiler_params=pltpu.CompilerParams(
            vmem_limit_bytes=60 * 2**20, dimension_semantics=("arbitrary", "arbitrary")
        ),
        cost_estimate=pl.CostEstimate(
            flops=tiles * rows * experts * 12 * D * FFE * 3 // 2,
            bytes_accessed=64 * 2**20,
            transcendentals=tiles * rows * experts * FFE,
        ),
        name="experts",
    )(*n2_parts, *dm_parts, c, weights, weights, *([] if first else before))


def on_device(
    ndp,
    nt,
    tokens,
    cotangent,
    routes,
    gate_weights,
    norm_gains,
    norm_gains_first,
    norm_gains_second,
    query_weight,
    query_first,
    query_second,
    keyval_weight,
    keyval_first,
    keyval_second,
    output_weight,
    output_first,
    output_second,
    expert_in,
    expert_in_first,
    expert_in_second,
    expert_down,
    expert_down_first,
    expert_down_second,
):
    nz = ndp // 2
    place_dp = lax.axis_index("dp")
    t = lax.axis_index("tensor")
    z, core = place_dp // 2, place_dp % 2
    place = jnp.stack([z, core, t]).astype(jnp.int32)
    rows = tokens.shape[0]
    sharers = max(1, SEQ_LEN // rows)

    def swap_core(x):
        return lax.ppermute(x, "dp", [(i, i ^ 1) for i in range(ndp)])

    def swap_z(x, j):
        return lax.ppermute(x, "dp", [(i, i ^ (2 * j)) for i in range(ndp)])

    def swap_t(x, k):
        return lax.ppermute(x, "tensor", [(i, i ^ k) for i in range(nt)])

    def spread_t(x):
        return [x] + [swap_t(x, k) for k in range(1, nt)]

    def spread_z(x):
        return [x] + [swap_z(x, j) for j in range(1, nz)]

    own = jnp.stack(
        [query_weight[0].astype(bf16), keyval_weight[0].astype(bf16), output_weight[0].T.astype(bf16)]
    )
    column = jnp.stack(spread_z(own))
    pieces = spread_t(column)
    pieces = pieces + [swap_core(piece) for piece in pieces]
    gains_z = jnp.stack(spread_z(norm_gains[0]))
    gains_t = jnp.stack(spread_t(gains_z))
    gains_all = jnp.stack([gains_t, swap_core(gains_t)])
    ids = jnp.arange(2 * nz * nt, dtype=jnp.int32)
    spot = (((ids // nt) % 2 ^ core) * nt + (ids % nt ^ t)) * nz + (ids // nt // 2 ^ z)
    gains = jnp.take(gains_all.reshape(2 * nz * nt, 2, -1), spot, axis=0)
    gains = gains.transpose(1, 0, 2).reshape(2, D)

    low = jnp.concatenate([expert_in[0].astype(bf16), expert_down[0].astype(bf16)], axis=1)
    half = low.shape[0] // 2
    mine = lax.dynamic_slice_in_dim(low, core * half, half, 0)
    theirs = lax.dynamic_slice_in_dim(low, (1 - core) * half, half, 0)
    got = swap_core(theirs)
    is_zero = core == 0
    shard = jnp.stack([jnp.where(is_zero, mine, got), jnp.where(is_zero, got, mine)], axis=1)
    groups = [[2 * i + c for i in range(nz)] for c in range(2)]
    per = half // PIECES
    weights = [
        lax.all_gather(shard[i * per : (i + 1) * per], "dp", axis=0, tiled=False, axis_index_groups=groups)
        for i in range(PIECES)
    ]

    dm_own = spread_t(cotangent)
    dm_parts = dm_own + [swap_core(part) for part in dm_own]

    ids = t * 2 * half + jnp.arange(2 * half, dtype=jnp.int32)
    chosen = routes[0].T[None, :, :] == ids[:, None, None]
    c_all = jnp.sum(jnp.where(chosen, gate_weights[0].T[None, :, :], 0.0), axis=1)
    c_mine = lax.dynamic_slice_in_dim(c_all, core * half, half, 0)
    c_got = swap_core(lax.dynamic_slice_in_dim(c_all, (1 - core) * half, half, 0))
    c_both = jnp.stack([c_mine, c_got]).reshape(2, half, nt, rows)
    order = jnp.arange(nt, dtype=jnp.int32) ^ t
    c_both = jnp.take(c_both, order, axis=2)
    c_rows = c_both.transpose(0, 2, 3, 1).reshape(2 * nt * rows, half)

    sequence = tokens
    if sharers > 1:
        seq_groups = [list(range(i, i + sharers)) for i in range(0, nt, sharers)]
        sequence = lax.all_gather(tokens, "tensor", axis=0, tiled=True, axis_index_groups=seq_groups)
    first_row = (t % sharers) * rows
    s1, n2, q, kv, o, lse = attend_forward((nz, nt), place, sequence, gains, pieces)
    if sharers > 1:
        s1 = lax.dynamic_slice_in_dim(s1, first_row, rows, 0)
        n2 = lax.dynamic_slice_in_dim(n2, first_row, rows, 0)

    n2_own = spread_t(n2)
    n2_parts = n2_own + [swap_core(part) for part in n2_own]
    before = None
    expert_grads = []
    for i in range(PIECES):
        m_sum, d_sum, gw = experts_step(
            n2_parts,
            dm_parts,
            c_rows[:, i * per : (i + 1) * per],
            weights[i],
            before,
            i == PIECES - 1,
        )
        before = (m_sum, d_sum)
        expert_grads.append(
            lax.psum_scatter(gw, "dp", scatter_dimension=0, tiled=False, axis_index_groups=groups)
        )

    def collect(partial_sums):
        block = nt * rows
        both = partial_sums[:block] + swap_core(partial_sums[block:])
        total = both[:rows].astype(f32)
        for k in range(1, nt):
            total = total + swap_t(both[k * rows : (k + 1) * rows], k).astype(f32)
        return total

    dn2 = collect(d_sum)
    block_out = s1 + collect(m_sum)

    grad = cotangent.astype(f32)
    inverse = rms_scale(s1)
    unit = s1 * inverse
    gain_two = jnp.sum(dn2 * unit, axis=0)
    scaled = dn2 * gains[1]
    gs1 = grad + inverse * (scaled - unit * jnp.mean(scaled * unit, axis=-1, keepdims=True))

    da = gs1.astype(bf16)
    if sharers > 1:
        da = lax.all_gather(da, "tensor", axis=0, tiled=True, axis_index_groups=seq_groups)
    dn1, gw_parts = attend_backward((nz, nt), place, sequence, da, gains, q, kv, o, lse, pieces)
    if sharers > 1:
        dn1 = lax.dynamic_slice_in_dim(dn1, first_row, rows, 0)

    stream = tokens.astype(f32)
    inverse = rms_scale(stream)
    unit = stream * inverse
    gain_one = jnp.sum(dn1 * unit, axis=0)
    scaled = dn1 * gains[0]
    input_grad = gs1 + inverse * (scaled - unit * jnp.mean(scaled * unit, axis=-1, keepdims=True))

    by_t = [gw_parts[k] + swap_core(gw_parts[nt + k]) for k in range(nt)]
    by_z = by_t[0].astype(f32)
    for k in range(1, nt):
        by_z = by_z + swap_t(by_t[k], k).astype(f32)
    by_z = by_z.astype(bf16)
    small = by_z[0].astype(f32)
    for j in range(1, nz):
        small = small + swap_z(by_z[j], j).astype(f32)
    small = small * (1.0 / sharers)

    gg = jnp.stack([gain_one, gain_two])
    gg = gg + swap_core(gg)
    gg = sum(spread_t(gg)[1:], gg)
    gg = sum(spread_z(gg)[1:], gg)
    width = norm_gains.shape[2]
    gg = lax.dynamic_slice_in_dim(gg, (place_dp * nt + t) * width, width, 1)[None]

    by_core = [[], []]
    for got in expert_grads:
        mine = lax.dynamic_index_in_dim(got, core, 1, keepdims=False)
        recv = swap_core(lax.dynamic_index_in_dim(got, 1 - core, 1, keepdims=False))
        by_core[0].append(jnp.where(is_zero, mine, recv))
        by_core[1].append(jnp.where(is_zero, recv, mine))
    expert_grad = jnp.concatenate(by_core[0] + by_core[1], axis=0).astype(f32)[None]
    rin = expert_in.shape[2]

    gains_new = adam_change(norm_gains_first, norm_gains_second, gg)
    query_new = adam_update(query_weight, query_first, query_second, small[0:1], WEIGHT_DECAY)
    keyval_new = adam_update(keyval_weight, keyval_first, keyval_second, small[1:2], WEIGHT_DECAY)
    output_new = adam_update(output_weight, output_first, output_second, small[2].T[None], WEIGHT_DECAY)
    in_new = adam_update(
        expert_in, expert_in_first, expert_in_second, expert_grad[:, :, :rin], WEIGHT_DECAY
    )
    down_new = adam_update(
        expert_down, expert_down_first, expert_down_second, expert_grad[:, :, rin:], WEIGHT_DECAY
    )
    return (block_out, input_grad) + gains_new + query_new + keyval_new + output_new + in_new + down_new


def solution(mesh):
    rows = P(("dp", "tensor"), None)
    by_rows = P(None, "dp", None)
    gains = P(None, None, ("dp", "tensor"))
    proj = P(None, "dp", "tensor")
    out_proj = P(None, "tensor", "dp")
    expert = P(None, "tensor", "dp", None)
    params = (gains,) * 3 + (proj,) * 6 + (out_proj,) * 3 + (expert,) * 6
    return jax.shard_map(
        functools.partial(on_device, mesh.shape["dp"], mesh.shape["tensor"]),
        mesh=mesh,
        in_specs=(rows, rows, by_rows, by_rows) + params,
        out_specs=(rows, rows) + params,
        check_vma=False,
    )
```

time: 1900 us -> 705 us (0.37)
  waiting for transfers between devices: 1040 us -> 238 us
  Pallas kernels: 0 us -> 277 us
  matrix products: 246 us -> 0 us
  local copies, waits for them, and re-layouts: 249 us -> 45.3 us
  other arithmetic: 222 us -> 56.4 us
  blocking collectives: 118 us -> 0 us
  starting transfers between devices: 1.3 us -> 69.1 us
    reduce_scatter x9 -> x2, waiting for transfers between devices: 762 us -> 0.02 us  [on_device(): lax.psum_scatter(gw, 'dp', scatter_dimension=0, tiled=False, axis_index_g...]
    pallas_call x0 -> x4, Pallas kernels: none -> 277 us  [the longest x2 218 us: experts_step(): pl.pallas_call(functools.partial(experts_kernel, first, last, tiles, None...]
    dot_general x21 -> x0, matrix products: 246 us -> none  [the longest x1 31.7 us: on_device(): jnp.einsum('ecd,efd->ecf', slot_grad, down_w, preferred_element_type=jnp....]
    ppermute x0 -> x60, waiting for transfers between devices: none -> 238 us  [the longest x24 195 us: swap_t(): return lax.ppermute(x, 'tensor', [(i, i ^ k) for i in range(nt)])]
    scatter-add x2 -> x0, other arithmetic: 150 us -> none  [the longest x1 74.8 us: on_device(): partial_sum = jnp.zeros((normed_two_all.shape[0], D), jnp.float32).at[ind...]
    all_gather x6 -> x2, waiting for transfers between devices: 148 us -> 0.02 us  [on_device(): lax.all_gather(shard[i * per:(i + 1) * per], 'dp', axis=0, tiled=False, a...]
    unnamed x17 -> x4, waiting for transfers between devices: 132 us -> 0.07 us
    unnamed x140 -> x104, local copies, waits for them, and re-layouts: 135 us -> 14.1 us
  transfers between devices with their start and end apart: 16 -> 64, of which waited for: 11 -> 22; matrix products, arithmetic and copies ran while one was open for 23% -> 10% of each run, Pallas kernels for 0% -> 40%
where the time goes in v1:
time: 705 us; the launch traced here: 700 us
  Pallas kernels  277 us (39%)
  waiting for transfers between devices  238 us (34%)
  starting transfers between devices  69.1 us (10%)
  other arithmetic  56.4 us (8%)
  local copies, waits for them, and re-layouts  45.3 us (6%)
  between operations  14.9 us (2%)
    pallas_call x2, Pallas kernels, experts_step(): pl.pallas_call(functools.partial(experts_kernel, first, last, tiles, None...  218 us
    ppermute x24, waiting for transfers between devices, swap_t(): return lax.ppermute(x, 'tensor', [(i, i ^ k) for i in range(nt)])  195 us
    ppermute x12, starting transfers between devices, swap_z(): return lax.ppermute(x, 'dp', [(i, i ^ 2 * j) for i in range(ndp)])  35.5 us
    ppermute x12, waiting for transfers between devices, swap_z(): return lax.ppermute(x, 'dp', [(i, i ^ 2 * j) for i in range(ndp)])  35.4 us
    pallas_call x1, Pallas kernels, attend_backward(): pl.pallas_call(functools.partial(attend_backward_kernel, nz, nt), out_sha...  33.7 us
    ppermute x24, starting transfers between devices, swap_t(): return lax.ppermute(x, 'tensor', [(i, i ^ k) for i in range(nt)])  28.2 us
    pallas_call x1, Pallas kernels, attend_forward(): pl.pallas_call(functools.partial(attend_forward_kernel, nz, nt), out_shap...  25.5 us
    unnamed x104, local copies, waits for them, and re-layouts  14.1 us
  transfers between devices with their start and end apart: 64, of which 22 were waited for; matrix products, arithmetic and copies ran while one was open for 10% of the time, Pallas kernels for 40%

profile of v1, /device:TPU:0, one launch (start us, length us, event | category | flops | bytes accessed | tf_op | source)
XLA Modules:
  0.0 700.5 jit_solution(15781794098284407346)
XLA Ops:
  7.3 2.7 convert_bitcast_fusion
  10.3 1.3 fusion.13
  12.0 3.4 collective-permute-done.32
  15.4 2.3 select_bitcast_fusion
  17.7 1.9 pad_maximum_fusion
  20.6 3.0 collective-permute-start.7
  23.6 2.6 collective-permute-start.8
  26.2 6.2 collective-permute-done.7
  32.4 13.6 %collective-permute-done.8 = bf16[3,128,256]{2,1,0:T(8,128)(2,1)S(1)} collective-permute-done((bf16[3,128,256]{2,1,0:T(8,128)(2,1)S(1)}, bf16[3,128,256]{2,1,0:T(8,128)(2,1)S(1)}, u32[]{:S(2)}, u32[]{:S(2)}) %collective-permute-start.8) | collective-permute-done | bytes 196640 | tf_op jit(solution)/shard_map/ppermute | solution.py:488
  46.1 1.6 collective-permute-start.10
  47.7 16.6 %collective-permute-start = (f32[2,32]{1,0:T(2,128)S(1)}, f32[2,32]{1,0:T(2,128)S(1)}, u32[]{:S(2)}, u32[]{:S(2)}) collective-permute-start(f32[2,32]{1,0:T(2,128)S(1)} %bitcast.144), channel_id=1, source_target_pairs={{0,8},{4,12},{8,0},{12,4},{16,24},{20,28},{24,16},{28,20},{1,9},{5... | collective-permute-start | bytes 776 | tf_op jit(solution)/shard_map/ppermute | solution.py:488
  64.2 1.9 collective-permute-start.1
  66.2 1.5 collective-permute-start.2
  67.6 1.6 collective-permute-done.1
  69.2 2.4 collective-permute-done.2
  71.6 1.6 collective-permute-start.5
  73.2 1.5 collective-permute-start.3
  75.2 1.5 collective-permute-start.12
  79.1 26.6 %collective-permute-done.4 = f32[4,2,32]{2,1,0:T(2,128)S(1)} collective-permute-done((f32[4,2,32]{2,1,0:T(2,128)S(1)}, f32[4,2,32]{2,1,0:T(2,128)S(1)}, u32[]{:S(2)}, u32[]{:S(2)}) %collective-permute-start.4) | collective-permute-done | bytes 1056 | tf_op jit(solution)/shard_map/ppermute | solution.py:491
  116.1 17.9 %collective-permute-done.24.rest_9_ = bf16[512,1024]{1,0:T(8,128)(2,1)} collective-permute-done((bf16[512,1024]{1,0:T(8,128)(2,1)}, bf16[512,1024]{1,0:T(8,128)(2,1)}, u32[]{:S(2)}, u32[]{:S(2)}) %collective-permute-start.24) | collective-permute-done | bytes 1048608 | tf_op jit(solution)/shard_map/ppermute | solution.py:491
  136.8 25.5 %attend_forward.1 = (f32[512,1024]{1,0:T(8,128)}, bf16[512,1024]{1,0:T(8,128)(2,1)}, bf16[512,1024]{1,0:T(8,128)(2,1)}, bf16[512,1024]{1,0:T(8,128)(2,1)}, bf16[...) custom-call(s32[3]{0:T(128)S(1)} %pad_add_fusion.place_ref, bf16[512,1024]{1,0:T(8,128)(2,1)} %tokens_ref.3, ...), custom_call_target="tpu_custom_call" | custom-call | flops 12000000000 | bytes 16777216 | tf_op jit(solution)/shard_map/attend_forward/pallas_call | solution.py:176
  164.3 1.5 collective-permute-start.18
  169.2 20.1 %collective-permute-done.17.rest_1_ = bf16[512,1024]{1,0:T(8,128)(2,1)} collective-permute-done((bf16[512,1024]{1,0:T(8,128)(2,1)}, bf16[512,1024]{1,0:T(8,128)(2,1)}, u32[]{:S(2)}, u32[]{:S(2)}) %collective-permute-start.17) | collective-permute-done | bytes 1048608 | tf_op jit(solution)/shard_map/ppermute | solution.py:491
  189.4 22.5 %collective-permute-done.18.rest_2_ = bf16[512,1024]{1,0:T(8,128)(2,1)} collective-permute-done((bf16[512,1024]{1,0:T(8,128)(2,1)}, bf16[512,1024]{1,0:T(8,128)(2,1)}, u32[]{:S(2)}, u32[]{:S(2)}) %collective-permute-start.18) | collective-permute-done | bytes 1048608 | tf_op jit(solution)/shard_map/ppermute | solution.py:491
  212.4 2.7 fusion.57
  215.1 6.5 copy.72
  221.6 108.3 %experts.2 = (f32[4096,1024]{1,0:T(8,128)}, f32[4096,1024]{1,0:T(8,128)}, bf16[4,2,2,192,1024]{4,3,2,1,0:T(8,128)(2,1)}) custom-call(bf16[512,1024]{1,0:T(8,128)(2,1)} %get-tuple-element.42.rest_0_, bf16[512,1024]{1,0:T(8,128)(2,1)} %collective-permute-done.17.rest_1_, bf16[512,1024]{1,0:T(8,128)(2,1)} %collective-permute-done.18.rest_2_, ...), custom_call_target="tpu_custom_call" | custom-call | flops 77309411328 | bytes 67108864 | tf_op jit(solution)/shard_map/experts/pallas_call | solution.py:417
  330.1 6.3 copy.71
  336.4 109.5 %experts.3 = (bf16[4096,1024]{1,0:T(8,128)(2,1)}, bf16[4096,1024]{1,0:T(8,128)(2,1)}, bf16[4,2,2,192,1024]{4,3,2,1,0:T(8,128)(2,1)}) custom-call(bf16[512,1024]{1,0:T(8,128)(2,1)} %get-tuple-element.42.rest_0_, bf16[512,1024]{1,0:T(8,128)(2,1)} %collective-permute-done.17.rest_1_, bf16[512,1024]{1,0:T(8,128)(2,1)} %collective-permute-done.18.rest_2_, ...), custom_call_target="tpu_custom_call" | custom-call | flops 77309411328 | bytes 67108864 | tf_op jit(solution)/shard_map/experts/pallas_call | solution.py:417
  445.9 4.6 slice.94
  450.6 4.7 slice.88
  456.3 1.8 collective-permute-done.37
  458.0 4.9 slice_add_fusion
  466.8 3.9 slice_add_fusion.1
  473.3 16.0 %collective-permute-done.38 = bf16[512,1024]{1,0:T(8,128)(2,1)S(1)} collective-permute-done((bf16[512,1024]{1,0:T(8,128)(2,1)S(1)}, bf16[512,1024]{1,0:T(8,128)(2,1)S(1)}, u32[]{:S(2)}, u32[]{:S(2)}) %collective-permute-start.38) | collective-permute-done | bytes 1048608 | tf_op jit(solution)/shard_map/ppermute | solution.py:491
  489.3 1.7 collective-permute-start.36
  491.2 21.6 %collective-permute-done.39 = bf16[512,1024]{1,0:T(8,128)(2,1)S(1)} collective-permute-done((bf16[512,1024]{1,0:T(8,128)(2,1)S(1)}, bf16[512,1024]{1,0:T(8,128)(2,1)S(1)}, u32[]{:S(2)}, u32[]{:S(2)}) %collective-permute-start.39) | collective-permute-done | bytes 1048608 | tf_op jit(solution)/shard_map/ppermute | solution.py:491
  514.0 20.3 %collective-permute-done.34 = bf16[512,1024]{1,0:T(8,128)(2,1)S(1)} collective-permute-done((bf16[512,1024]{1,0:T(8,128)(2,1)S(1)}, bf16[512,1024]{1,0:T(8,128)(2,1)S(1)}, u32[]{:S(2)}, u32[]{:S(2)}) %collective-permute-start.34) | collective-permute-done | bytes 1048608 | tf_op jit(solution)/shard_map/ppermute | solution.py:491
  534.3 21.1 %collective-permute-done.35 = bf16[512,1024]{1,0:T(8,128)(2,1)S(1)} collective-permute-done((bf16[512,1024]{1,0:T(8,128)(2,1)S(1)}, bf16[512,1024]{1,0:T(8,128)(2,1)S(1)}, u32[]{:S(2)}, u32[]{:S(2)}) %collective-permute-start.35) | collective-permute-done | bytes 1048608 | tf_op jit(solution)/shard_map/ppermute | solution.py:491
  555.4 1.7 collective-permute-done.36
  557.1 4.1 fusion.54
  561.2 33.7 %attend_backward.1 = (f32[512,1024]{1,0:T(8,128)}, bf16[4,3,128,256]{3,2,1,0:T(8,128)(2,1)S(1)}, bf16[4,3,128,256]{3,2,1,0:T(8,128)(2,1)}, bf16[4,3,128,256]{3,2...) custom-call(s32[3]{0:T(128)S(1)} %pad_add_fusion.place_ref, ...), custom_call_target="tpu_custom_call" | custom-call | flops 20000000000 | bytes 25165824 | tf_op jit(solution)/shard_map/attend_backward/pallas_call | solution.py:288
  595.7 2.3 fusion.8
  600.6 1.6 collective-permute-start.43
  602.3 1.7 add.386
  604.5 1.5 add.388
  606.1 1.4 collective-permute-start.52
  607.4 1.3 add.390
  608.8 1.7 collective-permute-start.54
  610.5 1.3 collective-permute-start.44
  611.8 1.9 fusion.7
  613.7 26.9 %collective-permute-done.44 = f32[2,1024]{1,0:T(2,128)S(1)} collective-permute-done((f32[2,1024]{1,0:T(2,128)S(1)}, f32[2,1024]{1,0:T(2,128)S(1)}, u32[]{:S(2)}, u32[]{:S(2)}) %collective-permute-start.44) | collective-permute-done | bytes 8224 | tf_op jit(solution)/shard_map/ppermute | solution.py:491
  640.6 3.0 collective-permute-start.45
  643.7 2.3 collective-permute-start.46
  647.9 3.2 collective-permute-start.56
  653.6 1.8 collective-permute-done.55
  655.4 9.6 %collective-permute-done.56 = bf16[3,128,256]{2,1,0:T(8,128)(2,1)S(1)} collective-permute-done((bf16[3,128,256]{2,1,0:T(8,128)(2,1)S(1)}, bf16[3,128,256]{2,1,0:T(8,128)(2,1)S(1)}, u32[]{:S(2)}, u32[]{:S(2)}) %collective-permute-start.56) | collective-permute-done | bytes 196640 | tf_op jit(solution)/shard_map/ppermute | solution.py:488
  666.0 2.1 dynamic-slice_bitcast_fusion
  668.9 1.7 copy.77
  670.6 1.7 copy.78
  673.0 2.2 multiply_subtract_fusion.3
  680.6 4.0 multiply_subtract_fusion.1
  684.6 1.7 copy-done.17
  687.4 6.2 multiply_subtract_fusion
  (250 shorter events, 50.1 us)
Async XLA Ops:
  7.2 207.9 %all-gather.7.cloned.1.call-start = ((), (), s32[]{:S(2)}) async-start(), calls=%async_computation.5 | async-start | bytes 7864320 | tf_op jit(solution)/shard_map/all_gather | solution.py:523
  11.5 3.8 collective-permute-start.32
  19.6 310.4 %all-gather.5.cloned.1.call-start = ((), (), s32[]{:S(2)}) async-start(), calls=%async_computation.4 | async-start | bytes 7864320 | tf_op jit(solution)/shard_map/all_gather | solution.py:523
  20.6 11.8 %collective-permute-start.7 = (bf16[3,128,256]{2,1,0:T(8,128)(2,1)S(1)}, bf16[3,128,256]{2,1,0:T(8,128)(2,1)S(1)}, u32[]{:S(2)}, u32[]{:S(2)}) collective-permute-start(bf16[3,128,256]{2,1,0:T(8,128)(2,1)S(1)} %get-tuple-element.172), channel_id=1, source_target_pairs={{0,8},{4,12},{8,0},{12,4},{16,24},{20,28},{24,16},{28,20},{1,9},{5... | collective-permute-start | bytes 589832 | tf_op jit(solution)/shard_map/ppermute | solution.py:488
  23.6 22.4 %collective-permute-start.8 = (bf16[3,128,256]{2,1,0:T(8,128)(2,1)S(1)}, bf16[3,128,256]{2,1,0:T(8,128)(2,1)S(1)}, u32[]{:S(2)}, u32[]{:S(2)}) collective-permute-start(bf16[3,128,256]{2,1,0:T(8,128)(2,1)S(1)} %get-tuple-element.172), channel_id=1, source_target_pairs={{0,16},{4,20},{8,24},{12,28},{16,0},{20,4},{24,8},{28,12},{1,17},{... | collective-permute-start | bytes 589832 | tf_op jit(solution)/shard_map/ppermute | solution.py:488
  26.2 19.8 %collective-permute-start.9 = (bf16[3,128,256]{2,1,0:T(8,128)(2,1)S(1)}, bf16[3,128,256]{2,1,0:T(8,128)(2,1)S(1)}, u32[]{:S(2)}, u32[]{:S(2)}) collective-permute-start(bf16[3,128,256]{2,1,0:T(8,128)(2,1)S(1)} %get-tuple-element.172), channel_id=1, source_target_pairs={{0,24},{4,28},{8,16},{12,20},{16,8},{20,12},{24,0},{28,4},{1,25},{... | collective-permute-start | bytes 589832 | tf_op jit(solution)/shard_map/ppermute | solution.py:488
  46.1 62.9 %collective-permute-start.10 = (bf16[4,3,128,256]{3,2,1,0:T(8,128)(2,1)S(1)}, bf16[4,3,128,256]{3,2,1,0:T(8,128)(2,1)S(1)}, u32[]{:S(2)}, u32[]{:S(2)}) collective-permute-start(bf16[4,3,128,256]{3,2,1,0:T(8,128)(2,1)S(1)} %pad_maximum_fusion.2.rest_0_), channel_id=1, source_target_pairs={{0,1},{1,0},{2,3},{3,2},{4,5},{5,4},{6,7},{7,6},{8,9},{9,8},{10,11... | collective-permute-start | bytes 2359304 | tf_op jit(solution)/shard_map/ppermute | solution.py:491
  47.7 19.9 %collective-permute-start = (f32[2,32]{1,0:T(2,128)S(1)}, f32[2,32]{1,0:T(2,128)S(1)}, u32[]{:S(2)}, u32[]{:S(2)}) collective-permute-start(f32[2,32]{1,0:T(2,128)S(1)} %bitcast.144), channel_id=1, source_target_pairs={{0,8},{4,12},{8,0},{12,4},{16,24},{20,28},{24,16},{28,20},{1,9},{5... | collective-permute-start | bytes 776 | tf_op jit(solution)/shard_map/ppermute | solution.py:488
  64.2 5.0 collective-permute-start.1
  66.2 5.4 collective-permute-start.2
  71.6 5.1 collective-permute-start.5
  73.2 4.0 collective-permute-start.3
  74.6 36.7 %collective-permute-start.11 = (bf16[4,3,128,256]{3,2,1,0:T(8,128)(2,1)S(1)}, bf16[4,3,128,256]{3,2,1,0:T(8,128)(2,1)S(1)}, u32[]{:S(2)}, u32[]{:S(2)}) collective-permute-start(bf16[4,3,128,256]{3,2,1,0:T(8,128)(2,1)S(1)} %pad_maximum_fusion.2.rest_0_), channel_id=1, source_target_pairs={{0,2},{1,3},{2,0},{3,1},{4,6},{5,7},{6,4},{7,5},{8,10},{9,11},{10,... | collective-permute-start | bytes 2359304 | tf_op jit(solution)/shard_map/ppermute | solution.py:491
  75.2 36.2 %collective-permute-start.12 = (bf16[4,3,128,256]{3,2,1,0:T(8,128)(2,1)S(1)}, bf16[4,3,128,256]{3,2,1,0:T(8,128)(2,1)S(1)}, u32[]{:S(2)}, u32[]{:S(2)}) collective-permute-start(bf16[4,3,128,256]{3,2,1,0:T(8,128)(2,1)S(1)} %pad_maximum_fusion.2.rest_0_), channel_id=1, source_target_pairs={{0,3},{1,2},{2,1},{3,0},{4,7},{5,6},{6,5},{7,4},{8,11},{9,10},{10,... | collective-permute-start | bytes 2359304 | tf_op jit(solution)/shard_map/ppermute | solution.py:491
  76.7 35.2 %collective-permute-start.13 = (bf16[4,3,128,256]{3,2,1,0:T(8,128)(2,1)S(1)}, bf16[4,3,128,256]{3,2,1,0:T(8,128)(2,1)}, u32[]{:S(2)}, u32[]{:S(2)}) collective-permute-start(bf16[4,3,128,256]{3,2,1,0:T(8,128)(2,1)S(1)} %pad_maximum_fusion.2.rest_0_), channel_id=1, source_target_pairs={{0,4},{4,0},{8,12},{12,8},{16,20},{20,16},{24,28},{28,24},{1,5},{5... | collective-permute-start | bytes 2359304 | tf_op jit(solution)/shard_map/ppermute | solution.py:485
  77.2 28.5 %collective-permute-start.4 = (f32[4,2,32]{2,1,0:T(2,128)S(1)}, f32[4,2,32]{2,1,0:T(2,128)S(1)}, u32[]{:S(2)}, u32[]{:S(2)}) collective-permute-start(f32[4,2,32]{2,1,0:T(2,128)S(1)} %pad_maximum_fusion.8), channel_id=1, source_target_pairs={{0,2},{1,3},{2,0},{3,1},{4,6},{5,7},{6,4},{7,5},{8,10},{9,11},{10,... | collective-permute-start | bytes 3080 | tf_op jit(solution)/shard_map/ppermute | solution.py:491
  107.0 1.5 collective-permute-start.6
  108.5 25.5 %collective-permute-start.24 = (bf16[512,1024]{1,0:T(8,128)(2,1)}, bf16[512,1024]{1,0:T(8,128)(2,1)}, u32[]{:S(2)}, u32[]{:S(2)}) collective-permute-start(bf16[512,1024]{1,0:T(8,128)(2,1)} %rest_8_.3), channel_id=1, source_target_pairs={{0,1},{1,0},{2,3},{3,2},{4,5},{5,4},{6,7},{7,6},{8,9},{9,8},{10,11... | collective-permute-start | bytes 3145736 | tf_op jit(solution)/shard_map/ppermute | solution.py:491
  109.0 25.8 %collective-permute-start.25 = (bf16[512,1024]{1,0:T(8,128)(2,1)}, bf16[512,1024]{1,0:T(8,128)(2,1)}, u32[]{:S(2)}, u32[]{:S(2)}) collective-permute-start(bf16[512,1024]{1,0:T(8,128)(2,1)} %rest_8_.3), channel_id=1, source_target_pairs={{0,2},{1,3},{2,0},{3,1},{4,6},{5,7},{6,4},{7,5},{8,10},{9,11},{10,... | collective-permute-start | bytes 3145736 | tf_op jit(solution)/shard_map/ppermute | solution.py:491
  111.3 23.5 %collective-permute-start.14 = (bf16[4,3,128,256]{3,2,1,0:T(8,128)(2,1)S(1)}, bf16[4,3,128,256]{3,2,1,0:T(8,128)(2,1)}, u32[]{:S(2)}, u32[]{:S(2)}) collective-permute-start(bf16[4,3,128,256]{3,2,1,0:T(8,128)(2,1)S(1)} %collective-permute-done.10.rest_1_), channel_id=1, source_target_pairs={{0,4},{4,0},{8,12},{12,8},{16,20},{20,16},{24,28},{28,24},{1,5},{5... | collective-permute-start | bytes 2359304 | tf_op jit(solution)/shard_map/ppermute | solution.py:485
  111.4 23.9 %collective-permute-start.15 = (bf16[4,3,128,256]{3,2,1,0:T(8,128)(2,1)S(1)}, bf16[4,3,128,256]{3,2,1,0:T(8,128)(2,1)}, u32[]{:S(2)}, u32[]{:S(2)}) collective-permute-start(bf16[4,3,128,256]{3,2,1,0:T(8,128)(2,1)S(1)} %collective-permute-done.11.rest_2_), channel_id=1, source_target_pairs={{0,4},{4,0},{8,12},{12,8},{16,20},{20,16},{24,28},{28,24},{1,5},{5... | collective-permute-start | bytes 2359304 | tf_op jit(solution)/shard_map/ppermute | solution.py:485
  111.9 23.5 %collective-permute-start.16 = (bf16[4,3,128,256]{3,2,1,0:T(8,128)(2,1)S(1)}, bf16[4,3,128,256]{3,2,1,0:T(8,128)(2,1)}, u32[]{:S(2)}, u32[]{:S(2)}) collective-permute-start(bf16[4,3,128,256]{3,2,1,0:T(8,128)(2,1)S(1)} %collective-permute-done.12.rest_3_), channel_id=1, source_target_pairs={{0,4},{4,0},{8,12},{12,8},{16,20},{20,16},{24,28},{28,24},{1,5},{5... | collective-permute-start | bytes 2359304 | tf_op jit(solution)/shard_map/ppermute | solution.py:485
  115.8 536.5 %reduce-scatter.3.cloned.1.call-start = ((), (), s32[]{:S(2)}) async-start(), calls=%async_computation.2 | async-start | bytes 7864320 | tf_op jit(solution)/shard_map/reduce_scatter | solution.py:565
  134.0 30.2 %collective-permute-start.26 = (bf16[512,1024]{1,0:T(8,128)(2,1)}, bf16[512,1024]{1,0:T(8,128)(2,1)S(1)}, u32[]{:S(2)}, u32[]{:S(2)}) collective-permute-start(bf16[512,1024]{1,0:T(8,128)(2,1)} %rest_8_.3), channel_id=1, source_target_pairs={{0,3},{1,2},{2,1},{3,0},{4,7},{5,6},{6,5},{7,4},{8,11},{9,10},{10,... | collective-permute-start | bytes 3145736 | tf_op jit(solution)/shard_map/ppermute | solution.py:491
  134.8 31.0 %collective-permute-start.27 = (bf16[512,1024]{1,0:T(8,128)(2,1)}, bf16[512,1024]{1,0:T(8,128)(2,1)S(1)}, u32[]{:S(2)}, u32[]{:S(2)}) collective-permute-start(bf16[512,1024]{1,0:T(8,128)(2,1)} %rest_8_.3), channel_id=1, source_target_pairs={{0,4},{4,0},{8,12},{12,8},{16,20},{20,16},{24,28},{28,24},{1,5},{5... | collective-permute-start | bytes 3145736 | tf_op jit(solution)/shard_map/ppermute | solution.py:485
  134.8 28.3 %collective-permute-start.31 = (f32[4,2048]{1,0:T(4,128)S(1)}, f32[4,2048]{1,0:T(4,128)S(1)}, u32[]{:S(2)}, u32[]{:S(2)}) collective-permute-start(f32[4,2048]{1,0:T(4,128)S(1)} %get-tuple-element.174), channel_id=1, source_target_pairs={{0,4},{4,0},{8,12},{12,8},{16,20},{20,16},{24,28},{28,24},{1,5},{5... | collective-permute-start | bytes 98312 | tf_op jit(solution)/shard_map/ppermute | solution.py:485
  135.3 32.8 %collective-permute-start.28 = (bf16[512,1024]{1,0:T(8,128)(2,1)}, bf16[512,1024]{1,0:T(8,128)(2,1)}, u32[]{:S(2)}, u32[]{:S(2)}) collective-permute-start(bf16[512,1024]{1,0:T(8,128)(2,1)} %collective-permute-done.24.rest_9_), channel_id=1, source_target_pairs={{0,4},{4,0},{8,12},{12,8},{16,20},{20,16},{24,28},{28,24},{1,5},{5... | collective-permute-start | bytes 3145736 | tf_op jit(solution)/shard_map/ppermute | solution.py:485
  135.4 33.3 %collective-permute-start.29 = (bf16[512,1024]{1,0:T(8,128)(2,1)}, bf16[512,1024]{1,0:T(8,128)(2,1)}, u32[]{:S(2)}, u32[]{:S(2)}) collective-permute-start(bf16[512,1024]{1,0:T(8,128)(2,1)} %collective-permute-done.25.rest_10_), channel_id=1, source_target_pairs={{0,4},{4,0},{8,12},{12,8},{16,20},{20,16},{24,28},{28,24},{1,5},{5... | collective-permute-start | bytes 3145736 | tf_op jit(solution)/shard_map/ppermute | solution.py:485
  163.1 26.3 %collective-permute-start.17 = (bf16[512,1024]{1,0:T(8,128)(2,1)}, bf16[512,1024]{1,0:T(8,128)(2,1)}, u32[]{:S(2)}, u32[]{:S(2)}) collective-permute-start(bf16[512,1024]{1,0:T(8,128)(2,1)} %get-tuple-element.42.rest_0_), channel_id=1, source_target_pairs={{0,1},{1,0},{2,3},{3,2},{4,5},{5,4},{6,7},{7,6},{8,9},{9,8},{10,11... | collective-permute-start | bytes 3145736 | tf_op jit(solution)/shard_map/ppermute | solution.py:491
  164.3 47.6 %collective-permute-start.18 = (bf16[512,1024]{1,0:T(8,128)(2,1)}, bf16[512,1024]{1,0:T(8,128)(2,1)}, u32[]{:S(2)}, u32[]{:S(2)}) collective-permute-start(bf16[512,1024]{1,0:T(8,128)(2,1)} %get-tuple-element.42.rest_0_), channel_id=1, source_target_pairs={{0,2},{1,3},{2,0},{3,1},{4,6},{5,7},{6,4},{7,5},{8,10},{9,11},{10,... | collective-permute-start | bytes 3145736 | tf_op jit(solution)/shard_map/ppermute | solution.py:491
  165.8 46.1 %collective-permute-start.19 = (bf16[512,1024]{1,0:T(8,128)(2,1)}, bf16[512,1024]{1,0:T(8,128)(2,1)}, u32[]{:S(2)}, u32[]{:S(2)}) collective-permute-start(bf16[512,1024]{1,0:T(8,128)(2,1)} %get-tuple-element.42.rest_0_), channel_id=1, source_target_pairs={{0,3},{1,2},{2,1},{3,0},{4,7},{5,6},{6,5},{7,4},{8,11},{9,10},{10,... | collective-permute-start | bytes 3145736 | tf_op jit(solution)/shard_map/ppermute | solution.py:491
  168.7 52.9 %collective-permute-start.30 = (bf16[512,1024]{1,0:T(8,128)(2,1)S(1)}, bf16[512,1024]{1,0:T(8,128)(2,1)}, u32[]{:S(2)}, u32[]{:S(2)}) collective-permute-start(bf16[512,1024]{1,0:T(8,128)(2,1)S(1)} %copy-done.47), channel_id=1, source_target_pairs={{0,4},{4,0},{8,12},{12,8},{16,20},{20,16},{24,28},{28,24},{1,5},{5... | collective-permute-start | bytes 3145736 | tf_op jit(solution)/shard_map/ppermute | solution.py:485
  168.7 52.9 %collective-permute-start.20 = (bf16[512,1024]{1,0:T(8,128)(2,1)}, bf16[512,1024]{1,0:T(8,128)(2,1)}, u32[]{:S(2)}, u32[]{:S(2)}) collective-permute-start(bf16[512,1024]{1,0:T(8,128)(2,1)} %get-tuple-element.42.rest_0_), channel_id=1, source_target_pairs={{0,4},{4,0},{8,12},{12,8},{16,20},{20,16},{24,28},{28,24},{1,5},{5... | collective-permute-start | bytes 3145736 | tf_op jit(solution)/shard_map/ppermute | solution.py:485
  189.4 32.2 %collective-permute-start.21 = (bf16[512,1024]{1,0:T(8,128)(2,1)}, bf16[512,1024]{1,0:T(8,128)(2,1)}, u32[]{:S(2)}, u32[]{:S(2)}) collective-permute-start(bf16[512,1024]{1,0:T(8,128)(2,1)} %collective-permute-done.17.rest_1_), channel_id=1, source_target_pairs={{0,4},{4,0},{8,12},{12,8},{16,20},{20,16},{24,28},{28,24},{1,5},{5... | collective-permute-start | bytes 3145736 | tf_op jit(solution)/shard_map/ppermute | solution.py:485
  211.9 9.7 %collective-permute-start.22 = (bf16[512,1024]{1,0:T(8,128)(2,1)}, bf16[512,1024]{1,0:T(8,128)(2,1)}, u32[]{:S(2)}, u32[]{:S(2)}) collective-permute-start(bf16[512,1024]{1,0:T(8,128)(2,1)} %collective-permute-done.18.rest_2_), channel_id=1, source_target_pairs={{0,4},{4,0},{8,12},{12,8},{16,20},{20,16},{24,28},{28,24},{1,5},{5... | collective-permute-start | bytes 3145736 | tf_op jit(solution)/shard_map/ppermute | solution.py:485
  211.9 9.7 %collective-permute-start.23 = (bf16[512,1024]{1,0:T(8,128)(2,1)}, bf16[512,1024]{1,0:T(8,128)(2,1)}, u32[]{:S(2)}, u32[]{:S(2)}) collective-permute-start(bf16[512,1024]{1,0:T(8,128)(2,1)} %collective-permute-done.19.rest_3_), channel_id=1, source_target_pairs={{0,4},{4,0},{8,12},{12,8},{16,20},{20,16},{24,28},{28,24},{1,5},{5... | collective-permute-start | bytes 3145736 | tf_op jit(solution)/shard_map/ppermute | solution.py:485
  330.0 336.0 %reduce-scatter.5.cloned.1.call-start = ((), (), s32[]{:S(2)}) async-start(), calls=%async_computation.3 | async-start | bytes 7864320 | tf_op jit(solution)/shard_map/reduce_scatter | solution.py:565
  450.5 7.5 %collective-permute-start.37 = (bf16[2048,1024]{1,0:T(8,128)(2,1)}, bf16[2048,1024]{1,0:T(8,128)(2,1)}, u32[]{:S(2)}, u32[]{:S(2)}) collective-permute-start(bf16[2048,1024]{1,0:T(8,128)(2,1)} %slice.94), channel_id=1, source_target_pairs={{0,4},{4,0},{8,12},{12,8},{16,20},{20,16},{24,28},{28,24},{1,5},{5... | collective-permute-start | bytes 12582920 | tf_op jit(solution)/shard_map/ppermute | solution.py:485
  455.3 11.5 %collective-permute-start.33 = (bf16[2048,1024]{1,0:T(8,128)(2,1)}, bf16[2048,1024]{1,0:T(8,128)(2,1)}, u32[]{:S(2)}, u32[]{:S(2)}) collective-permute-start(bf16[2048,1024]{1,0:T(8,128)(2,1)} %slice.88), channel_id=1, source_target_pairs={{0,4},{4,0},{8,12},{12,8},{16,20},{20,16},{24,28},{28,24},{1,5},{5... | collective-permute-start | bytes 12582920 | tf_op jit(solution)/shard_map/ppermute | solution.py:485
  463.2 26.1 %collective-permute-start.38 = (bf16[512,1024]{1,0:T(8,128)(2,1)S(1)}, bf16[512,1024]{1,0:T(8,128)(2,1)S(1)}, u32[]{:S(2)}, u32[]{:S(2)}) collective-permute-start(bf16[512,1024]{1,0:T(8,128)(2,1)S(1)} %get-tuple-element.150), channel_id=1, source_target_pairs={{0,1},{1,0},{2,3},{3,2},{4,5},{5,4},{6,7},{7,6},{8,9},{9,8},{10,11... | collective-permute-start | bytes 3145736 | tf_op jit(solution)/shard_map/ppermute | solution.py:491
  464.4 48.4 %collective-permute-start.39 = (bf16[512,1024]{1,0:T(8,128)(2,1)S(1)}, bf16[512,1024]{1,0:T(8,128)(2,1)S(1)}, u32[]{:S(2)}, u32[]{:S(2)}) collective-permute-start(bf16[512,1024]{1,0:T(8,128)(2,1)S(1)} %get-tuple-element.152), channel_id=1, source_target_pairs={{0,2},{1,3},{2,0},{3,1},{4,6},{5,7},{6,4},{7,5},{8,10},{9,11},{10,... | collective-permute-start | bytes 3145736 | tf_op jit(solution)/shard_map/ppermute | solution.py:491
  465.5 47.4 %collective-permute-start.40 = (bf16[512,1024]{1,0:T(8,128)(2,1)S(1)}, bf16[512,1024]{1,0:T(8,128)(2,1)S(1)}, u32[]{:S(2)}, u32[]{:S(2)}) collective-permute-start(bf16[512,1024]{1,0:T(8,128)(2,1)S(1)} %get-tuple-element.151), channel_id=1, source_target_pairs={{0,3},{1,2},{2,1},{3,0},{4,7},{5,6},{6,5},{7,4},{8,11},{9,10},{10,... | collective-permute-start | bytes 3145736 | tf_op jit(solution)/shard_map/ppermute | solution.py:491
  471.0 63.3 %collective-permute-start.34 = (bf16[512,1024]{1,0:T(8,128)(2,1)S(1)}, bf16[512,1024]{1,0:T(8,128)(2,1)S(1)}, u32[]{:S(2)}, u32[]{:S(2)}) collective-permute-start(bf16[512,1024]{1,0:T(8,128)(2,1)S(1)} %get-tuple-element.153), channel_id=1, source_target_pairs={{0,1},{1,0},{2,3},{3,2},{4,5},{5,4},{6,7},{7,6},{8,9},{9,8},{10,11... | collective-permute-start | bytes 3145736 | tf_op jit(solution)/shard_map/ppermute | solution.py:491
  472.2 83.3 %collective-permute-start.35 = (bf16[512,1024]{1,0:T(8,128)(2,1)S(1)}, bf16[512,1024]{1,0:T(8,128)(2,1)S(1)}, u32[]{:S(2)}, u32[]{:S(2)}) collective-permute-start(bf16[512,1024]{1,0:T(8,128)(2,1)S(1)} %get-tuple-element.155), channel_id=1, source_target_pairs={{0,2},{1,3},{2,0},{3,1},{4,6},{5,7},{6,4},{7,5},{8,10},{9,11},{10,... | collective-permute-start | bytes 3145736 | tf_op jit(solution)/shard_map/ppermute | solution.py:491
  489.3 67.8 %collective-permute-start.36 = (bf16[512,1024]{1,0:T(8,128)(2,1)S(1)}, bf16[512,1024]{1,0:T(8,128)(2,1)S(1)}, u32[]{:S(2)}, u32[]{:S(2)}) collective-permute-start(bf16[512,1024]{1,0:T(8,128)(2,1)S(1)} %get-tuple-element.154), channel_id=1, source_target_pairs={{0,3},{1,2},{2,1},{3,0},{4,7},{5,6},{6,5},{7,4},{8,11},{9,10},{10,... | collective-permute-start | bytes 3145736 | tf_op jit(solution)/shard_map/ppermute | solution.py:491
  594.9 5.7 collective-permute-start.49
  595.0 8.9 %collective-permute-start.51 = (bf16[4,3,128,256]{3,2,1,0:T(8,128)(2,1)}, bf16[4,3,128,256]{3,2,1,0:T(8,128)(2,1)}, u32[]{:S(2)}, u32[]{:S(2)}) collective-permute-start(bf16[4,3,128,256]{3,2,1,0:T(8,128)(2,1)} %get-tuple-element.57), channel_id=1, source_target_pairs={{0,4},{4,0},{8,12},{12,8},{16,20},{20,16},{24,28},{28,24},{1,5},{5... | collective-permute-start | bytes 2359304 | tf_op jit(solution)/shard_map/ppermute | solution.py:485
  595.5 10.6 %collective-permute-start.53 = (bf16[4,3,128,256]{3,2,1,0:T(8,128)(2,1)}, bf16[4,3,128,256]{3,2,1,0:T(8,128)(2,1)}, u32[]{:S(2)}, u32[]{:S(2)}) collective-permute-start(bf16[4,3,128,256]{3,2,1,0:T(8,128)(2,1)} %get-tuple-element.59), channel_id=1, source_target_pairs={{0,4},{4,0},{8,12},{12,8},{16,20},{20,16},{24,28},{28,24},{1,5},{5... | collective-permute-start | bytes 2359304 | tf_op jit(solution)/shard_map/ppermute | solution.py:485
  598.0 1.6 collective-permute-start.41
  599.6 9.2 %collective-permute-start.42 = (f32[2,1024]{1,0:T(2,128)S(1)}, f32[2,1024]{1,0:T(2,128)S(1)}, u32[]{:S(2)}, u32[]{:S(2)}) collective-permute-start(f32[2,1024]{1,0:T(2,128)S(1)} %fusion.45), channel_id=1, source_target_pairs={{0,1},{1,0},{2,3},{3,2},{4,5},{5,4},{6,7},{7,6},{8,9},{9,8},{10,11... | collective-permute-start | bytes 24584 | tf_op jit(solution)/shard_map/ppermute | solution.py:491
  600.5 43.1 %collective-permute-start.48 = (bf16[4,3,128,256]{3,2,1,0:T(8,128)(2,1)}, bf16[4,3,128,256]{3,2,1,0:T(8,128)(2,1)S(1)}, u32[]{:S(2)}, u32[]{:S(2)}) collective-permute-start(bf16[4,3,128,256]{3,2,1,0:T(8,128)(2,1)} %get-tuple-element.53), channel_id=1, source_target_pairs={{0,4},{4,0},{8,12},{12,8},{16,20},{20,16},{24,28},{28,24},{1,5},{5... | collective-permute-start | bytes 2359304 | tf_op jit(solution)/shard_map/ppermute | solution.py:485
  600.6 9.9 %collective-permute-start.43 = (f32[2,1024]{1,0:T(2,128)S(1)}, f32[2,1024]{1,0:T(2,128)S(1)}, u32[]{:S(2)}, u32[]{:S(2)}) collective-permute-start(f32[2,1024]{1,0:T(2,128)S(1)} %fusion.45), channel_id=1, source_target_pairs={{0,2},{1,3},{2,0},{3,1},{4,6},{5,7},{6,4},{7,5},{8,10},{9,11},{10,... | collective-permute-start | bytes 24584 | tf_op jit(solution)/shard_map/ppermute | solution.py:491
  603.9 42.0 %collective-permute-start.50 = (bf16[4,3,128,256]{3,2,1,0:T(8,128)(2,1)S(1)}, bf16[4,3,128,256]{3,2,1,0:T(8,128)(2,1)S(1)}, u32[]{:S(2)}, u32[]{:S(2)}) collective-permute-start(bf16[4,3,128,256]{3,2,1,0:T(8,128)(2,1)S(1)} %add.386), channel_id=1, source_target_pairs={{0,1},{1,0},{2,3},{3,2},{4,5},{5,4},{6,7},{7,6},{8,9},{9,8},{10,11... | collective-permute-start | bytes 2359304 | tf_op jit(solution)/shard_map/ppermute | solution.py:491
  606.1 40.0 %collective-permute-start.52 = (bf16[4,3,128,256]{3,2,1,0:T(8,128)(2,1)S(1)}, bf16[4,3,128,256]{3,2,1,0:T(8,128)(2,1)S(1)}, u32[]{:S(2)}, u32[]{:S(2)}) collective-permute-start(bf16[4,3,128,256]{3,2,1,0:T(8,128)(2,1)S(1)} %add.388), channel_id=1, source_target_pairs={{0,2},{1,3},{2,0},{3,1},{4,6},{5,7},{6,4},{7,5},{8,10},{9,11},{10,... | collective-permute-start | bytes 2359304 | tf_op jit(solution)/shard_map/ppermute | solution.py:491
  608.8 37.3 %collective-permute-start.54 = (bf16[4,3,128,256]{3,2,1,0:T(8,128)(2,1)S(1)}, bf16[4,3,128,256]{3,2,1,0:T(8,128)(2,1)S(1)}, u32[]{:S(2)}, u32[]{:S(2)}) collective-permute-start(bf16[4,3,128,256]{3,2,1,0:T(8,128)(2,1)S(1)} %add.390), channel_id=1, source_target_pairs={{0,3},{1,2},{2,1},{3,0},{4,7},{5,6},{6,5},{7,4},{8,11},{9,10},{10,... | collective-permute-start | bytes 2359304 | tf_op jit(solution)/shard_map/ppermute | solution.py:491
  610.5 30.1 %collective-permute-start.44 = (f32[2,1024]{1,0:T(2,128)S(1)}, f32[2,1024]{1,0:T(2,128)S(1)}, u32[]{:S(2)}, u32[]{:S(2)}) collective-permute-start(f32[2,1024]{1,0:T(2,128)S(1)} %fusion.45), channel_id=1, source_target_pairs={{0,3},{1,2},{2,1},{3,0},{4,7},{5,6},{6,5},{7,4},{8,11},{9,10},{10,... | collective-permute-start | bytes 24584 | tf_op jit(solution)/shard_map/ppermute | solution.py:491
  640.6 10.4 %collective-permute-start.45 = (f32[2,1024]{1,0:T(2,128)S(1)}, f32[2,1024]{1,0:T(2,128)S(1)}, u32[]{:S(2)}, u32[]{:S(2)}) collective-permute-start(f32[2,1024]{1,0:T(2,128)S(1)} %add_add_fusion.1), channel_id=1, source_target_pairs={{0,8},{4,12},{8,0},{12,4},{16,24},{20,28},{24,16},{28,20},{1,9},{5... | collective-permute-start | bytes 24584 | tf_op jit(solution)/shard_map/ppermute | solution.py:488
  643.7 7.6 %collective-permute-start.46 = (f32[2,1024]{1,0:T(2,128)S(1)}, f32[2,1024]{1,0:T(2,128)S(1)}, u32[]{:S(2)}, u32[]{:S(2)}) collective-permute-start(f32[2,1024]{1,0:T(2,128)S(1)} %add_add_fusion.1), channel_id=1, source_target_pairs={{0,16},{4,20},{8,24},{12,28},{16,0},{20,4},{24,8},{28,12},{1,17},{... | collective-permute-start | bytes 24584 | tf_op jit(solution)/shard_map/ppermute | solution.py:488
  645.9 5.7 collective-permute-start.47
  646.8 8.6 %collective-permute-start.55 = (bf16[3,128,256]{2,1,0:T(8,128)(2,1)S(1)}, bf16[3,128,256]{2,1,0:T(8,128)(2,1)S(1)}, u32[]{:S(2)}, u32[]{:S(2)}) collective-permute-start(bf16[3,128,256]{2,1,0:T(8,128)(2,1)S(1)} %get-tuple-element.165), channel_id=1, source_target_pairs={{0,8},{4,12},{8,0},{12,4},{16,24},{20,28},{24,16},{28,20},{1,9},{5... | collective-permute-start | bytes 589832 | tf_op jit(solution)/shard_map/ppermute | solution.py:488
  647.9 17.0 %collective-permute-start.56 = (bf16[3,128,256]{2,1,0:T(8,128)(2,1)S(1)}, bf16[3,128,256]{2,1,0:T(8,128)(2,1)S(1)}, u32[]{:S(2)}, u32[]{:S(2)}) collective-permute-start(bf16[3,128,256]{2,1,0:T(8,128)(2,1)S(1)} %get-tuple-element.167), channel_id=1, source_target_pairs={{0,16},{4,20},{8,24},{12,28},{16,0},{20,4},{24,8},{28,12},{1,17},{... | collective-permute-start | bytes 589832 | tf_op jit(solution)/shard_map/ppermute | solution.py:488
  651.1 13.9 %collective-permute-start.57 = (bf16[3,128,256]{2,1,0:T(8,128)(2,1)S(1)}, bf16[3,128,256]{2,1,0:T(8,128)(2,1)}, u32[]{:S(2)}, u32[]{:S(2)}) collective-permute-start(bf16[3,128,256]{2,1,0:T(8,128)(2,1)S(1)} %get-tuple-element.166), channel_id=1, source_target_pairs={{0,24},{4,28},{8,16},{12,20},{16,8},{20,12},{24,0},{28,4},{1,25},{... | collective-permute-start | bytes 589832 | tf_op jit(solution)/shard_map/ppermute | solution.py:488
  653.5 21.7 %collective-permute-start.58 = (bf16[2,192,1024]{2,1,0:T(8,128)(2,1)S(1)}, bf16[2,192,1024]{2,1,0:T(8,128)(2,1)}, u32[]{:S(2)}, u32[]{:S(2)}) collective-permute-start(bf16[2,192,1024]{2,1,0:T(8,128)(2,1)S(1)} %dynamic-slice_bitcast_fusion.1), channel_id=1, source_target_pairs={{0,4},{4,0},{8,12},{12,8},{16,20},{20,16},{24,28},{28,24},{1,5},{5... | collective-permute-start | bytes 2359304 | tf_op jit(solution)/shard_map/ppermute | solution.py:485
  668.1 8.3 %collective-permute-start.59 = (bf16[2,192,1024]{2,1,0:T(8,128)(2,1)}, bf16[2,192,1024]{2,1,0:T(8,128)(2,1)}, u32[]{:S(2)}, u32[]{:S(2)}) collective-permute-start(bf16[2,192,1024]{2,1,0:T(8,128)(2,1)} %dynamic-slice_bitcast_fusion), channel_id=1, source_target_pairs={{0,4},{4,0},{8,12},{12,8},{16,20},{20,16},{24,28},{28,24},{1,5},{5... | collective-permute-start | bytes 2359304 | tf_op jit(solution)/shard_map/ppermute | solution.py:485
  (49 other events, 989.7 us)
Sparse Core Ops, SparseCore 0:
  19.8 125.9 all-gather.6
  147.9 115.4 all-gather.4
  330.1 112.7 reduce-scatter.2
  450.7 112.7 reduce-scatter.4

commit v2 on v1

v2 whole, which is shorter than its diff:
```python
import functools
import math

import jax
import jax.numpy as jnp
import numpy as np
from jax import lax
from jax.experimental import pallas as pl
from jax.experimental.pallas import tpu as pltpu
from jax.sharding import PartitionSpec as P

D = 1024
HD = 64
FFE = 512
SEQ_LEN = 512
STEP = 10
CALLS = (((0, 2),), ((2, 3), (3, 4)))
GATHERS = ((0, 2), (2, 3), (3, 4))
QBLK = 256
SUB = 256
CHUNK = 256
SLOTS = 2560
AHEAD = 4
HELD = 3072

NORM_EPS = 1e-05
ROPE_BASE = 10000.0
BETA_ONE = 0.9
BETA_TWO = 0.95
ADAM_EPS = 1e-08
LEARN_RATE = 0.1
WEIGHT_DECAY = 0.1
MASK_FILL = -1e30
SCALE = 1.0 / math.sqrt(HD)

bf16 = jnp.bfloat16
f32 = jnp.float32
ANY = pl.BlockSpec(memory_space=pl.ANY)
COST = pl.CostEstimate(flops=1, bytes_accessed=1, transcendentals=0)
HBM = pl.BlockSpec(memory_space=pltpu.HBM)
SMEM = pl.BlockSpec(memory_space=pltpu.SMEM)
VMEM = pl.BlockSpec(memory_space=pltpu.VMEM)


def dot(a, b):
    return jnp.dot(a, b, preferred_element_type=f32)


def dot_t(a, b):
    return lax.dot_general(a, b, (((1,), (1,)), ((), ())), preferred_element_type=f32)


def t_dot(a, b):
    return lax.dot_general(a, b, (((0,), (0,)), ((), ())), preferred_element_type=f32)


def rope_tables():
    half = HD // 2
    position = np.arange(SEQ_LEN, dtype=np.float32)
    exponent = np.arange(half, dtype=np.float32) * np.float32(-2.0 / HD)
    frequency = np.exp(exponent * np.float32(math.log(ROPE_BASE))).astype(np.float32)
    angle = (position[:, None] * frequency[None, :]).astype(np.float32)
    cosine = np.cos(angle).astype(np.float32)
    sine = np.sin(angle).astype(np.float32)
    return np.tile(cosine, (1, 4)), np.concatenate([-sine, sine, -sine, sine], axis=1)


def adam_update(master, first_moment, second_moment, gradient, decay_rate):
    first_new = BETA_ONE * first_moment + (1.0 - BETA_ONE) * gradient
    second_new = BETA_TWO * second_moment + (1.0 - BETA_TWO) * gradient * gradient
    first_fixed = first_new / (1.0 - BETA_ONE**STEP)
    second_fixed = second_new / (1.0 - BETA_TWO**STEP)
    master_new = master - LEARN_RATE * (
        first_fixed / (jnp.sqrt(second_fixed) + ADAM_EPS) + decay_rate * master
    )
    return (master_new, first_new, second_new)


def adam_change(first_moment, second_moment, gradient):
    first_new = BETA_ONE * first_moment + (1.0 - BETA_ONE) * gradient
    second_new = BETA_TWO * second_moment + (1.0 - BETA_TWO) * gradient * gradient
    first_fixed = first_new / (1.0 - BETA_ONE**STEP)
    second_fixed = second_new / (1.0 - BETA_TWO**STEP)
    change = -LEARN_RATE * (first_fixed / (jnp.sqrt(second_fixed) + ADAM_EPS))
    return (change, first_new, second_new)


def rms_scale(values):
    return lax.rsqrt(jnp.mean(values * values, axis=-1, keepdims=True) + NORM_EPS)


def weight_spots(place_ref, nz, nt):
    rows, cols = D // (2 * nz), D // nt
    z, core, t = place_ref[0], place_ref[1], place_ref[2]
    for c in range(2):
        for k in range(nt):
            for j in range(nz):
                row = pl.multiple_of(((z ^ j) * 2 + (core ^ c)) * rows, rows)
                col = pl.multiple_of((t ^ k) * cols, cols)
                yield c, k, j, (pl.ds(row, rows), pl.ds(col, cols))


def gather_copies(place_ref, pieces, first, w_ref, sem, nz, nt):
    rows = D // (2 * nz)
    return [
        pltpu.make_async_copy(
            pieces[c * nt + k].at[j, (first + member) * rows : (first + member + 1) * rows, :],
            w_ref.at[(member,) + spot],
            sem.at[((c * nt + k) * nz + j) * w_ref.shape[0] + member],
        )
        for c, k, j, spot in weight_spots(place_ref, nz, nt)
        for member in range(w_ref.shape[0])
    ]


def rotate(x, cosine, sine, first_half):
    width = x.shape[-1]
    swapped = jnp.where(
        first_half, pltpu.roll(x, width - HD // 2, 1), pltpu.roll(x, HD // 2, 1)
    )
    return x * cosine + swapped * sine


def join_gains(parts, width):
    owners = parts.shape[0]
    both = jnp.sum(parts[:, :, :128].astype(f32), axis=1)
    lane = lax.broadcasted_iota(jnp.int32, (owners, 128), 1)
    owner = lax.broadcasted_iota(jnp.int32, (owners, D), 0)
    mine = lax.broadcasted_iota(jnp.int32, (owners, D), 1) // width == owner
    out = []
    for values in (both, pltpu.roll(both, 128 - width, 1)):
        values = jnp.where(lane < width, values, 0.0)
        shift = width
        while shift < 128:
            values = values + pltpu.roll(values, shift, 1)
            shift *= 2
        wide = jnp.concatenate([values] * (D // 128), axis=1)
        out.append(jnp.sum(jnp.where(mine, wide, 0.0), axis=0, keepdims=True))
    return jnp.concatenate(out, axis=0)


def attend_forward_kernel(nz, nt, place_ref, tokens_ref, cos_ref, sin_ref, *rest):
    pieces = rest[: 2 * nt]
    q_ref, kv_ref, o_ref, lse_ref, w_ref, gains_ref = rest[2 * nt : 2 * nt + 6]
    qlin_ref, kvlin_ref, parts_ref, sems, gain_sems = rest[2 * nt + 6 :]
    length = tokens_ref.shape[0]
    rows = D // (2 * nz)
    z, core, t = place_ref[0], place_ref[1], place_ref[2]
    gain_copies = [
        pltpu.make_async_copy(
            pieces[c * nt + k].at[j, 2 * rows :, :],
            parts_ref.at[((z ^ j) * 2 + (core ^ c)) * nt + (t ^ k)],
            gain_sems.at[(c * nt + k) * nz + j],
        )
        for c in range(2)
        for k in range(nt)
        for j in range(nz)
    ]
    for copy in gain_copies:
        copy.start()
    copies = gather_copies(place_ref, pieces, 0, w_ref, sems, nz, nt)
    for copy in copies:
        copy.start()
    lse_ref[...] = jnp.zeros_like(lse_ref)
    for copy in gain_copies:
        copy.wait()
    gains_ref[...] = join_gains(parts_ref[...], D // (2 * nz * nt))
    stream = tokens_ref[...].astype(f32)
    n1 = (stream * rms_scale(stream) * gains_ref[0:1, :]).astype(bf16)
    for copy in copies:
        copy.wait()
    qlin_ref[...] = dot(n1, w_ref[0])
    kvlin_ref[...] = dot(n1, w_ref[1])

    def group(g, carry):
        part = pl.ds(pl.multiple_of(g * 128, 128), 128)
        lane = lax.broadcasted_iota(jnp.int32, (length, 128), 1)
        low = lane < HD
        first_half = (lane & (HD // 2)) == 0
        cosine, sine = cos_ref[...], sin_ref[...]
        q = rotate(qlin_ref[:, part], cosine, sine, first_half)
        kv = kvlin_ref[:, part]
        kv = jnp.where(low, rotate(kv, cosine, sine, first_half), kv)
        q_ref[:, part] = q.astype(bf16)
        kv_ref[:, part] = kv.astype(bf16)
        vk = pltpu.roll(kv, HD, 1).astype(bf16)
        kv = kv.astype(bf16)
        heads = (
            (jnp.where(low, q, 0.0).astype(bf16), kv, vk),
            (jnp.where(low, 0.0, q).astype(bf16), vk, kv),
        )
        for b in range(length // QBLK):
            rows = slice(b * QBLK, (b + 1) * QBLK)
            keys = (b + 1) * QBLK
            row = lax.broadcasted_iota(jnp.int32, (QBLK, keys), 0) + b * QBLK
            column = lax.broadcasted_iota(jnp.int32, (QBLK, keys), 1)
            seen = column <= row
            outs = []
            lses = lse_ref[rows, :]
            lane_b = lax.broadcasted_iota(jnp.int32, (QBLK, 128), 1)
            for h, (qh, key_side, value_side) in enumerate(heads):
                scores = dot_t(qh[rows], key_side[:keys]) * SCALE
                scores = jnp.where(seen, scores, MASK_FILL)
                top = jnp.max(scores, axis=-1, keepdims=True)
                e = jnp.exp(scores - top)
                total = jnp.sum(e, axis=-1, keepdims=True)
                p = (e * (1.0 / total)).astype(bf16)
                outs.append(dot(p, value_side[:keys]))
                lses = jnp.where(lane_b == 2 * g + h, top + jnp.log(total), lses)
            lse_ref[rows, :] = lses
            o_ref[rows, part] = jnp.where(lane_b < HD, outs[0], outs[1]).astype(bf16)
        return carry

    lax.fori_loop(0, D // 128, group, 0)


def attend_forward(mesh_sizes, place, tokens, pieces):
    nz, nt = mesh_sizes
    length = tokens.shape[0]
    cosine, sine = rope_tables()
    return pl.pallas_call(
        functools.partial(attend_forward_kernel, nz, nt),
        out_shape=(
            jax.ShapeDtypeStruct((length, D), bf16),
            jax.ShapeDtypeStruct((length, D), bf16),
            jax.ShapeDtypeStruct((length, D), bf16),
            jax.ShapeDtypeStruct((length, 128), f32),
            jax.ShapeDtypeStruct((2, D, D), bf16),
            jax.ShapeDtypeStruct((2, D), f32),
        ),
        in_specs=[SMEM] + [VMEM] * 3 + [ANY] * len(pieces),
        out_specs=[VMEM] * 6,
        scratch_shapes=[
            pltpu.VMEM((length, D), f32),
            pltpu.VMEM((length, D), f32),
            pltpu.VMEM((2 * nz * nt, 16, D // nt), bf16),
            pltpu.SemaphoreType.DMA((2 * nt * nz * 2,)),
            pltpu.SemaphoreType.DMA((2 * nt * nz,)),
        ],
        compiler_params=pltpu.CompilerParams(vmem_limit_bytes=40 * 2**20),
        cost_estimate=COST,
        name="attend_forward",
    )(place, tokens, jnp.asarray(cosine), jnp.asarray(sine), *pieces)


def attend_out_kernel(nz, nt, place_ref, tokens_ref, gains_ref, o_ref, *rest):
    pieces = rest[: 2 * nt]
    s1_ref, n2_ref, w_ref, sems = rest[2 * nt :]
    copies = gather_copies(place_ref, pieces, 0, w_ref, sems, nz, nt)
    for copy in copies:
        copy.start()
    for copy in copies:
        copy.wait()
    s1 = tokens_ref[...].astype(f32) + dot_t(o_ref[...], w_ref[0])
    s1_ref[...] = s1
    n2_ref[...] = (s1 * rms_scale(s1) * gains_ref[1:2, :]).astype(bf16)


def attend_out(mesh_sizes, place, tokens, gains, o, pieces):
    nz, nt = mesh_sizes
    length = tokens.shape[0]
    return pl.pallas_call(
        functools.partial(attend_out_kernel, nz, nt),
        out_shape=(
            jax.ShapeDtypeStruct((length, D), f32),
            jax.ShapeDtypeStruct((length, D), bf16),
            jax.ShapeDtypeStruct((1, D, D), bf16),
        ),
        in_specs=[SMEM] + [VMEM] * 3 + [ANY] * len(pieces),
        out_specs=[VMEM] * 3,
        scratch_shapes=[pltpu.SemaphoreType.DMA((2 * nt * nz,))],
        compiler_params=pltpu.CompilerParams(vmem_limit_bytes=32 * 2**20),
        cost_estimate=COST,
        name="attend_out",
    )(place, tokens, gains, o, *pieces)


def attend_backward_kernel(
    nz, nt, place_ref, tokens_ref, da_ref, gains_ref, gain_two_ref, cos_ref, sin_ref, q_ref, kv_ref, o_ref,
    lse_ref, w_ref, wo_ref, dn1_ref, own_ref, other_ref, gw_ref, gg_ref, do_ref, dq_ref, dkv_ref, lse_t_ref, sems
):
    length = tokens_ref.shape[0]
    rows, cols = D // (2 * nz), D // nt
    sides = (own_ref, other_ref)

    def member_copies(members):
        return [
            pltpu.make_async_copy(
                gw_ref.at[(member,) + spot],
                sides[c].at[k, j, member * rows : (member + 1) * rows, :],
                sems.at[member, (c * nt + k) * nz + j],
            )
            for member in members
            for c, k, j, spot in weight_spots(place_ref, nz, nt)
        ]

    gw_ref[2] = t_dot(da_ref[...], o_ref[...]).astype(bf16)
    first = member_copies((2,))
    for copy in first:
        copy.start()
    do_ref[...] = dot(da_ref[...], wo_ref[0]).astype(bf16)
    lse_t_ref[...] = lse_ref[...].T

    def group(g, carry):
        part = pl.ds(pl.multiple_of(g * 128, 128), 128)
        lane = lax.broadcasted_iota(jnp.int32, (length, 128), 1)
        low = lane < HD
        first_half = (lane & (HD // 2)) == 0
        cosine, sine = cos_ref[...], sin_ref[...]
        q = q_ref[:, part].astype(f32)
        kv = kv_ref[:, part].astype(f32)
        do = do_ref[:, part].astype(f32)
        vk = pltpu.roll(kv, HD, 1).astype(bf16)
        kv = kv.astype(bf16)
        q_low = jnp.where(low, q, 0.0).astype(bf16)
        q_high = jnp.where(low, 0.0, q).astype(bf16)
        q_moved = jnp.where(low, pltpu.roll(q, HD, 1), 0.0).astype(bf16)
        do_low = jnp.where(low, do, 0.0).astype(bf16)
        do_high = jnp.where(low, 0.0, do).astype(bf16)
        do_moved = jnp.where(low, 0.0, pltpu.roll(do, HD, 1)).astype(bf16)
        heads = (
            (q_low, kv, vk, do_low, q_low, do_moved),
            (q_high, vk, kv, do_high, q_moved, do_high),
        )
        blocks = length // QBLK
        dkv = [jnp.zeros((QBLK, 128), f32) for _ in range(blocks)]
        dqs = []
        for b in range(blocks):
            rows = slice(b * QBLK, (b + 1) * QBLK)
            keys = (b + 1) * QBLK
            row = lax.broadcasted_iota(jnp.int32, (keys, QBLK), 0)
            column = lax.broadcasted_iota(jnp.int32, (keys, QBLK), 1) + b * QBLK
            seen = row <= column
            both = []
            for h, (qh, key_side, value_side, doh, q_for_k, do_for_v) in enumerate(heads):
                scores = dot_t(key_side[:keys], qh[rows]) * SCALE
                scores = jnp.where(seen, scores, MASK_FILL)
                e = jnp.exp(scores - lse_t_ref[pl.ds(2 * g + h, 1), rows])
                dp = dot_t(value_side[:keys], doh[rows])
                mean = jnp.sum(e * dp, axis=0, keepdims=True)
                dz = (e * (dp - mean)).astype(bf16)
                both.append(t_dot(dz, key_side[:keys]))
                add = dot(dz, q_for_k[rows]) + dot(e.astype(bf16), do_for_v[rows])
                for i in range(b + 1):
                    dkv[i] = dkv[i] + add[i * QBLK : (i + 1) * QBLK]
            lane_b = lax.broadcasted_iota(jnp.int32, (QBLK, 128), 1)
            dqs.append(jnp.where(lane_b < HD, both[0], both[1]))
        dq = jnp.concatenate(dqs, axis=0) * SCALE
        dkv_all = jnp.concatenate(dkv, axis=0)
        dq_ref[:, part] = rotate(dq, cosine, -sine, first_half).astype(bf16)
        dk = rotate(dkv_all * SCALE, cosine, -sine, first_half)
        dkv_ref[:, part] = jnp.where(low, dk, dkv_all).astype(bf16)
        return carry

    lax.fori_loop(0, D // 128, group, 0)
    stream = tokens_ref[...].astype(f32)
    unit = stream * rms_scale(stream)
    n1 = (unit * gains_ref[0:1, :]).astype(bf16)
    gw_ref[0] = t_dot(n1, dq_ref[...]).astype(bf16)
    gw_ref[1] = t_dot(n1, dkv_ref[...]).astype(bf16)
    second = member_copies((0, 1))
    for copy in second:
        copy.start()
    dn1 = dot_t(dq_ref[...], w_ref[0]) + dot_t(dkv_ref[...], w_ref[1])
    dn1_ref[...] = dn1
    gain_one = jnp.sum(dn1 * unit, axis=0, keepdims=True)
    gg_ref[...] = jnp.zeros_like(gg_ref)
    for i in range(nt):
        gg_ref[i : i + 1, :] = gain_one[:, i * cols : (i + 1) * cols].astype(bf16)
        gg_ref[nt + i : nt + i + 1, :] = gain_two_ref[:, i * cols : (i + 1) * cols].astype(bf16)
    third = [
        pltpu.make_async_copy(gg_ref, sides[c].at[k, j, 3 * rows :, :], sems.at[3, (c * nt + k) * nz + j])
        for c in range(2)
        for k in range(nt)
        for j in range(nz)
    ]
    for copy in third:
        copy.start()
    for copy in first + second + third:
        copy.wait()


def attend_backward(mesh_sizes, place, tokens, da, gains, gain_two, q, kv, o, lse, weights, out_weight):
    nz, nt = mesh_sizes
    length = tokens.shape[0]
    cosine, sine = rope_tables()
    part = jax.ShapeDtypeStruct((nt, nz, 3 * D // (2 * nz) + 16, D // nt), bf16)
    return pl.pallas_call(
        functools.partial(attend_backward_kernel, nz, nt),
        out_shape=(jax.ShapeDtypeStruct((length, D), f32), part, part),
        in_specs=[SMEM] + [VMEM] * 12,
        out_specs=[VMEM, ANY, ANY],
        scratch_shapes=[
            pltpu.VMEM((3, D, D), bf16),
            pltpu.VMEM((16, D // nt), bf16),
            pltpu.VMEM((length, D), bf16),
            pltpu.VMEM((length, D), bf16),
            pltpu.VMEM((length, D), bf16),
            pltpu.VMEM((128, length), f32),
            pltpu.SemaphoreType.DMA((4, 2 * nt * nz)),
        ],
        compiler_params=pltpu.CompilerParams(vmem_limit_bytes=48 * 2**20),
        cost_estimate=COST,
        name="attend_backward",
    )(
        place, tokens, da, gains, gain_two, jnp.asarray(cosine), jnp.asarray(sine), q, kv, o, lse, weights, out_weight
    )


def gather_kernel(starts, experts, offs_ref, pos_ref, c_ref, *rest):
    tiles = len(starts) - 1
    n2_parts, dm_parts, rest = rest[:tiles], rest[tiles : 2 * tiles], rest[2 * tiles :]
    n2_out, dm_out, c_out, n2_in, dm_in, n2_slots, dm_slots, c_slots, in_sems, out_sems = rest
    subs = starts[-1] // SUB

    def block_copies(s):
        j = max(i for i in range(tiles) if starts[i] <= s * SUB)
        spot = pl.ds(s * SUB - starts[j], SUB)
        return (
            pltpu.make_async_copy(n2_parts[j].at[spot], n2_in.at[s % AHEAD], in_sems.at[0, s % AHEAD]),
            pltpu.make_async_copy(dm_parts[j].at[spot], dm_in.at[s % AHEAD], in_sems.at[1, s % AHEAD]),
        )

    def flush(e, chunk):
        spot = pl.ds(pl.multiple_of(chunk * CHUNK, CHUNK), CHUNK)
        return [
            pltpu.make_async_copy(slots.at[e, spot, :], out.at[e, spot, :], out_sems.at[i, e, chunk])
            for i, (slots, out) in enumerate(((n2_slots, n2_out), (dm_slots, dm_out), (c_slots, c_out)))
        ]

    for s in range(AHEAD - 1):
        for copy in block_copies(s):
            copy.start()

    def block(s, carry):
        for ahead in range(AHEAD - 1, subs):

            @pl.when(s + AHEAD - 1 == ahead)
            def _():
                for copy in block_copies(ahead):
                    copy.start()

        slot = lax.rem(s, AHEAD)
        pltpu.make_async_copy(n2_parts[0].at[pl.ds(0, SUB)], n2_in.at[slot], in_sems.at[0, slot]).wait()
        pltpu.make_async_copy(dm_parts[0].at[pl.ds(0, SUB)], dm_in.at[slot], in_sems.at[1, slot]).wait()
        begin = [offs_ref[e * (subs + 1) + s] for e in range(experts)]
        end = [offs_ref[e * (subs + 1) + s + 1] for e in range(experts)]
        most = functools.reduce(jnp.maximum, [end[e] - begin[e] for e in range(experts)])

        def fill(count):
            slots = lax.broadcasted_iota(jnp.int32, (count, SUB), 0).astype(f32)
            picks = []
            for e in range(experts):
                spot = pl.ds(pl.multiple_of(begin[e], 16), count)
                hit = slots == pos_ref[pl.ds(e * subs + s, 1), :]
                picks.append(jnp.where(hit, 1.0, 0.0).astype(bf16))
                c = jnp.sum(jnp.where(hit, c_ref[pl.ds(e * subs + s, 1), :], 0.0), axis=1, keepdims=True)
                c_slots[e, spot, :] = jnp.broadcast_to(c, (count, 128))
            pick = jnp.concatenate(picks, axis=0)
            for source, target in ((n2_in, n2_slots), (dm_in, dm_slots)):
                rows = dot(pick, source[slot]).astype(bf16)
                for e in range(experts):
                    spot = pl.ds(pl.multiple_of(begin[e], 16), count)
                    target[e, spot, :] = rows[e * count : (e + 1) * count]

        @pl.when(most <= SUB // 2)
        def _():
            fill(SUB // 2)

        @pl.when(most > SUB // 2)
        def _():
            fill(SUB)

        for e in range(experts):

            @pl.when(end[e] // CHUNK > begin[e] // CHUNK)
            def _():
                for copy in flush(e, begin[e] // CHUNK):
                    copy.start()

        return carry

    lax.fori_loop(0, subs, block, 0)
    for e in range(experts):
        total = offs_ref[e * (subs + 1) + subs]
        tail = pl.ds(pl.multiple_of(total, 16), CHUNK)
        n2_slots[e, tail, :] = jnp.zeros((CHUNK, D), bf16)
        dm_slots[e, tail, :] = jnp.zeros((CHUNK, D), bf16)
        c_slots[e, tail, :] = jnp.zeros((CHUNK, 128), f32)
        for copy in flush(e, total // CHUNK):
            copy.start()
    for e in range(experts):

        def drain(chunk, carry):
            for copy in flush(e, chunk):
                copy.wait()
            return carry

        lax.fori_loop(0, offs_ref[e * (subs + 1) + subs] // CHUNK + 1, drain, 0)


def gather(n2_parts, dm_parts, offs, pos, c):
    starts = [0]
    for n2_part in n2_parts:
        starts.append(starts[-1] + n2_part.shape[0])
    experts = pos.shape[0] * SUB // starts[-1]
    rows = jax.ShapeDtypeStruct((experts, SLOTS, D), bf16)
    return pl.pallas_call(
        functools.partial(gather_kernel, tuple(starts), experts),
        out_shape=(rows, rows, jax.ShapeDtypeStruct((experts, SLOTS, 128), f32)),
        in_specs=[SMEM, VMEM, VMEM] + [HBM] * (2 * len(n2_parts)),
        out_specs=(HBM, HBM, HBM),
        scratch_shapes=[
            pltpu.VMEM((AHEAD, SUB, D), bf16),
            pltpu.VMEM((AHEAD, SUB, D), bf16),
            pltpu.VMEM((experts, SLOTS, D), bf16),
            pltpu.VMEM((experts, SLOTS, D), bf16),
            pltpu.VMEM((experts, SLOTS, 128), f32),
            pltpu.SemaphoreType.DMA((2, AHEAD)),
            pltpu.SemaphoreType.DMA((3, experts, SLOTS // CHUNK)),
        ],
        compiler_params=pltpu.CompilerParams(vmem_limit_bytes=62 * 2**20),
        cost_estimate=COST,
        name="gather_rows",
    )(offs, pos, c, *n2_parts, *dm_parts)


def experts_kernel(first, subs, sources, kept, place_ref, offs_ref, n2_ref, dm_ref, c_ref, *rest):
    arrays = 1 + sources[-1][0]
    weights, rest = rest[:arrays], rest[arrays + kept :]
    m_ref, d_ref, gw_ref = rest[:3]
    win_buf, wdown_buf, n2_in, dm_in, c_in, m_out, d_out, zeros, gin, gdown, w_sems, in_sems, out_sems = rest[3:]
    e = pl.program_id(0)
    nz, cores, _, wrows, _ = gw_ref.shape
    rin, rdown = D // (nz * cores), FFE // (nz * cores)
    core = place_ref[1]
    total = offs_ref[(first + e) * (subs + 1) + subs]
    chunks = jnp.maximum((total + CHUNK - 1) // CHUNK, 1)

    def weight_copies(index):
        i, place = sources[index]
        slot = index % 2
        return [
            pltpu.make_async_copy(
                weights[i].at[:, side, place, spot, :], buf.at[slot, :, core ^ side], w_sems.at[2 * side + j, slot]
            )
            for side in range(2)
            for j, (spot, buf) in enumerate(((slice(0, rin), win_buf), (slice(rin, wrows), wdown_buf)))
        ]

    def in_copies(k, slot):
        spot = pl.ds(pl.multiple_of(k * CHUNK, CHUNK), CHUNK)
        return [
            pltpu.make_async_copy(source.at[first + e, spot, :], target.at[slot], in_sems.at[i, slot])
            for i, (source, target) in enumerate(((n2_ref, n2_in), (dm_ref, dm_in), (c_ref, c_in)))
        ]

    def out_copies(k, slot):
        spot = pl.ds(pl.multiple_of(k * CHUNK, CHUNK), CHUNK)
        return (
            pltpu.make_async_copy(m_out.at[slot], m_ref.at[e, spot, :], out_sems.at[0, slot]),
            pltpu.make_async_copy(d_out.at[slot], d_ref.at[e, spot, :], out_sems.at[1, slot]),
        )

    for copy in in_copies(0, 0):
        copy.start()

    @pl.when(e == 0)
    def _():
        for copy in weight_copies(0):
            copy.start()
        zeros[...] = jnp.zeros_like(zeros)

    for index in range(len(sources)):

        @pl.when(e == index)
        def _():
            for copy in weight_copies(index):
                copy.wait()
            if index + 1 < len(sources):
                for copy in weight_copies(index + 1):
                    copy.start()

    at = lax.rem(e, 2)

    def one_chunk(k, carry):
        slot = lax.rem(k, 2)
        for copy in in_copies(k, slot):
            copy.wait()

        @pl.when(k + 1 < chunks)
        def _():
            for copy in in_copies(k + 1, 1 - slot):
                copy.start()

        @pl.when(k >= 2)
        def _():
            for copy in out_copies(k - 2, slot):
                copy.wait()

        win = win_buf[at].reshape(D, D)
        wdown = wdown_buf[at].reshape(FFE, D)
        n2, dm, c = n2_in[slot], dm_in[slot], c_in[slot][:, 0:1]
        hidden = dot(n2, win)
        gate, up = hidden[:, :FFE], hidden[:, FFE:]
        sigma = jax.nn.sigmoid(gate)
        silu = gate * sigma
        active = (c * silu * up).astype(bf16)
        m_out[slot] = dot(active, wdown).astype(bf16)
        gdown[...] = jnp.where(k == 0, 0.0, gdown[...]) + dot(active.T, dm)
        da = c * dot_t(dm, wdown)
        dgate = da * up * (sigma + silu * (1.0 - sigma))
        dup = da * silu
        dh = jnp.concatenate([dgate.astype(bf16), dup.astype(bf16)], axis=1)
        gin[...] = jnp.where(k == 0, 0.0, gin[...]) + dot(n2.T, dh)
        d_out[slot] = dot_t(dh, win).astype(bf16)
        for copy in out_copies(k, slot):
            copy.start()
        return carry

    lax.fori_loop(0, chunks, one_chunk, 0)
    spot = pl.ds(pl.multiple_of(chunks * CHUNK, CHUNK), CHUNK)
    ends = (
        pltpu.make_async_copy(zeros, m_ref.at[e, spot, :], out_sems.at[0, 2]),
        pltpu.make_async_copy(zeros, d_ref.at[e, spot, :], out_sems.at[1, 2]),
    )
    for copy in ends:
        copy.start()
    for j in range(nz):
        for side in range(2):
            owner = 2 * j + (core ^ side)
            at_in, at_down = pl.multiple_of(owner * rin, rin), pl.multiple_of(owner * rdown, rdown)
            gw_ref[j, side, 0, :rin, :] = gin[pl.ds(at_in, rin), :].astype(bf16)
            gw_ref[j, side, 0, rin:, :] = gdown[pl.ds(at_down, rdown), :].astype(bf16)
    for copy in ends:
        copy.wait()
    for back in (1, 2):

        @pl.when(chunks >= back)
        def _():
            for copy in out_copies(chunks - back, lax.rem(chunks - back, 2)):
                copy.wait()


def experts_step(place, slots, offs, first, weights, sources, before, spot, count):
    nz, cores, _, wrows, _ = weights[0].shape
    experts = len(sources)
    rin, rdown = D // (nz * cores), FFE // (nz * cores)
    part = jax.ShapeDtypeStruct((experts, HELD, D), bf16)
    kept = [] if before is None else [before]
    subs = offs.shape[1] - 1
    return pl.pallas_call(
        functools.partial(experts_kernel, first, subs, sources, len(kept)),
        grid=(experts,),
        out_shape=(part, part, jax.ShapeDtypeStruct((nz, cores, count, wrows, D), bf16)),
        in_specs=[SMEM, SMEM] + [HBM] * (3 + len(weights) + len(kept)),
        out_specs=(HBM, HBM, pl.BlockSpec((nz, cores, 1, wrows, D), lambda e: (0, 0, spot + e, 0, 0))),
        scratch_shapes=[
            pltpu.VMEM((2, nz, cores, rin, D), bf16),
            pltpu.VMEM((2, nz, cores, rdown, D), bf16),
            pltpu.VMEM((2, CHUNK, D), bf16),
            pltpu.VMEM((2, CHUNK, D), bf16),
            pltpu.VMEM((2, CHUNK, 128), f32),
            pltpu.VMEM((2, CHUNK, D), bf16),
            pltpu.VMEM((2, CHUNK, D), bf16),
            pltpu.VMEM((CHUNK, D), bf16),
            pltpu.VMEM((D, D), f32),
            pltpu.VMEM((FFE, D), f32),
            pltpu.SemaphoreType.DMA((4, 2)),
            pltpu.SemaphoreType.DMA((3, 2)),
            pltpu.SemaphoreType.DMA((2, 3)),
        ],
        input_output_aliases={5 + len(weights): 2} if kept else {},
        compiler_params=pltpu.CompilerParams(
            vmem_limit_bytes=60 * 2**20, dimension_semantics=("arbitrary",)
        ),
        cost_estimate=COST,
        name="experts",
    )(place, offs.reshape(-1), *slots, *weights, *kept)


def scatter_kernel(halves, sources, experts, subs, offs_ref, pos_ref, *rest):
    arrays = 1 + sources[-1][1]
    parts, rest = rest[:arrays], rest[arrays:]
    outs, (slots, sems) = rest[: len(halves)], rest[len(halves) :]
    i, steps = pl.program_id(0), subs // 2
    low = min(halves) * steps
    high = low + len(halves) * steps

    @pl.when(i == 0)
    def _():
        def each(act):
            for spot, (e, array, index) in enumerate(sources):

                def one(chunk, carry):
                    rows = pl.ds(pl.multiple_of(chunk * CHUNK, CHUNK), CHUNK)
                    act(pltpu.make_async_copy(parts[array].at[index, rows, :], slots.at[spot, rows, :], sems.at[spot, chunk]))
                    return carry

                begin = offs_ref[e * (subs + 1) + low] // CHUNK
                end = (offs_ref[e * (subs + 1) + high] + CHUNK - 1) // CHUNK + 1
                lax.fori_loop(begin, end, one, 0)

        each(lambda copy: copy.start())
        each(lambda copy: copy.wait())

    block = lax.rem(i + halves[0] * steps, subs)
    lane = lax.broadcasted_iota(jnp.int32, (SUB, SUB), 1).astype(f32)
    picks = [jnp.where(lane == pos_ref[:, e : e + 1], 1.0, 0.0).astype(bf16) for e, _, _ in sources]
    windows = [
        slots[spot, pl.ds(pl.multiple_of(offs_ref[e * (subs + 1) + block], 16), SUB), :]
        for spot, (e, _, _) in enumerate(sources)
    ]
    total = dot(jnp.concatenate(picks, axis=1), jnp.concatenate(windows, axis=0))
    for j, out_ref in enumerate(outs):

        @pl.when(i // steps == j)
        def _():
            out_ref[...] = total.astype(bf16)


def scatter(offs, pos_columns, parts, halves):
    tokens, experts = pos_columns.shape
    sources = [
        (first + index, i, index) for i, (part, first) in enumerate(parts) for index in range(part.shape[0])
    ]
    subs = tokens // SUB
    steps = subs // 2
    shift = halves[0] * steps
    blocks = [
        pl.BlockSpec((SUB, D), lambda i, j=j: (jnp.clip(i - j * steps, 0, steps - 1), 0))
        for j in range(len(halves))
    ]
    return pl.pallas_call(
        functools.partial(scatter_kernel, halves, sources, experts, subs),
        grid=(len(halves) * steps,),
        out_shape=[jax.ShapeDtypeStruct((steps * SUB, D), bf16)] * len(halves),
        in_specs=[SMEM, pl.BlockSpec((SUB, experts), lambda i: (lax.rem(i + shift, subs), 0))]
        + [HBM] * len(parts),
        out_specs=blocks,
        scratch_shapes=[
            pltpu.VMEM((len(sources), HELD, D), bf16),
            pltpu.SemaphoreType.DMA((len(sources), HELD // CHUNK)),
        ],
        compiler_params=pltpu.CompilerParams(
            vmem_limit_bytes=60 * 2**20, dimension_semantics=("arbitrary",)
        ),
        cost_estimate=COST,
        name="scatter_rows",
    )(offs.reshape(-1), pos_columns, *[part for part, _ in parts])


def adam_kernel(per, place_ref, mine_ref, recv_ref, *rest):
    states, news = rest[:6], rest[-6:]
    here = pl.program_id(0) // per == place_ref[1]
    grad = jnp.where(here, mine_ref[0, 0], recv_ref[0]).astype(f32)
    rin = states[0].shape[2]
    for i, part in ((0, grad[:rin]), (3, grad[rin:])):
        masters = [ref[0, 0] for ref in states[i : i + 3]]
        for ref, new in zip(news[i : i + 3], adam_update(*masters, part, WEIGHT_DECAY)):
            ref[0, 0] = new


def adam_experts(place, a, mine, recv, states, before):
    experts, rin = states[0].shape[1:3]
    rdown = states[3].shape[2]
    per = recv.shape[0]
    half = experts // 2
    spec = [
        pl.BlockSpec((1, 1, r, D), lambda i, place: (0, i // per * half + a + i % per, 0, 0))
        for r in (rin, rdown)
    ]
    specs = [spec[0]] * 3 + [spec[1]] * 3
    kept = [] if before is None else list(before)
    return pl.pallas_call(
        functools.partial(adam_kernel, per),
        grid_spec=pltpu.PrefetchScalarGridSpec(
            num_scalar_prefetch=1,
            grid=(2 * per,),
            in_specs=[
                pl.BlockSpec((1, 1, rin + rdown, D), lambda i, place: (0, i % per, 0, 0)),
                pl.BlockSpec((1, rin + rdown, D), lambda i, place: (i % per, 0, 0)),
            ]
            + specs
            + [HBM] * len(kept),
            out_specs=specs,
        ),
        out_shape=[jax.ShapeDtypeStruct(state.shape, f32) for state in states],
        input_output_aliases={9 + i: i for i in range(len(kept))},
        compiler_params=pltpu.CompilerParams(
            vmem_limit_bytes=60 * 2**20, dimension_semantics=("arbitrary",)
        ),
        cost_estimate=COST,
        name="adam_experts",
    )(place, mine, recv, *states, *kept)


def on_device(
    ndp,
    nt,
    tokens,
    cotangent,
    routes,
    gate_weights,
    norm_gains,
    norm_gains_first,
    norm_gains_second,
    query_weight,
    query_first,
    query_second,
    keyval_weight,
    keyval_first,
    keyval_second,
    output_weight,
    output_first,
    output_second,
    expert_in,
    expert_in_first,
    expert_in_second,
    expert_down,
    expert_down_first,
    expert_down_second,
):
    nz = ndp // 2
    place_dp = lax.axis_index("dp")
    t = lax.axis_index("tensor")
    z, core = place_dp // 2, place_dp % 2
    place = jnp.stack([z, core, t]).astype(jnp.int32)
    rows = tokens.shape[0]
    sharers = max(1, SEQ_LEN // rows)

    def swap_core(x):
        return lax.ppermute(x, "dp", [(i, i ^ 1) for i in range(ndp)])

    def swap_z(x, j):
        return lax.ppermute(x, "dp", [(i, i ^ (2 * j)) for i in range(ndp)])

    def swap_t(x, k):
        return lax.ppermute(x, "tensor", [(i, i ^ k) for i in range(nt)])

    def spread_t(x):
        return [x] + [swap_t(x, k) for k in range(1, nt)]

    def spread_z(x):
        return [x] + [swap_z(x, j) for j in range(1, nz)]

    def after(x, *others):
        return lax.optimization_barrier((x,) + others)[0]

    def near(x):
        return [swap_t(x, k) for k in range(1, nt)] if nt != 4 else [swap_t(x, 1), swap_t(x, 2)]

    def far(x, others):
        mid = x.shape[0] // 2
        return [] if nt != 4 else [swap_t(others[0][:mid], 2), swap_t(others[1][mid:], 1)]

    width = norm_gains.shape[2]
    wrows, wcols = query_weight.shape[1:]
    high = lax.reduce_precision(norm_gains[0], 8, 7)
    middle = lax.reduce_precision(norm_gains[0] - high, 8, 7)
    gain_rows = jnp.stack([high, middle, norm_gains[0] - high - middle]).astype(bf16).reshape(3, 2 * width)
    own = jnp.concatenate(
        [
            query_weight[0].astype(bf16),
            keyval_weight[0].astype(bf16),
            jnp.pad(gain_rows, ((0, 13), (0, wcols - 2 * width))),
            output_weight[0].T.astype(bf16),
        ],
        axis=0,
    )
    own_z = spread_z(own)
    half = expert_in.shape[1] // 2
    groups = [[2 * i + c for i in range(nz)] for c in range(2)]

    def cut(quarters):
        return quarters[0] * half // 4, quarters[1] * half // 4

    def shard(a, b, *ready):
        masters = lax.optimization_barrier((expert_in, expert_down, own, *ready))[:2]

        def low(side):
            return jnp.concatenate(
                [lax.dynamic_slice_in_dim(w[0], side * half + a, b - a, 0).astype(bf16) for w in masters], axis=1
            )

        return jnp.stack([low(core), swap_core(low(1 - core))])

    spans = [cut(quarters) for quarters in GATHERS]
    spans = [(a, b) for a, b in spans if a < b]
    shards = [shard(*spans[0])]
    for a, b in spans[1:]:
        shards.append(shard(a, b, own_z[1]))
    own_z[1:], shards = lax.optimization_barrier((own_z[1:], shards))
    column = jnp.stack(own_z)
    held = {}
    for (a, b), part in zip(spans, shards):
        whole = lax.all_gather(after(part, column), "dp", axis=0, tiled=False, axis_index_groups=groups)
        held.update({i: (whole, i - a) for i in range(a, b)})
    pieces = spread_t(column[:, : 2 * wrows + 16])
    pieces_out = spread_t(after(column[:, 2 * wrows + 16 :], pieces[nt - 1]))
    dm_near = near(after(cotangent, *pieces_out[1:nt]))
    pieces = pieces + [swap_core(piece) for piece in pieces]
    pieces_out = pieces_out + [swap_core(piece) for piece in pieces_out]

    ids = t * 2 * half + jnp.arange(2 * half, dtype=jnp.int32)
    chosen = routes[0].T[None, :, :] == ids[:, None, None]
    c_all = jnp.sum(jnp.where(chosen, gate_weights[0].T[None, :, :], 0.0), axis=1)
    c_mine = lax.dynamic_slice_in_dim(c_all, core * half, half, 0)
    c_got = swap_core(lax.dynamic_slice_in_dim(c_all, (1 - core) * half, half, 0))
    c_both = jnp.stack([c_mine, c_got], axis=1).reshape(half, 2, nt, rows)
    c_both = jnp.take(c_both, jnp.arange(nt, dtype=jnp.int32) ^ t, axis=2)
    subs = 2 * nt * rows // SUB
    c_rows = c_both.reshape(half * subs, SUB)
    taken = c_rows != 0.0
    upto = lax.broadcasted_iota(jnp.int32, (SUB, SUB), 0) <= lax.broadcasted_iota(jnp.int32, (SUB, SUB), 1)
    rank = dot(taken.astype(bf16), upto.astype(bf16))
    pos = jnp.where(taken, rank - 1.0, -1.0)
    sizes = (rank[:, SUB - 1].astype(jnp.int32).reshape(half, subs) + 15) // 16 * 16
    offs = jnp.pad(jnp.cumsum(sizes, axis=1), ((0, 0), (1, 0)))
    pos_columns = pos.reshape(half, subs * SUB).T

    sequence = after(tokens, offs, pos, c_rows, pos_columns)
    if sharers > 1:
        seq_groups = [list(range(i, i + sharers)) for i in range(0, nt, sharers)]
        sequence = lax.all_gather(tokens, "tensor", axis=0, tiled=True, axis_index_groups=seq_groups)
    first_row = (t % sharers) * rows
    q, kv, o, lse, qkv_weights, gains = attend_forward((nz, nt), place, sequence, pieces)
    s1, n2, out_weight = attend_out((nz, nt), place, sequence, gains, o, pieces_out)
    if sharers > 1:
        s1 = lax.dynamic_slice_in_dim(s1, first_row, rows, 0)
        n2 = lax.dynamic_slice_in_dim(n2, first_row, rows, 0)

    n2_near = near(n2)
    n2_own = [n2] + n2_near + far(n2, n2_near)
    dm_near = list(lax.optimization_barrier((*dm_near, *n2_near))[: len(dm_near)])
    dm_own = [cotangent] + dm_near + far(cotangent, dm_near)
    dm_parts = dm_own + [swap_core(part) for part in dm_own]
    n2_parts = n2_own + [swap_core(part) for part in n2_own]
    slots = gather(n2_parts, dm_parts, offs.reshape(-1), pos, c_rows)
    m_parts, d_parts, expert_grads = [], [], []
    for calls in CALLS:
        start, stop = cut((calls[0][0], calls[-1][1]))
        gw = None
        for quarters in calls:
            a, b = cut(quarters)
            if a == b:
                continue
            arrays, sources = [], []
            for i in range(a, b):
                array, index = held[i]
                if not arrays or arrays[-1] is not array:
                    arrays.append(array)
                sources.append((len(arrays) - 1, index))
            m_part, d_part, gw = experts_step(
                place, slots, offs, a, arrays, tuple(sources), gw, a - start, stop - start
            )
            m_parts.append((m_part, a))
            d_parts.append((d_part, a))
        grad = lax.psum_scatter(gw, "dp", scatter_dimension=0, tiled=False, axis_index_groups=groups)
        expert_grads.append((start, grad))

    def both_cores(own, other):
        both = [
            own[k * rows : (k + 1) * rows].astype(f32) + other[k * rows : (k + 1) * rows].astype(f32)
            for k in range(nt)
        ]
        return both[0], [part.astype(bf16) for part in both[1:]]

    def to_tokens(parts, last=()):
        if nt != 4:
            return [swap_t(parts[k], k) for k in range(1, nt)], parts[nt - 1]
        mid = parts[3].shape[0] // 2
        by_x, by_y = swap_t(parts[3][:mid], 1), swap_t(parts[3][mid:], 2)
        x_first, y_last = swap_t(parts[1][:mid], 1), swap_t(parts[2][mid:], 2)
        by_x, by_y, *_ = lax.optimization_barrier((by_x, by_y, *last))
        x_part = (parts[1][mid:].astype(f32) + by_y.astype(f32)).astype(bf16)
        y_part = (parts[2][:mid].astype(f32) + by_x.astype(f32)).astype(bf16)
        return [x_first, swap_t(x_part, 1), swap_t(y_part, 2), y_last], y_part

    def collect(total, received):
        if nt != 4:
            for part in received:
                total = total + part.astype(f32)
            return total
        x_first, x_last, y_first, y_last = (part.astype(f32) for part in received)
        return total + jnp.concatenate([x_first + y_first, x_last + y_last], axis=0)

    (d_other,) = scatter(offs, pos_columns, d_parts, (1,))
    (d_own,) = scatter(offs, pos_columns, d_parts, (0,))
    d_own, d_sent = both_cores(d_own, swap_core(d_other))
    d_received, d_last = to_tokens([None] + d_sent)
    dn2 = collect(d_own, d_received)
    m_pos = after(pos_columns, d_last)
    m_other, m_own = scatter(offs, m_pos, m_parts, (1, 0))
    m_other = jnp.concatenate([swap_core(m_other[k * rows : (k + 1) * rows]) for k in range(nt)])
    m_own, m_sent = both_cores(m_own, m_other)

    grad = cotangent.astype(f32)
    inverse = rms_scale(s1)
    unit = s1 * inverse
    gain_two = jnp.sum(dn2 * unit, axis=0)
    scaled = dn2 * gains[1]
    gs1 = grad + inverse * (scaled - unit * jnp.mean(scaled * unit, axis=-1, keepdims=True))

    da, *m_sent = lax.optimization_barrier((gs1.astype(bf16), *m_sent))
    m_received = [swap_t(part, k + 1) for k, part in enumerate(m_sent)]
    if sharers > 1:
        da = lax.all_gather(da, "tensor", axis=0, tiled=True, axis_index_groups=seq_groups)
    dn1, grads_own, grads_other = attend_backward(
        (nz, nt), place, sequence, da, gains, gain_two[None] * sharers, q, kv, o, lse, qkv_weights, out_weight
    )
    block_out = m_own + s1
    for part in m_received:
        block_out = block_out + part.astype(f32)
    if sharers > 1:
        dn1 = lax.dynamic_slice_in_dim(dn1, first_row, rows, 0)

    stream = tokens.astype(f32)
    inverse = rms_scale(stream)
    unit = stream * inverse
    scaled = dn1 * gains[0]
    input_grad = gs1 + inverse * (scaled - unit * jnp.mean(scaled * unit, axis=-1, keepdims=True))

    grads_other = after(grads_other, *m_received)
    both = (grads_own.astype(f32) + swap_core(grads_other).astype(f32)).astype(bf16)
    received, _ = to_tokens([both[k] for k in range(nt)])

    states = [expert_in, expert_in_first, expert_in_second, expert_down, expert_down_first, expert_down_second]
    experts_new = None
    for start, got in expert_grads[:-1]:
        experts_new = adam_experts(place, start, got, swap_core(got[1]), states, experts_new)
    block_out, experts_new, received = lax.optimization_barrier((block_out, experts_new, received))

    total = collect(both[0].astype(f32), received)
    owned = total[0]
    sent = [total[j].astype(bf16) for j in range(1, nz)]
    received = [swap_z(part, j + 1) for j, part in enumerate(sent)]
    for start, got in expert_grads[-1:]:
        got = after(got, *sent, *experts_new)
        experts_new = adam_experts(place, start, got, swap_core(got[1]), states, experts_new)
    received, experts_new = lax.optimization_barrier((received, experts_new))
    for part in received:
        owned = owned + part.astype(f32)
    owned = owned * (1.0 / sharers)
    query_grad, keyval_grad, out_grad = (owned[i * wrows : (i + 1) * wrows] for i in range(3))
    gg = owned[3 * wrows : 3 * wrows + 2 * nt].reshape(1, 2, D)
    gg = lax.dynamic_slice_in_dim(gg, (place_dp * nt + t) * width, width, 2)

    gains_new = adam_change(norm_gains_first, norm_gains_second, gg)
    query_new = adam_update(query_weight, query_first, query_second, query_grad[None], WEIGHT_DECAY)
    keyval_new = adam_update(keyval_weight, keyval_first, keyval_second, keyval_grad[None], WEIGHT_DECAY)
    output_new = adam_update(output_weight, output_first, output_second, out_grad.T[None], WEIGHT_DECAY)
    return (block_out, input_grad) + gains_new + query_new + keyval_new + output_new + tuple(experts_new)


def solution(mesh):
    rows = P(("dp", "tensor"), None)
    by_rows = P(None, "dp", None)
    gains = P(None, None, ("dp", "tensor"))
    proj = P(None, "dp", "tensor")
    out_proj = P(None, "tensor", "dp")
    expert = P(None, "tensor", "dp", None)
    params = (gains,) * 3 + (proj,) * 6 + (out_proj,) * 3 + (expert,) * 6
    return jax.shard_map(
        functools.partial(on_device, mesh.shape["dp"], mesh.shape["tensor"]),
        mesh=mesh,
        in_specs=(rows, rows, by_rows, by_rows) + params,
        out_specs=(rows, rows) + params,
        check_vma=False,
    )
```

time: 705 us -> 557 us (0.79); the launches traced: 700 us -> 563 us
  waiting for transfers between devices: 238 us -> 155 us
  Pallas kernels: 277 us -> 217 us
  starting transfers between devices: 69.1 us -> 97.2 us
  other arithmetic: 56.4 us -> 44.5 us
  local copies, waits for them, and re-layouts: 45.3 us -> 34 us
    ppermute x24 -> x29, waiting for transfers between devices: 195 us -> 123 us  [swap_t(): return lax.ppermute(x, 'tensor', [(i, i ^ k) for i in range(nt)])]
    pallas_call x2 -> x10, Pallas kernels: 218 us -> 161 us  [the longest x3 71.2 us: experts_step(): pl.pallas_call(functools.partial(experts_kernel, first, subs, sources, le...]
    ppermute x24 -> x29, starting transfers between devices: 28.2 us -> 70.6 us  [swap_t(): return lax.ppermute(x, 'tensor', [(i, i ^ k) for i in range(nt)])]
    ppermute x12 -> x6, waiting for transfers between devices: 35.4 us -> 5.74 us  [swap_z(): return lax.ppermute(x, 'dp', [(i, i ^ 2 * j) for i in range(ndp)])]
    ppermute x12 -> x6, starting transfers between devices: 35.5 us -> 17.3 us  [swap_z(): return lax.ppermute(x, 'dp', [(i, i ^ 2 * j) for i in range(ndp)])]
    all_gather x2 -> x3, waiting for transfers between devices: 0.02 us -> 14.6 us  [on_device(): lax.all_gather(after(part, column), 'dp', axis=0, tiled=False, axis_index...]
    all_gather x2 -> x0, local copies, waits for them, and re-layouts: 12.9 us -> none  [on_device(): lax.all_gather(shard[i * per:(i + 1) * per], 'dp', axis=0, tiled=False, a...]
    sub x4 -> x2, other arithmetic: 13.2 us -> 2.07 us  [adam_update(): master - LEARN_RATE * (first_fixed / (jnp.sqrt(second_fixed) + ADAM_EPS)...]
  transfers between devices with their start and end apart: 64 -> 70, of which waited for: 22 -> 23; matrix products, arithmetic and copies ran while one was open for 10% -> 10% of each run, Pallas kernels for 40% -> 39%
where the time goes in v2:
time: 557 us; the launch traced here: 563 us
  Pallas kernels  217 us (39%)
  waiting for transfers between devices  155 us (28%)
  starting transfers between devices  97.2 us (17%)
  other arithmetic  44.5 us (8%)
  local copies, waits for them, and re-layouts  34 us (6%)
  between operations  15.2 us (3%)
    ppermute x29, waiting for transfers between devices, swap_t(): return lax.ppermute(x, 'tensor', [(i, i ^ k) for i in range(nt)])  123 us
    pallas_call x3, Pallas kernels, experts_step(): pl.pallas_call(functools.partial(experts_kernel, first, subs, sources, le...  71.2 us
    ppermute x29, starting transfers between devices, swap_t(): return lax.ppermute(x, 'tensor', [(i, i ^ k) for i in range(nt)])  70.6 us
    pallas_call x3, Pallas kernels, scatter(): pl.pallas_call(functools.partial(scatter_kernel, halves, sources, experts...  47.5 us
    pallas_call x1, Pallas kernels, attend_backward(): pl.pallas_call(functools.partial(attend_backward_kernel, nz, nt), out_sha...  34 us
    pallas_call x1, Pallas kernels, attend_forward(): pl.pallas_call(functools.partial(attend_forward_kernel, nz, nt), out_shap...  21.9 us
    pallas_call x2, Pallas kernels, adam_experts(): pl.pallas_call(functools.partial(adam_kernel, per), grid_spec=pltpu.Prefe...  19.7 us
    pallas_call x1, Pallas kernels, gather(): pl.pallas_call(functools.partial(gather_kernel, tuple(starts), experts),...  18.9 us
  transfers between devices with their start and end apart: 70, of which 23 were waited for; matrix products, arithmetic and copies ran while one was open for 10% of the time, Pallas kernels for 39%

profile of v2, /device:TPU:0, one launch (start us, length us, event | category | flops | bytes accessed | tf_op | source)
XLA Modules:
  0.0 562.8 jit_solution(16181643959896015275)
XLA Ops:
  11.1 3.0 collective-permute-start.1
  14.2 2.6 collective-permute-start.2
  16.7 2.5 fusion.9
  21.0 2.1 collective-permute-done.1
  23.7 1.7 fusion.18
  29.3 2.4 pad_maximum_fusion
  34.4 2.5 collective-permute-start.9
  40.0 11.0 %collective-permute-done.9.rest_3_ = bf16[4,272,256]{2,1,0:T(8,128)(2,1)S(1)} collective-permute-done((bf16[4,272,256]{2,1,0:T(8,128)(2,1)S(1)}, bf16[4,272,256]{2,1,0:T(8,128)(2,1)S(1)}, u32[]{:S(2)}, u32[]{:S(2)}) %collective-permute-start.9) | collective-permute-done | bytes 557088 | tf_op jit(solution)/shard_map/ppermute | solution.py:839
  51.0 1.5 collective-permute-start.14
  52.5 10.6 %collective-permute-done.7.rest_1_ = bf16[4,272,256]{2,1,0:T(8,128)(2,1)} collective-permute-done((bf16[4,272,256]{2,1,0:T(8,128)(2,1)S(1)}, bf16[4,272,256]{2,1,0:T(8,128)(2,1)}, u32[]{:S(2)}, u32[]{:S(2)}) %collective-permute-start.7) | collective-permute-done | bytes 557088 | tf_op jit(solution)/shard_map/ppermute | solution.py:839
  64.8 2.4 collective-permute-start.16
  67.8 10.4 %collective-permute-done.15.rest_2_ = bf16[4,128,256]{2,1,0:T(8,128)(2,1)} collective-permute-done((bf16[4,128,256]{2,1,0:T(8,128)(2,1)S(1)}, bf16[4,128,256]{2,1,0:T(8,128)(2,1)}, u32[]{:S(2)}, u32[]{:S(2)}) %collective-permute-start.15) | collective-permute-done | bytes 262176 | tf_op jit(solution)/shard_map/ppermute | solution.py:839
  79.5 2.0 copy.82
  81.8 1.6 collective-permute-start.30
  83.4 21.9 %attend_forward.1 = (bf16[512,1024]{1,0:T(8,128)(2,1)S(1)}, bf16[512,1024]{1,0:T(8,128)(2,1)S(1)}, bf16[512,1024]{1,0:T(8,128)(2,1)S(1)}, f32[512,128]{1,0:T(8,1...) custom-call(s32[3]{0:T(128)S(1)} %pad_add_fusion.place_ref, bf16[512,1024]{1,0:T(8,128)(2,1)S(1)} %copy-done, ...), custom_call_target="tpu_custom_call" | custom-call | flops 1 | bytes 1 | tf_op jit(solution)/shard_map/attend_forward/pallas_call | solution.py:221
  105.3 2.0 copy-done.5
  107.9 3.9 attend_out.1
  112.4 1.5 collective-permute-start.22
  114.4 19.1 %collective-permute-done.31.rest_12_ = bf16[512,1024]{1,0:T(8,128)(2,1)} collective-permute-done((bf16[512,1024]{1,0:T(8,128)(2,1)S(1)}, bf16[512,1024]{1,0:T(8,128)(2,1)}, u32[]{:S(2)}, u32[]{:S(2)}) %collective-permute-start.31) | collective-permute-done | bytes 1048608 | tf_op jit(solution)/shard_map/ppermute | solution.py:839
  133.5 3.1 collective-permute-done.21.rest_1_
  136.7 18.0 %collective-permute-done.22.rest_2_ = bf16[512,1024]{1,0:T(8,128)(2,1)S(1)} collective-permute-done((bf16[512,1024]{1,0:T(8,128)(2,1)S(1)}, bf16[512,1024]{1,0:T(8,128)(2,1)S(1)}, u32[]{:S(2)}, u32[]{:S(2)}) %collective-permute-start.22) | collective-permute-done | bytes 1048608 | tf_op jit(solution)/shard_map/ppermute | solution.py:839
  158.4 1.6 collective-permute-start.23
  160.1 1.6 collective-permute-start.24
  161.7 9.4 %collective-permute-done.32.rest_13_ = bf16[256,1024]{1,0:T(8,128)(2,1)S(1)} collective-permute-done((bf16[256,1024]{1,0:T(8,128)(2,1)S(1)}, bf16[256,1024]{1,0:T(8,128)(2,1)S(1)}, u32[]{:S(2)}, u32[]{:S(2)}) %collective-permute-start.32) | collective-permute-done | bytes 524320 | tf_op jit(solution)/shard_map/ppermute | solution.py:839
  171.0 1.7 collective-permute-done.33.rest_14_
  173.2 6.9 %collective-permute-done.23.rest_3_ = bf16[256,1024]{1,0:T(8,128)(2,1)S(1)} collective-permute-done((bf16[256,1024]{1,0:T(8,128)(2,1)S(1)}, bf16[256,1024]{1,0:T(8,128)(2,1)S(1)}, u32[]{:S(2)}, u32[]{:S(2)}) %collective-permute-start.23) | collective-permute-done | bytes 524320 | tf_op jit(solution)/shard_map/ppermute | solution.py:839
  184.5 3.1 collective-permute-done.29.rest_9_
  188.1 18.9 %gather_rows.1 = (bf16[4,2560,1024]{2,1,0:T(8,128)(2,1)}, bf16[4,2560,1024]{2,1,0:T(8,128)(2,1)}, f32[4,2560,128]{2,1,0:T(8,128)}) custom-call(s32[68]{0:T(128)} %reshape.277.offs_ref, f32[64,256]{1,0:T(8,128)} %copy-done.40, f32[64,256]{1,0:T(8,128)} %copy-done.39, bf16[512,1024]{1,0:T(8,128)(2,1)} %copy-done.11, bf16[512,1024]{1,0:T(8,128)(2,1)} %copy-done.29, ...), custom_call_target="tpu_custom_call" | custom-call | flops 1 | bytes 1 | tf_op jit(solution)/shard_map/gather_rows/pallas_call | solution.py:508
  207.0 33.0 %experts.3 = (bf16[2,3072,1024]{2,1,0:T(8,128)(2,1)}, bf16[2,3072,1024]{2,1,0:T(8,128)(2,1)}, bf16[4,2,2,192,1024]{4,3,2,1,0:T(8,128)(2,1)}) custom-call(s32[3]{0:T(128)} %copy-done.17, s32[68]{0:T(128)} %reshape.277.offs_ref, bf16[4,2560,1024]{2,1,0:T(8,128)(2,1)} %get-tuple-element.122.n2_ref, bf16[4,2560,1024]{2,1,0:T(8,128)(2,1)} %get-tuple-element.123.dm_ref, ...), custom_call_target="tpu_custom_call" | custom-call | flops 1 | bytes 1 | tf_op jit(solution)/shard_map/experts/pallas_call | solution.py:652
  240.1 23.5 %experts.4 = (bf16[1,3072,1024]{2,1,0:T(8,128)(2,1)}, bf16[1,3072,1024]{2,1,0:T(8,128)(2,1)}, bf16[4,2,2,192,1024]{4,3,2,1,0:T(8,128)(2,1)}) custom-call(s32[3]{0:T(128)} %copy-done.17, s32[68]{0:T(128)} %reshape.277.offs_ref, bf16[4,2560,1024]{2,1,0:T(8,128)(2,1)} %get-tuple-element.122.n2_ref, bf16[4,2560,1024]{2,1,0:T(8,128)(2,1)} %get-tuple-element.123.dm_ref, ...), custom_call_target="tpu_custom_call" | custom-call | flops 1 | bytes 1 | tf_op jit(solution)/shard_map/experts/pallas_call | solution.py:652
  263.6 14.6 %all-gather.11.cloned.1.call-done = bf16[8,1,192,1024]{3,2,1,0:T(8,128)(2,1)} async-done(((bf16[2,1,192,1024]{3,2,1,0:T(8,128)(2,1)}), bf16[8,1,192,1024]{3,2,1,0:T(8,128)(2,1)}) %all-gather.11.cloned.1.call-update) | async-done | bytes 3145744 | tf_op jit(solution)/shard_map/all_gather | solution.py:897
  278.2 14.7 %experts.5 = (bf16[1,3072,1024]{2,1,0:T(8,128)(2,1)}, bf16[1,3072,1024]{2,1,0:T(8,128)(2,1)}, bf16[4,2,2,192,1024]{4,3,2,1,0:T(8,128)(2,1)}) custom-call(s32[3]{0:T(128)} %copy-done.17, s32[68]{0:T(128)} %reshape.277.offs_ref, bf16[4,2560,1024]{2,1,0:T(8,128)(2,1)} %get-tuple-element.122.n2_ref, ...), custom_call_target="tpu_custom_call", output_to_operand_aliasing={{2}: (6, {})} | custom-call | flops 1 | bytes 1 | tf_op jit(solution)/shard_map/experts/pallas_call | solution.py:652
  292.8 12.8 %scatter_rows.4 = bf16[2048,1024]{1,0:T(8,128)(2,1)} custom-call(s32[68]{0:T(128)} %reshape.277.offs_ref, f32[4096,4]{1,0:T(8,128)} %bitcast.145, bf16[2,3072,1024]{2,1,0:T(8,128)(2,1)} %get-tuple-element.127.rest_0_, bf16[1,3072,1024]{2,1,0:T(8,128)(2,1)} %get-tuple-element.130.rest_1_, bf16[1,3072,1024]{2,1,0:T(8,128)(2,1)} %get-tuple-element.134.rest_2_), custom_call_target="tpu_custom_call" | custom-call | flops 1 | bytes 1 | tf_op jit(solution)/shard_map/scatter_rows/pallas_call | solution.py:734
  305.7 2.9 collective-permute-start.39
  308.7 12.7 %scatter_rows.3 = bf16[2048,1024]{1,0:T(8,128)(2,1)} custom-call(s32[68]{0:T(128)} %reshape.277.offs_ref, f32[4096,4]{1,0:T(8,128)} %bitcast.146, bf16[2,3072,1024]{2,1,0:T(8,128)(2,1)} %get-tuple-element.127.rest_0_, bf16[1,3072,1024]{2,1,0:T(8,128)(2,1)} %get-tuple-element.130.rest_1_, bf16[1,3072,1024]{2,1,0:T(8,128)(2,1)} %get-tuple-element.134.rest_2_), custom_call_target="tpu_custom_call" | custom-call | flops 1 | bytes 1 | tf_op jit(solution)/shard_map/scatter_rows/pallas_call | solution.py:734
  321.4 4.3 add_convert_fusion.4
  325.8 1.9 collective-permute-start.40
  327.7 38.1 %collective-permute-start.41 = (bf16[256,1024]{1,0:T(8,128)(2,1)S(1)}, bf16[256,1024]{1,0:T(8,128)(2,1)S(1)}, u32[]{:S(2)}, u32[]{:S(2)}) collective-permute-start(bf16[256,1024]{1,0:T(8,128)(2,1)S(1)} %get-tuple-element.321), channel_id=1, source_target_pairs={{0,2},{1,3},{2,0},{3,1},{4,6},{5,7},{6,4},{7,5},{8,10},{9,11},{10,... | collective-permute-start | bytes 1572872 | tf_op jit(solution)/shard_map/ppermute | solution.py:839
  369.2 9.5 %collective-permute-done.41 = bf16[256,1024]{1,0:T(8,128)(2,1)S(1)} collective-permute-done((bf16[256,1024]{1,0:T(8,128)(2,1)S(1)}, bf16[256,1024]{1,0:T(8,128)(2,1)S(1)}, u32[]{:S(2)}, u32[]{:S(2)}) %collective-permute-start.41) | collective-permute-done | bytes 524320 | tf_op jit(solution)/shard_map/ppermute | solution.py:839
  379.7 2.0 collective-permute-start.44
  382.8 22.0 %scatter_rows.5 = (bf16[2048,1024]{1,0:T(8,128)(2,1)}, bf16[2048,1024]{1,0:T(8,128)(2,1)}) custom-call(s32[68]{0:T(128)} %reshape.277.offs_ref, f32[4096,4]{1,0:T(8,128)} %bitcast.147, bf16[2,3072,1024]{2,1,0:T(8,128)(2,1)} %get-tuple-element.137.rest_0_, bf16[1,3072,1024]{2,1,0:T(8,128)(2,1)} %get-tuple-element.138.rest_1_, ...), custom_call_target="tpu_custom_call" | custom-call | flops 1 | bytes 1 | tf_op jit(solution)/shard_map/scatter_rows/pallas_call | solution.py:734
  404.8 3.6 fusion.56
  411.8 2.6 multiply_reduce_fusion
  415.8 1.6 copy-done.27
  417.4 2.8 add_convert_fusion.1
  420.2 2.1 collective-permute-start.50
  422.3 2.0 collective-permute-start.51
  424.3 34.0 %attend_backward.1 = (f32[512,1024]{1,0:T(8,128)}, bf16[4,4,400,256]{3,2,1,0:T(8,128)(2,1)}, bf16[4,4,400,256]{3,2,1,0:T(8,128)(2,1)}) custom-call(s32[3]{0:T(128)S(1)} %copy-done.18, bf16[512,1024]{1,0:T(8,128)(2,1)S(1)} %copy-done, bf16[512,1024]{1,0:T(8,128)(2,1)S(1)} %fusion.50.da_ref, f32[2,1024]{1,0:T(2,128)S(1)} %get-tuple-element.115.gains_ref, ...), custom_call_target="tpu_custom_call" | custom-call | flops 1 | bytes 1 | tf_op jit(solution)/shard_map/attend_backward/pallas_call | solution.py:388
  458.3 12.1 %collective-permute-done.51 = bf16[512,1024]{1,0:T(8,128)(2,1)S(1)} collective-permute-done((bf16[512,1024]{1,0:T(8,128)(2,1)}, bf16[512,1024]{1,0:T(8,128)(2,1)S(1)}, u32[]{:S(2)}, u32[]{:S(2)}) %collective-permute-start.51) | collective-permute-done | bytes 1048608 | tf_op jit(solution)/shard_map/ppermute | solution.py:839
  471.4 6.2 %collective-permute-done.54 = bf16[4,4,400,256]{3,2,1,0:T(8,128)(2,1)S(1)} collective-permute-done((bf16[4,4,400,256]{3,2,1,0:T(8,128)(2,1)}, bf16[4,4,400,256]{3,2,1,0:T(8,128)(2,1)S(1)}, u32[]{:S(2)}, u32[]{:S(2)}) %collective-permute-start.54) | collective-permute-done | bytes 3276832 | tf_op jit(solution)/shard_map/ppermute | solution.py:833
  477.6 2.9 add_convert_fusion
  480.5 1.7 copy-done.21
  485.8 1.8 collective-permute-start.55
  487.9 7.7 %collective-permute-done.56 = bf16[2,400,256]{2,1,0:T(8,128)(2,1)} collective-permute-done((bf16[2,400,256]{2,1,0:T(8,128)(2,1)S(1)}, bf16[2,400,256]{2,1,0:T(8,128)(2,1)}, u32[]{:S(2)}, u32[]{:S(2)}) %collective-permute-start.56) | collective-permute-done | bytes 409632 | tf_op jit(solution)/shard_map/ppermute | solution.py:839
  495.6 1.5 collective-permute-done.57
  498.6 2.3 fusion.7
  501.5 1.7 collective-permute-start.59
  503.2 5.4 fusion.5
  508.7 9.9 %adam_experts.2 = (f32[1,8,128,1024]{3,2,1,0:T(8,128)}, f32[1,8,128,1024]{3,2,1,0:T(8,128)}, f32[1,8,128,1024]{3,2,1,0:T(8,128)}, f32[1,8,64,1024]{3,2,1,0:T(8,1...) custom-call(s32[3]{0:T(128)} %copy-done.17, bf16[2,2,192,1024]{3,2,1,0:T(8,128)(2,1)} %bitcast.149, ...), custom_call_target="tpu_custom_call" | custom-call | flops 1 | bytes 1 | tf_op jit(solution)/shard_map/adam_experts/pallas_call | solution.py:775
  523.7 9.3 %collective-permute-start.61 = (bf16[400,256]{1,0:T(8,128)(2,1)S(1)}, bf16[400,256]{1,0:T(8,128)(2,1)}, u32[]{:S(2)}, u32[]{:S(2)}) collective-permute-start(bf16[400,256]{1,0:T(8,128)(2,1)S(1)} %get-tuple-element.325), channel_id=1, source_target_pairs={{0,8},{4,12},{8,0},{12,4},{16,24},{20,28},{24,16},{28,20},{1,9},{5... | collective-permute-start | bytes 614408 | tf_op jit(solution)/shard_map/ppermute | solution.py:836
  533.0 2.4 collective-permute-start.63
  536.6 9.9 %adam_experts.3 = (f32[1,8,128,1024]{3,2,1,0:T(8,128)}, f32[1,8,128,1024]{3,2,1,0:T(8,128)}, f32[1,8,128,1024]{3,2,1,0:T(8,128)}, f32[1,8,64,1024]{3,2,1,0:T(8,1...) custom-call(s32[3]{0:T(128)} %copy-done.17, ...), custom_call_target="tpu_custom_call", output_to_operand_aliasing={{0}: (9, {}), {1}: (10, {}), {2}: (11, {}), {3}: (12, {}), ... | custom-call | flops 1 | bytes 1 | tf_op jit(solution)/shard_map/adam_experts/pallas_call | solution.py:775
  546.5 3.2 collective-permute-done.62
  553.4 2.0 multiply_subtract_fusion.1
  (312 shorter events, 57.9 us)
Async XLA Ops:
  7.2 199.8 %all-gather.7.cloned.1.call-start = ((), (), s32[]{:S(2)}) async-start(), calls=%async_computation.4 | async-start | bytes 7864320 | tf_op jit(solution)/shard_map/all_gather | solution.py:897
  11.1 11.9 %collective-permute-start.1 = (bf16[400,256]{1,0:T(8,128)(2,1)}, bf16[400,256]{1,0:T(8,128)(2,1)S(1)}, u32[]{:S(2)}, u32[]{:S(2)}) collective-permute-start(bf16[400,256]{1,0:T(8,128)(2,1)} %get-tuple-element.330), channel_id=1, source_target_pairs={{0,8},{4,12},{8,0},{12,4},{16,24},{20,28},{24,16},{28,20},{1,9},{5... | collective-permute-start | bytes 614408 | tf_op jit(solution)/shard_map/ppermute | solution.py:836
  14.2 18.0 %collective-permute-start.2 = (bf16[400,256]{1,0:T(8,128)(2,1)}, bf16[400,256]{1,0:T(8,128)(2,1)}, u32[]{:S(2)}, u32[]{:S(2)}) collective-permute-start(bf16[400,256]{1,0:T(8,128)(2,1)} %get-tuple-element.330), channel_id=1, source_target_pairs={{0,16},{4,20},{8,24},{12,28},{16,0},{20,4},{24,8},{28,12},{1,17},{... | collective-permute-start | bytes 614408 | tf_op jit(solution)/shard_map/ppermute | solution.py:836
  16.7 15.4 %collective-permute-start.3 = (bf16[400,256]{1,0:T(8,128)(2,1)}, bf16[400,256]{1,0:T(8,128)(2,1)}, u32[]{:S(2)}, u32[]{:S(2)}) collective-permute-start(bf16[400,256]{1,0:T(8,128)(2,1)} %get-tuple-element.330), channel_id=1, source_target_pairs={{0,24},{4,28},{8,16},{12,20},{16,8},{20,12},{24,0},{28,4},{1,25},{... | collective-permute-start | bytes 614408 | tf_op jit(solution)/shard_map/ppermute | solution.py:836
  21.0 8.3 %collective-permute-start.4 = (bf16[2,192,1024]{2,1,0:T(8,128)(2,1)}, bf16[2,192,1024]{2,1,0:T(8,128)(2,1)}, u32[]{:S(2)}, u32[]{:S(2)}) collective-permute-start(bf16[2,192,1024]{2,1,0:T(8,128)(2,1)} %pad_maximum_fusion.2), channel_id=1, source_target_pairs={{0,4},{4,0},{8,12},{12,8},{16,20},{20,16},{24,28},{28,24},{1,5},{5... | collective-permute-start | bytes 2359304 | tf_op jit(solution)/shard_map/ppermute | solution.py:833
  33.3 206.8 %all-gather.9.cloned.1.call-start = ((), (), s32[]{:S(2)}) async-start(), calls=%async_computation.5 | async-start | bytes 3932160 | tf_op jit(solution)/shard_map/all_gather | solution.py:897
  34.1 244.1 %all-gather.11.cloned.1.call-start = ((), (), s32[]{:S(2)}) async-start(), calls=%async_computation.6 | async-start | bytes 3932160 | tf_op jit(solution)/shard_map/all_gather | solution.py:897
  34.4 16.5 %collective-permute-start.9 = (bf16[4,272,256]{2,1,0:T(8,128)(2,1)S(1)}, bf16[4,272,256]{2,1,0:T(8,128)(2,1)S(1)}, u32[]{:S(2)}, u32[]{:S(2)}) collective-permute-start(bf16[4,272,256]{2,1,0:T(8,128)(2,1)S(1)} %slice.226.rest_0_), channel_id=1, source_target_pairs={{0,3},{1,2},{2,1},{3,0},{4,7},{5,6},{6,5},{7,4},{8,11},{9,10},{10,... | collective-permute-start | bytes 1671176 | tf_op jit(solution)/shard_map/ppermute | solution.py:839
  37.0 26.1 %collective-permute-start.7 = (bf16[4,272,256]{2,1,0:T(8,128)(2,1)S(1)}, bf16[4,272,256]{2,1,0:T(8,128)(2,1)}, u32[]{:S(2)}, u32[]{:S(2)}) collective-permute-start(bf16[4,272,256]{2,1,0:T(8,128)(2,1)S(1)} %slice.226.rest_0_), channel_id=1, source_target_pairs={{0,1},{1,0},{2,3},{3,2},{4,5},{5,4},{6,7},{7,6},{8,9},{9,8},{10,11... | collective-permute-start | bytes 1671176 | tf_op jit(solution)/shard_map/ppermute | solution.py:839
  37.5 25.6 %collective-permute-start.8 = (bf16[4,272,256]{2,1,0:T(8,128)(2,1)S(1)}, bf16[4,272,256]{2,1,0:T(8,128)(2,1)}, u32[]{:S(2)}, u32[]{:S(2)}) collective-permute-start(bf16[4,272,256]{2,1,0:T(8,128)(2,1)S(1)} %slice.226.rest_0_), channel_id=1, source_target_pairs={{0,2},{1,3},{2,0},{3,1},{4,6},{5,7},{6,4},{7,5},{8,10},{9,11},{10,... | collective-permute-start | bytes 1671176 | tf_op jit(solution)/shard_map/ppermute | solution.py:839
  38.1 459.1 %reduce-scatter.3.cloned.1.call-start = ((), (), s32[]{:S(2)}) async-start(), calls=%async_computation.2 | async-start | bytes 7864320 | tf_op jit(solution)/shard_map/reduce_scatter | solution.py:959
  38.4 25.2 %collective-permute-start = (f32[4,2048]{1,0:T(4,128)S(1)}, f32[4,2048]{1,0:T(4,128)S(1)}, u32[]{:S(2)}, u32[]{:S(2)}) collective-permute-start(f32[4,2048]{1,0:T(4,128)S(1)} %get-tuple-element.332), channel_id=1, source_target_pairs={{0,4},{4,0},{8,12},{12,8},{16,20},{20,16},{24,28},{28,24},{1,5},{5... | collective-permute-start | bytes 98312 | tf_op jit(solution)/shard_map/ppermute | solution.py:833
  38.4 26.3 %collective-permute-start.10 = (bf16[4,272,256]{2,1,0:T(8,128)(2,1)S(1)}, bf16[4,272,256]{2,1,0:T(8,128)(2,1)}, u32[]{:S(2)}, u32[]{:S(2)}) collective-permute-start(bf16[4,272,256]{2,1,0:T(8,128)(2,1)S(1)} %slice.226.rest_0_), channel_id=1, source_target_pairs={{0,4},{4,0},{8,12},{12,8},{16,20},{20,16},{24,28},{28,24},{1,5},{5... | collective-permute-start | bytes 1671176 | tf_op jit(solution)/shard_map/ppermute | solution.py:833
  51.0 16.6 %collective-permute-start.14 = (bf16[4,128,256]{2,1,0:T(8,128)(2,1)S(1)}, bf16[4,128,256]{2,1,0:T(8,128)(2,1)}, u32[]{:S(2)}, u32[]{:S(2)}) collective-permute-start(bf16[4,128,256]{2,1,0:T(8,128)(2,1)S(1)} %slice.227.rest_0_), channel_id=1, source_target_pairs={{0,1},{1,0},{2,3},{3,2},{4,5},{5,4},{6,7},{7,6},{8,9},{9,8},{10,11... | collective-permute-start | bytes 786440 | tf_op jit(solution)/shard_map/ppermute | solution.py:839
  63.1 15.7 %collective-permute-start.11 = (bf16[4,272,256]{2,1,0:T(8,128)(2,1)}, bf16[4,272,256]{2,1,0:T(8,128)(2,1)}, u32[]{:S(2)}, u32[]{:S(2)}) collective-permute-start(bf16[4,272,256]{2,1,0:T(8,128)(2,1)} %collective-permute-done.7.rest_1_), channel_id=1, source_target_pairs={{0,4},{4,0},{8,12},{12,8},{16,20},{20,16},{24,28},{28,24},{1,5},{5... | collective-permute-start | bytes 1671176 | tf_op jit(solution)/shard_map/ppermute | solution.py:833
  63.1 15.7 %collective-permute-start.12 = (bf16[4,272,256]{2,1,0:T(8,128)(2,1)}, bf16[4,272,256]{2,1,0:T(8,128)(2,1)}, u32[]{:S(2)}, u32[]{:S(2)}) collective-permute-start(bf16[4,272,256]{2,1,0:T(8,128)(2,1)} %collective-permute-done.8.rest_2_), channel_id=1, source_target_pairs={{0,4},{4,0},{8,12},{12,8},{16,20},{20,16},{24,28},{28,24},{1,5},{5... | collective-permute-start | bytes 1671176 | tf_op jit(solution)/shard_map/ppermute | solution.py:833
  64.2 14.0 %collective-permute-start.15 = (bf16[4,128,256]{2,1,0:T(8,128)(2,1)S(1)}, bf16[4,128,256]{2,1,0:T(8,128)(2,1)}, u32[]{:S(2)}, u32[]{:S(2)}) collective-permute-start(bf16[4,128,256]{2,1,0:T(8,128)(2,1)S(1)} %slice.227.rest_0_), channel_id=1, source_target_pairs={{0,2},{1,3},{2,0},{3,1},{4,6},{5,7},{6,4},{7,5},{8,10},{9,11},{10,... | collective-permute-start | bytes 786440 | tf_op jit(solution)/shard_map/ppermute | solution.py:839
  64.8 13.4 %collective-permute-start.16 = (bf16[4,128,256]{2,1,0:T(8,128)(2,1)S(1)}, bf16[4,128,256]{2,1,0:T(8,128)(2,1)}, u32[]{:S(2)}, u32[]{:S(2)}) collective-permute-start(bf16[4,128,256]{2,1,0:T(8,128)(2,1)S(1)} %slice.227.rest_0_), channel_id=1, source_target_pairs={{0,3},{1,2},{2,1},{3,0},{4,7},{5,6},{6,5},{7,4},{8,11},{9,10},{10,... | collective-permute-start | bytes 786440 | tf_op jit(solution)/shard_map/ppermute | solution.py:839
  67.6 14.2 %collective-permute-start.13 = (bf16[4,272,256]{2,1,0:T(8,128)(2,1)S(1)}, bf16[4,272,256]{2,1,0:T(8,128)(2,1)}, u32[]{:S(2)}, u32[]{:S(2)}) collective-permute-start(bf16[4,272,256]{2,1,0:T(8,128)(2,1)S(1)} %collective-permute-done.9.rest_3_), channel_id=1, source_target_pairs={{0,4},{4,0},{8,12},{12,8},{16,20},{20,16},{24,28},{28,24},{1,5},{5... | collective-permute-start | bytes 1671176 | tf_op jit(solution)/shard_map/ppermute | solution.py:833
  78.2 29.1 %collective-permute-start.17 = (bf16[4,128,256]{2,1,0:T(8,128)(2,1)S(1)}, bf16[4,128,256]{2,1,0:T(8,128)(2,1)}, u32[]{:S(2)}, u32[]{:S(2)}) collective-permute-start(bf16[4,128,256]{2,1,0:T(8,128)(2,1)S(1)} %slice.227.rest_0_), channel_id=1, source_target_pairs={{0,4},{4,0},{8,12},{12,8},{16,20},{20,16},{24,28},{28,24},{1,5},{5... | collective-permute-start | bytes 786440 | tf_op jit(solution)/shard_map/ppermute | solution.py:833
  78.2 29.6 %collective-permute-start.18 = (bf16[4,128,256]{2,1,0:T(8,128)(2,1)}, bf16[4,128,256]{2,1,0:T(8,128)(2,1)}, u32[]{:S(2)}, u32[]{:S(2)}) collective-permute-start(bf16[4,128,256]{2,1,0:T(8,128)(2,1)} %collective-permute-done.14.rest_1_), channel_id=1, source_target_pairs={{0,4},{4,0},{8,12},{12,8},{16,20},{20,16},{24,28},{28,24},{1,5},{5... | collective-permute-start | bytes 786440 | tf_op jit(solution)/shard_map/ppermute | solution.py:833
  78.7 29.1 %collective-permute-start.19 = (bf16[4,128,256]{2,1,0:T(8,128)(2,1)}, bf16[4,128,256]{2,1,0:T(8,128)(2,1)}, u32[]{:S(2)}, u32[]{:S(2)}) collective-permute-start(bf16[4,128,256]{2,1,0:T(8,128)(2,1)} %collective-permute-done.15.rest_2_), channel_id=1, source_target_pairs={{0,4},{4,0},{8,12},{12,8},{16,20},{20,16},{24,28},{28,24},{1,5},{5... | collective-permute-start | bytes 786440 | tf_op jit(solution)/shard_map/ppermute | solution.py:833
  78.8 29.1 %collective-permute-start.20 = (bf16[4,128,256]{2,1,0:T(8,128)(2,1)}, bf16[4,128,256]{2,1,0:T(8,128)(2,1)}, u32[]{:S(2)}, u32[]{:S(2)}) collective-permute-start(bf16[4,128,256]{2,1,0:T(8,128)(2,1)} %collective-permute-done.16.rest_3_), channel_id=1, source_target_pairs={{0,4},{4,0},{8,12},{12,8},{16,20},{20,16},{24,28},{28,24},{1,5},{5... | collective-permute-start | bytes 786440 | tf_op jit(solution)/shard_map/ppermute | solution.py:833
  81.8 32.1 %collective-permute-start.30 = (bf16[512,1024]{1,0:T(8,128)(2,1)}, bf16[512,1024]{1,0:T(8,128)(2,1)}, u32[]{:S(2)}, u32[]{:S(2)}) collective-permute-start(bf16[512,1024]{1,0:T(8,128)(2,1)} %rest_10_.1), channel_id=1, source_target_pairs={{0,1},{1,0},{2,3},{3,2},{4,5},{5,4},{6,7},{7,6},{8,9},{9,8},{10,11... | collective-permute-start | bytes 3145736 | tf_op jit(solution)/shard_map/ppermute | solution.py:839
  107.3 26.2 %collective-permute-start.31 = (bf16[512,1024]{1,0:T(8,128)(2,1)S(1)}, bf16[512,1024]{1,0:T(8,128)(2,1)}, u32[]{:S(2)}, u32[]{:S(2)}) collective-permute-start(bf16[512,1024]{1,0:T(8,128)(2,1)S(1)} %copy-done.23), channel_id=1, source_target_pairs={{0,2},{1,3},{2,0},{3,1},{4,6},{5,7},{6,4},{7,5},{8,10},{9,11},{10,... | collective-permute-start | bytes 3145736 | tf_op jit(solution)/shard_map/ppermute | solution.py:839
  111.8 24.8 %collective-permute-start.21 = (bf16[512,1024]{1,0:T(8,128)(2,1)S(1)}, bf16[512,1024]{1,0:T(8,128)(2,1)S(1)}, u32[]{:S(2)}, u32[]{:S(2)}) collective-permute-start(bf16[512,1024]{1,0:T(8,128)(2,1)S(1)} %get-tuple-element.118.rest_0_), channel_id=1, source_target_pairs={{0,1},{1,0},{2,3},{3,2},{4,5},{5,4},{6,7},{7,6},{8,9},{9,8},{10,11... | collective-permute-start | bytes 3145736 | tf_op jit(solution)/shard_map/ppermute | solution.py:839
  112.4 42.3 %collective-permute-start.22 = (bf16[512,1024]{1,0:T(8,128)(2,1)S(1)}, bf16[512,1024]{1,0:T(8,128)(2,1)S(1)}, u32[]{:S(2)}, u32[]{:S(2)}) collective-permute-start(bf16[512,1024]{1,0:T(8,128)(2,1)S(1)} %get-tuple-element.118.rest_0_), channel_id=1, source_target_pairs={{0,2},{1,3},{2,0},{3,1},{4,6},{5,7},{6,4},{7,5},{8,10},{9,11},{10,... | collective-permute-start | bytes 3145736 | tf_op jit(solution)/shard_map/ppermute | solution.py:839
  113.9 46.1 %collective-permute-start.34 = (bf16[512,1024]{1,0:T(8,128)(2,1)S(1)}, bf16[512,1024]{1,0:T(8,128)(2,1)S(1)}, u32[]{:S(2)}, u32[]{:S(2)}) collective-permute-start(bf16[512,1024]{1,0:T(8,128)(2,1)S(1)} %copy-done.23), channel_id=1, source_target_pairs={{0,4},{4,0},{8,12},{12,8},{16,20},{20,16},{24,28},{28,24},{1,5},{5... | collective-permute-start | bytes 3145736 | tf_op jit(solution)/shard_map/ppermute | solution.py:833
  113.9 58.8 %collective-permute-start.25 = (bf16[512,1024]{1,0:T(8,128)(2,1)S(1)}, bf16[512,1024]{1,0:T(8,128)(2,1)S(1)}, u32[]{:S(2)}, u32[]{:S(2)}) collective-permute-start(bf16[512,1024]{1,0:T(8,128)(2,1)S(1)} %get-tuple-element.118.rest_0_), channel_id=1, source_target_pairs={{0,4},{4,0},{8,12},{12,8},{16,20},{20,16},{24,28},{28,24},{1,5},{5... | collective-permute-start | bytes 3145736 | tf_op jit(solution)/shard_map/ppermute | solution.py:833
  156.1 14.9 %collective-permute-start.32 = (bf16[256,1024]{1,0:T(8,128)(2,1)S(1)}, bf16[256,1024]{1,0:T(8,128)(2,1)S(1)}, u32[]{:S(2)}, u32[]{:S(2)}) collective-permute-start(bf16[256,1024]{1,0:T(8,128)(2,1)S(1)} %slice.176), channel_id=1, source_target_pairs={{0,2},{1,3},{2,0},{3,1},{4,6},{5,7},{6,4},{7,5},{8,10},{9,11},{10,... | collective-permute-start | bytes 1572872 | tf_op jit(solution)/shard_map/ppermute | solution.py:839
  157.8 14.9 %collective-permute-start.33 = (bf16[256,1024]{1,0:T(8,128)(2,1)S(1)}, bf16[256,1024]{1,0:T(8,128)(2,1)S(1)}, u32[]{:S(2)}, u32[]{:S(2)}) collective-permute-start(bf16[256,1024]{1,0:T(8,128)(2,1)S(1)} %slice.177), channel_id=1, source_target_pairs={{0,1},{1,0},{2,3},{3,2},{4,5},{5,4},{6,7},{7,6},{8,9},{9,8},{10,11... | collective-permute-start | bytes 1572872 | tf_op jit(solution)/shard_map/ppermute | solution.py:839
  158.4 21.7 %collective-permute-start.23 = (bf16[256,1024]{1,0:T(8,128)(2,1)S(1)}, bf16[256,1024]{1,0:T(8,128)(2,1)S(1)}, u32[]{:S(2)}, u32[]{:S(2)}) collective-permute-start(bf16[256,1024]{1,0:T(8,128)(2,1)S(1)} %slice.228), channel_id=1, source_target_pairs={{0,2},{1,3},{2,0},{3,1},{4,6},{5,7},{6,4},{7,5},{8,10},{9,11},{10,... | collective-permute-start | bytes 1572872 | tf_op jit(solution)/shard_map/ppermute | solution.py:839
  160.1 21.5 %collective-permute-start.24 = (bf16[256,1024]{1,0:T(8,128)(2,1)S(1)}, bf16[256,1024]{1,0:T(8,128)(2,1)}, u32[]{:S(2)}, u32[]{:S(2)}) collective-permute-start(bf16[256,1024]{1,0:T(8,128)(2,1)S(1)} %slice.229), channel_id=1, source_target_pairs={{0,1},{1,0},{2,3},{3,2},{4,5},{5,4},{6,7},{7,6},{8,9},{9,8},{10,11... | collective-permute-start | bytes 1572872 | tf_op jit(solution)/shard_map/ppermute | solution.py:839
  171.0 10.5 %collective-permute-start.37 = (bf16[256,1024]{1,0:T(8,128)(2,1)S(1)}, bf16[256,1024]{1,0:T(8,128)(2,1)S(1)}, u32[]{:S(2)}, u32[]{:S(2)}) collective-permute-start(bf16[256,1024]{1,0:T(8,128)(2,1)S(1)} %collective-permute-done.32.rest_13_), channel_id=1, source_target_pairs={{0,4},{4,0},{8,12},{12,8},{16,20},{20,16},{24,28},{28,24},{1,5},{5... | collective-permute-start | bytes 1572872 | tf_op jit(solution)/shard_map/ppermute | solution.py:833
  172.7 9.5 %collective-permute-start.38 = (bf16[256,1024]{1,0:T(8,128)(2,1)S(1)}, bf16[256,1024]{1,0:T(8,128)(2,1)S(1)}, u32[]{:S(2)}, u32[]{:S(2)}) collective-permute-start(bf16[256,1024]{1,0:T(8,128)(2,1)S(1)} %collective-permute-done.33.rest_14_), channel_id=1, source_target_pairs={{0,4},{4,0},{8,12},{12,8},{16,20},{20,16},{24,28},{28,24},{1,5},{5... | collective-permute-start | bytes 1572872 | tf_op jit(solution)/shard_map/ppermute | solution.py:833
  172.7 14.9 %collective-permute-start.35 = (bf16[512,1024]{1,0:T(8,128)(2,1)}, bf16[512,1024]{1,0:T(8,128)(2,1)}, u32[]{:S(2)}, u32[]{:S(2)}) collective-permute-start(bf16[512,1024]{1,0:T(8,128)(2,1)} %collective-permute-done.30.rest_11_), channel_id=1, source_target_pairs={{0,4},{4,0},{8,12},{12,8},{16,20},{20,16},{24,28},{28,24},{1,5},{5... | collective-permute-start | bytes 3145736 | tf_op jit(solution)/shard_map/ppermute | solution.py:833
  181.6 6.0 %collective-permute-start.36 = (bf16[512,1024]{1,0:T(8,128)(2,1)}, bf16[512,1024]{1,0:T(8,128)(2,1)}, u32[]{:S(2)}, u32[]{:S(2)}) collective-permute-start(bf16[512,1024]{1,0:T(8,128)(2,1)} %collective-permute-done.31.rest_12_), channel_id=1, source_target_pairs={{0,4},{4,0},{8,12},{12,8},{16,20},{20,16},{24,28},{28,24},{1,5},{5... | collective-permute-start | bytes 3145736 | tf_op jit(solution)/shard_map/ppermute | solution.py:833
  240.0 282.4 %reduce-scatter.5.cloned.1.call-start = ((), (), s32[]{:S(2)}) async-start(), calls=%async_computation.3 | async-start | bytes 7864320 | tf_op jit(solution)/shard_map/reduce_scatter | solution.py:959
  305.7 15.7 %collective-permute-start.39 = (bf16[2048,1024]{1,0:T(8,128)(2,1)}, bf16[2048,1024]{1,0:T(8,128)(2,1)}, u32[]{:S(2)}, u32[]{:S(2)}) collective-permute-start(bf16[2048,1024]{1,0:T(8,128)(2,1)} %scatter_rows.4), channel_id=1, source_target_pairs={{0,4},{4,0},{8,12},{12,8},{16,20},{20,16},{24,28},{28,24},{1,5},{5... | collective-permute-start | bytes 12582920 | tf_op jit(solution)/shard_map/ppermute | solution.py:833
  325.8 43.4 %collective-permute-start.40 = (bf16[256,1024]{1,0:T(8,128)(2,1)S(1)}, bf16[256,1024]{1,0:T(8,128)(2,1)S(1)}, u32[]{:S(2)}, u32[]{:S(2)}) collective-permute-start(bf16[256,1024]{1,0:T(8,128)(2,1)S(1)} %get-tuple-element.322), channel_id=1, source_target_pairs={{0,1},{1,0},{2,3},{3,2},{4,5},{5,4},{6,7},{7,6},{8,9},{9,8},{10,11... | collective-permute-start | bytes 1572872 | tf_op jit(solution)/shard_map/ppermute | solution.py:839
  327.7 51.0 %collective-permute-start.41 = (bf16[256,1024]{1,0:T(8,128)(2,1)S(1)}, bf16[256,1024]{1,0:T(8,128)(2,1)S(1)}, u32[]{:S(2)}, u32[]{:S(2)}) collective-permute-start(bf16[256,1024]{1,0:T(8,128)(2,1)S(1)} %get-tuple-element.321), channel_id=1, source_target_pairs={{0,2},{1,3},{2,0},{3,1},{4,6},{5,7},{6,4},{7,5},{8,10},{9,11},{10,... | collective-permute-start | bytes 1572872 | tf_op jit(solution)/shard_map/ppermute | solution.py:839
  366.9 41.5 %collective-permute-start.43 = (bf16[256,1024]{1,0:T(8,128)(2,1)}, bf16[256,1024]{1,0:T(8,128)(2,1)}, u32[]{:S(2)}, u32[]{:S(2)}) collective-permute-start(bf16[256,1024]{1,0:T(8,128)(2,1)} %slice.241), channel_id=1, source_target_pairs={{0,1},{1,0},{2,3},{3,2},{4,5},{5,4},{6,7},{7,6},{8,9},{9,8},{10,11... | collective-permute-start | bytes 1572872 | tf_op jit(solution)/shard_map/ppermute | solution.py:839
  367.8 42.5 %collective-permute-start.46 = (bf16[256,1024]{1,0:T(8,128)(2,1)}, bf16[256,1024]{1,0:T(8,128)(2,1)}, u32[]{:S(2)}, u32[]{:S(2)}) collective-permute-start(bf16[256,1024]{1,0:T(8,128)(2,1)} %slice.243), channel_id=1, source_target_pairs={{0,2},{1,3},{2,0},{3,1},{4,6},{5,7},{6,4},{7,5},{8,10},{9,11},{10,... | collective-permute-start | bytes 1572872 | tf_op jit(solution)/shard_map/ppermute | solution.py:839
  379.7 29.2 %collective-permute-start.44 = (bf16[256,1024]{1,0:T(8,128)(2,1)}, bf16[256,1024]{1,0:T(8,128)(2,1)}, u32[]{:S(2)}, u32[]{:S(2)}) collective-permute-start(bf16[256,1024]{1,0:T(8,128)(2,1)} %add_convert_fusion.8), channel_id=1, source_target_pairs={{0,2},{1,3},{2,0},{3,1},{4,6},{5,7},{6,4},{7,5},{8,10},{9,11},{10,... | collective-permute-start | bytes 1572872 | tf_op jit(solution)/shard_map/ppermute | solution.py:839
  382.7 27.7 %collective-permute-start.45 = (bf16[256,1024]{1,0:T(8,128)(2,1)}, bf16[256,1024]{1,0:T(8,128)(2,1)}, u32[]{:S(2)}, u32[]{:S(2)}) collective-permute-start(bf16[256,1024]{1,0:T(8,128)(2,1)} %add_convert_fusion.7), channel_id=1, source_target_pairs={{0,1},{1,0},{2,3},{3,2},{4,5},{5,4},{6,7},{7,6},{8,9},{9,8},{10,11... | collective-permute-start | bytes 1572872 | tf_op jit(solution)/shard_map/ppermute | solution.py:839
  408.4 7.3 %collective-permute-start.47 = (bf16[512,1024]{1,0:T(8,128)(2,1)S(1)}, bf16[512,1024]{1,0:T(8,128)(2,1)S(1)}, u32[]{:S(2)}, u32[]{:S(2)}) collective-permute-start(bf16[512,1024]{1,0:T(8,128)(2,1)S(1)} %get-tuple-element.297), channel_id=1, source_target_pairs={{0,4},{4,0},{8,12},{12,8},{16,20},{20,16},{24,28},{28,24},{1,5},{5... | collective-permute-start | bytes 3145736 | tf_op jit(solution)/shard_map/ppermute | solution.py:833
  408.4 7.3 %collective-permute-start.48 = (bf16[512,1024]{1,0:T(8,128)(2,1)S(1)}, bf16[512,1024]{1,0:T(8,128)(2,1)S(1)}, u32[]{:S(2)}, u32[]{:S(2)}) collective-permute-start(bf16[512,1024]{1,0:T(8,128)(2,1)S(1)} %get-tuple-element.296), channel_id=1, source_target_pairs={{0,4},{4,0},{8,12},{12,8},{16,20},{20,16},{24,28},{28,24},{1,5},{5... | collective-permute-start | bytes 3145736 | tf_op jit(solution)/shard_map/ppermute | solution.py:833
  408.9 6.8 %collective-permute-start.49 = (bf16[512,1024]{1,0:T(8,128)(2,1)S(1)}, bf16[512,1024]{1,0:T(8,128)(2,1)S(1)}, u32[]{:S(2)}, u32[]{:S(2)}) collective-permute-start(bf16[512,1024]{1,0:T(8,128)(2,1)S(1)} %get-tuple-element.295), channel_id=1, source_target_pairs={{0,4},{4,0},{8,12},{12,8},{16,20},{20,16},{24,28},{28,24},{1,5},{5... | collective-permute-start | bytes 3145736 | tf_op jit(solution)/shard_map/ppermute | solution.py:833
  420.2 38.1 %collective-permute-start.50 = (bf16[512,1024]{1,0:T(8,128)(2,1)}, bf16[512,1024]{1,0:T(8,128)(2,1)S(1)}, u32[]{:S(2)}, u32[]{:S(2)}) collective-permute-start(bf16[512,1024]{1,0:T(8,128)(2,1)} %get-tuple-element.144), channel_id=1, source_target_pairs={{0,1},{1,0},{2,3},{3,2},{4,5},{5,4},{6,7},{7,6},{8,9},{9,8},{10,11... | collective-permute-start | bytes 3145736 | tf_op jit(solution)/shard_map/ppermute | solution.py:839
  422.3 48.1 %collective-permute-start.51 = (bf16[512,1024]{1,0:T(8,128)(2,1)}, bf16[512,1024]{1,0:T(8,128)(2,1)S(1)}, u32[]{:S(2)}, u32[]{:S(2)}) collective-permute-start(bf16[512,1024]{1,0:T(8,128)(2,1)} %get-tuple-element.145), channel_id=1, source_target_pairs={{0,2},{1,3},{2,0},{3,1},{4,6},{5,7},{6,4},{7,5},{8,10},{9,11},{10,... | collective-permute-start | bytes 3145736 | tf_op jit(solution)/shard_map/ppermute | solution.py:839
  424.3 46.2 %collective-permute-start.52 = (bf16[512,1024]{1,0:T(8,128)(2,1)}, bf16[512,1024]{1,0:T(8,128)(2,1)S(1)}, u32[]{:S(2)}, u32[]{:S(2)}) collective-permute-start(bf16[512,1024]{1,0:T(8,128)(2,1)} %get-tuple-element.146), channel_id=1, source_target_pairs={{0,3},{1,2},{2,1},{3,0},{4,7},{5,6},{6,5},{7,4},{8,11},{9,10},{10,... | collective-permute-start | bytes 3145736 | tf_op jit(solution)/shard_map/ppermute | solution.py:839
  470.4 7.1 %collective-permute-start.54 = (bf16[4,4,400,256]{3,2,1,0:T(8,128)(2,1)}, bf16[4,4,400,256]{3,2,1,0:T(8,128)(2,1)S(1)}, u32[]{:S(2)}, u32[]{:S(2)}) collective-permute-start(bf16[4,4,400,256]{3,2,1,0:T(8,128)(2,1)} %get-tuple-element.162), channel_id=1, source_target_pairs={{0,4},{4,0},{8,12},{12,8},{16,20},{20,16},{24,28},{28,24},{1,5},{5... | collective-permute-start | bytes 9830408 | tf_op jit(solution)/shard_map/ppermute | solution.py:833
  470.8 30.7 %collective-permute-start.42 = (bf16[512,1024]{1,0:T(8,128)(2,1)}, bf16[512,1024]{1,0:T(8,128)(2,1)}, u32[]{:S(2)}, u32[]{:S(2)}) collective-permute-start(bf16[512,1024]{1,0:T(8,128)(2,1)} %get-tuple-element.294), channel_id=1, source_target_pairs={{0,4},{4,0},{8,12},{12,8},{16,20},{20,16},{24,28},{28,24},{1,5},{5... | collective-permute-start | bytes 3145736 | tf_op jit(solution)/shard_map/ppermute | solution.py:833
  483.2 12.4 %collective-permute-start.56 = (bf16[2,400,256]{2,1,0:T(8,128)(2,1)S(1)}, bf16[2,400,256]{2,1,0:T(8,128)(2,1)}, u32[]{:S(2)}, u32[]{:S(2)}) collective-permute-start(bf16[2,400,256]{2,1,0:T(8,128)(2,1)S(1)} %get-tuple-element.309), channel_id=1, source_target_pairs={{0,1},{1,0},{2,3},{3,2},{4,5},{5,4},{6,7},{7,6},{8,9},{9,8},{10,11... | collective-permute-start | bytes 1228808 | tf_op jit(solution)/shard_map/ppermute | solution.py:839
  484.7 12.5 %collective-permute-start.57 = (bf16[2,400,256]{2,1,0:T(8,128)(2,1)S(1)}, bf16[2,400,256]{2,1,0:T(8,128)(2,1)}, u32[]{:S(2)}, u32[]{:S(2)}) collective-permute-start(bf16[2,400,256]{2,1,0:T(8,128)(2,1)S(1)} %get-tuple-element.308), channel_id=1, source_target_pairs={{0,2},{1,3},{2,0},{3,1},{4,6},{5,7},{6,4},{7,5},{8,10},{9,11},{10,... | collective-permute-start | bytes 1228808 | tf_op jit(solution)/shard_map/ppermute | solution.py:839
  485.8 32.7 %collective-permute-start.55 = (bf16[2,400,256]{2,1,0:T(8,128)(2,1)}, bf16[2,400,256]{2,1,0:T(8,128)(2,1)}, u32[]{:S(2)}, u32[]{:S(2)}) collective-permute-start(bf16[2,400,256]{2,1,0:T(8,128)(2,1)} %get-tuple-element.310), channel_id=1, source_target_pairs={{0,1},{1,0},{2,3},{3,2},{4,5},{5,4},{6,7},{7,6},{8,9},{9,8},{10,11... | collective-permute-start | bytes 1228808 | tf_op jit(solution)/shard_map/ppermute | solution.py:839
  487.6 30.9 %collective-permute-start.60 = (bf16[2,400,256]{2,1,0:T(8,128)(2,1)}, bf16[2,400,256]{2,1,0:T(8,128)(2,1)}, u32[]{:S(2)}, u32[]{:S(2)}) collective-permute-start(bf16[2,400,256]{2,1,0:T(8,128)(2,1)} %get-tuple-element.307), channel_id=1, source_target_pairs={{0,2},{1,3},{2,0},{3,1},{4,6},{5,7},{6,4},{7,5},{8,10},{9,11},{10,... | collective-permute-start | bytes 1228808 | tf_op jit(solution)/shard_map/ppermute | solution.py:839
  498.5 10.2 %collective-permute-start.53 = (bf16[2,192,1024]{2,1,0:T(8,128)(2,1)S(1)}, bf16[2,192,1024]{2,1,0:T(8,128)(2,1)}, u32[]{:S(2)}, u32[]{:S(2)}) collective-permute-start(bf16[2,192,1024]{2,1,0:T(8,128)(2,1)S(1)} %slice_bitcast_fusion.1), channel_id=1, source_target_pairs={{0,4},{4,0},{8,12},{12,8},{16,20},{20,16},{24,28},{28,24},{1,5},{5... | collective-permute-start | bytes 2359304 | tf_op jit(solution)/shard_map/ppermute | solution.py:833
  500.9 17.7 %collective-permute-start.58 = (bf16[2,400,256]{2,1,0:T(8,128)(2,1)}, bf16[2,400,256]{2,1,0:T(8,128)(2,1)}, u32[]{:S(2)}, u32[]{:S(2)}) collective-permute-start(bf16[2,400,256]{2,1,0:T(8,128)(2,1)} %get-tuple-element.312), channel_id=1, source_target_pairs={{0,1},{1,0},{2,3},{3,2},{4,5},{5,4},{6,7},{7,6},{8,9},{9,8},{10,11... | collective-permute-start | bytes 1228808 | tf_op jit(solution)/shard_map/ppermute | solution.py:839
  501.5 17.1 %collective-permute-start.59 = (bf16[2,400,256]{2,1,0:T(8,128)(2,1)S(1)}, bf16[2,400,256]{2,1,0:T(8,128)(2,1)}, u32[]{:S(2)}, u32[]{:S(2)}) collective-permute-start(bf16[2,400,256]{2,1,0:T(8,128)(2,1)S(1)} %get-tuple-element.311), channel_id=1, source_target_pairs={{0,2},{1,3},{2,0},{3,1},{4,6},{5,7},{6,4},{7,5},{8,10},{9,11},{10,... | collective-permute-start | bytes 1228808 | tf_op jit(solution)/shard_map/ppermute | solution.py:839
  523.7 12.9 %collective-permute-start.64 = (bf16[2,192,1024]{2,1,0:T(8,128)(2,1)S(1)}, bf16[2,192,1024]{2,1,0:T(8,128)(2,1)}, u32[]{:S(2)}, u32[]{:S(2)}) collective-permute-start(bf16[2,192,1024]{2,1,0:T(8,128)(2,1)S(1)} %slice_bitcast_fusion.2), channel_id=1, source_target_pairs={{0,4},{4,0},{8,12},{12,8},{16,20},{20,16},{24,28},{28,24},{1,5},{5... | collective-permute-start | bytes 2359304 | tf_op jit(solution)/shard_map/ppermute | solution.py:833
  523.7 22.8 %collective-permute-start.61 = (bf16[400,256]{1,0:T(8,128)(2,1)S(1)}, bf16[400,256]{1,0:T(8,128)(2,1)}, u32[]{:S(2)}, u32[]{:S(2)}) collective-permute-start(bf16[400,256]{1,0:T(8,128)(2,1)S(1)} %get-tuple-element.325), channel_id=1, source_target_pairs={{0,8},{4,12},{8,0},{12,4},{16,24},{20,28},{24,16},{28,20},{1,9},{5... | collective-permute-start | bytes 614408 | tf_op jit(solution)/shard_map/ppermute | solution.py:836
  533.0 16.7 %collective-permute-start.62 = (bf16[400,256]{1,0:T(8,128)(2,1)S(1)}, bf16[400,256]{1,0:T(8,128)(2,1)}, u32[]{:S(2)}, u32[]{:S(2)}) collective-permute-start(bf16[400,256]{1,0:T(8,128)(2,1)S(1)} %get-tuple-element.324), channel_id=1, source_target_pairs={{0,16},{4,20},{8,24},{12,28},{16,0},{20,4},{24,8},{28,12},{1,17},{... | collective-permute-start | bytes 614408 | tf_op jit(solution)/shard_map/ppermute | solution.py:836
  533.0 16.7 %collective-permute-start.63 = (bf16[400,256]{1,0:T(8,128)(2,1)S(1)}, bf16[400,256]{1,0:T(8,128)(2,1)}, u32[]{:S(2)}, u32[]{:S(2)}) collective-permute-start(bf16[400,256]{1,0:T(8,128)(2,1)S(1)} %get-tuple-element.323), channel_id=1, source_target_pairs={{0,24},{4,28},{8,16},{12,20},{16,8},{20,12},{24,0},{28,4},{1,25},{... | collective-permute-start | bytes 614408 | tf_op jit(solution)/shard_map/ppermute | solution.py:836
  (70 other events, 1039.2 us)
Sparse Core Ops, SparseCore 0:
  33.5 117.5 all-gather.6
  152.6 61.7 all-gather.8
  216.0 62.1 all-gather.10
  280.3 111.1 reduce-scatter.2
  393.7 111.2 reduce-scatter.4

commit v3 on v2

--- a/solution.py
+++ b/solution.py
@@ -15,12 +15,13 @@
 SEQ_LEN = 512
 STEP = 10
 CALLS = (((0, 2),), ((2, 3), (3, 4)))
-GATHERS = ((0, 2), (2, 3), (3, 4))
+GATHERS = ((0, 3), (3, 4))
 QBLK = 256
 SUB = 256
 CHUNK = 256
 SLOTS = 2560
-AHEAD = 4
+DEEP = 8
+PAIR = 2
 HELD = 3072
 
 NORM_EPS = 1e-05
@@ -85,17 +86,25 @@
     return (change, first_new, second_new)
 
 
+def sum_received(received, nt):
+    received = [part.astype(f32) for part in received]
+    if nt != 4:
+        return functools.reduce(jnp.add, received)
+    x_first, x_last, y_first, y_last = received
+    return jnp.concatenate([x_first + y_first, x_last + y_last], axis=0)
+
+
 def rms_scale(values):
     return lax.rsqrt(jnp.mean(values * values, axis=-1, keepdims=True) + NORM_EPS)
 
 
-def weight_spots(place_ref, nz, nt):
+def weight_spots(place_ref, nz, nt, relative):
     rows, cols = D // (2 * nz), D // nt
     z, core, t = place_ref[0], place_ref[1], place_ref[2]
     for c in range(2):
         for k in range(nt):
             for j in range(nz):
-                row = pl.multiple_of(((z ^ j) * 2 + (core ^ c)) * rows, rows)
+                row = pl.multiple_of(((z ^ j if relative else j) * 2 + (core ^ c)) * rows, rows)
                 col = pl.multiple_of((t ^ k) * cols, cols)
                 yield c, k, j, (pl.ds(row, rows), pl.ds(col, cols))
 
@@ -108,7 +117,7 @@
             w_ref.at[(member,) + spot],
             sem.at[((c * nt + k) * nz + j) * w_ref.shape[0] + member],
         )
-        for c, k, j, spot in weight_spots(place_ref, nz, nt)
+        for c, k, j, spot in weight_spots(place_ref, nz, nt, False)
         for member in range(w_ref.shape[0])
     ]
 
@@ -145,11 +154,11 @@
     qlin_ref, kvlin_ref, parts_ref, sems, gain_sems = rest[2 * nt + 6 :]
     length = tokens_ref.shape[0]
     rows = D // (2 * nz)
-    z, core, t = place_ref[0], place_ref[1], place_ref[2]
+    core, t = place_ref[1], place_ref[2]
     gain_copies = [
         pltpu.make_async_copy(
             pieces[c * nt + k].at[j, 2 * rows :, :],
-            parts_ref.at[((z ^ j) * 2 + (core ^ c)) * nt + (t ^ k)],
+            parts_ref.at[(j * 2 + (core ^ c)) * nt + (t ^ k)],
             gain_sems.at[(c * nt + k) * nz + j],
         )
         for c in range(2)
@@ -186,26 +195,26 @@
         vk = pltpu.roll(kv, HD, 1).astype(bf16)
         kv = kv.astype(bf16)
         heads = (
-            (jnp.where(low, q, 0.0).astype(bf16), kv, vk),
-            (jnp.where(low, 0.0, q).astype(bf16), vk, kv),
+            (jnp.where(low, q * SCALE, 0.0).astype(bf16), kv, vk),
+            (jnp.where(low, 0.0, q * SCALE).astype(bf16), vk, kv),
         )
+        row = lax.broadcasted_iota(jnp.int32, (QBLK, QBLK), 0)
+        column = lax.broadcasted_iota(jnp.int32, (QBLK, QBLK), 1)
+        seen = column <= row
         for b in range(length // QBLK):
             rows = slice(b * QBLK, (b + 1) * QBLK)
             keys = (b + 1) * QBLK
-            row = lax.broadcasted_iota(jnp.int32, (QBLK, keys), 0) + b * QBLK
-            column = lax.broadcasted_iota(jnp.int32, (QBLK, keys), 1)
-            seen = column <= row
             outs = []
             lses = lse_ref[rows, :]
             lane_b = lax.broadcasted_iota(jnp.int32, (QBLK, 128), 1)
             for h, (qh, key_side, value_side) in enumerate(heads):
-                scores = dot_t(qh[rows], key_side[:keys]) * SCALE
-                scores = jnp.where(seen, scores, MASK_FILL)
+                scores = jnp.where(seen, dot_t(qh[rows], key_side[rows]), MASK_FILL)
+                if b > 0:
+                    scores = jnp.concatenate([dot_t(qh[rows], key_side[: b * QBLK]), scores], axis=1)
                 top = jnp.max(scores, axis=-1, keepdims=True)
                 e = jnp.exp(scores - top)
                 total = jnp.sum(e, axis=-1, keepdims=True)
-                p = (e * (1.0 / total)).astype(bf16)
-                outs.append(dot(p, value_side[:keys]))
+                outs.append(dot(e.astype(bf16), value_side[:keys]) * (1.0 / total))
                 lses = jnp.where(lane_b == 2 * g + h, top + jnp.log(total), lses)
             lse_ref[rows, :] = lses
             o_ref[rows, part] = jnp.where(lane_b < HD, outs[0], outs[1]).astype(bf16)
@@ -238,7 +247,7 @@
             pltpu.SemaphoreType.DMA((2 * nt * nz,)),
         ],
         compiler_params=pltpu.CompilerParams(vmem_limit_bytes=40 * 2**20),
-        cost_estimate=COST,
+        cost_estimate=pl.CostEstimate(flops=25 * 10**9, bytes_accessed=12 * 2**20, transcendentals=4 * 2**20),
         name="attend_forward",
     )(place, tokens, jnp.asarray(cosine), jnp.asarray(sine), *pieces)
 
@@ -275,30 +284,42 @@
     )(place, tokens, gains, o, *pieces)
 
 
-def attend_backward_kernel(
-    nz, nt, place_ref, tokens_ref, da_ref, gains_ref, gain_two_ref, cos_ref, sin_ref, q_ref, kv_ref, o_ref,
-    lse_ref, w_ref, wo_ref, dn1_ref, own_ref, other_ref, gw_ref, gg_ref, do_ref, dq_ref, dkv_ref, lse_t_ref, sems
-):
+def norm_backward(grad, stream, gain, given):
+    inverse = rms_scale(stream)
+    unit = stream * inverse
+    scaled = grad * gain
+    through = inverse * (scaled - unit * jnp.mean(scaled * unit, axis=-1, keepdims=True))
+    return given + through, jnp.sum(grad * unit, axis=0, keepdims=True)
+
+
+def attend_backward_kernel(nz, nt, whole, place_ref, tokens_ref, gains_ref, cos_ref, sin_ref, q_ref, kv_ref, o_ref, *rest):
+    lse_ref, w_ref, wo_ref, rest = rest[0], rest[1], rest[2], rest[3:]
+    da_ref, gain_two_ref, rest = rest[0], rest[1], rest[2:]
+    if whole:
+        gs1_ref, rest = rest[0], rest[1:]
+    out_ref, own_ref, others, rest = rest[0], rest[1], rest[2 : 2 + nt], rest[2 + nt :]
+    gw_ref, gg_ref, do_ref, dq_ref, dkv_ref, lse_t_ref, sems = rest
     length = tokens_ref.shape[0]
     rows, cols = D // (2 * nz), D // nt
-    sides = (own_ref, other_ref)
+    sides = ([own_ref.at[k] for k in range(nt)], others)
+    da, gain_two = da_ref[...], gain_two_ref[...]
 
     def member_copies(members):
         return [
             pltpu.make_async_copy(
                 gw_ref.at[(member,) + spot],
-                sides[c].at[k, j, member * rows : (member + 1) * rows, :],
+                sides[c][k].at[j, member * rows : (member + 1) * rows, :],
                 sems.at[member, (c * nt + k) * nz + j],
             )
             for member in members
-            for c, k, j, spot in weight_spots(place_ref, nz, nt)
+            for c, k, j, spot in weight_spots(place_ref, nz, nt, True)
         ]
 
-    gw_ref[2] = t_dot(da_ref[...], o_ref[...]).astype(bf16)
+    gw_ref[2] = t_dot(da, o_ref[...]).astype(bf16)
     first = member_copies((2,))
     for copy in first:
         copy.start()
-    do_ref[...] = dot(da_ref[...], wo_ref[0]).astype(bf16)
+    do_ref[...] = dot(da, wo_ref[0]).astype(bf16)
     lse_t_ref[...] = lse_ref[...].T
 
     def group(g, carry):
@@ -313,28 +334,30 @@
         vk = pltpu.roll(kv, HD, 1).astype(bf16)
         kv = kv.astype(bf16)
         q_low = jnp.where(low, q, 0.0).astype(bf16)
-        q_high = jnp.where(low, 0.0, q).astype(bf16)
+        scaled_low = jnp.where(low, q * SCALE, 0.0).astype(bf16)
+        scaled_high = jnp.where(low, 0.0, q * SCALE).astype(bf16)
         q_moved = jnp.where(low, pltpu.roll(q, HD, 1), 0.0).astype(bf16)
         do_low = jnp.where(low, do, 0.0).astype(bf16)
         do_high = jnp.where(low, 0.0, do).astype(bf16)
         do_moved = jnp.where(low, 0.0, pltpu.roll(do, HD, 1)).astype(bf16)
         heads = (
-            (q_low, kv, vk, do_low, q_low, do_moved),
-            (q_high, vk, kv, do_high, q_moved, do_high),
+            (scaled_low, kv, vk, do_low, q_low, do_moved),
+            (scaled_high, vk, kv, do_high, q_moved, do_high),
         )
+        row = lax.broadcasted_iota(jnp.int32, (QBLK, QBLK), 0)
+        column = lax.broadcasted_iota(jnp.int32, (QBLK, QBLK), 1)
+        seen = row <= column
         blocks = length // QBLK
         dkv = [jnp.zeros((QBLK, 128), f32) for _ in range(blocks)]
         dqs = []
         for b in range(blocks):
             rows = slice(b * QBLK, (b + 1) * QBLK)
             keys = (b + 1) * QBLK
-            row = lax.broadcasted_iota(jnp.int32, (keys, QBLK), 0)
-            column = lax.broadcasted_iota(jnp.int32, (keys, QBLK), 1) + b * QBLK
-            seen = row <= column
             both = []
             for h, (qh, key_side, value_side, doh, q_for_k, do_for_v) in enumerate(heads):
-                scores = dot_t(key_side[:keys], qh[rows]) * SCALE
-                scores = jnp.where(seen, scores, MASK_FILL)
+                scores = jnp.where(seen, dot_t(key_side[rows], qh[rows]), MASK_FILL)
+                if b > 0:
+                    scores = jnp.concatenate([dot_t(key_side[: b * QBLK], qh[rows]), scores], axis=0)
                 e = jnp.exp(scores - lse_t_ref[pl.ds(2 * g + h, 1), rows])
                 dp = dot_t(value_side[:keys], doh[rows])
                 mean = jnp.sum(e * dp, axis=0, keepdims=True)
@@ -354,22 +377,21 @@
 
     lax.fori_loop(0, D // 128, group, 0)
     stream = tokens_ref[...].astype(f32)
-    unit = stream * rms_scale(stream)
-    n1 = (unit * gains_ref[0:1, :]).astype(bf16)
+    n1 = (stream * rms_scale(stream) * gains_ref[0:1, :]).astype(bf16)
     gw_ref[0] = t_dot(n1, dq_ref[...]).astype(bf16)
     gw_ref[1] = t_dot(n1, dkv_ref[...]).astype(bf16)
     second = member_copies((0, 1))
     for copy in second:
         copy.start()
     dn1 = dot_t(dq_ref[...], w_ref[0]) + dot_t(dkv_ref[...], w_ref[1])
-    dn1_ref[...] = dn1
-    gain_one = jnp.sum(dn1 * unit, axis=0, keepdims=True)
+    input_grad, gain_one = norm_backward(dn1, stream, gains_ref[0:1, :], gs1_ref[...] if whole else 0.0)
+    out_ref[...] = input_grad if whole else dn1
     gg_ref[...] = jnp.zeros_like(gg_ref)
     for i in range(nt):
         gg_ref[i : i + 1, :] = gain_one[:, i * cols : (i + 1) * cols].astype(bf16)
-        gg_ref[nt + i : nt + i + 1, :] = gain_two_ref[:, i * cols : (i + 1) * cols].astype(bf16)
+        gg_ref[nt + i : nt + i + 1, :] = gain_two[:, i * cols : (i + 1) * cols].astype(bf16)
     third = [
-        pltpu.make_async_copy(gg_ref, sides[c].at[k, j, 3 * rows :, :], sems.at[3, (c * nt + k) * nz + j])
+        pltpu.make_async_copy(gg_ref, sides[c][k].at[j, 3 * rows :, :], sems.at[3, (c * nt + k) * nz + j])
         for c in range(2)
         for k in range(nt)
         for j in range(nz)
@@ -380,16 +402,17 @@
         copy.wait()
 
 
-def attend_backward(mesh_sizes, place, tokens, da, gains, gain_two, q, kv, o, lse, weights, out_weight):
+def attend_backward(mesh_sizes, whole, place, tokens, gains, q, kv, o, lse, weights, out_weight, *given):
     nz, nt = mesh_sizes
     length = tokens.shape[0]
     cosine, sine = rope_tables()
-    part = jax.ShapeDtypeStruct((nt, nz, 3 * D // (2 * nz) + 16, D // nt), bf16)
-    return pl.pallas_call(
-        functools.partial(attend_backward_kernel, nz, nt),
-        out_shape=(jax.ShapeDtypeStruct((length, D), f32), part, part),
-        in_specs=[SMEM] + [VMEM] * 12,
-        out_specs=[VMEM, ANY, ANY],
+    part = (nz, 3 * D // (2 * nz) + 16, D // nt)
+    out = pl.pallas_call(
+        functools.partial(attend_backward_kernel, nz, nt, whole),
+        out_shape=[jax.ShapeDtypeStruct((length, D), f32), jax.ShapeDtypeStruct((nt,) + part, bf16)]
+        + [jax.ShapeDtypeStruct(part, bf16)] * nt,
+        in_specs=[SMEM] + [VMEM] * (10 + len(given)),
+        out_specs=[VMEM] + [ANY] * (1 + nt),
         scratch_shapes=[
             pltpu.VMEM((3, D, D), bf16),
             pltpu.VMEM((16, D // nt), bf16),
@@ -399,69 +422,66 @@
             pltpu.VMEM((128, length), f32),
             pltpu.SemaphoreType.DMA((4, 2 * nt * nz)),
         ],
-        compiler_params=pltpu.CompilerParams(vmem_limit_bytes=48 * 2**20),
+        compiler_params=pltpu.CompilerParams(vmem_limit_bytes=60 * 2**20),
         cost_estimate=COST,
         name="attend_backward",
     )(
-        place, tokens, da, gains, gain_two, jnp.asarray(cosine), jnp.asarray(sine), q, kv, o, lse, weights, out_weight
+        place, tokens, gains, jnp.asarray(cosine), jnp.asarray(sine), q, kv, o, lse, weights, out_weight, *given
     )
-
-
-def gather_kernel(starts, experts, offs_ref, pos_ref, c_ref, *rest):
+    return out[0], out[1], out[2:]
+
+
+def gather_kernel(starts, experts, with_c, offs_ref, pos_ref, *rest):
     tiles = len(starts) - 1
-    n2_parts, dm_parts, rest = rest[:tiles], rest[tiles : 2 * tiles], rest[2 * tiles :]
-    n2_out, dm_out, c_out, n2_in, dm_in, n2_slots, dm_slots, c_slots, in_sems, out_sems = rest
+    if with_c:
+        c_ref, rest = rest[0], rest[1:]
+    parts, rest = rest[:tiles], rest[tiles:]
+    outs, rest = rest[: 1 + with_c], rest[1 + with_c :]
+    held, (buf, in_sems, out_sems) = rest[: 1 + with_c], rest[1 + with_c :]
     subs = starts[-1] // SUB
 
-    def block_copies(s):
+    def block_copy(s):
         j = max(i for i in range(tiles) if starts[i] <= s * SUB)
-        spot = pl.ds(s * SUB - starts[j], SUB)
-        return (
-            pltpu.make_async_copy(n2_parts[j].at[spot], n2_in.at[s % AHEAD], in_sems.at[0, s % AHEAD]),
-            pltpu.make_async_copy(dm_parts[j].at[spot], dm_in.at[s % AHEAD], in_sems.at[1, s % AHEAD]),
+        return pltpu.make_async_copy(
+            parts[j].at[pl.ds(s * SUB - starts[j], SUB)], buf.at[s % DEEP], in_sems.at[s % DEEP]
         )
 
     def flush(e, chunk):
         spot = pl.ds(pl.multiple_of(chunk * CHUNK, CHUNK), CHUNK)
         return [
             pltpu.make_async_copy(slots.at[e, spot, :], out.at[e, spot, :], out_sems.at[i, e, chunk])
-            for i, (slots, out) in enumerate(((n2_slots, n2_out), (dm_slots, dm_out), (c_slots, c_out)))
+            for i, (slots, out) in enumerate(zip(held, outs))
         ]
 
-    for s in range(AHEAD - 1):
-        for copy in block_copies(s):
-            copy.start()
+    for s in range(DEEP - 1):
+        block_copy(s).start()
 
     def block(s, carry):
-        for ahead in range(AHEAD - 1, subs):
-
-            @pl.when(s + AHEAD - 1 == ahead)
+        for ahead in range(DEEP - 1, subs):
+
+            @pl.when(s + DEEP - 1 == ahead)
             def _():
-                for copy in block_copies(ahead):
-                    copy.start()
-
-        slot = lax.rem(s, AHEAD)
-        pltpu.make_async_copy(n2_parts[0].at[pl.ds(0, SUB)], n2_in.at[slot], in_sems.at[0, slot]).wait()
-        pltpu.make_async_copy(dm_parts[0].at[pl.ds(0, SUB)], dm_in.at[slot], in_sems.at[1, slot]).wait()
+                block_copy(ahead).start()
+
+        slot = lax.rem(s, DEEP)
         begin = [offs_ref[e * (subs + 1) + s] for e in range(experts)]
         end = [offs_ref[e * (subs + 1) + s + 1] for e in range(experts)]
         most = functools.reduce(jnp.maximum, [end[e] - begin[e] for e in range(experts)])
+        pltpu.make_async_copy(parts[0].at[pl.ds(0, SUB)], buf.at[slot], in_sems.at[slot]).wait()
 
         def fill(count):
             slots = lax.broadcasted_iota(jnp.int32, (count, SUB), 0).astype(f32)
+            spots = [pl.ds(pl.multiple_of(begin[e], 16), count) for e in range(experts)]
             picks = []
             for e in range(experts):
-                spot = pl.ds(pl.multiple_of(begin[e], 16), count)
                 hit = slots == pos_ref[pl.ds(e * subs + s, 1), :]
                 picks.append(jnp.where(hit, 1.0, 0.0).astype(bf16))
-                c = jnp.sum(jnp.where(hit, c_ref[pl.ds(e * subs + s, 1), :], 0.0), axis=1, keepdims=True)
-                c_slots[e, spot, :] = jnp.broadcast_to(c, (count, 128))
-            pick = jnp.concatenate(picks, axis=0)
-            for source, target in ((n2_in, n2_slots), (dm_in, dm_slots)):
-                rows = dot(pick, source[slot]).astype(bf16)
-                for e in range(experts):
-                    spot = pl.ds(pl.multiple_of(begin[e], 16), count)
-                    target[e, spot, :] = rows[e * count : (e + 1) * count]
+                if with_c:
+                    c = jnp.sum(jnp.where(hit, c_ref[pl.ds(e * subs + s, 1), :], 0.0), axis=1, keepdims=True)
+                    held[1][e, spots[e], :] = jnp.broadcast_to(c, (count, 128))
+            rows = dot(jnp.concatenate(picks, axis=0), buf[slot]).astype(bf16)
+            for e in range(experts):
+                held[0][e, spots[e], :] = rows[e * count : (e + 1) * count]
 
         @pl.when(most <= SUB // 2)
         def _():
@@ -484,9 +504,8 @@
     for e in range(experts):
         total = offs_ref[e * (subs + 1) + subs]
         tail = pl.ds(pl.multiple_of(total, 16), CHUNK)
-        n2_slots[e, tail, :] = jnp.zeros((CHUNK, D), bf16)
-        dm_slots[e, tail, :] = jnp.zeros((CHUNK, D), bf16)
-        c_slots[e, tail, :] = jnp.zeros((CHUNK, 128), f32)
+        for slots in held:
+            slots[e, tail, :] = jnp.zeros((CHUNK, slots.shape[2]), slots.dtype)
         for copy in flush(e, total // CHUNK):
             copy.start()
     for e in range(experts):
@@ -499,30 +518,28 @@
         lax.fori_loop(0, offs_ref[e * (subs + 1) + subs] // CHUNK + 1, drain, 0)
 
 
-def gather(n2_parts, dm_parts, offs, pos, c):
+def gather(parts, offs, pos, c=None):
     starts = [0]
-    for n2_part in n2_parts:
-        starts.append(starts[-1] + n2_part.shape[0])
+    for part in parts:
+        starts.append(starts[-1] + part.shape[0])
     experts = pos.shape[0] * SUB // starts[-1]
-    rows = jax.ShapeDtypeStruct((experts, SLOTS, D), bf16)
+    with_c = c is not None
+    held = [((experts, SLOTS, D), bf16)] + [((experts, SLOTS, 128), f32)] * with_c
     return pl.pallas_call(
-        functools.partial(gather_kernel, tuple(starts), experts),
-        out_shape=(rows, rows, jax.ShapeDtypeStruct((experts, SLOTS, 128), f32)),
-        in_specs=[SMEM, VMEM, VMEM] + [HBM] * (2 * len(n2_parts)),
-        out_specs=(HBM, HBM, HBM),
-        scratch_shapes=[
-            pltpu.VMEM((AHEAD, SUB, D), bf16),
-            pltpu.VMEM((AHEAD, SUB, D), bf16),
-            pltpu.VMEM((experts, SLOTS, D), bf16),
-            pltpu.VMEM((experts, SLOTS, D), bf16),
-            pltpu.VMEM((experts, SLOTS, 128), f32),
-            pltpu.SemaphoreType.DMA((2, AHEAD)),
-            pltpu.SemaphoreType.DMA((3, experts, SLOTS // CHUNK)),
+        functools.partial(gather_kernel, tuple(starts), experts, with_c),
+        out_shape=[jax.ShapeDtypeStruct(*kind) for kind in held],
+        in_specs=[SMEM, VMEM] + [VMEM] * with_c + [HBM] * len(parts),
+        out_specs=[HBM] * len(held),
+        scratch_shapes=[pltpu.VMEM(*kind) for kind in held]
+        + [
+            pltpu.VMEM((DEEP, SUB, D), bf16),
+            pltpu.SemaphoreType.DMA((DEEP,)),
+            pltpu.SemaphoreType.DMA((1 + with_c, experts, SLOTS // CHUNK)),
         ],
         compiler_params=pltpu.CompilerParams(vmem_limit_bytes=62 * 2**20),
         cost_estimate=COST,
         name="gather_rows",
-    )(offs, pos, c, *n2_parts, *dm_parts)
+    )(offs, pos, *([c] if with_c else []), *parts)
 
 
 def experts_kernel(first, subs, sources, kept, place_ref, offs_ref, n2_ref, dm_ref, c_ref, *rest):
@@ -548,7 +565,7 @@
             for j, (spot, buf) in enumerate(((slice(0, rin), win_buf), (slice(rin, wrows), wdown_buf)))
         ]
 
-    def in_copies(k, slot):
+    def in_copies(e, k, slot):
         spot = pl.ds(pl.multiple_of(k * CHUNK, CHUNK), CHUNK)
         return [
             pltpu.make_async_copy(source.at[first + e, spot, :], target.at[slot], in_sems.at[i, slot])
@@ -562,12 +579,9 @@
             pltpu.make_async_copy(d_out.at[slot], d_ref.at[e, spot, :], out_sems.at[1, slot]),
         )
 
-    for copy in in_copies(0, 0):
-        copy.start()
-
     @pl.when(e == 0)
     def _():
-        for copy in weight_copies(0):
+        for copy in in_copies(e, 0, 0) + weight_copies(0):
             copy.start()
         zeros[...] = jnp.zeros_like(zeros)
 
@@ -585,12 +599,12 @@
 
     def one_chunk(k, carry):
         slot = lax.rem(k, 2)
-        for copy in in_copies(k, slot):
+        for copy in in_copies(e, k, slot):
             copy.wait()
 
         @pl.when(k + 1 < chunks)
         def _():
-            for copy in in_copies(k + 1, 1 - slot):
+            for copy in in_copies(e, k + 1, 1 - slot):
                 copy.start()
 
         @pl.when(k >= 2)
@@ -619,6 +633,12 @@
         return carry
 
     lax.fori_loop(0, chunks, one_chunk, 0)
+
+    @pl.when(e + 1 < len(sources))
+    def _():
+        for copy in in_copies(e + 1, 0, 0):
+            copy.start()
+
     spot = pl.ds(pl.multiple_of(chunks * CHUNK, CHUNK), CHUNK)
     ends = (
         pltpu.make_async_copy(zeros, m_ref.at[e, spot, :], out_sems.at[0, 2]),
@@ -683,40 +703,55 @@
     arrays = 1 + sources[-1][1]
     parts, rest = rest[:arrays], rest[arrays:]
     outs, (slots, sems) = rest[: len(halves)], rest[len(halves) :]
-    i, steps = pl.program_id(0), subs // 2
-    low = min(halves) * steps
-    high = low + len(halves) * steps
+    i, steps = pl.program_id(0), subs // (2 * PAIR)
+    first = lax.rem(i * PAIR + halves[0] * (subs // 2), subs)
+
+    half = subs // 2
+
+    def each(low, high, act):
+        for spot, (e, array, index) in enumerate(sources):
+
+            def one(chunk, carry):
+                rows = pl.ds(pl.multiple_of(chunk * CHUNK, CHUNK), CHUNK)
+                act(pltpu.make_async_copy(parts[array].at[index, rows, :], slots.at[spot, rows, :], sems.at[spot, chunk]))
+                return carry
+
+            lax.fori_loop(*spans(e, low, high), one, 0)
+
+    def spans(e, low, high):
+        middle = offs_ref[e * (subs + 1) + half] // CHUNK
+        last_low = (offs_ref[e * (subs + 1) + low] + CHUNK - 1) // CHUNK + 1
+        begin = jnp.where(lax.rem(low, half) == 0, offs_ref[e * (subs + 1) + low] // CHUNK, last_low)
+        end = (offs_ref[e * (subs + 1) + high] + CHUNK - 1) // CHUNK + 1
+        if len(halves) == 2:
+            early = jnp.asarray(low) < half
+            begin = jnp.where(early, jnp.minimum(begin, middle), begin)
+            end = jnp.where(early, jnp.minimum(end, middle), end)
+        return begin, end
 
     @pl.when(i == 0)
     def _():
-        def each(act):
-            for spot, (e, array, index) in enumerate(sources):
-
-                def one(chunk, carry):
-                    rows = pl.ds(pl.multiple_of(chunk * CHUNK, CHUNK), CHUNK)
-                    act(pltpu.make_async_copy(parts[array].at[index, rows, :], slots.at[spot, rows, :], sems.at[spot, chunk]))
-                    return carry
-
-                begin = offs_ref[e * (subs + 1) + low] // CHUNK
-                end = (offs_ref[e * (subs + 1) + high] + CHUNK - 1) // CHUNK + 1
-                lax.fori_loop(begin, end, one, 0)
-
-        each(lambda copy: copy.start())
-        each(lambda copy: copy.wait())
-
-    block = lax.rem(i + halves[0] * steps, subs)
+        for h in halves:
+            each(h * half, (h + 1) * half, lambda copy: copy.start())
+
+    each(first, first + PAIR, lambda copy: copy.wait())
     lane = lax.broadcasted_iota(jnp.int32, (SUB, SUB), 1).astype(f32)
-    picks = [jnp.where(lane == pos_ref[:, e : e + 1], 1.0, 0.0).astype(bf16) for e, _, _ in sources]
-    windows = [
-        slots[spot, pl.ds(pl.multiple_of(offs_ref[e * (subs + 1) + block], 16), SUB), :]
-        for spot, (e, _, _) in enumerate(sources)
-    ]
-    total = dot(jnp.concatenate(picks, axis=1), jnp.concatenate(windows, axis=0))
+    totals = []
+    for p in range(PAIR):
+        picks = [
+            jnp.where(lane == pos_ref[p * SUB : (p + 1) * SUB, e : e + 1], 1.0, 0.0).astype(bf16) for e, _, _ in sources
+        ]
+        windows = [
+            slots[spot, pl.ds(pl.multiple_of(offs_ref[e * (subs + 1) + first + p], 16), SUB), :]
+            for spot, (e, _, _) in enumerate(sources)
+        ]
+        totals.append(dot(jnp.concatenate(picks, axis=1), jnp.concatenate(windows, axis=0)).astype(bf16))
     for j, out_ref in enumerate(outs):
 
         @pl.when(i // steps == j)
         def _():
-            out_ref[...] = total.astype(bf16)
+            for p in range(PAIR):
+                out_ref[p * SUB : (p + 1) * SUB, :] = totals[p]
 
 
 def scatter(offs, pos_columns, parts, halves):
@@ -725,17 +760,17 @@
         (first + index, i, index) for i, (part, first) in enumerate(parts) for index in range(part.shape[0])
     ]
     subs = tokens // SUB
-    steps = subs // 2
+    steps = subs // (2 * PAIR)
     shift = halves[0] * steps
     blocks = [
-        pl.BlockSpec((SUB, D), lambda i, j=j: (jnp.clip(i - j * steps, 0, steps - 1), 0))
+        pl.BlockSpec((PAIR * SUB, D), lambda i, j=j: (jnp.clip(i - j * steps, 0, steps - 1), 0))
         for j in range(len(halves))
     ]
     return pl.pallas_call(
         functools.partial(scatter_kernel, halves, sources, experts, subs),
         grid=(len(halves) * steps,),
-        out_shape=[jax.ShapeDtypeStruct((steps * SUB, D), bf16)] * len(halves),
-        in_specs=[SMEM, pl.BlockSpec((SUB, experts), lambda i: (lax.rem(i + shift, subs), 0))]
+        out_shape=[jax.ShapeDtypeStruct((tokens // 2, D), bf16)] * len(halves),
+        in_specs=[SMEM, pl.BlockSpec((PAIR * SUB, experts), lambda i: (lax.rem(i + shift, 2 * steps), 0))]
         + [HBM] * len(parts),
         out_specs=blocks,
         scratch_shapes=[
@@ -795,6 +830,43 @@
     )(place, mine, recv, *states, *kept)
 
 
+def adam_rest_kernel(scale, place_ref, mine_ref, *rest):
+    count = len(rest) - 25
+    received, states, news, (grad_ref,) = rest[:count], rest[count : count + 12], rest[count + 12 : count + 24], rest[-1:]
+    total = mine_ref[...]
+    for part in received:
+        total = total + part[...].astype(f32)
+    grad_ref[...] = total * scale
+    rows, cols = states[0].shape[1:]
+    width = states[9].shape[2]
+    for i, turned in ((0, False), (1, False), (2, True)):
+        part = grad_ref[i * rows : (i + 1) * rows, :]
+        refs = slice(3 * i, 3 * i + 3)
+        masters = [ref[0] for ref in states[refs]]
+        for ref, new in zip(news[refs], adam_update(*masters, part.T if turned else part, WEIGHT_DECAY)):
+            ref[0] = new
+    start = place_ref[3] * width
+    for i in range(2):
+        row = grad_ref[pl.ds(3 * rows + i * (D // cols) + start // cols, 1), :]
+        part = pltpu.roll(row, lax.rem(cols - lax.rem(start, cols), cols), 1)[:, :width]
+        moments = [ref[0, i : i + 1, :] for ref in states[9:11]]
+        for ref, new in zip(news[9:], adam_change(*moments, part)):
+            ref[0, i : i + 1, :] = new
+
+
+def adam_rest(place, scale, mine, received, states):
+    return pl.pallas_call(
+        functools.partial(adam_rest_kernel, scale),
+        out_shape=[jax.ShapeDtypeStruct(state.shape, f32) for state in states],
+        in_specs=[SMEM] + [VMEM] * (1 + len(received) + len(states)),
+        out_specs=[VMEM] * len(states),
+        scratch_shapes=[pltpu.VMEM(mine.shape, f32)],
+        compiler_params=pltpu.CompilerParams(vmem_limit_bytes=32 * 2**20),
+        cost_estimate=COST,
+        name="adam_rest",
+    )(place, mine, *received, *states)
+
+
 def on_device(
     ndp,
     nt,
@@ -825,7 +897,7 @@
     place_dp = lax.axis_index("dp")
     t = lax.axis_index("tensor")
     z, core = place_dp // 2, place_dp % 2
-    place = jnp.stack([z, core, t]).astype(jnp.int32)
+    place = jnp.stack([z, core, t, place_dp * nt + t]).astype(jnp.int32)
     rows = tokens.shape[0]
     sharers = max(1, SEQ_LEN // rows)
 
@@ -868,7 +940,6 @@
         ],
         axis=0,
     )
-    own_z = spread_z(own)
     half = expert_in.shape[1] // 2
     groups = [[2 * i + c for i in range(nz)] for c in range(2)]
 
@@ -889,16 +960,16 @@
     spans = [(a, b) for a, b in spans if a < b]
     shards = [shard(*spans[0])]
     for a, b in spans[1:]:
-        shards.append(shard(a, b, own_z[1]))
-    own_z[1:], shards = lax.optimization_barrier((own_z[1:], shards))
-    column = jnp.stack(own_z)
+        shards.append(shard(a, b))
+    column = lax.all_gather(own, "dp", axis=0, tiled=False, axis_index_groups=groups)
     held = {}
     for (a, b), part in zip(spans, shards):
-        whole = lax.all_gather(after(part, column), "dp", axis=0, tiled=False, axis_index_groups=groups)
+        whole = lax.all_gather(part, "dp", axis=0, tiled=False, axis_index_groups=groups)
         held.update({i: (whole, i - a) for i in range(a, b)})
-    pieces = spread_t(column[:, : 2 * wrows + 16])
-    pieces_out = spread_t(after(column[:, 2 * wrows + 16 :], pieces[nt - 1]))
-    dm_near = near(after(cotangent, *pieces_out[1:nt]))
+    dm_near = near(cotangent)
+    dm_far = far(cotangent, dm_near)
+    pieces = spread_t(after(column[:, : 2 * wrows + 16], *dm_near))
+    pieces_out = spread_t(after(column[:, 2 * wrows + 16 :], *pieces[1:], *dm_far))
     pieces = pieces + [swap_core(piece) for piece in pieces]
     pieces_out = pieces_out + [swap_core(piece) for piece in pieces_out]
 
@@ -931,12 +1002,16 @@
         n2 = lax.dynamic_slice_in_dim(n2, first_row, rows, 0)
 
     n2_near = near(n2)
-    n2_own = [n2] + n2_near + far(n2, n2_near)
-    dm_near = list(lax.optimization_barrier((*dm_near, *n2_near))[: len(dm_near)])
-    dm_own = [cotangent] + dm_near + far(cotangent, dm_near)
+    n2_far = far(n2, n2_near)
+    n2_own = [n2] + n2_near
+    dm_own = [cotangent] + dm_near + dm_far
     dm_parts = dm_own + [swap_core(part) for part in dm_own]
+    dm_slots, c_slots = gather(dm_parts, offs.reshape(-1), pos, c_rows)
+    dm_slots, c_slots, *n2_far = lax.optimization_barrier((dm_slots, c_slots, *n2_far))
+    n2_own = n2_own + n2_far
     n2_parts = n2_own + [swap_core(part) for part in n2_own]
-    slots = gather(n2_parts, dm_parts, offs.reshape(-1), pos, c_rows)
+    (n2_slots,) = gather(n2_parts, offs.reshape(-1), pos)
+    slots = (n2_slots, dm_slots, c_slots)
     m_parts, d_parts, expert_grads = [], [], []
     for calls in CALLS:
         start, stop = cut((calls[0][0], calls[-1][1]))
@@ -968,70 +1043,71 @@
 
     def to_tokens(parts, last=()):
         if nt != 4:
-            return [swap_t(parts[k], k) for k in range(1, nt)], parts[nt - 1]
+            return [swap_t(parts[k], k) for k in range(1, nt)], parts[1:]
         mid = parts[3].shape[0] // 2
         by_x, by_y = swap_t(parts[3][:mid], 1), swap_t(parts[3][mid:], 2)
         x_first, y_last = swap_t(parts[1][:mid], 1), swap_t(parts[2][mid:], 2)
         by_x, by_y, *_ = lax.optimization_barrier((by_x, by_y, *last))
         x_part = (parts[1][mid:].astype(f32) + by_y.astype(f32)).astype(bf16)
         y_part = (parts[2][:mid].astype(f32) + by_x.astype(f32)).astype(bf16)
-        return [x_first, swap_t(x_part, 1), swap_t(y_part, 2), y_last], y_part
-
-    def collect(total, received):
-        if nt != 4:
-            for part in received:
-                total = total + part.astype(f32)
-            return total
-        x_first, x_last, y_first, y_last = (part.astype(f32) for part in received)
-        return total + jnp.concatenate([x_first + y_first, x_last + y_last], axis=0)
+        return [x_first, swap_t(x_part, 1), swap_t(y_part, 2), y_last], (x_part, y_part)
 
     (d_other,) = scatter(offs, pos_columns, d_parts, (1,))
     (d_own,) = scatter(offs, pos_columns, d_parts, (0,))
     d_own, d_sent = both_cores(d_own, swap_core(d_other))
+    def to_owners(parts, meanwhile):
+        if nt != 4:
+            return sum_received([swap_t(parts[k], k) for k in range(1, nt)], nt), meanwhile
+        mid = parts[3].shape[0] // 2
+        by_x = swap_t(jnp.concatenate([parts[3][:mid], parts[1][:mid]]), 1)
+        by_y = swap_t(jnp.concatenate([parts[3][mid:], parts[2][mid:]]), 2)
+        by_x, by_y, meanwhile = lax.optimization_barrier((by_x, by_y, meanwhile))
+        x_last = swap_t((parts[1][mid:].astype(f32) + by_y[:mid].astype(f32)).astype(bf16), 1)
+        y_first = swap_t((parts[2][:mid].astype(f32) + by_x[:mid].astype(f32)).astype(bf16), 2)
+        return sum_received([by_x[mid:], x_last, y_first, by_y[mid:]], nt), meanwhile
+
     d_received, d_last = to_tokens([None] + d_sent)
-    dn2 = collect(d_own, d_received)
-    m_pos = after(pos_columns, d_last)
+    m_pos = after(pos_columns, *d_last)
     m_other, m_own = scatter(offs, m_pos, m_parts, (1, 0))
     m_other = jnp.concatenate([swap_core(m_other[k * rows : (k + 1) * rows]) for k in range(nt)])
     m_own, m_sent = both_cores(m_own, m_other)
 
-    grad = cotangent.astype(f32)
-    inverse = rms_scale(s1)
-    unit = s1 * inverse
-    gain_two = jnp.sum(dn2 * unit, axis=0)
-    scaled = dn2 * gains[1]
-    gs1 = grad + inverse * (scaled - unit * jnp.mean(scaled * unit, axis=-1, keepdims=True))
-
+    whole = sharers == 1
+    gs1, gain_two = norm_backward(d_own + sum_received(d_received, nt), s1, gains[1:2], cotangent.astype(f32))
     da, *m_sent = lax.optimization_barrier((gs1.astype(bf16), *m_sent))
-    m_received = [swap_t(part, k + 1) for k, part in enumerate(m_sent)]
-    if sharers > 1:
+    if nt == 4:
+        mid = rows // 2
+        m_step = [swap_t(m_sent[2][:mid], 1), swap_t(m_sent[2][mid:], 2)]
+        m_step += [swap_t(m_sent[0][:mid], 1), swap_t(m_sent[1][mid:], 2)]
+    else:
+        m_step = [swap_t(part, k + 1) for k, part in enumerate(m_sent)]
+    if not whole:
         da = lax.all_gather(da, "tensor", axis=0, tiled=True, axis_index_groups=seq_groups)
-    dn1, grads_own, grads_other = attend_backward(
-        (nz, nt), place, sequence, da, gains, gain_two[None] * sharers, q, kv, o, lse, qkv_weights, out_weight
+    input_grad, grads_own, grads_other = attend_backward(
+        (nz, nt), whole, place, sequence, gains, q, kv, o, lse, qkv_weights, out_weight,
+        da, gain_two * sharers, *([gs1] if whole else []),
     )
-    block_out = m_own + s1
-    for part in m_received:
-        block_out = block_out + part.astype(f32)
-    if sharers > 1:
-        dn1 = lax.dynamic_slice_in_dim(dn1, first_row, rows, 0)
-
-    stream = tokens.astype(f32)
-    inverse = rms_scale(stream)
-    unit = stream * inverse
-    scaled = dn1 * gains[0]
-    input_grad = gs1 + inverse * (scaled - unit * jnp.mean(scaled * unit, axis=-1, keepdims=True))
-
-    grads_other = after(grads_other, *m_received)
-    both = (grads_own.astype(f32) + swap_core(grads_other).astype(f32)).astype(bf16)
-    received, _ = to_tokens([both[k] for k in range(nt)])
-
+    if not whole:
+        dn1 = lax.dynamic_slice_in_dim(input_grad, first_row, rows, 0)
+        input_grad, _ = norm_backward(dn1, tokens.astype(f32), gains[0], gs1)
+
+    grads_other, m_step = lax.optimization_barrier((grads_other, m_step))
+    swapped = [swap_core(part) for part in grads_other]
+    both = [(grads_own[k].astype(f32) + swapped[k].astype(f32)).astype(bf16) for k in range(nt)]
+    if nt == 4:
+        by_x, by_y, x_first, y_last = m_step
+        by_x, by_y, *_ = lax.optimization_barrier((by_x, by_y, grads_own))
+        x_last = swap_t((m_sent[0][mid:].astype(f32) + by_y.astype(f32)).astype(bf16), 1)
+        y_first = swap_t((m_sent[1][:mid].astype(f32) + by_x.astype(f32)).astype(bf16), 2)
+        m_step = [x_first, x_last, y_first, y_last]
+    block_out = s1 + m_own + sum_received(m_step, nt)
     states = [expert_in, expert_in_first, expert_in_second, expert_down, expert_down_first, expert_down_second]
     experts_new = None
     for start, got in expert_grads[:-1]:
+        got = after(got, grads_own)
         experts_new = adam_experts(place, start, got, swap_core(got[1]), states, experts_new)
-    block_out, experts_new, received = lax.optimization_barrier((block_out, experts_new, received))
-
-    total = collect(both[0].astype(f32), received)
+    received, (experts_new, block_out) = to_owners(both, (experts_new, block_out))
+    total = both[0].astype(f32) + received
     owned = total[0]
     sent = [total[j].astype(bf16) for j in range(1, nz)]
     received = [swap_z(part, j + 1) for j, part in enumerate(sent)]
@@ -1039,18 +1115,10 @@
         got = after(got, *sent, *experts_new)
         experts_new = adam_experts(place, start, got, swap_core(got[1]), states, experts_new)
     received, experts_new = lax.optimization_barrier((received, experts_new))
-    for part in received:
-        owned = owned + part.astype(f32)
-    owned = owned * (1.0 / sharers)
-    query_grad, keyval_grad, out_grad = (owned[i * wrows : (i + 1) * wrows] for i in range(3))
-    gg = owned[3 * wrows : 3 * wrows + 2 * nt].reshape(1, 2, D)
-    gg = lax.dynamic_slice_in_dim(gg, (place_dp * nt + t) * width, width, 2)
-
-    gains_new = adam_change(norm_gains_first, norm_gains_second, gg)
-    query_new = adam_update(query_weight, query_first, query_second, query_grad[None], WEIGHT_DECAY)
-    keyval_new = adam_update(keyval_weight, keyval_first, keyval_second, keyval_grad[None], WEIGHT_DECAY)
-    output_new = adam_update(output_weight, output_first, output_second, out_grad.T[None], WEIGHT_DECAY)
-    return (block_out, input_grad) + gains_new + query_new + keyval_new + output_new + tuple(experts_new)
+    states = [query_weight, query_first, query_second, keyval_weight, keyval_first, keyval_second]
+    states += [output_weight, output_first, output_second, norm_gains, norm_gains_first, norm_gains_second]
+    rest_new = adam_rest(place, 1.0 / sharers, owned, received, states[:9] + states[10:] + states[9:10])
+    return (block_out, input_grad, *rest_new[9:], *rest_new[:9], *experts_new)
 
 
 def solution(mesh):

time: 557 us -> 528 us (0.948); the launches traced: 563 us -> 520 us
  waiting for transfers between devices: 155 us -> 103 us
  blocking collectives: 0 us -> 32.5 us
  starting transfers between devices: 97.2 us -> 82.5 us
  Pallas kernels: 217 us -> 207 us
    all_gather x0 -> x1, blocking collectives: none -> 32.5 us  [on_device(): lax.all_gather(own, 'dp', axis=0, tiled=False, axis_index_groups=groups)]
    ppermute x29 -> x30, waiting for transfers between devices: 123 us -> 90.1 us  [swap_t(): return lax.ppermute(x, 'tensor', [(i, i ^ k) for i in range(nt)])]
    ppermute x29 -> x30, starting transfers between devices: 70.6 us -> 49.4 us  [swap_t(): return lax.ppermute(x, 'tensor', [(i, i ^ k) for i in range(nt)])]
    ppermute x30 -> x32, starting transfers between devices: 8.79 us -> 23.8 us  [swap_core(): return lax.ppermute(x, 'dp', [(i, i ^ 1) for i in range(ndp)])]
    all_gather x3 -> x2, waiting for transfers between devices: 14.6 us -> 3.5 us  [on_device(): lax.all_gather(part, 'dp', axis=0, tiled=False, axis_index_groups=groups)]
    pallas_call x3, Pallas kernels: 71.2 us -> 60.9 us  [experts_step(): pl.pallas_call(functools.partial(experts_kernel, first, subs, sources, le...]
    pallas_call x2 -> x4, Pallas kernels: 52.8 us -> 62.8 us  [the longest x1 35.6 us: attend_backward(): pl.pallas_call(functools.partial(attend_backward_kernel, nz, nt, whole),...]
    ppermute x6 -> x3, starting transfers between devices: 17.3 us -> 8.53 us  [swap_z(): return lax.ppermute(x, 'dp', [(i, i ^ 2 * j) for i in range(ndp)])]
  transfers between devices with their start and end apart: 70 -> 69, of which waited for: 23 -> 21; matrix products, arithmetic and copies ran while one was open for 10% -> 12% of each run, Pallas kernels for 39% -> 39%
where the time goes in v3:
time: 528 us; the launch traced here: 520 us
  Pallas kernels  207 us (39%)
  waiting for transfers between devices  103 us (20%)
  starting transfers between devices  82.5 us (16%)
  other arithmetic  43.7 us (8%)
  local copies, waits for them, and re-layouts  37 us (7%)
  blocking collectives  32.5 us (6%)
  between operations  15.2 us (3%)
    ppermute x30, waiting for transfers between devices, swap_t(): return lax.ppermute(x, 'tensor', [(i, i ^ k) for i in range(nt)])  90.1 us
    pallas_call x3, Pallas kernels, experts_step(): pl.pallas_call(functools.partial(experts_kernel, first, subs, sources, le...  60.9 us
    ppermute x30, starting transfers between devices, swap_t(): return lax.ppermute(x, 'tensor', [(i, i ^ k) for i in range(nt)])  49.4 us
    pallas_call x3, Pallas kernels, scatter(): pl.pallas_call(functools.partial(scatter_kernel, halves, sources, experts...  40.9 us
    pallas_call x1, Pallas kernels, attend_backward(): pl.pallas_call(functools.partial(attend_backward_kernel, nz, nt, whole),...  35.6 us
    all_gather x1, blocking collectives, on_device(): lax.all_gather(own, 'dp', axis=0, tiled=False, axis_index_groups=groups)  32.5 us
    pallas_call x2, Pallas kernels, gather(): pl.pallas_call(functools.partial(gather_kernel, tuple(starts), experts, w...  25.2 us
    ppermute x32, starting transfers between devices, swap_core(): return lax.ppermute(x, 'dp', [(i, i ^ 1) for i in range(ndp)])  23.8 us
  transfers between devices with their start and end apart: 69, of which 21 were waited for; matrix products, arithmetic and copies ran while one was open for 12% of the time, Pallas kernels for 39%

profile of v3, /device:TPU:0, one launch (start us, length us, event | category | flops | bytes accessed | tf_op | source)
XLA Modules:
  0.0 520.5 jit_solution(16092030979723872370)
XLA Ops:
  10.4 2.1 fusion.4
  13.4 2.4 collective-permute-done.33
  15.8 1.6 pad_maximum_fusion
  18.6 2.9 collective-permute-start.1
  21.5 1.5 collective-permute-start.2
  25.2 32.5 %all-gather = bf16[1600,256]{1,0:T(8,128)(2,1)S(1)} all-gather(bf16[400,256]{1,0:T(8,128)(2,1)S(1)} %pad_maximum_fusion.6), channel_id=2, replica_groups={{0,8,16,24},{4,12,20,28},{1,9,17,25},{5,13,21,29},{2,10,18,26},{6,14,22..., dimensions={0}, use_global_device_ids=true | all-gather | bytes 1024000 | tf_op jit(solution)/shard_map/all_gather | solution.py:964
  57.7 1.9 slice.232
  61.7 2.1 collective-permute-start.3
  63.7 2.0 collective-permute-start.4
  65.8 9.0 %collective-permute-done.10.rest_4_ = bf16[256,1024]{1,0:T(8,128)(2,1)} collective-permute-done((bf16[256,1024]{1,0:T(8,128)(2,1)}, bf16[256,1024]{1,0:T(8,128)(2,1)}, u32[]{:S(2)}, u32[]{:S(2)}) %collective-permute-start.10) | collective-permute-done | bytes 524320 | tf_op jit(solution)/shard_map/ppermute | solution.py:911
  77.3 11.1 %collective-permute-done.3.rest_1_ = bf16[4,272,256]{2,1,0:T(8,128)(2,1)} collective-permute-done((bf16[4,272,256]{2,1,0:T(8,128)(2,1)S(1)}, bf16[4,272,256]{2,1,0:T(8,128)(2,1)}, u32[]{:S(2)}, u32[]{:S(2)}) %collective-permute-start.3) | collective-permute-done | bytes 557088 | tf_op jit(solution)/shard_map/ppermute | solution.py:911
  88.4 11.9 %collective-permute-done.5.rest_3_ = bf16[4,272,256]{2,1,0:T(8,128)(2,1)} collective-permute-done((bf16[4,272,256]{2,1,0:T(8,128)(2,1)S(1)}, bf16[4,272,256]{2,1,0:T(8,128)(2,1)}, u32[]{:S(2)}, u32[]{:S(2)}) %collective-permute-start.5) | collective-permute-done | bytes 557088 | tf_op jit(solution)/shard_map/ppermute | solution.py:911
  102.7 4.4 collective-permute-done.12.rest_1_
  108.1 2.0 copy.67
  110.1 2.1 pad_maximum_fusion.4
  112.4 4.3 collective-permute-done.13.rest_2_
  118.8 18.7 %attend_forward.1 = (bf16[512,1024]{1,0:T(8,128)(2,1)S(1)}, bf16[512,1024]{1,0:T(8,128)(2,1)S(1)}, bf16[512,1024]{1,0:T(8,128)(2,1)S(1)}, f32[512,128]{1,0:T(8,1...) custom-call(s32[4]{0:T(128)S(1)} %pad_add_fusion.place_ref, bf16[512,1024]{1,0:T(8,128)(2,1)S(1)} %copy-done.3, ...), custom_call_target="tpu_custom_call" | custom-call | flops 24999999488 | bytes 12582912 | tf_op jit(solution)/shard_map/attend_forward/pallas_call | solution.py:230
  140.2 3.6 attend_out.1
  147.5 1.8 collective-permute-start.19
  150.0 22.8 %collective-permute-done.19.rest_1_ = bf16[512,1024]{1,0:T(8,128)(2,1)S(1)} collective-permute-done((bf16[512,1024]{1,0:T(8,128)(2,1)}, bf16[512,1024]{1,0:T(8,128)(2,1)S(1)}, u32[]{:S(2)}, u32[]{:S(2)}) %collective-permute-start.19) | collective-permute-done | bytes 1048608 | tf_op jit(solution)/shard_map/ppermute | solution.py:911
  172.8 1.6 collective-permute-done.20.rest_2_
  175.2 1.9 slice.235
  180.5 13.0 %gather_rows.2 = (bf16[4,2560,1024]{2,1,0:T(8,128)(2,1)}, f32[4,2560,128]{2,1,0:T(8,128)}) custom-call(s32[68]{0:T(128)} %reshape.193.offs_ref, f32[64,256]{1,0:T(8,128)} %copy-done.38, f32[64,256]{1,0:T(8,128)} %copy-done.42, bf16[512,1024]{1,0:T(8,128)(2,1)} %rest_1_.3, bf16[512,1024]{1,0:T(8,128)(2,1)} %collective-permute-done.1.rest_2_, ...), custom_call_target="tpu_custom_call" | custom-call | flops 1 | bytes 1 | tf_op jit(solution)/shard_map/gather_rows/pallas_call | solution.py:528
  194.1 1.4 collective-permute-done.31.rest_8_
  197.2 12.3 %gather_rows.3.n2_ref = bf16[4,2560,1024]{2,1,0:T(8,128)(2,1)} custom-call(s32[68]{0:T(128)} %reshape.193.offs_ref, f32[64,256]{1,0:T(8,128)} %copy-done.38, bf16[512,1024]{1,0:T(8,128)(2,1)} %get-tuple-element.129.rest_0_, bf16[512,1024]{1,0:T(8,128)(2,1)} %copy-done.37, bf16[512,1024]{1,0:T(8,128)(2,1)} %collective-permute-done.20.rest_2_, ...), custom_call_target="tpu_custom_call" | custom-call | flops 1 | bytes 1 | tf_op jit(solution)/shard_map/gather_rows/pallas_call | solution.py:528
  209.5 34.5 %experts.3 = (bf16[2,3072,1024]{2,1,0:T(8,128)(2,1)}, bf16[2,3072,1024]{2,1,0:T(8,128)(2,1)}, bf16[4,2,2,192,1024]{4,3,2,1,0:T(8,128)(2,1)}) custom-call(s32[4]{0:T(128)} %copy-done.21, s32[68]{0:T(128)} %reshape.193.offs_ref, bf16[4,2560,1024]{2,1,0:T(8,128)(2,1)} %gather_rows.3.n2_ref, bf16[4,2560,1024]{2,1,0:T(8,128)(2,1)} %get-tuple-element.134.dm_ref, ...), custom_call_target="tpu_custom_call" | custom-call | flops 1 | bytes 1 | tf_op jit(solution)/shard_map/experts/pallas_call | solution.py:672
  244.5 11.8 %experts.4 = (bf16[1,3072,1024]{2,1,0:T(8,128)(2,1)}, bf16[1,3072,1024]{2,1,0:T(8,128)(2,1)}, bf16[4,2,2,192,1024]{4,3,2,1,0:T(8,128)(2,1)}) custom-call(s32[4]{0:T(128)} %copy-done.21, s32[68]{0:T(128)} %reshape.193.offs_ref, bf16[4,2560,1024]{2,1,0:T(8,128)(2,1)} %gather_rows.3.n2_ref, bf16[4,2560,1024]{2,1,0:T(8,128)(2,1)} %get-tuple-element.134.dm_ref, ...), custom_call_target="tpu_custom_call" | custom-call | flops 1 | bytes 1 | tf_op jit(solution)/shard_map/experts/pallas_call | solution.py:672
  256.3 3.5 all-gather.8.cloned.1.call-done
  259.8 14.7 %experts.5 = (bf16[1,3072,1024]{2,1,0:T(8,128)(2,1)}, bf16[1,3072,1024]{2,1,0:T(8,128)(2,1)}, bf16[4,2,2,192,1024]{4,3,2,1,0:T(8,128)(2,1)}) custom-call(s32[4]{0:T(128)} %copy-done.21, s32[68]{0:T(128)} %reshape.193.offs_ref, bf16[4,2560,1024]{2,1,0:T(8,128)(2,1)} %gather_rows.3.n2_ref, ...), custom_call_target="tpu_custom_call", output_to_operand_aliasing={{2}: (6, {})} | custom-call | flops 1 | bytes 1 | tf_op jit(solution)/shard_map/experts/pallas_call | solution.py:672
  274.5 11.2 %scatter_rows.4 = bf16[2048,1024]{1,0:T(8,128)(2,1)} custom-call(s32[68]{0:T(128)} %reshape.193.offs_ref, f32[4096,4]{1,0:T(8,128)} %bitcast.82, bf16[2,3072,1024]{2,1,0:T(8,128)(2,1)} %get-tuple-element.138.rest_0_, bf16[1,3072,1024]{2,1,0:T(8,128)(2,1)} %get-tuple-element.139.rest_1_, bf16[1,3072,1024]{2,1,0:T(8,128)(2,1)} %get-tuple-element.141.rest_2_), custom_call_target="tpu_custom_call" | custom-call | flops 1 | bytes 1 | tf_op jit(solution)/shard_map/scatter_rows/pallas_call | solution.py:769
  285.7 17.9 %collective-permute-start.35 = (bf16[2048,1024]{1,0:T(8,128)(2,1)}, bf16[2048,1024]{1,0:T(8,128)(2,1)}, u32[]{:S(2)}, u32[]{:S(2)}) collective-permute-start(bf16[2048,1024]{1,0:T(8,128)(2,1)} %scatter_rows.4), channel_id=1, source_target_pairs={{0,4},{4,0},{8,12},{12,8},{16,20},{20,16},{24,28},{28,24},{1,5},{5... | collective-permute-start | bytes 12582920 | tf_op jit(solution)/shard_map/ppermute | solution.py:905
  303.6 11.2 %scatter_rows.3 = bf16[2048,1024]{1,0:T(8,128)(2,1)} custom-call(s32[68]{0:T(128)} %reshape.193.offs_ref, f32[4096,4]{1,0:T(8,128)} %bitcast.83, bf16[2,3072,1024]{2,1,0:T(8,128)(2,1)} %get-tuple-element.138.rest_0_, bf16[1,3072,1024]{2,1,0:T(8,128)(2,1)} %get-tuple-element.139.rest_1_, bf16[1,3072,1024]{2,1,0:T(8,128)(2,1)} %get-tuple-element.141.rest_2_), custom_call_target="tpu_custom_call" | custom-call | flops 1 | bytes 1 | tf_op jit(solution)/shard_map/scatter_rows/pallas_call | solution.py:769
  314.8 4.3 add_convert_fusion.5
  319.3 20.4 %collective-permute-start.38 = (bf16[256,1024]{1,0:T(8,128)(2,1)S(1)}, bf16[256,1024]{1,0:T(8,128)(2,1)S(1)}, u32[]{:S(2)}, u32[]{:S(2)}) collective-permute-start(bf16[256,1024]{1,0:T(8,128)(2,1)S(1)} %get-tuple-element.245), channel_id=1, source_target_pairs={{0,2},{1,3},{2,0},{3,1},{4,6},{5,7},{6,4},{7,5},{8,10},{9,11},{10,... | collective-permute-start | bytes 1572872 | tf_op jit(solution)/shard_map/ppermute | solution.py:911
  340.9 1.4 collective-permute-start.41
  342.4 10.1 %collective-permute-done.38 = bf16[256,1024]{1,0:T(8,128)(2,1)S(1)} collective-permute-done((bf16[256,1024]{1,0:T(8,128)(2,1)S(1)}, bf16[256,1024]{1,0:T(8,128)(2,1)S(1)}, u32[]{:S(2)}, u32[]{:S(2)}) %collective-permute-start.38) | collective-permute-done | bytes 524320 | tf_op jit(solution)/shard_map/ppermute | solution.py:911
  352.6 2.1 collective-permute-start.39
  355.1 18.4 %scatter_rows.5 = (bf16[2048,1024]{1,0:T(8,128)(2,1)}, bf16[2048,1024]{1,0:T(8,128)(2,1)}) custom-call(s32[68]{0:T(128)} %reshape.193.offs_ref, f32[4096,4]{1,0:T(8,128)} %bitcast.84, bf16[2,3072,1024]{2,1,0:T(8,128)(2,1)} %get-tuple-element.145.rest_0_, bf16[1,3072,1024]{2,1,0:T(8,128)(2,1)} %get-tuple-element.146.rest_1_, ...), custom_call_target="tpu_custom_call" | custom-call | flops 1 | bytes 1 | tf_op jit(solution)/shard_map/scatter_rows/pallas_call | solution.py:769
  373.5 3.6 fusion.31
  377.7 1.5 convert_add_fusion.7
  380.6 2.8 multiply_reduce_fusion
  383.4 4.0 fusion.30
  387.4 1.6 add_convert_fusion
  390.2 2.2 collective-permute-start.45
  396.1 35.6 %attend_backward.1 = (f32[512,1024]{1,0:T(8,128)}, bf16[4,4,400,256]{3,2,1,0:T(8,128)(2,1)}, bf16[4,400,256]{2,1,0:T(8,128)(2,1)}, bf16[4,400,256]{2,1,0:T(8,128...) custom-call(s32[4]{0:T(128)} %copy-done.21, bf16[512,1024]{1,0:T(8,128)(2,1)} %tokens_ref.2, ...), custom_call_target="tpu_custom_call" | custom-call | flops 1 | bytes 1 | tf_op jit(solution)/shard_map/attend_backward/pallas_call | solution.py:410
  432.8 2.2 add_convert_fusion.7
  436.9 1.7 collective-permute-start.57
  438.6 2.2 fusion.1
  442.0 1.5 collective-permute-start.53
  446.4 3.8 collective-permute-done.56
  450.1 1.4 convert_add_fusion.5
  453.2 3.5 maximum_add_fusion.1
  456.7 10.0 %adam_experts.2 = (f32[1,8,128,1024]{3,2,1,0:T(8,128)}, f32[1,8,128,1024]{3,2,1,0:T(8,128)}, f32[1,8,128,1024]{3,2,1,0:T(8,128)}, f32[1,8,64,1024]{3,2,1,0:T(8,1...) custom-call(s32[4]{0:T(128)} %copy-done.21, bf16[2,2,192,1024]{3,2,1,0:T(8,128)(2,1)} %bitcast.86, ...), custom_call_target="tpu_custom_call" | custom-call | flops 1 | bytes 1 | tf_op jit(solution)/shard_map/adam_experts/pallas_call | solution.py:810
  466.8 1.6 collective-permute-done.51
  469.5 1.5 collective-permute-start.59
  472.2 1.8 collective-permute-start.60
  474.0 6.0 %collective-permute-done.59 = bf16[2,400,256]{2,1,0:T(8,128)(2,1)S(1)} collective-permute-done((bf16[2,400,256]{2,1,0:T(8,128)(2,1)S(1)}, bf16[2,400,256]{2,1,0:T(8,128)(2,1)S(1)}, u32[]{:S(2)}, u32[]{:S(2)}) %collective-permute-start.59) | collective-permute-done | bytes 409632 | tf_op jit(solution)/shard_map/ppermute | solution.py:911
  481.0 3.1 collective-permute-done.60
  485.2 1.5 fusion.29
  488.5 2.6 collective-permute-start.61
  491.1 5.9 %collective-permute-start.62 = (bf16[400,256]{1,0:T(8,128)(2,1)S(1)}, bf16[400,256]{1,0:T(8,128)(2,1)S(1)}, u32[]{:S(2)}, u32[]{:S(2)}) collective-permute-start(bf16[400,256]{1,0:T(8,128)(2,1)S(1)} %get-tuple-element.248), channel_id=1, source_target_pairs={{0,16},{4,20},{8,24},{12,28},{16,0},{20,4},{24,8},{28,12},{1,17},{... | collective-permute-start | bytes 614408 | tf_op jit(solution)/shard_map/ppermute | solution.py:908
  498.1 9.9 %adam_experts.3 = (f32[1,8,128,1024]{3,2,1,0:T(8,128)}, f32[1,8,128,1024]{3,2,1,0:T(8,128)}, f32[1,8,128,1024]{3,2,1,0:T(8,128)}, f32[1,8,64,1024]{3,2,1,0:T(8,1...) custom-call(s32[4]{0:T(128)} %copy-done.21, ...), custom_call_target="tpu_custom_call", output_to_operand_aliasing={{0}: (9, {}), {1}: (10, {}), {2}: (11, {}), {3}: (12, {}), ... | custom-call | flops 1 | bytes 1 | tf_op jit(solution)/shard_map/adam_experts/pallas_call | solution.py:810
  507.9 3.7 collective-permute-done.62.rest_1_
  511.7 2.0 adam_rest.1
  (285 shorter events, 56.2 us)
Async XLA Ops:
  7.2 202.3 %all-gather.6.cloned.1.call-start = ((), (), s32[]{:S(2)}) async-start(), calls=%async_computation.4 | async-start | bytes 11796480 | tf_op jit(solution)/shard_map/all_gather | solution.py:967
  17.4 242.4 %all-gather.8.cloned.1.call-start = ((), (), s32[]{:S(2)}) async-start(), calls=%async_computation.5 | async-start | bytes 3932160 | tf_op jit(solution)/shard_map/all_gather | solution.py:967
  18.6 39.1 %collective-permute-start.1 = (bf16[512,1024]{1,0:T(8,128)(2,1)S(1)}, bf16[512,1024]{1,0:T(8,128)(2,1)}, u32[]{:S(2)}, u32[]{:S(2)}) collective-permute-start(bf16[512,1024]{1,0:T(8,128)(2,1)S(1)} %copy-done.30), channel_id=1, source_target_pairs={{0,1},{1,0},{2,3},{3,2},{4,5},{5,4},{6,7},{7,6},{8,9},{9,8},{10,11... | collective-permute-start | bytes 3145736 | tf_op jit(solution)/shard_map/ppermute | solution.py:911
  21.5 39.0 %collective-permute-start.2 = (bf16[512,1024]{1,0:T(8,128)(2,1)S(1)}, bf16[512,1024]{1,0:T(8,128)(2,1)}, u32[]{:S(2)}, u32[]{:S(2)}) collective-permute-start(bf16[512,1024]{1,0:T(8,128)(2,1)S(1)} %copy-done.30), channel_id=1, source_target_pairs={{0,2},{1,3},{2,0},{3,1},{4,6},{5,7},{6,4},{7,5},{8,10},{9,11},{10,... | collective-permute-start | bytes 3145736 | tf_op jit(solution)/shard_map/ppermute | solution.py:911
  23.9 41.9 %collective-permute-start = (f32[4,2048]{1,0:T(4,128)}, f32[4,2048]{1,0:T(4,128)}, u32[]{:S(2)}, u32[]{:S(2)}) collective-permute-start(f32[4,2048]{1,0:T(4,128)} %get-tuple-element.253), channel_id=1, source_target_pairs={{0,4},{4,0},{8,12},{12,8},{16,20},{20,16},{24,28},{28,24},{1,5},{5... | collective-permute-start | bytes 98312 | tf_op jit(solution)/shard_map/ppermute | solution.py:905
  59.6 15.1 %collective-permute-start.10 = (bf16[256,1024]{1,0:T(8,128)(2,1)}, bf16[256,1024]{1,0:T(8,128)(2,1)}, u32[]{:S(2)}, u32[]{:S(2)}) collective-permute-start(bf16[256,1024]{1,0:T(8,128)(2,1)} %slice.232), channel_id=1, source_target_pairs={{0,2},{1,3},{2,0},{3,1},{4,6},{5,7},{6,4},{7,5},{8,10},{9,11},{10,... | collective-permute-start | bytes 1572872 | tf_op jit(solution)/shard_map/ppermute | solution.py:911
  61.5 14.9 %collective-permute-start.11 = (bf16[256,1024]{1,0:T(8,128)(2,1)S(1)}, bf16[256,1024]{1,0:T(8,128)(2,1)S(1)}, u32[]{:S(2)}, u32[]{:S(2)}) collective-permute-start(bf16[256,1024]{1,0:T(8,128)(2,1)S(1)} %slice.233), channel_id=1, source_target_pairs={{0,1},{1,0},{2,3},{3,2},{4,5},{5,4},{6,7},{7,6},{8,9},{9,8},{10,11... | collective-permute-start | bytes 1572872 | tf_op jit(solution)/shard_map/ppermute | solution.py:911
  61.7 26.8 %collective-permute-start.3 = (bf16[4,272,256]{2,1,0:T(8,128)(2,1)S(1)}, bf16[4,272,256]{2,1,0:T(8,128)(2,1)}, u32[]{:S(2)}, u32[]{:S(2)}) collective-permute-start(bf16[4,272,256]{2,1,0:T(8,128)(2,1)S(1)} %slice.230.rest_0_), channel_id=1, source_target_pairs={{0,1},{1,0},{2,3},{3,2},{4,5},{5,4},{6,7},{7,6},{8,9},{9,8},{10,11... | collective-permute-start | bytes 1671176 | tf_op jit(solution)/shard_map/ppermute | solution.py:911
  63.7 24.7 %collective-permute-start.4 = (bf16[4,272,256]{2,1,0:T(8,128)(2,1)S(1)}, bf16[4,272,256]{2,1,0:T(8,128)(2,1)}, u32[]{:S(2)}, u32[]{:S(2)}) collective-permute-start(bf16[4,272,256]{2,1,0:T(8,128)(2,1)S(1)} %slice.230.rest_0_), channel_id=1, source_target_pairs={{0,2},{1,3},{2,0},{3,1},{4,6},{5,7},{6,4},{7,5},{8,10},{9,11},{10,... | collective-permute-start | bytes 1671176 | tf_op jit(solution)/shard_map/ppermute | solution.py:911
  65.8 34.5 %collective-permute-start.5 = (bf16[4,272,256]{2,1,0:T(8,128)(2,1)S(1)}, bf16[4,272,256]{2,1,0:T(8,128)(2,1)}, u32[]{:S(2)}, u32[]{:S(2)}) collective-permute-start(bf16[4,272,256]{2,1,0:T(8,128)(2,1)S(1)} %slice.230.rest_0_), channel_id=1, source_target_pairs={{0,3},{1,2},{2,1},{3,0},{4,7},{5,6},{6,5},{7,4},{8,11},{9,10},{10,... | collective-permute-start | bytes 1671176 | tf_op jit(solution)/shard_map/ppermute | solution.py:911
  74.7 26.4 %collective-permute-start.34 = (bf16[1,192,1024]{2,1,0:T(8,128)(2,1)S(1)}, bf16[1,192,1024]{2,1,0:T(8,128)(2,1)S(1)}, u32[]{:S(2)}, u32[]{:S(2)}) collective-permute-start(bf16[1,192,1024]{2,1,0:T(8,128)(2,1)S(1)} %pad_maximum_fusion.5), channel_id=1, source_target_pairs={{0,4},{4,0},{8,12},{12,8},{16,20},{20,16},{24,28},{28,24},{1,5},{5... | collective-permute-start | bytes 1179656 | tf_op jit(solution)/shard_map/ppermute | solution.py:905
  76.4 25.2 %collective-permute-start.6 = (bf16[4,272,256]{2,1,0:T(8,128)(2,1)S(1)}, bf16[4,272,256]{2,1,0:T(8,128)(2,1)S(1)}, u32[]{:S(2)}, u32[]{:S(2)}) collective-permute-start(bf16[4,272,256]{2,1,0:T(8,128)(2,1)S(1)} %slice.230.rest_0_), channel_id=1, source_target_pairs={{0,4},{4,0},{8,12},{12,8},{16,20},{20,16},{24,28},{28,24},{1,5},{5... | collective-permute-start | bytes 1671176 | tf_op jit(solution)/shard_map/ppermute | solution.py:905
  100.3 6.8 %collective-permute-start.12 = (bf16[4,128,256]{2,1,0:T(8,128)(2,1)S(1)}, bf16[4,128,256]{2,1,0:T(8,128)(2,1)S(1)}, u32[]{:S(2)}, u32[]{:S(2)}) collective-permute-start(bf16[4,128,256]{2,1,0:T(8,128)(2,1)S(1)} %slice.231.rest_0_), channel_id=1, source_target_pairs={{0,1},{1,0},{2,3},{3,2},{4,5},{5,4},{6,7},{7,6},{8,9},{9,8},{10,11... | collective-permute-start | bytes 786440 | tf_op jit(solution)/shard_map/ppermute | solution.py:911
  100.6 16.6 %collective-permute-start.7 = (bf16[4,272,256]{2,1,0:T(8,128)(2,1)}, bf16[4,272,256]{2,1,0:T(8,128)(2,1)}, u32[]{:S(2)}, u32[]{:S(2)}) collective-permute-start(bf16[4,272,256]{2,1,0:T(8,128)(2,1)} %collective-permute-done.3.rest_1_), channel_id=1, source_target_pairs={{0,4},{4,0},{8,12},{12,8},{16,20},{20,16},{24,28},{28,24},{1,5},{5... | collective-permute-start | bytes 1671176 | tf_op jit(solution)/shard_map/ppermute | solution.py:905
  100.6 16.7 %collective-permute-start.8 = (bf16[4,272,256]{2,1,0:T(8,128)(2,1)}, bf16[4,272,256]{2,1,0:T(8,128)(2,1)}, u32[]{:S(2)}, u32[]{:S(2)}) collective-permute-start(bf16[4,272,256]{2,1,0:T(8,128)(2,1)} %collective-permute-done.4.rest_2_), channel_id=1, source_target_pairs={{0,4},{4,0},{8,12},{12,8},{16,20},{20,16},{24,28},{28,24},{1,5},{5... | collective-permute-start | bytes 1671176 | tf_op jit(solution)/shard_map/ppermute | solution.py:905
  101.1 16.6 %collective-permute-start.9 = (bf16[4,272,256]{2,1,0:T(8,128)(2,1)}, bf16[4,272,256]{2,1,0:T(8,128)(2,1)}, u32[]{:S(2)}, u32[]{:S(2)}) collective-permute-start(bf16[4,272,256]{2,1,0:T(8,128)(2,1)} %collective-permute-done.5.rest_3_), channel_id=1, source_target_pairs={{0,4},{4,0},{8,12},{12,8},{16,20},{20,16},{24,28},{28,24},{1,5},{5... | collective-permute-start | bytes 1671176 | tf_op jit(solution)/shard_map/ppermute | solution.py:905
  102.4 14.3 %collective-permute-start.13 = (bf16[4,128,256]{2,1,0:T(8,128)(2,1)S(1)}, bf16[4,128,256]{2,1,0:T(8,128)(2,1)S(1)}, u32[]{:S(2)}, u32[]{:S(2)}) collective-permute-start(bf16[4,128,256]{2,1,0:T(8,128)(2,1)S(1)} %slice.231.rest_0_), channel_id=1, source_target_pairs={{0,2},{1,3},{2,0},{3,1},{4,6},{5,7},{6,4},{7,5},{8,10},{9,11},{10,... | collective-permute-start | bytes 786440 | tf_op jit(solution)/shard_map/ppermute | solution.py:911
  107.1 9.6 %collective-permute-start.14 = (bf16[4,128,256]{2,1,0:T(8,128)(2,1)S(1)}, bf16[4,128,256]{2,1,0:T(8,128)(2,1)S(1)}, u32[]{:S(2)}, u32[]{:S(2)}) collective-permute-start(bf16[4,128,256]{2,1,0:T(8,128)(2,1)S(1)} %slice.231.rest_0_), channel_id=1, source_target_pairs={{0,3},{1,2},{2,1},{3,0},{4,7},{5,6},{6,5},{7,4},{8,11},{9,10},{10,... | collective-permute-start | bytes 786440 | tf_op jit(solution)/shard_map/ppermute | solution.py:911
  112.2 333.0 %reduce-scatter.3.cloned.1.call-start = ((), (), s32[]{:S(2)}) async-start(), calls=%async_computation.2 | async-start | bytes 7864320 | tf_op jit(solution)/shard_map/reduce_scatter | solution.py:1034
  116.7 23.4 %collective-permute-start.15 = (bf16[4,128,256]{2,1,0:T(8,128)(2,1)S(1)}, bf16[4,128,256]{2,1,0:T(8,128)(2,1)S(1)}, u32[]{:S(2)}, u32[]{:S(2)}) collective-permute-start(bf16[4,128,256]{2,1,0:T(8,128)(2,1)S(1)} %slice.231.rest_0_), channel_id=1, source_target_pairs={{0,4},{4,0},{8,12},{12,8},{16,20},{20,16},{24,28},{28,24},{1,5},{5... | collective-permute-start | bytes 786440 | tf_op jit(solution)/shard_map/ppermute | solution.py:905
  116.7 23.4 %collective-permute-start.16 = (bf16[4,128,256]{2,1,0:T(8,128)(2,1)S(1)}, bf16[4,128,256]{2,1,0:T(8,128)(2,1)S(1)}, u32[]{:S(2)}, u32[]{:S(2)}) collective-permute-start(bf16[4,128,256]{2,1,0:T(8,128)(2,1)S(1)} %collective-permute-done.12.rest_1_), channel_id=1, source_target_pairs={{0,4},{4,0},{8,12},{12,8},{16,20},{20,16},{24,28},{28,24},{1,5},{5... | collective-permute-start | bytes 786440 | tf_op jit(solution)/shard_map/ppermute | solution.py:905
  117.2 22.9 %collective-permute-start.17 = (bf16[4,128,256]{2,1,0:T(8,128)(2,1)S(1)}, bf16[4,128,256]{2,1,0:T(8,128)(2,1)S(1)}, u32[]{:S(2)}, u32[]{:S(2)}) collective-permute-start(bf16[4,128,256]{2,1,0:T(8,128)(2,1)S(1)} %collective-permute-done.13.rest_2_), channel_id=1, source_target_pairs={{0,4},{4,0},{8,12},{12,8},{16,20},{20,16},{24,28},{28,24},{1,5},{5... | collective-permute-start | bytes 786440 | tf_op jit(solution)/shard_map/ppermute | solution.py:905
  117.3 22.9 %collective-permute-start.18 = (bf16[4,128,256]{2,1,0:T(8,128)(2,1)S(1)}, bf16[4,128,256]{2,1,0:T(8,128)(2,1)S(1)}, u32[]{:S(2)}, u32[]{:S(2)}) collective-permute-start(bf16[4,128,256]{2,1,0:T(8,128)(2,1)S(1)} %collective-permute-done.14.rest_3_), channel_id=1, source_target_pairs={{0,4},{4,0},{8,12},{12,8},{16,20},{20,16},{24,28},{28,24},{1,5},{5... | collective-permute-start | bytes 786440 | tf_op jit(solution)/shard_map/ppermute | solution.py:905
  147.5 25.4 %collective-permute-start.19 = (bf16[512,1024]{1,0:T(8,128)(2,1)}, bf16[512,1024]{1,0:T(8,128)(2,1)S(1)}, u32[]{:S(2)}, u32[]{:S(2)}) collective-permute-start(bf16[512,1024]{1,0:T(8,128)(2,1)} %get-tuple-element.129.rest_0_), channel_id=1, source_target_pairs={{0,1},{1,0},{2,3},{3,2},{4,5},{5,4},{6,7},{7,6},{8,9},{9,8},{10,11... | collective-permute-start | bytes 3145736 | tf_op jit(solution)/shard_map/ppermute | solution.py:911
  149.2 25.2 %collective-permute-start.20 = (bf16[512,1024]{1,0:T(8,128)(2,1)}, bf16[512,1024]{1,0:T(8,128)(2,1)}, u32[]{:S(2)}, u32[]{:S(2)}) collective-permute-start(bf16[512,1024]{1,0:T(8,128)(2,1)} %get-tuple-element.129.rest_0_), channel_id=1, source_target_pairs={{0,2},{1,3},{2,0},{3,1},{4,6},{5,7},{6,4},{7,5},{8,10},{9,11},{10,... | collective-permute-start | bytes 3145736 | tf_op jit(solution)/shard_map/ppermute | solution.py:911
  149.5 27.6 %collective-permute-start.21 = (bf16[512,1024]{1,0:T(8,128)(2,1)S(1)}, bf16[512,1024]{1,0:T(8,128)(2,1)S(1)}, u32[]{:S(2)}, u32[]{:S(2)}) collective-permute-start(bf16[512,1024]{1,0:T(8,128)(2,1)S(1)} %copy-done.31), channel_id=1, source_target_pairs={{0,4},{4,0},{8,12},{12,8},{16,20},{20,16},{24,28},{28,24},{1,5},{5... | collective-permute-start | bytes 3145736 | tf_op jit(solution)/shard_map/ppermute | solution.py:905
  149.5 28.6 %collective-permute-start.22 = (bf16[512,1024]{1,0:T(8,128)(2,1)}, bf16[512,1024]{1,0:T(8,128)(2,1)S(1)}, u32[]{:S(2)}, u32[]{:S(2)}) collective-permute-start(bf16[512,1024]{1,0:T(8,128)(2,1)} %collective-permute-done.1.rest_2_), channel_id=1, source_target_pairs={{0,4},{4,0},{8,12},{12,8},{16,20},{20,16},{24,28},{28,24},{1,5},{5... | collective-permute-start | bytes 3145736 | tf_op jit(solution)/shard_map/ppermute | solution.py:905
  150.0 29.6 %collective-permute-start.23 = (bf16[512,1024]{1,0:T(8,128)(2,1)}, bf16[512,1024]{1,0:T(8,128)(2,1)}, u32[]{:S(2)}, u32[]{:S(2)}) collective-permute-start(bf16[512,1024]{1,0:T(8,128)(2,1)} %collective-permute-done.2.rest_3_), channel_id=1, source_target_pairs={{0,4},{4,0},{8,12},{12,8},{16,20},{20,16},{24,28},{28,24},{1,5},{5... | collective-permute-start | bytes 3145736 | tf_op jit(solution)/shard_map/ppermute | solution.py:905
  177.1 16.4 %collective-permute-start.26 = (bf16[256,1024]{1,0:T(8,128)(2,1)}, bf16[256,1024]{1,0:T(8,128)(2,1)S(1)}, u32[]{:S(2)}, u32[]{:S(2)}) collective-permute-start(bf16[256,1024]{1,0:T(8,128)(2,1)} %slice.234), channel_id=1, source_target_pairs={{0,2},{1,3},{2,0},{3,1},{4,6},{5,7},{6,4},{7,5},{8,10},{9,11},{10,... | collective-permute-start | bytes 1572872 | tf_op jit(solution)/shard_map/ppermute | solution.py:911
  177.4 16.1 %collective-permute-start.27 = (bf16[256,1024]{1,0:T(8,128)(2,1)}, bf16[256,1024]{1,0:T(8,128)(2,1)}, u32[]{:S(2)}, u32[]{:S(2)}) collective-permute-start(bf16[256,1024]{1,0:T(8,128)(2,1)} %slice.235), channel_id=1, source_target_pairs={{0,1},{1,0},{2,3},{3,2},{4,5},{5,4},{6,7},{7,6},{8,9},{9,8},{10,11... | collective-permute-start | bytes 1572872 | tf_op jit(solution)/shard_map/ppermute | solution.py:911
  178.1 16.0 %collective-permute-start.28 = (bf16[512,1024]{1,0:T(8,128)(2,1)}, bf16[512,1024]{1,0:T(8,128)(2,1)}, u32[]{:S(2)}, u32[]{:S(2)}) collective-permute-start(bf16[512,1024]{1,0:T(8,128)(2,1)} %get-tuple-element.129.rest_0_), channel_id=1, source_target_pairs={{0,4},{4,0},{8,12},{12,8},{16,20},{20,16},{24,28},{28,24},{1,5},{5... | collective-permute-start | bytes 3145736 | tf_op jit(solution)/shard_map/ppermute | solution.py:905
  179.3 17.2 %collective-permute-start.29 = (bf16[512,1024]{1,0:T(8,128)(2,1)S(1)}, bf16[512,1024]{1,0:T(8,128)(2,1)}, u32[]{:S(2)}, u32[]{:S(2)}) collective-permute-start(bf16[512,1024]{1,0:T(8,128)(2,1)S(1)} %collective-permute-done.19.rest_1_), channel_id=1, source_target_pairs={{0,4},{4,0},{8,12},{12,8},{16,20},{20,16},{24,28},{28,24},{1,5},{5... | collective-permute-start | bytes 3145736 | tf_op jit(solution)/shard_map/ppermute | solution.py:905
  179.7 17.6 %collective-permute-start.30 = (bf16[512,1024]{1,0:T(8,128)(2,1)}, bf16[512,1024]{1,0:T(8,128)(2,1)}, u32[]{:S(2)}, u32[]{:S(2)}) collective-permute-start(bf16[512,1024]{1,0:T(8,128)(2,1)} %collective-permute-done.20.rest_2_), channel_id=1, source_target_pairs={{0,4},{4,0},{8,12},{12,8},{16,20},{20,16},{24,28},{28,24},{1,5},{5... | collective-permute-start | bytes 3145736 | tf_op jit(solution)/shard_map/ppermute | solution.py:905
  244.0 243.2 %reduce-scatter.5.cloned.1.call-start = ((), (), s32[]{:S(2)}) async-start(), calls=%async_computation.3 | async-start | bytes 7864320 | tf_op jit(solution)/shard_map/reduce_scatter | solution.py:1034
  285.7 29.1 %collective-permute-start.35 = (bf16[2048,1024]{1,0:T(8,128)(2,1)}, bf16[2048,1024]{1,0:T(8,128)(2,1)}, u32[]{:S(2)}, u32[]{:S(2)}) collective-permute-start(bf16[2048,1024]{1,0:T(8,128)(2,1)} %scatter_rows.4), channel_id=1, source_target_pairs={{0,4},{4,0},{8,12},{12,8},{16,20},{20,16},{24,28},{28,24},{1,5},{5... | collective-permute-start | bytes 12582920 | tf_op jit(solution)/shard_map/ppermute | solution.py:905
  319.3 23.1 %collective-permute-start.37 = (bf16[256,1024]{1,0:T(8,128)(2,1)S(1)}, bf16[256,1024]{1,0:T(8,128)(2,1)S(1)}, u32[]{:S(2)}, u32[]{:S(2)}) collective-permute-start(bf16[256,1024]{1,0:T(8,128)(2,1)S(1)} %get-tuple-element.246), channel_id=1, source_target_pairs={{0,1},{1,0},{2,3},{3,2},{4,5},{5,4},{6,7},{7,6},{8,9},{9,8},{10,11... | collective-permute-start | bytes 1572872 | tf_op jit(solution)/shard_map/ppermute | solution.py:911
  319.3 33.1 %collective-permute-start.38 = (bf16[256,1024]{1,0:T(8,128)(2,1)S(1)}, bf16[256,1024]{1,0:T(8,128)(2,1)S(1)}, u32[]{:S(2)}, u32[]{:S(2)}) collective-permute-start(bf16[256,1024]{1,0:T(8,128)(2,1)S(1)} %get-tuple-element.245), channel_id=1, source_target_pairs={{0,2},{1,3},{2,0},{3,1},{4,6},{5,7},{6,4},{7,5},{8,10},{9,11},{10,... | collective-permute-start | bytes 1572872 | tf_op jit(solution)/shard_map/ppermute | solution.py:911
  340.8 36.3 %collective-permute-start.36 = (bf16[256,1024]{1,0:T(8,128)(2,1)}, bf16[256,1024]{1,0:T(8,128)(2,1)}, u32[]{:S(2)}, u32[]{:S(2)}) collective-permute-start(bf16[256,1024]{1,0:T(8,128)(2,1)} %slice.240), channel_id=1, source_target_pairs={{0,1},{1,0},{2,3},{3,2},{4,5},{5,4},{6,7},{7,6},{8,9},{9,8},{10,11... | collective-permute-start | bytes 1572872 | tf_op jit(solution)/shard_map/ppermute | solution.py:911
  340.9 38.3 %collective-permute-start.41 = (bf16[256,1024]{1,0:T(8,128)(2,1)S(1)}, bf16[256,1024]{1,0:T(8,128)(2,1)}, u32[]{:S(2)}, u32[]{:S(2)}) collective-permute-start(bf16[256,1024]{1,0:T(8,128)(2,1)S(1)} %slice.249), channel_id=1, source_target_pairs={{0,2},{1,3},{2,0},{3,1},{4,6},{5,7},{6,4},{7,5},{8,10},{9,11},{10,... | collective-permute-start | bytes 1572872 | tf_op jit(solution)/shard_map/ppermute | solution.py:911
  352.6 25.0 %collective-permute-start.39 = (bf16[256,1024]{1,0:T(8,128)(2,1)S(1)}, bf16[256,1024]{1,0:T(8,128)(2,1)}, u32[]{:S(2)}, u32[]{:S(2)}) collective-permute-start(bf16[256,1024]{1,0:T(8,128)(2,1)S(1)} %add_convert_fusion.9), channel_id=1, source_target_pairs={{0,2},{1,3},{2,0},{3,1},{4,6},{5,7},{6,4},{7,5},{8,10},{9,11},{10,... | collective-permute-start | bytes 1572872 | tf_op jit(solution)/shard_map/ppermute | solution.py:911
  355.0 24.2 %collective-permute-start.40 = (bf16[256,1024]{1,0:T(8,128)(2,1)S(1)}, bf16[256,1024]{1,0:T(8,128)(2,1)}, u32[]{:S(2)}, u32[]{:S(2)}) collective-permute-start(bf16[256,1024]{1,0:T(8,128)(2,1)S(1)} %add_convert_fusion.8), channel_id=1, source_target_pairs={{0,1},{1,0},{2,3},{3,2},{4,5},{5,4},{6,7},{7,6},{8,9},{9,8},{10,11... | collective-permute-start | bytes 1572872 | tf_op jit(solution)/shard_map/ppermute | solution.py:911
  377.1 10.3 %collective-permute-start.42 = (bf16[512,1024]{1,0:T(8,128)(2,1)S(1)}, bf16[512,1024]{1,0:T(8,128)(2,1)S(1)}, u32[]{:S(2)}, u32[]{:S(2)}) collective-permute-start(bf16[512,1024]{1,0:T(8,128)(2,1)S(1)} %get-tuple-element.228), channel_id=1, source_target_pairs={{0,4},{4,0},{8,12},{12,8},{16,20},{20,16},{24,28},{28,24},{1,5},{5... | collective-permute-start | bytes 3145736 | tf_op jit(solution)/shard_map/ppermute | solution.py:905
  377.1 10.3 %collective-permute-start.43 = (bf16[512,1024]{1,0:T(8,128)(2,1)S(1)}, bf16[512,1024]{1,0:T(8,128)(2,1)S(1)}, u32[]{:S(2)}, u32[]{:S(2)}) collective-permute-start(bf16[512,1024]{1,0:T(8,128)(2,1)S(1)} %get-tuple-element.227), channel_id=1, source_target_pairs={{0,4},{4,0},{8,12},{12,8},{16,20},{20,16},{24,28},{28,24},{1,5},{5... | collective-permute-start | bytes 3145736 | tf_op jit(solution)/shard_map/ppermute | solution.py:905
  377.6 9.8 %collective-permute-start.44 = (bf16[512,1024]{1,0:T(8,128)(2,1)S(1)}, bf16[512,1024]{1,0:T(8,128)(2,1)S(1)}, u32[]{:S(2)}, u32[]{:S(2)}) collective-permute-start(bf16[512,1024]{1,0:T(8,128)(2,1)S(1)} %get-tuple-element.226), channel_id=1, source_target_pairs={{0,4},{4,0},{8,12},{12,8},{16,20},{20,16},{24,28},{28,24},{1,5},{5... | collective-permute-start | bytes 3145736 | tf_op jit(solution)/shard_map/ppermute | solution.py:905
  390.2 41.5 %collective-permute-start.45 = (bf16[256,1024]{1,0:T(8,128)(2,1)}, bf16[256,1024]{1,0:T(8,128)(2,1)}, u32[]{:S(2)}, u32[]{:S(2)}) collective-permute-start(bf16[256,1024]{1,0:T(8,128)(2,1)} %get-tuple-element.244), channel_id=1, source_target_pairs={{0,1},{1,0},{2,3},{3,2},{4,5},{5,4},{6,7},{7,6},{8,9},{9,8},{10,11... | collective-permute-start | bytes 1572872 | tf_op jit(solution)/shard_map/ppermute | solution.py:911
  392.4 39.3 %collective-permute-start.46 = (bf16[256,1024]{1,0:T(8,128)(2,1)}, bf16[256,1024]{1,0:T(8,128)(2,1)S(1)}, u32[]{:S(2)}, u32[]{:S(2)}) collective-permute-start(bf16[256,1024]{1,0:T(8,128)(2,1)} %get-tuple-element.243), channel_id=1, source_target_pairs={{0,2},{1,3},{2,0},{3,1},{4,6},{5,7},{6,4},{7,5},{8,10},{9,11},{10,... | collective-permute-start | bytes 1572872 | tf_op jit(solution)/shard_map/ppermute | solution.py:911
  393.8 37.9 %collective-permute-start.47 = (bf16[256,1024]{1,0:T(8,128)(2,1)}, bf16[256,1024]{1,0:T(8,128)(2,1)}, u32[]{:S(2)}, u32[]{:S(2)}) collective-permute-start(bf16[256,1024]{1,0:T(8,128)(2,1)} %slice.202), channel_id=1, source_target_pairs={{0,1},{1,0},{2,3},{3,2},{4,5},{5,4},{6,7},{7,6},{8,9},{9,8},{10,11... | collective-permute-start | bytes 1572872 | tf_op jit(solution)/shard_map/ppermute | solution.py:911
  395.0 36.8 %collective-permute-start.48 = (bf16[256,1024]{1,0:T(8,128)(2,1)}, bf16[256,1024]{1,0:T(8,128)(2,1)}, u32[]{:S(2)}, u32[]{:S(2)}) collective-permute-start(bf16[256,1024]{1,0:T(8,128)(2,1)} %slice.203), channel_id=1, source_target_pairs={{0,2},{1,3},{2,0},{3,1},{4,6},{5,7},{6,4},{7,5},{8,10},{9,11},{10,... | collective-permute-start | bytes 1572872 | tf_op jit(solution)/shard_map/ppermute | solution.py:911
  431.8 5.2 collective-permute-start.49
  431.8 6.8 %collective-permute-start.50 = (bf16[4,400,256]{2,1,0:T(8,128)(2,1)}, bf16[4,400,256]{2,1,0:T(8,128)(2,1)S(1)}, u32[]{:S(2)}, u32[]{:S(2)}) collective-permute-start(bf16[4,400,256]{2,1,0:T(8,128)(2,1)} %get-tuple-element.160), channel_id=1, source_target_pairs={{0,4},{4,0},{8,12},{12,8},{16,20},{20,16},{24,28},{28,24},{1,5},{5... | collective-permute-start | bytes 2457608 | tf_op jit(solution)/shard_map/ppermute | solution.py:905
  432.3 6.3 %collective-permute-start.52 = (bf16[4,400,256]{2,1,0:T(8,128)(2,1)}, bf16[4,400,256]{2,1,0:T(8,128)(2,1)S(1)}, u32[]{:S(2)}, u32[]{:S(2)}) collective-permute-start(bf16[4,400,256]{2,1,0:T(8,128)(2,1)} %get-tuple-element.161), channel_id=1, source_target_pairs={{0,4},{4,0},{8,12},{12,8},{16,20},{20,16},{24,28},{28,24},{1,5},{5... | collective-permute-start | bytes 2457608 | tf_op jit(solution)/shard_map/ppermute | solution.py:905
  432.4 20.7 %collective-permute-start.55 = (bf16[512,1024]{1,0:T(8,128)(2,1)}, bf16[512,1024]{1,0:T(8,128)(2,1)}, u32[]{:S(2)}, u32[]{:S(2)}) collective-permute-start(bf16[512,1024]{1,0:T(8,128)(2,1)} %get-tuple-element.225), channel_id=1, source_target_pairs={{0,4},{4,0},{8,12},{12,8},{16,20},{20,16},{24,28},{28,24},{1,5},{5... | collective-permute-start | bytes 3145736 | tf_op jit(solution)/shard_map/ppermute | solution.py:905
  435.0 15.1 %collective-permute-start.56 = (bf16[256,1024]{1,0:T(8,128)(2,1)}, bf16[256,1024]{1,0:T(8,128)(2,1)}, u32[]{:S(2)}, u32[]{:S(2)}) collective-permute-start(bf16[256,1024]{1,0:T(8,128)(2,1)} %add_convert_fusion.7), channel_id=1, source_target_pairs={{0,2},{1,3},{2,0},{3,1},{4,6},{5,7},{6,4},{7,5},{8,10},{9,11},{10,... | collective-permute-start | bytes 1572872 | tf_op jit(solution)/shard_map/ppermute | solution.py:911
  436.9 15.0 %collective-permute-start.57 = (bf16[256,1024]{1,0:T(8,128)(2,1)}, bf16[256,1024]{1,0:T(8,128)(2,1)S(1)}, u32[]{:S(2)}, u32[]{:S(2)}) collective-permute-start(bf16[256,1024]{1,0:T(8,128)(2,1)} %add_convert_fusion.6), channel_id=1, source_target_pairs={{0,1},{1,0},{2,3},{3,2},{4,5},{5,4},{6,7},{7,6},{8,9},{9,8},{10,11... | collective-permute-start | bytes 1572872 | tf_op jit(solution)/shard_map/ppermute | solution.py:911
  442.0 24.8 %collective-permute-start.53 = (bf16[4,400,256]{2,1,0:T(8,128)(2,1)}, bf16[4,400,256]{2,1,0:T(8,128)(2,1)}, u32[]{:S(2)}, u32[]{:S(2)}) collective-permute-start(bf16[4,400,256]{2,1,0:T(8,128)(2,1)} %pad_maximum_fusion.3), channel_id=1, source_target_pairs={{0,2},{1,3},{2,0},{3,1},{4,6},{5,7},{6,4},{7,5},{8,10},{9,11},{10,... | collective-permute-start | bytes 2457608 | tf_op jit(solution)/shard_map/ppermute | solution.py:911
  444.5 23.9 %collective-permute-start.51 = (bf16[4,400,256]{2,1,0:T(8,128)(2,1)}, bf16[4,400,256]{2,1,0:T(8,128)(2,1)}, u32[]{:S(2)}, u32[]{:S(2)}) collective-permute-start(bf16[4,400,256]{2,1,0:T(8,128)(2,1)} %pad_maximum_fusion.2), channel_id=1, source_target_pairs={{0,1},{1,0},{2,3},{3,2},{4,5},{5,4},{6,7},{7,6},{8,9},{9,8},{10,11... | collective-permute-start | bytes 2457608 | tf_op jit(solution)/shard_map/ppermute | solution.py:911
  450.1 6.5 %collective-permute-start.54 = (bf16[2,192,1024]{2,1,0:T(8,128)(2,1)S(1)}, bf16[2,192,1024]{2,1,0:T(8,128)(2,1)}, u32[]{:S(2)}, u32[]{:S(2)}) collective-permute-start(bf16[2,192,1024]{2,1,0:T(8,128)(2,1)S(1)} %slice_bitcast_fusion.1), channel_id=1, source_target_pairs={{0,4},{4,0},{8,12},{12,8},{16,20},{20,16},{24,28},{28,24},{1,5},{5... | collective-permute-start | bytes 2359304 | tf_op jit(solution)/shard_map/ppermute | solution.py:905
  469.5 10.4 %collective-permute-start.59 = (bf16[2,400,256]{2,1,0:T(8,128)(2,1)S(1)}, bf16[2,400,256]{2,1,0:T(8,128)(2,1)S(1)}, u32[]{:S(2)}, u32[]{:S(2)}) collective-permute-start(bf16[2,400,256]{2,1,0:T(8,128)(2,1)S(1)} %add_convert_fusion.11), channel_id=1, source_target_pairs={{0,2},{1,3},{2,0},{3,1},{4,6},{5,7},{6,4},{7,5},{8,10},{9,11},{10,... | collective-permute-start | bytes 1228808 | tf_op jit(solution)/shard_map/ppermute | solution.py:911
  471.0 14.2 %collective-permute-start.58 = (bf16[4,400,256]{2,1,0:T(8,128)(2,1)S(1)}, bf16[4,400,256]{2,1,0:T(8,128)(2,1)S(1)}, u32[]{:S(2)}, u32[]{:S(2)}) collective-permute-start(bf16[4,400,256]{2,1,0:T(8,128)(2,1)S(1)} %copy-done.53), channel_id=1, source_target_pairs={{0,4},{4,0},{8,12},{12,8},{16,20},{20,16},{24,28},{28,24},{1,5},{5... | collective-permute-start | bytes 2457608 | tf_op jit(solution)/shard_map/ppermute | solution.py:905
  472.2 11.9 %collective-permute-start.60 = (bf16[2,400,256]{2,1,0:T(8,128)(2,1)S(1)}, bf16[2,400,256]{2,1,0:T(8,128)(2,1)S(1)}, u32[]{:S(2)}, u32[]{:S(2)}) collective-permute-start(bf16[2,400,256]{2,1,0:T(8,128)(2,1)S(1)} %add_convert_fusion.10), channel_id=1, source_target_pairs={{0,1},{1,0},{2,3},{3,2},{4,5},{5,4},{6,7},{7,6},{8,9},{9,8},{10,11... | collective-permute-start | bytes 1228808 | tf_op jit(solution)/shard_map/ppermute | solution.py:911
  488.4 8.8 %collective-permute-start.64 = (bf16[2,192,1024]{2,1,0:T(8,128)(2,1)S(1)}, bf16[2,192,1024]{2,1,0:T(8,128)(2,1)S(1)}, u32[]{:S(2)}, u32[]{:S(2)}) collective-permute-start(bf16[2,192,1024]{2,1,0:T(8,128)(2,1)S(1)} %slice_bitcast_fusion), channel_id=1, source_target_pairs={{0,4},{4,0},{8,12},{12,8},{16,20},{20,16},{24,28},{28,24},{1,5},{5... | collective-permute-start | bytes 2359304 | tf_op jit(solution)/shard_map/ppermute | solution.py:905
  488.5 19.5 %collective-permute-start.61 = (bf16[400,256]{1,0:T(8,128)(2,1)S(1)}, bf16[400,256]{1,0:T(8,128)(2,1)S(1)}, u32[]{:S(2)}, u32[]{:S(2)}) collective-permute-start(bf16[400,256]{1,0:T(8,128)(2,1)S(1)} %get-tuple-element.249), channel_id=1, source_target_pairs={{0,8},{4,12},{8,0},{12,4},{16,24},{20,28},{24,16},{28,20},{1,9},{5... | collective-permute-start | bytes 614408 | tf_op jit(solution)/shard_map/ppermute | solution.py:908
  491.1 20.5 %collective-permute-start.62 = (bf16[400,256]{1,0:T(8,128)(2,1)S(1)}, bf16[400,256]{1,0:T(8,128)(2,1)S(1)}, u32[]{:S(2)}, u32[]{:S(2)}) collective-permute-start(bf16[400,256]{1,0:T(8,128)(2,1)S(1)} %get-tuple-element.248), channel_id=1, source_target_pairs={{0,16},{4,20},{8,24},{12,28},{16,0},{20,4},{24,8},{28,12},{1,17},{... | collective-permute-start | bytes 614408 | tf_op jit(solution)/shard_map/ppermute | solution.py:908
  497.0 14.6 %collective-permute-start.63 = (bf16[400,256]{1,0:T(8,128)(2,1)S(1)}, bf16[400,256]{1,0:T(8,128)(2,1)S(1)}, u32[]{:S(2)}, u32[]{:S(2)}) collective-permute-start(bf16[400,256]{1,0:T(8,128)(2,1)S(1)} %get-tuple-element.247), channel_id=1, source_target_pairs={{0,24},{4,28},{8,16},{12,20},{16,8},{20,12},{24,0},{28,4},{1,25},{... | collective-permute-start | bytes 614408 | tf_op jit(solution)/shard_map/ppermute | solution.py:908
  (59 other events, 749.5 us)
Sparse Core Ops, SparseCore 0:
  17.5 179.0 all-gather.5
  198.2 61.5 all-gather.7
  262.1 111.6 reduce-scatter.2
  375.9 111.2 reduce-scatter.4

commit v4 on v3

--- a/solution.py
+++ b/solution.py
@@ -362,13 +362,12 @@
                 dp = dot_t(value_side[:keys], doh[rows])
                 mean = jnp.sum(e * dp, axis=0, keepdims=True)
                 dz = (e * (dp - mean)).astype(bf16)
-                both.append(t_dot(dz, key_side[:keys]))
+                both.append(t_dot(key_side[:keys], dz))
                 add = dot(dz, q_for_k[rows]) + dot(e.astype(bf16), do_for_v[rows])
                 for i in range(b + 1):
                     dkv[i] = dkv[i] + add[i * QBLK : (i + 1) * QBLK]
-            lane_b = lax.broadcasted_iota(jnp.int32, (QBLK, 128), 1)
-            dqs.append(jnp.where(lane_b < HD, both[0], both[1]))
-        dq = jnp.concatenate(dqs, axis=0) * SCALE
+            dqs.append(jnp.concatenate([both[0][:HD], both[1][HD:]], axis=0))
+        dq = jnp.concatenate(dqs, axis=1).T * SCALE
         dkv_all = jnp.concatenate(dkv, axis=0)
         dq_ref[:, part] = rotate(dq, cosine, -sine, first_half).astype(bf16)
         dk = rotate(dkv_all * SCALE, cosine, -sine, first_half)
@@ -967,11 +966,10 @@
         whole = lax.all_gather(part, "dp", axis=0, tiled=False, axis_index_groups=groups)
         held.update({i: (whole, i - a) for i in range(a, b)})
     dm_near = near(cotangent)
-    dm_far = far(cotangent, dm_near)
     pieces = spread_t(after(column[:, : 2 * wrows + 16], *dm_near))
-    pieces_out = spread_t(after(column[:, 2 * wrows + 16 :], *pieces[1:], *dm_far))
+    pieces_out = spread_t(after(column[:, 2 * wrows + 16 :], *pieces[1:]))
+    dm_far = far(cotangent, list(lax.optimization_barrier((*dm_near, *pieces[1:])))[: len(dm_near)])
     pieces = pieces + [swap_core(piece) for piece in pieces]
-    pieces_out = pieces_out + [swap_core(piece) for piece in pieces_out]
 
     ids = t * 2 * half + jnp.arange(2 * half, dtype=jnp.int32)
     chosen = routes[0].T[None, :, :] == ids[:, None, None]
@@ -996,6 +994,8 @@
         sequence = lax.all_gather(tokens, "tensor", axis=0, tiled=True, axis_index_groups=seq_groups)
     first_row = (t % sharers) * rows
     q, kv, o, lse, qkv_weights, gains = attend_forward((nz, nt), place, sequence, pieces)
+    o, *pieces_out = lax.optimization_barrier((o, *pieces_out))
+    pieces_out = pieces_out + [swap_core(piece) for piece in pieces_out]
     s1, n2, out_weight = attend_out((nz, nt), place, sequence, gains, o, pieces_out)
     if sharers > 1:
         s1 = lax.dynamic_slice_in_dim(s1, first_row, rows, 0)

time: 528 us -> 522 us (0.989)
  starting transfers between devices: 82.5 us -> 63.1 us
  Pallas kernels: 207 us -> 215 us
  waiting for transfers between devices: 103 us -> 110 us
    reduce_scatter x2, waiting for transfers between devices: 0.46 us -> 18.1 us  [on_device(): lax.psum_scatter(gw, 'dp', scatter_dimension=0, tiled=False, axis_index_g...]
    ppermute x32, starting transfers between devices: 23.8 us -> 6.29 us  [swap_core(): return lax.ppermute(x, 'dp', [(i, i ^ 1) for i in range(ndp)])]
    ppermute x30, waiting for transfers between devices: 90.1 us -> 72.8 us  [swap_t(): return lax.ppermute(x, 'tensor', [(i, i ^ k) for i in range(nt)])]
    pallas_call x3, Pallas kernels: 60.9 us -> 69.7 us  [experts_step(): pl.pallas_call(functools.partial(experts_kernel, first, subs, sources, le...]
    all_gather x2, waiting for transfers between devices: 3.5 us -> 10.6 us  [on_device(): lax.all_gather(part, 'dp', axis=0, tiled=False, axis_index_groups=groups)]
    unnamed x109 -> x113, local copies, waits for them, and re-layouts: 13.5 us -> 11.7 us
  transfers between devices with their start and end apart: 69 -> 69, of which waited for: 21 -> 19; matrix products, arithmetic and copies ran while one was open for 12% -> 12% of each run, Pallas kernels for 39% -> 41%
where the time goes in v4:
time: 522 us; the launch traced here: 515 us
  Pallas kernels  215 us (41%)
  waiting for transfers between devices  110 us (21%)
  starting transfers between devices  63.1 us (12%)
  other arithmetic  43.6 us (8%)
  local copies, waits for them, and re-layouts  35.4 us (7%)
  blocking collectives  32.9 us (6%)
  between operations  15.2 us (3%)
    ppermute x30, waiting for transfers between devices, swap_t(): return lax.ppermute(x, 'tensor', [(i, i ^ k) for i in range(nt)])  72.8 us
    pallas_call x3, Pallas kernels, experts_step(): pl.pallas_call(functools.partial(experts_kernel, first, subs, sources, le...  69.7 us
    ppermute x30, starting transfers between devices, swap_t(): return lax.ppermute(x, 'tensor', [(i, i ^ k) for i in range(nt)])  52 us
    pallas_call x3, Pallas kernels, scatter(): pl.pallas_call(functools.partial(scatter_kernel, halves, sources, experts...  41.7 us
    pallas_call x1, Pallas kernels, attend_backward(): pl.pallas_call(functools.partial(attend_backward_kernel, nz, nt, whole),...  34 us
    all_gather x1, blocking collectives, on_device(): lax.all_gather(own, 'dp', axis=0, tiled=False, axis_index_groups=groups)  32.9 us
    pallas_call x2, Pallas kernels, gather(): pl.pallas_call(functools.partial(gather_kernel, tuple(starts), experts, w...  25.3 us
    pallas_call x2, Pallas kernels, adam_experts(): pl.pallas_call(functools.partial(adam_kernel, per), grid_spec=pltpu.Prefe...  19.9 us
  transfers between devices with their start and end apart: 69, of which 19 were waited for; matrix products, arithmetic and copies ran while one was open for 12% of the time, Pallas kernels for 41%

profile of v4, /device:TPU:0, one launch (start us, length us, event | category | flops | bytes accessed | tf_op | source)
XLA Modules:
  0.0 515.5 jit_solution(7935652615081896549)
XLA Ops:
  10.4 2.1 fusion.4
  13.4 2.4 collective-permute-done.33
  15.8 1.6 pad_maximum_fusion
  18.6 2.9 collective-permute-start.1
  21.5 1.5 collective-permute-start.2
  27.2 32.9 %all-gather = bf16[1600,256]{1,0:T(8,128)(2,1)S(1)} all-gather(bf16[400,256]{1,0:T(8,128)(2,1)S(1)} %pad_maximum_fusion.6), channel_id=2, replica_groups={{0,8,16,24},{4,12,20,28},{1,9,17,25},{5,13,21,29},{2,10,18,26},{6,14,22..., dimensions={0}, use_global_device_ids=true | all-gather | bytes 1024000 | tf_op jit(solution)/shard_map/all_gather | solution.py:963
  60.5 3.3 collective-permute-start.5
  65.6 10.4 %collective-permute-done.3.rest_1_ = bf16[4,272,256]{2,1,0:T(8,128)(2,1)} collective-permute-done((bf16[4,272,256]{2,1,0:T(8,128)(2,1)S(1)}, bf16[4,272,256]{2,1,0:T(8,128)(2,1)}, u32[]{:S(2)}, u32[]{:S(2)}) %collective-permute-start.3) | collective-permute-done | bytes 557088 | tf_op jit(solution)/shard_map/ppermute | solution.py:910
  76.0 9.6 %collective-permute-done.4.rest_2_ = bf16[4,272,256]{2,1,0:T(8,128)(2,1)} collective-permute-done((bf16[4,272,256]{2,1,0:T(8,128)(2,1)S(1)}, bf16[4,272,256]{2,1,0:T(8,128)(2,1)}, u32[]{:S(2)}, u32[]{:S(2)}) %collective-permute-start.4) | collective-permute-done | bytes 557088 | tf_op jit(solution)/shard_map/ppermute | solution.py:910
  86.9 2.0 copy.67
  88.9 2.0 pad_maximum_fusion.4
  91.1 1.7 collective-permute-start.10
  93.9 1.5 collective-permute-start.12
  96.6 18.7 %attend_forward.1 = (bf16[512,1024]{1,0:T(8,128)(2,1)S(1)}, bf16[512,1024]{1,0:T(8,128)(2,1)S(1)}, bf16[512,1024]{1,0:T(8,128)(2,1)S(1)}, f32[512,128]{1,0:T(8,1...) custom-call(s32[4]{0:T(128)S(1)} %pad_add_fusion.place_ref, bf16[512,1024]{1,0:T(8,128)(2,1)S(1)} %copy-done.3, ...), custom_call_target="tpu_custom_call" | custom-call | flops 24999999488 | bytes 12582912 | tf_op jit(solution)/shard_map/attend_forward/pallas_call | solution.py:230
  118.1 1.5 slice.174
  122.8 3.7 attend_out.1
  131.2 3.0 collective-permute-done.19.rest_4_
  134.2 2.2 collective-permute-done.20.rest_5_
  136.5 21.3 %collective-permute-done.17.rest_1_ = bf16[512,1024]{1,0:T(8,128)(2,1)S(1)} collective-permute-done((bf16[512,1024]{1,0:T(8,128)(2,1)}, bf16[512,1024]{1,0:T(8,128)(2,1)S(1)}, u32[]{:S(2)}, u32[]{:S(2)}) %collective-permute-start.17) | collective-permute-done | bytes 1048608 | tf_op jit(solution)/shard_map/ppermute | solution.py:910
  159.1 1.9 slice.233
  161.8 1.6 collective-permute-start.27
  166.2 12.8 %gather_rows.2 = (bf16[4,2560,1024]{2,1,0:T(8,128)(2,1)}, f32[4,2560,128]{2,1,0:T(8,128)}) custom-call(s32[68]{0:T(128)} %reshape.193.offs_ref, f32[64,256]{1,0:T(8,128)} %copy-done.38, f32[64,256]{1,0:T(8,128)} %copy-done.43, bf16[512,1024]{1,0:T(8,128)(2,1)} %rest_1_.3, bf16[512,1024]{1,0:T(8,128)(2,1)} %collective-permute-done.1.rest_2_, ...), custom_call_target="tpu_custom_call" | custom-call | flops 1 | bytes 1 | tf_op jit(solution)/shard_map/gather_rows/pallas_call | solution.py:527
  179.6 1.5 collective-permute-done.31.rest_8_
  182.8 12.5 %gather_rows.3.n2_ref = bf16[4,2560,1024]{2,1,0:T(8,128)(2,1)} custom-call(s32[68]{0:T(128)} %reshape.193.offs_ref, f32[64,256]{1,0:T(8,128)} %copy-done.38, bf16[512,1024]{1,0:T(8,128)(2,1)} %get-tuple-element.141.rest_0_, bf16[512,1024]{1,0:T(8,128)(2,1)} %copy-done.37, bf16[512,1024]{1,0:T(8,128)(2,1)} %collective-permute-done.18.rest_2_, ...), custom_call_target="tpu_custom_call" | custom-call | flops 1 | bytes 1 | tf_op jit(solution)/shard_map/gather_rows/pallas_call | solution.py:527
  195.3 2.8 all-gather.6.cloned.1.call-done
  198.1 37.3 %experts.3 = (bf16[2,3072,1024]{2,1,0:T(8,128)(2,1)}, bf16[2,3072,1024]{2,1,0:T(8,128)(2,1)}, bf16[4,2,2,192,1024]{4,3,2,1,0:T(8,128)(2,1)}) custom-call(s32[4]{0:T(128)} %copy-done.21, s32[68]{0:T(128)} %reshape.193.offs_ref, bf16[4,2560,1024]{2,1,0:T(8,128)(2,1)} %gather_rows.3.n2_ref, bf16[4,2560,1024]{2,1,0:T(8,128)(2,1)} %get-tuple-element.148.dm_ref, ...), custom_call_target="tpu_custom_call" | custom-call | flops 1 | bytes 1 | tf_op jit(solution)/shard_map/experts/pallas_call | solution.py:671
  235.5 17.7 %experts.4 = (bf16[1,3072,1024]{2,1,0:T(8,128)(2,1)}, bf16[1,3072,1024]{2,1,0:T(8,128)(2,1)}, bf16[4,2,2,192,1024]{4,3,2,1,0:T(8,128)(2,1)}) custom-call(s32[4]{0:T(128)} %copy-done.21, s32[68]{0:T(128)} %reshape.193.offs_ref, bf16[4,2560,1024]{2,1,0:T(8,128)(2,1)} %gather_rows.3.n2_ref, bf16[4,2560,1024]{2,1,0:T(8,128)(2,1)} %get-tuple-element.148.dm_ref, ...), custom_call_target="tpu_custom_call" | custom-call | flops 1 | bytes 1 | tf_op jit(solution)/shard_map/experts/pallas_call | solution.py:671
  253.2 7.8 %all-gather.8.cloned.1.call-done = bf16[8,1,192,1024]{3,2,1,0:T(8,128)(2,1)} async-done(((bf16[2,1,192,1024]{3,2,1,0:T(8,128)(2,1)}), bf16[8,1,192,1024]{3,2,1,0:T(8,128)(2,1)}) %all-gather.8.cloned.1.call-update) | async-done | bytes 3145744 | tf_op jit(solution)/shard_map/all_gather | solution.py:966
  260.9 14.7 %experts.5 = (bf16[1,3072,1024]{2,1,0:T(8,128)(2,1)}, bf16[1,3072,1024]{2,1,0:T(8,128)(2,1)}, bf16[4,2,2,192,1024]{4,3,2,1,0:T(8,128)(2,1)}) custom-call(s32[4]{0:T(128)} %copy-done.21, s32[68]{0:T(128)} %reshape.193.offs_ref, bf16[4,2560,1024]{2,1,0:T(8,128)(2,1)} %gather_rows.3.n2_ref, ...), custom_call_target="tpu_custom_call", output_to_operand_aliasing={{2}: (6, {})} | custom-call | flops 1 | bytes 1 | tf_op jit(solution)/shard_map/experts/pallas_call | solution.py:671
  275.7 11.7 %scatter_rows.4 = bf16[2048,1024]{1,0:T(8,128)(2,1)} custom-call(s32[68]{0:T(128)} %reshape.193.offs_ref, f32[4096,4]{1,0:T(8,128)} %bitcast.82, bf16[2,3072,1024]{2,1,0:T(8,128)(2,1)} %get-tuple-element.152.rest_0_, bf16[1,3072,1024]{2,1,0:T(8,128)(2,1)} %get-tuple-element.153.rest_1_, bf16[1,3072,1024]{2,1,0:T(8,128)(2,1)} %get-tuple-element.155.rest_2_), custom_call_target="tpu_custom_call" | custom-call | flops 1 | bytes 1 | tf_op jit(solution)/shard_map/scatter_rows/pallas_call | solution.py:768
  287.5 11.2 %scatter_rows.3 = bf16[2048,1024]{1,0:T(8,128)(2,1)} custom-call(s32[68]{0:T(128)} %reshape.193.offs_ref, f32[4096,4]{1,0:T(8,128)} %bitcast.83, bf16[2,3072,1024]{2,1,0:T(8,128)(2,1)} %get-tuple-element.152.rest_0_, bf16[1,3072,1024]{2,1,0:T(8,128)(2,1)} %get-tuple-element.153.rest_1_, bf16[1,3072,1024]{2,1,0:T(8,128)(2,1)} %get-tuple-element.155.rest_2_), custom_call_target="tpu_custom_call" | custom-call | flops 1 | bytes 1 | tf_op jit(solution)/shard_map/scatter_rows/pallas_call | solution.py:768
  298.7 4.3 add_convert_fusion.5
  303.2 19.0 %collective-permute-start.37 = (bf16[256,1024]{1,0:T(8,128)(2,1)S(1)}, bf16[256,1024]{1,0:T(8,128)(2,1)S(1)}, u32[]{:S(2)}, u32[]{:S(2)}) collective-permute-start(bf16[256,1024]{1,0:T(8,128)(2,1)S(1)} %get-tuple-element.260), channel_id=1, source_target_pairs={{0,1},{1,0},{2,3},{3,2},{4,5},{5,4},{6,7},{7,6},{8,9},{9,8},{10,11... | collective-permute-start | bytes 1572872 | tf_op jit(solution)/shard_map/ppermute | solution.py:910
  325.4 9.5 %collective-permute-done.37 = bf16[256,1024]{1,0:T(8,128)(2,1)S(1)} collective-permute-done((bf16[256,1024]{1,0:T(8,128)(2,1)S(1)}, bf16[256,1024]{1,0:T(8,128)(2,1)S(1)}, u32[]{:S(2)}, u32[]{:S(2)}) %collective-permute-start.37) | collective-permute-done | bytes 524320 | tf_op jit(solution)/shard_map/ppermute | solution.py:910
  334.9 2.0 collective-permute-done.38
  337.5 18.8 %scatter_rows.5 = (bf16[2048,1024]{1,0:T(8,128)(2,1)}, bf16[2048,1024]{1,0:T(8,128)(2,1)}) custom-call(s32[68]{0:T(128)} %reshape.193.offs_ref, f32[4096,4]{1,0:T(8,128)} %bitcast.84, bf16[2,3072,1024]{2,1,0:T(8,128)(2,1)} %get-tuple-element.159.rest_0_, bf16[1,3072,1024]{2,1,0:T(8,128)(2,1)} %get-tuple-element.160.rest_1_, ...), custom_call_target="tpu_custom_call" | custom-call | flops 1 | bytes 1 | tf_op jit(solution)/shard_map/scatter_rows/pallas_call | solution.py:768
  356.3 3.6 fusion.31
  360.5 1.5 convert_add_fusion.7
  363.5 2.9 multiply_reduce_fusion
  366.3 3.9 fusion.30
  370.3 1.6 add_convert_fusion
  373.0 1.8 collective-permute-start.45
  374.8 2.3 collective-permute-start.46
  379.0 34.0 %attend_backward.1 = (f32[512,1024]{1,0:T(8,128)}, bf16[4,4,400,256]{3,2,1,0:T(8,128)(2,1)}, bf16[4,400,256]{2,1,0:T(8,128)(2,1)}, bf16[4,400,256]{2,1,0:T(8,128...) custom-call(s32[4]{0:T(128)} %copy-done.21, bf16[512,1024]{1,0:T(8,128)(2,1)} %tokens_ref.2, ...), custom_call_target="tpu_custom_call" | custom-call | flops 1 | bytes 1 | tf_op jit(solution)/shard_map/attend_backward/pallas_call | solution.py:409
  414.1 2.2 add_convert_fusion.7
  416.3 2.0 collective-permute-start.56
  419.3 1.8 collective-permute-start.57
  421.1 2.2 fusion.1
  425.9 1.8 collective-permute-start.51
  428.9 2.5 collective-permute-done.56
  432.7 1.6 collective-permute-done.57
  435.6 3.5 maximum_add_fusion.1
  439.1 10.1 %adam_experts.2 = (f32[1,8,128,1024]{3,2,1,0:T(8,128)}, f32[1,8,128,1024]{3,2,1,0:T(8,128)}, f32[1,8,128,1024]{3,2,1,0:T(8,128)}, f32[1,8,64,1024]{3,2,1,0:T(8,1...) custom-call(s32[4]{0:T(128)} %copy-done.21, bf16[2,2,192,1024]{3,2,1,0:T(8,128)(2,1)} %bitcast.86, ...), custom_call_target="tpu_custom_call" | custom-call | flops 1 | bytes 1 | tf_op jit(solution)/shard_map/adam_experts/pallas_call | solution.py:809
  449.1 1.7 collective-permute-done.51
  453.4 1.8 collective-permute-start.60
  455.2 7.1 %collective-permute-done.59 = bf16[2,400,256]{2,1,0:T(8,128)(2,1)S(1)} collective-permute-done((bf16[2,400,256]{2,1,0:T(8,128)(2,1)S(1)}, bf16[2,400,256]{2,1,0:T(8,128)(2,1)S(1)}, u32[]{:S(2)}, u32[]{:S(2)}) %collective-permute-start.59) | collective-permute-done | bytes 409632 | tf_op jit(solution)/shard_map/ppermute | solution.py:910
  463.5 1.9 collective-permute-done.60
  466.5 1.5 fusion.29
  468.0 18.1 %reduce-scatter.5.cloned.1.call-done = bf16[1,2,2,192,1024]{4,3,2,1,0:T(8,128)(2,1)} async-done(((bf16[4,2,2,192,1024]{4,3,2,1,0:T(8,128)(2,1)}), bf16[1,2,2,192,1024]{4,3,2,1,0:T(8,128)(2,1)}) %reduce-scatter.5.cloned.1.call-update) | async-done | bytes 1572880 | tf_op jit(solution)/shard_map/reduce_scatter | solution.py:1034
  487.4 1.5 collective-permute-start.61
  489.0 1.7 collective-permute-start.62
  493.0 9.9 %adam_experts.3 = (f32[1,8,128,1024]{3,2,1,0:T(8,128)}, f32[1,8,128,1024]{3,2,1,0:T(8,128)}, f32[1,8,128,1024]{3,2,1,0:T(8,128)}, f32[1,8,64,1024]{3,2,1,0:T(8,1...) custom-call(s32[4]{0:T(128)} %copy-done.21, ...), custom_call_target="tpu_custom_call", output_to_operand_aliasing={{0}: (9, {}), {1}: (10, {}), {2}: (11, {}), {3}: (12, {}), ... | custom-call | flops 1 | bytes 1 | tf_op jit(solution)/shard_map/adam_experts/pallas_call | solution.py:809
  502.8 3.8 collective-permute-done.62.rest_1_
  506.7 2.0 adam_rest.1
  (289 shorter events, 59.0 us)
Async XLA Ops:
  7.2 190.9 %all-gather.6.cloned.1.call-start = ((), (), s32[]{:S(2)}) async-start(), calls=%async_computation.4 | async-start | bytes 11796480 | tf_op jit(solution)/shard_map/all_gather | solution.py:966
  17.4 243.5 %all-gather.8.cloned.1.call-start = ((), (), s32[]{:S(2)}) async-start(), calls=%async_computation.5 | async-start | bytes 3932160 | tf_op jit(solution)/shard_map/all_gather | solution.py:966
  18.6 41.6 %collective-permute-start.1 = (bf16[512,1024]{1,0:T(8,128)(2,1)S(1)}, bf16[512,1024]{1,0:T(8,128)(2,1)}, u32[]{:S(2)}, u32[]{:S(2)}) collective-permute-start(bf16[512,1024]{1,0:T(8,128)(2,1)S(1)} %copy-done.30), channel_id=1, source_target_pairs={{0,1},{1,0},{2,3},{3,2},{4,5},{5,4},{6,7},{7,6},{8,9},{9,8},{10,11... | collective-permute-start | bytes 3145736 | tf_op jit(solution)/shard_map/ppermute | solution.py:910
  21.5 38.8 %collective-permute-start.2 = (bf16[512,1024]{1,0:T(8,128)(2,1)S(1)}, bf16[512,1024]{1,0:T(8,128)(2,1)}, u32[]{:S(2)}, u32[]{:S(2)}) collective-permute-start(bf16[512,1024]{1,0:T(8,128)(2,1)S(1)} %copy-done.30), channel_id=1, source_target_pairs={{0,2},{1,3},{2,0},{3,1},{4,6},{5,7},{6,4},{7,5},{8,10},{9,11},{10,... | collective-permute-start | bytes 3145736 | tf_op jit(solution)/shard_map/ppermute | solution.py:910
  23.9 40.0 %collective-permute-start = (f32[4,2048]{1,0:T(4,128)}, f32[4,2048]{1,0:T(4,128)}, u32[]{:S(2)}, u32[]{:S(2)}) collective-permute-start(f32[4,2048]{1,0:T(4,128)} %get-tuple-element.267), channel_id=1, source_target_pairs={{0,4},{4,0},{8,12},{12,8},{16,20},{20,16},{24,28},{28,24},{1,5},{5... | collective-permute-start | bytes 98312 | tf_op jit(solution)/shard_map/ppermute | solution.py:904
  26.7 62.2 %collective-permute-start.34 = (bf16[1,192,1024]{2,1,0:T(8,128)(2,1)}, bf16[1,192,1024]{2,1,0:T(8,128)(2,1)}, u32[]{:S(2)}, u32[]{:S(2)}) collective-permute-start(bf16[1,192,1024]{2,1,0:T(8,128)(2,1)} %pad_maximum_fusion.5), channel_id=1, source_target_pairs={{0,4},{4,0},{8,12},{12,8},{16,20},{20,16},{24,28},{28,24},{1,5},{5... | collective-permute-start | bytes 1179656 | tf_op jit(solution)/shard_map/ppermute | solution.py:904
  60.2 15.7 %collective-permute-start.3 = (bf16[4,272,256]{2,1,0:T(8,128)(2,1)S(1)}, bf16[4,272,256]{2,1,0:T(8,128)(2,1)}, u32[]{:S(2)}, u32[]{:S(2)}) collective-permute-start(bf16[4,272,256]{2,1,0:T(8,128)(2,1)S(1)} %slice.230.rest_0_), channel_id=1, source_target_pairs={{0,1},{1,0},{2,3},{3,2},{4,5},{5,4},{6,7},{7,6},{8,9},{9,8},{10,11... | collective-permute-start | bytes 1671176 | tf_op jit(solution)/shard_map/ppermute | solution.py:910
  60.5 25.1 %collective-permute-start.4 = (bf16[4,272,256]{2,1,0:T(8,128)(2,1)S(1)}, bf16[4,272,256]{2,1,0:T(8,128)(2,1)}, u32[]{:S(2)}, u32[]{:S(2)}) collective-permute-start(bf16[4,272,256]{2,1,0:T(8,128)(2,1)S(1)} %slice.230.rest_0_), channel_id=1, source_target_pairs={{0,2},{1,3},{2,0},{3,1},{4,6},{5,7},{6,4},{7,5},{8,10},{9,11},{10,... | collective-permute-start | bytes 1671176 | tf_op jit(solution)/shard_map/ppermute | solution.py:910
  60.5 25.1 %collective-permute-start.5 = (bf16[4,272,256]{2,1,0:T(8,128)(2,1)S(1)}, bf16[4,272,256]{2,1,0:T(8,128)(2,1)}, u32[]{:S(2)}, u32[]{:S(2)}) collective-permute-start(bf16[4,272,256]{2,1,0:T(8,128)(2,1)S(1)} %slice.230.rest_0_), channel_id=1, source_target_pairs={{0,3},{1,2},{2,1},{3,0},{4,7},{5,6},{6,5},{7,4},{8,11},{9,10},{10,... | collective-permute-start | bytes 1671176 | tf_op jit(solution)/shard_map/ppermute | solution.py:910
  65.5 27.3 %collective-permute-start.6 = (bf16[4,272,256]{2,1,0:T(8,128)(2,1)S(1)}, bf16[4,272,256]{2,1,0:T(8,128)(2,1)S(1)}, u32[]{:S(2)}, u32[]{:S(2)}) collective-permute-start(bf16[4,272,256]{2,1,0:T(8,128)(2,1)S(1)} %slice.230.rest_0_), channel_id=1, source_target_pairs={{0,4},{4,0},{8,12},{12,8},{16,20},{20,16},{24,28},{28,24},{1,5},{5... | collective-permute-start | bytes 1671176 | tf_op jit(solution)/shard_map/ppermute | solution.py:904
  76.0 17.9 %collective-permute-start.7 = (bf16[4,272,256]{2,1,0:T(8,128)(2,1)}, bf16[4,272,256]{2,1,0:T(8,128)(2,1)}, u32[]{:S(2)}, u32[]{:S(2)}) collective-permute-start(bf16[4,272,256]{2,1,0:T(8,128)(2,1)} %collective-permute-done.3.rest_1_), channel_id=1, source_target_pairs={{0,4},{4,0},{8,12},{12,8},{16,20},{20,16},{24,28},{28,24},{1,5},{5... | collective-permute-start | bytes 1671176 | tf_op jit(solution)/shard_map/ppermute | solution.py:904
  85.5 9.9 %collective-permute-start.8 = (bf16[4,272,256]{2,1,0:T(8,128)(2,1)}, bf16[4,272,256]{2,1,0:T(8,128)(2,1)}, u32[]{:S(2)}, u32[]{:S(2)}) collective-permute-start(bf16[4,272,256]{2,1,0:T(8,128)(2,1)} %collective-permute-done.4.rest_2_), channel_id=1, source_target_pairs={{0,4},{4,0},{8,12},{12,8},{16,20},{20,16},{24,28},{28,24},{1,5},{5... | collective-permute-start | bytes 1671176 | tf_op jit(solution)/shard_map/ppermute | solution.py:904
  85.5 9.9 %collective-permute-start.9 = (bf16[4,272,256]{2,1,0:T(8,128)(2,1)}, bf16[4,272,256]{2,1,0:T(8,128)(2,1)}, u32[]{:S(2)}, u32[]{:S(2)}) collective-permute-start(bf16[4,272,256]{2,1,0:T(8,128)(2,1)} %collective-permute-done.5.rest_3_), channel_id=1, source_target_pairs={{0,4},{4,0},{8,12},{12,8},{16,20},{20,16},{24,28},{28,24},{1,5},{5... | collective-permute-start | bytes 1671176 | tf_op jit(solution)/shard_map/ppermute | solution.py:904
  90.9 336.8 %reduce-scatter.3.cloned.1.call-start = ((), (), s32[]{:S(2)}) async-start(), calls=%async_computation.2 | async-start | bytes 7864320 | tf_op jit(solution)/shard_map/reduce_scatter | solution.py:1034
  91.1 25.9 %collective-permute-start.10 = (bf16[4,128,256]{2,1,0:T(8,128)(2,1)S(1)}, bf16[4,128,256]{2,1,0:T(8,128)(2,1)S(1)}, u32[]{:S(2)}, u32[]{:S(2)}) collective-permute-start(bf16[4,128,256]{2,1,0:T(8,128)(2,1)S(1)} %slice.231.rest_0_), channel_id=1, source_target_pairs={{0,1},{1,0},{2,3},{3,2},{4,5},{5,4},{6,7},{7,6},{8,9},{9,8},{10,11... | collective-permute-start | bytes 786440 | tf_op jit(solution)/shard_map/ppermute | solution.py:910
  93.6 23.3 %collective-permute-start.11 = (bf16[4,128,256]{2,1,0:T(8,128)(2,1)S(1)}, bf16[4,128,256]{2,1,0:T(8,128)(2,1)S(1)}, u32[]{:S(2)}, u32[]{:S(2)}) collective-permute-start(bf16[4,128,256]{2,1,0:T(8,128)(2,1)S(1)} %slice.231.rest_0_), channel_id=1, source_target_pairs={{0,2},{1,3},{2,0},{3,1},{4,6},{5,7},{6,4},{7,5},{8,10},{9,11},{10,... | collective-permute-start | bytes 786440 | tf_op jit(solution)/shard_map/ppermute | solution.py:910
  93.9 23.1 %collective-permute-start.12 = (bf16[4,128,256]{2,1,0:T(8,128)(2,1)S(1)}, bf16[4,128,256]{2,1,0:T(8,128)(2,1)S(1)}, u32[]{:S(2)}, u32[]{:S(2)}) collective-permute-start(bf16[4,128,256]{2,1,0:T(8,128)(2,1)S(1)} %slice.231.rest_0_), channel_id=1, source_target_pairs={{0,3},{1,2},{2,1},{3,0},{4,7},{5,6},{6,5},{7,4},{8,11},{9,10},{10,... | collective-permute-start | bytes 786440 | tf_op jit(solution)/shard_map/ppermute | solution.py:910
  117.1 5.6 %collective-permute-start.14 = (bf16[4,128,256]{2,1,0:T(8,128)(2,1)S(1)}, bf16[4,128,256]{2,1,0:T(8,128)(2,1)S(1)}, u32[]{:S(2)}, u32[]{:S(2)}) collective-permute-start(bf16[4,128,256]{2,1,0:T(8,128)(2,1)S(1)} %collective-permute-done.10.rest_1_), channel_id=1, source_target_pairs={{0,4},{4,0},{8,12},{12,8},{16,20},{20,16},{24,28},{28,24},{1,5},{5... | collective-permute-start | bytes 786440 | tf_op jit(solution)/shard_map/ppermute | solution.py:904
  117.6 5.2 collective-permute-start.15
  117.7 5.1 collective-permute-start.16
  119.6 14.7 %collective-permute-start.19 = (bf16[256,1024]{1,0:T(8,128)(2,1)S(1)}, bf16[256,1024]{1,0:T(8,128)(2,1)S(1)}, u32[]{:S(2)}, u32[]{:S(2)}) collective-permute-start(bf16[256,1024]{1,0:T(8,128)(2,1)S(1)} %slice.174), channel_id=1, source_target_pairs={{0,2},{1,3},{2,0},{3,1},{4,6},{5,7},{6,4},{7,5},{8,10},{9,11},{10,... | collective-permute-start | bytes 1572872 | tf_op jit(solution)/shard_map/ppermute | solution.py:910
  121.6 14.9 %collective-permute-start.20 = (bf16[256,1024]{1,0:T(8,128)(2,1)S(1)}, bf16[256,1024]{1,0:T(8,128)(2,1)S(1)}, u32[]{:S(2)}, u32[]{:S(2)}) collective-permute-start(bf16[256,1024]{1,0:T(8,128)(2,1)S(1)} %slice.175), channel_id=1, source_target_pairs={{0,1},{1,0},{2,3},{3,2},{4,5},{5,4},{6,7},{7,6},{8,9},{9,8},{10,11... | collective-permute-start | bytes 1572872 | tf_op jit(solution)/shard_map/ppermute | solution.py:910
  129.1 28.6 %collective-permute-start.17 = (bf16[512,1024]{1,0:T(8,128)(2,1)}, bf16[512,1024]{1,0:T(8,128)(2,1)S(1)}, u32[]{:S(2)}, u32[]{:S(2)}) collective-permute-start(bf16[512,1024]{1,0:T(8,128)(2,1)} %get-tuple-element.141.rest_0_), channel_id=1, source_target_pairs={{0,1},{1,0},{2,3},{3,2},{4,5},{5,4},{6,7},{7,6},{8,9},{9,8},{10,11... | collective-permute-start | bytes 3145736 | tf_op jit(solution)/shard_map/ppermute | solution.py:910
  130.0 27.7 %collective-permute-start.18 = (bf16[512,1024]{1,0:T(8,128)(2,1)}, bf16[512,1024]{1,0:T(8,128)(2,1)}, u32[]{:S(2)}, u32[]{:S(2)}) collective-permute-start(bf16[512,1024]{1,0:T(8,128)(2,1)} %get-tuple-element.141.rest_0_), channel_id=1, source_target_pairs={{0,2},{1,3},{2,0},{3,1},{4,6},{5,7},{6,4},{7,5},{8,10},{9,11},{10,... | collective-permute-start | bytes 3145736 | tf_op jit(solution)/shard_map/ppermute | solution.py:910
  131.2 29.8 %collective-permute-start.21 = (bf16[512,1024]{1,0:T(8,128)(2,1)S(1)}, bf16[512,1024]{1,0:T(8,128)(2,1)S(1)}, u32[]{:S(2)}, u32[]{:S(2)}) collective-permute-start(bf16[512,1024]{1,0:T(8,128)(2,1)S(1)} %copy-done.31), channel_id=1, source_target_pairs={{0,4},{4,0},{8,12},{12,8},{16,20},{20,16},{24,28},{28,24},{1,5},{5... | collective-permute-start | bytes 3145736 | tf_op jit(solution)/shard_map/ppermute | solution.py:904
  134.2 27.6 %collective-permute-start.22 = (bf16[512,1024]{1,0:T(8,128)(2,1)}, bf16[512,1024]{1,0:T(8,128)(2,1)S(1)}, u32[]{:S(2)}, u32[]{:S(2)}) collective-permute-start(bf16[512,1024]{1,0:T(8,128)(2,1)} %collective-permute-done.1.rest_2_), channel_id=1, source_target_pairs={{0,4},{4,0},{8,12},{12,8},{16,20},{20,16},{24,28},{28,24},{1,5},{5... | collective-permute-start | bytes 3145736 | tf_op jit(solution)/shard_map/ppermute | solution.py:904
  136.5 27.0 %collective-permute-start.23 = (bf16[512,1024]{1,0:T(8,128)(2,1)}, bf16[512,1024]{1,0:T(8,128)(2,1)S(1)}, u32[]{:S(2)}, u32[]{:S(2)}) collective-permute-start(bf16[512,1024]{1,0:T(8,128)(2,1)} %collective-permute-done.2.rest_3_), channel_id=1, source_target_pairs={{0,4},{4,0},{8,12},{12,8},{16,20},{20,16},{24,28},{28,24},{1,5},{5... | collective-permute-start | bytes 3145736 | tf_op jit(solution)/shard_map/ppermute | solution.py:904
  157.7 5.8 %collective-permute-start.24 = (bf16[256,1024]{1,0:T(8,128)(2,1)S(1)}, bf16[256,1024]{1,0:T(8,128)(2,1)S(1)}, u32[]{:S(2)}, u32[]{:S(2)}) collective-permute-start(bf16[256,1024]{1,0:T(8,128)(2,1)S(1)} %collective-permute-done.19.rest_4_), channel_id=1, source_target_pairs={{0,4},{4,0},{8,12},{12,8},{16,20},{20,16},{24,28},{28,24},{1,5},{5... | collective-permute-start | bytes 1572872 | tf_op jit(solution)/shard_map/ppermute | solution.py:904
  157.7 6.8 %collective-permute-start.25 = (bf16[256,1024]{1,0:T(8,128)(2,1)S(1)}, bf16[256,1024]{1,0:T(8,128)(2,1)S(1)}, u32[]{:S(2)}, u32[]{:S(2)}) collective-permute-start(bf16[256,1024]{1,0:T(8,128)(2,1)S(1)} %collective-permute-done.20.rest_5_), channel_id=1, source_target_pairs={{0,4},{4,0},{8,12},{12,8},{16,20},{20,16},{24,28},{28,24},{1,5},{5... | collective-permute-start | bytes 1572872 | tf_op jit(solution)/shard_map/ppermute | solution.py:904
  161.0 18.0 %collective-permute-start.26 = (bf16[256,1024]{1,0:T(8,128)(2,1)}, bf16[256,1024]{1,0:T(8,128)(2,1)S(1)}, u32[]{:S(2)}, u32[]{:S(2)}) collective-permute-start(bf16[256,1024]{1,0:T(8,128)(2,1)} %slice.232), channel_id=1, source_target_pairs={{0,2},{1,3},{2,0},{3,1},{4,6},{5,7},{6,4},{7,5},{8,10},{9,11},{10,... | collective-permute-start | bytes 1572872 | tf_op jit(solution)/shard_map/ppermute | solution.py:910
  161.8 17.2 %collective-permute-start.27 = (bf16[256,1024]{1,0:T(8,128)(2,1)}, bf16[256,1024]{1,0:T(8,128)(2,1)}, u32[]{:S(2)}, u32[]{:S(2)}) collective-permute-start(bf16[256,1024]{1,0:T(8,128)(2,1)} %slice.233), channel_id=1, source_target_pairs={{0,1},{1,0},{2,3},{3,2},{4,5},{5,4},{6,7},{7,6},{8,9},{9,8},{10,11... | collective-permute-start | bytes 1572872 | tf_op jit(solution)/shard_map/ppermute | solution.py:910
  163.5 16.1 %collective-permute-start.28 = (bf16[512,1024]{1,0:T(8,128)(2,1)}, bf16[512,1024]{1,0:T(8,128)(2,1)}, u32[]{:S(2)}, u32[]{:S(2)}) collective-permute-start(bf16[512,1024]{1,0:T(8,128)(2,1)} %get-tuple-element.141.rest_0_), channel_id=1, source_target_pairs={{0,4},{4,0},{8,12},{12,8},{16,20},{20,16},{24,28},{28,24},{1,5},{5... | collective-permute-start | bytes 3145736 | tf_op jit(solution)/shard_map/ppermute | solution.py:904
  163.5 18.5 %collective-permute-start.29 = (bf16[512,1024]{1,0:T(8,128)(2,1)S(1)}, bf16[512,1024]{1,0:T(8,128)(2,1)}, u32[]{:S(2)}, u32[]{:S(2)}) collective-permute-start(bf16[512,1024]{1,0:T(8,128)(2,1)S(1)} %collective-permute-done.17.rest_1_), channel_id=1, source_target_pairs={{0,4},{4,0},{8,12},{12,8},{16,20},{20,16},{24,28},{28,24},{1,5},{5... | collective-permute-start | bytes 3145736 | tf_op jit(solution)/shard_map/ppermute | solution.py:904
  165.5 17.3 %collective-permute-start.30 = (bf16[512,1024]{1,0:T(8,128)(2,1)}, bf16[512,1024]{1,0:T(8,128)(2,1)}, u32[]{:S(2)}, u32[]{:S(2)}) collective-permute-start(bf16[512,1024]{1,0:T(8,128)(2,1)} %collective-permute-done.18.rest_2_), channel_id=1, source_target_pairs={{0,4},{4,0},{8,12},{12,8},{16,20},{20,16},{24,28},{28,24},{1,5},{5... | collective-permute-start | bytes 3145736 | tf_op jit(solution)/shard_map/ppermute | solution.py:904
  235.4 250.7 %reduce-scatter.5.cloned.1.call-start = ((), (), s32[]{:S(2)}) async-start(), calls=%async_computation.3 | async-start | bytes 7864320 | tf_op jit(solution)/shard_map/reduce_scatter | solution.py:1034
  287.4 11.4 %collective-permute-start.35 = (bf16[2048,1024]{1,0:T(8,128)(2,1)}, bf16[2048,1024]{1,0:T(8,128)(2,1)}, u32[]{:S(2)}, u32[]{:S(2)}) collective-permute-start(bf16[2048,1024]{1,0:T(8,128)(2,1)} %scatter_rows.4), channel_id=1, source_target_pairs={{0,4},{4,0},{8,12},{12,8},{16,20},{20,16},{24,28},{28,24},{1,5},{5... | collective-permute-start | bytes 12582920 | tf_op jit(solution)/shard_map/ppermute | solution.py:904
  303.2 31.7 %collective-permute-start.37 = (bf16[256,1024]{1,0:T(8,128)(2,1)S(1)}, bf16[256,1024]{1,0:T(8,128)(2,1)S(1)}, u32[]{:S(2)}, u32[]{:S(2)}) collective-permute-start(bf16[256,1024]{1,0:T(8,128)(2,1)S(1)} %get-tuple-element.260), channel_id=1, source_target_pairs={{0,1},{1,0},{2,3},{3,2},{4,5},{5,4},{6,7},{7,6},{8,9},{9,8},{10,11... | collective-permute-start | bytes 1572872 | tf_op jit(solution)/shard_map/ppermute | solution.py:910
  322.1 14.8 %collective-permute-start.38 = (bf16[256,1024]{1,0:T(8,128)(2,1)S(1)}, bf16[256,1024]{1,0:T(8,128)(2,1)S(1)}, u32[]{:S(2)}, u32[]{:S(2)}) collective-permute-start(bf16[256,1024]{1,0:T(8,128)(2,1)S(1)} %get-tuple-element.259), channel_id=1, source_target_pairs={{0,2},{1,3},{2,0},{3,1},{4,6},{5,7},{6,4},{7,5},{8,10},{9,11},{10,... | collective-permute-start | bytes 1572872 | tf_op jit(solution)/shard_map/ppermute | solution.py:910
  323.2 36.7 %collective-permute-start.36 = (bf16[256,1024]{1,0:T(8,128)(2,1)}, bf16[256,1024]{1,0:T(8,128)(2,1)}, u32[]{:S(2)}, u32[]{:S(2)}) collective-permute-start(bf16[256,1024]{1,0:T(8,128)(2,1)} %slice.238), channel_id=1, source_target_pairs={{0,1},{1,0},{2,3},{3,2},{4,5},{5,4},{6,7},{7,6},{8,9},{9,8},{10,11... | collective-permute-start | bytes 1572872 | tf_op jit(solution)/shard_map/ppermute | solution.py:910
  324.6 37.4 %collective-permute-start.41 = (bf16[256,1024]{1,0:T(8,128)(2,1)S(1)}, bf16[256,1024]{1,0:T(8,128)(2,1)}, u32[]{:S(2)}, u32[]{:S(2)}) collective-permute-start(bf16[256,1024]{1,0:T(8,128)(2,1)S(1)} %slice.247), channel_id=1, source_target_pairs={{0,2},{1,3},{2,0},{3,1},{4,6},{5,7},{6,4},{7,5},{8,10},{9,11},{10,... | collective-permute-start | bytes 1572872 | tf_op jit(solution)/shard_map/ppermute | solution.py:910
  337.1 23.4 %collective-permute-start.39 = (bf16[256,1024]{1,0:T(8,128)(2,1)S(1)}, bf16[256,1024]{1,0:T(8,128)(2,1)}, u32[]{:S(2)}, u32[]{:S(2)}) collective-permute-start(bf16[256,1024]{1,0:T(8,128)(2,1)S(1)} %add_convert_fusion.9), channel_id=1, source_target_pairs={{0,2},{1,3},{2,0},{3,1},{4,6},{5,7},{6,4},{7,5},{8,10},{9,11},{10,... | collective-permute-start | bytes 1572872 | tf_op jit(solution)/shard_map/ppermute | solution.py:910
  337.4 24.7 %collective-permute-start.40 = (bf16[256,1024]{1,0:T(8,128)(2,1)S(1)}, bf16[256,1024]{1,0:T(8,128)(2,1)}, u32[]{:S(2)}, u32[]{:S(2)}) collective-permute-start(bf16[256,1024]{1,0:T(8,128)(2,1)S(1)} %add_convert_fusion.8), channel_id=1, source_target_pairs={{0,1},{1,0},{2,3},{3,2},{4,5},{5,4},{6,7},{7,6},{8,9},{9,8},{10,11... | collective-permute-start | bytes 1572872 | tf_op jit(solution)/shard_map/ppermute | solution.py:910
  359.9 10.3 %collective-permute-start.42 = (bf16[512,1024]{1,0:T(8,128)(2,1)S(1)}, bf16[512,1024]{1,0:T(8,128)(2,1)S(1)}, u32[]{:S(2)}, u32[]{:S(2)}) collective-permute-start(bf16[512,1024]{1,0:T(8,128)(2,1)S(1)} %get-tuple-element.242), channel_id=1, source_target_pairs={{0,4},{4,0},{8,12},{12,8},{16,20},{20,16},{24,28},{28,24},{1,5},{5... | collective-permute-start | bytes 3145736 | tf_op jit(solution)/shard_map/ppermute | solution.py:904
  359.9 10.3 %collective-permute-start.43 = (bf16[512,1024]{1,0:T(8,128)(2,1)S(1)}, bf16[512,1024]{1,0:T(8,128)(2,1)S(1)}, u32[]{:S(2)}, u32[]{:S(2)}) collective-permute-start(bf16[512,1024]{1,0:T(8,128)(2,1)S(1)} %get-tuple-element.241), channel_id=1, source_target_pairs={{0,4},{4,0},{8,12},{12,8},{16,20},{20,16},{24,28},{28,24},{1,5},{5... | collective-permute-start | bytes 3145736 | tf_op jit(solution)/shard_map/ppermute | solution.py:904
  360.4 9.8 %collective-permute-start.44 = (bf16[512,1024]{1,0:T(8,128)(2,1)S(1)}, bf16[512,1024]{1,0:T(8,128)(2,1)S(1)}, u32[]{:S(2)}, u32[]{:S(2)}) collective-permute-start(bf16[512,1024]{1,0:T(8,128)(2,1)S(1)} %get-tuple-element.240), channel_id=1, source_target_pairs={{0,4},{4,0},{8,12},{12,8},{16,20},{20,16},{24,28},{28,24},{1,5},{5... | collective-permute-start | bytes 3145736 | tf_op jit(solution)/shard_map/ppermute | solution.py:904
  373.0 40.0 %collective-permute-start.45 = (bf16[256,1024]{1,0:T(8,128)(2,1)}, bf16[256,1024]{1,0:T(8,128)(2,1)}, u32[]{:S(2)}, u32[]{:S(2)}) collective-permute-start(bf16[256,1024]{1,0:T(8,128)(2,1)} %get-tuple-element.258), channel_id=1, source_target_pairs={{0,1},{1,0},{2,3},{3,2},{4,5},{5,4},{6,7},{7,6},{8,9},{9,8},{10,11... | collective-permute-start | bytes 1572872 | tf_op jit(solution)/shard_map/ppermute | solution.py:910
  374.8 38.2 %collective-permute-start.46 = (bf16[256,1024]{1,0:T(8,128)(2,1)}, bf16[256,1024]{1,0:T(8,128)(2,1)S(1)}, u32[]{:S(2)}, u32[]{:S(2)}) collective-permute-start(bf16[256,1024]{1,0:T(8,128)(2,1)} %get-tuple-element.257), channel_id=1, source_target_pairs={{0,2},{1,3},{2,0},{3,1},{4,6},{5,7},{6,4},{7,5},{8,10},{9,11},{10,... | collective-permute-start | bytes 1572872 | tf_op jit(solution)/shard_map/ppermute | solution.py:910
  377.9 35.1 %collective-permute-start.47 = (bf16[256,1024]{1,0:T(8,128)(2,1)}, bf16[256,1024]{1,0:T(8,128)(2,1)}, u32[]{:S(2)}, u32[]{:S(2)}) collective-permute-start(bf16[256,1024]{1,0:T(8,128)(2,1)} %slice.202), channel_id=1, source_target_pairs={{0,1},{1,0},{2,3},{3,2},{4,5},{5,4},{6,7},{7,6},{8,9},{9,8},{10,11... | collective-permute-start | bytes 1572872 | tf_op jit(solution)/shard_map/ppermute | solution.py:910
  379.0 34.0 %collective-permute-start.48 = (bf16[256,1024]{1,0:T(8,128)(2,1)}, bf16[256,1024]{1,0:T(8,128)(2,1)}, u32[]{:S(2)}, u32[]{:S(2)}) collective-permute-start(bf16[256,1024]{1,0:T(8,128)(2,1)} %slice.203), channel_id=1, source_target_pairs={{0,2},{1,3},{2,0},{3,1},{4,6},{5,7},{6,4},{7,5},{8,10},{9,11},{10,... | collective-permute-start | bytes 1572872 | tf_op jit(solution)/shard_map/ppermute | solution.py:910
  413.0 6.3 %collective-permute-start.49 = (bf16[4,400,256]{2,1,0:T(8,128)(2,1)}, bf16[4,400,256]{2,1,0:T(8,128)(2,1)S(1)}, u32[]{:S(2)}, u32[]{:S(2)}) collective-permute-start(bf16[4,400,256]{2,1,0:T(8,128)(2,1)} %get-tuple-element.173), channel_id=1, source_target_pairs={{0,4},{4,0},{8,12},{12,8},{16,20},{20,16},{24,28},{28,24},{1,5},{5... | collective-permute-start | bytes 2457608 | tf_op jit(solution)/shard_map/ppermute | solution.py:904
  413.1 8.0 %collective-permute-start.50 = (bf16[4,400,256]{2,1,0:T(8,128)(2,1)}, bf16[4,400,256]{2,1,0:T(8,128)(2,1)S(1)}, u32[]{:S(2)}, u32[]{:S(2)}) collective-permute-start(bf16[4,400,256]{2,1,0:T(8,128)(2,1)} %get-tuple-element.174), channel_id=1, source_target_pairs={{0,4},{4,0},{8,12},{12,8},{16,20},{20,16},{24,28},{28,24},{1,5},{5... | collective-permute-start | bytes 2457608 | tf_op jit(solution)/shard_map/ppermute | solution.py:904
  413.6 7.5 %collective-permute-start.52 = (bf16[4,400,256]{2,1,0:T(8,128)(2,1)}, bf16[4,400,256]{2,1,0:T(8,128)(2,1)S(1)}, u32[]{:S(2)}, u32[]{:S(2)}) collective-permute-start(bf16[4,400,256]{2,1,0:T(8,128)(2,1)} %get-tuple-element.175), channel_id=1, source_target_pairs={{0,4},{4,0},{8,12},{12,8},{16,20},{20,16},{24,28},{28,24},{1,5},{5... | collective-permute-start | bytes 2457608 | tf_op jit(solution)/shard_map/ppermute | solution.py:904
  413.7 21.9 %collective-permute-start.55 = (bf16[512,1024]{1,0:T(8,128)(2,1)}, bf16[512,1024]{1,0:T(8,128)(2,1)}, u32[]{:S(2)}, u32[]{:S(2)}) collective-permute-start(bf16[512,1024]{1,0:T(8,128)(2,1)} %get-tuple-element.239), channel_id=1, source_target_pairs={{0,4},{4,0},{8,12},{12,8},{16,20},{20,16},{24,28},{28,24},{1,5},{5... | collective-permute-start | bytes 3145736 | tf_op jit(solution)/shard_map/ppermute | solution.py:904
  416.3 15.1 %collective-permute-start.56 = (bf16[256,1024]{1,0:T(8,128)(2,1)}, bf16[256,1024]{1,0:T(8,128)(2,1)}, u32[]{:S(2)}, u32[]{:S(2)}) collective-permute-start(bf16[256,1024]{1,0:T(8,128)(2,1)} %add_convert_fusion.7), channel_id=1, source_target_pairs={{0,2},{1,3},{2,0},{3,1},{4,6},{5,7},{6,4},{7,5},{8,10},{9,11},{10,... | collective-permute-start | bytes 1572872 | tf_op jit(solution)/shard_map/ppermute | solution.py:910
  419.3 15.0 %collective-permute-start.57 = (bf16[256,1024]{1,0:T(8,128)(2,1)}, bf16[256,1024]{1,0:T(8,128)(2,1)S(1)}, u32[]{:S(2)}, u32[]{:S(2)}) collective-permute-start(bf16[256,1024]{1,0:T(8,128)(2,1)} %add_convert_fusion.6), channel_id=1, source_target_pairs={{0,1},{1,0},{2,3},{3,2},{4,5},{5,4},{6,7},{7,6},{8,9},{9,8},{10,11... | collective-permute-start | bytes 1572872 | tf_op jit(solution)/shard_map/ppermute | solution.py:910
  424.5 24.7 %collective-permute-start.53 = (bf16[4,400,256]{2,1,0:T(8,128)(2,1)}, bf16[4,400,256]{2,1,0:T(8,128)(2,1)}, u32[]{:S(2)}, u32[]{:S(2)}) collective-permute-start(bf16[4,400,256]{2,1,0:T(8,128)(2,1)} %pad_maximum_fusion.3), channel_id=1, source_target_pairs={{0,2},{1,3},{2,0},{3,1},{4,6},{5,7},{6,4},{7,5},{8,10},{9,11},{10,... | collective-permute-start | bytes 2457608 | tf_op jit(solution)/shard_map/ppermute | solution.py:910
  425.9 24.9 %collective-permute-start.51 = (bf16[4,400,256]{2,1,0:T(8,128)(2,1)}, bf16[4,400,256]{2,1,0:T(8,128)(2,1)}, u32[]{:S(2)}, u32[]{:S(2)}) collective-permute-start(bf16[4,400,256]{2,1,0:T(8,128)(2,1)} %pad_maximum_fusion.2), channel_id=1, source_target_pairs={{0,1},{1,0},{2,3},{3,2},{4,5},{5,4},{6,7},{7,6},{8,9},{9,8},{10,11... | collective-permute-start | bytes 2457608 | tf_op jit(solution)/shard_map/ppermute | solution.py:910
  431.3 7.7 %collective-permute-start.54 = (bf16[2,192,1024]{2,1,0:T(8,128)(2,1)S(1)}, bf16[2,192,1024]{2,1,0:T(8,128)(2,1)}, u32[]{:S(2)}, u32[]{:S(2)}) collective-permute-start(bf16[2,192,1024]{2,1,0:T(8,128)(2,1)S(1)} %slice_bitcast_fusion.1), channel_id=1, source_target_pairs={{0,4},{4,0},{8,12},{12,8},{16,20},{20,16},{24,28},{28,24},{1,5},{5... | collective-permute-start | bytes 2359304 | tf_op jit(solution)/shard_map/ppermute | solution.py:904
  451.9 10.4 %collective-permute-start.59 = (bf16[2,400,256]{2,1,0:T(8,128)(2,1)S(1)}, bf16[2,400,256]{2,1,0:T(8,128)(2,1)S(1)}, u32[]{:S(2)}, u32[]{:S(2)}) collective-permute-start(bf16[2,400,256]{2,1,0:T(8,128)(2,1)S(1)} %add_convert_fusion.11), channel_id=1, source_target_pairs={{0,2},{1,3},{2,0},{3,1},{4,6},{5,7},{6,4},{7,5},{8,10},{9,11},{10,... | collective-permute-start | bytes 1228808 | tf_op jit(solution)/shard_map/ppermute | solution.py:910
  452.3 14.2 %collective-permute-start.58 = (bf16[4,400,256]{2,1,0:T(8,128)(2,1)S(1)}, bf16[4,400,256]{2,1,0:T(8,128)(2,1)S(1)}, u32[]{:S(2)}, u32[]{:S(2)}) collective-permute-start(bf16[4,400,256]{2,1,0:T(8,128)(2,1)S(1)} %copy-done.55), channel_id=1, source_target_pairs={{0,4},{4,0},{8,12},{12,8},{16,20},{20,16},{24,28},{28,24},{1,5},{5... | collective-permute-start | bytes 2457608 | tf_op jit(solution)/shard_map/ppermute | solution.py:904
  453.4 11.9 %collective-permute-start.60 = (bf16[2,400,256]{2,1,0:T(8,128)(2,1)S(1)}, bf16[2,400,256]{2,1,0:T(8,128)(2,1)S(1)}, u32[]{:S(2)}, u32[]{:S(2)}) collective-permute-start(bf16[2,400,256]{2,1,0:T(8,128)(2,1)S(1)} %add_convert_fusion.10), channel_id=1, source_target_pairs={{0,1},{1,0},{2,3},{3,2},{4,5},{5,4},{6,7},{7,6},{8,9},{9,8},{10,11... | collective-permute-start | bytes 1228808 | tf_op jit(solution)/shard_map/ppermute | solution.py:910
  487.4 15.4 %collective-permute-start.61 = (bf16[400,256]{1,0:T(8,128)(2,1)S(1)}, bf16[400,256]{1,0:T(8,128)(2,1)S(1)}, u32[]{:S(2)}, u32[]{:S(2)}) collective-permute-start(bf16[400,256]{1,0:T(8,128)(2,1)S(1)} %get-tuple-element.263), channel_id=1, source_target_pairs={{0,8},{4,12},{8,0},{12,4},{16,24},{20,28},{24,16},{28,20},{1,9},{5... | collective-permute-start | bytes 614408 | tf_op jit(solution)/shard_map/ppermute | solution.py:907
  489.0 17.6 %collective-permute-start.62 = (bf16[400,256]{1,0:T(8,128)(2,1)S(1)}, bf16[400,256]{1,0:T(8,128)(2,1)S(1)}, u32[]{:S(2)}, u32[]{:S(2)}) collective-permute-start(bf16[400,256]{1,0:T(8,128)(2,1)S(1)} %get-tuple-element.262), channel_id=1, source_target_pairs={{0,16},{4,20},{8,24},{12,28},{16,0},{20,4},{24,8},{28,12},{1,17},{... | collective-permute-start | bytes 614408 | tf_op jit(solution)/shard_map/ppermute | solution.py:907
  490.6 16.0 %collective-permute-start.63 = (bf16[400,256]{1,0:T(8,128)(2,1)S(1)}, bf16[400,256]{1,0:T(8,128)(2,1)S(1)}, u32[]{:S(2)}, u32[]{:S(2)}) collective-permute-start(bf16[400,256]{1,0:T(8,128)(2,1)S(1)} %get-tuple-element.261), channel_id=1, source_target_pairs={{0,24},{4,28},{8,16},{12,20},{16,8},{20,12},{24,0},{28,4},{1,25},{... | collective-permute-start | bytes 614408 | tf_op jit(solution)/shard_map/ppermute | solution.py:907
  (61 other events, 809.5 us)
Sparse Core Ops, SparseCore 0:
  17.5 180.5 all-gather.5
  199.6 61.2 all-gather.7
  263.2 109.3 reduce-scatter.2
  374.8 111.2 reduce-scatter.4

commit v5 on v4

--- a/solution.py
+++ b/solution.py
@@ -556,11 +556,9 @@
     def weight_copies(index):
         i, place = sources[index]
         slot = index % 2
+        expert = core * (weights[i].shape[1] // 2) + place
         return [
-            pltpu.make_async_copy(
-                weights[i].at[:, side, place, spot, :], buf.at[slot, :, core ^ side], w_sems.at[2 * side + j, slot]
-            )
-            for side in range(2)
+            pltpu.make_async_copy(weights[i].at[:, expert, spot, :], buf.at[slot], w_sems.at[j, slot])
             for j, (spot, buf) in enumerate(((slice(0, rin), win_buf), (slice(rin, wrows), wdown_buf)))
         ]
 
@@ -662,7 +660,8 @@
 
 
 def experts_step(place, slots, offs, first, weights, sources, before, spot, count):
-    nz, cores, _, wrows, _ = weights[0].shape
+    owners, _, wrows, _ = weights[0].shape
+    nz, cores = owners // 2, 2
     experts = len(sources)
     rin, rdown = D // (nz * cores), FFE // (nz * cores)
     part = jax.ShapeDtypeStruct((experts, HELD, D), bf16)
@@ -675,8 +674,8 @@
         in_specs=[SMEM, SMEM] + [HBM] * (3 + len(weights) + len(kept)),
         out_specs=(HBM, HBM, pl.BlockSpec((nz, cores, 1, wrows, D), lambda e: (0, 0, spot + e, 0, 0))),
         scratch_shapes=[
-            pltpu.VMEM((2, nz, cores, rin, D), bf16),
-            pltpu.VMEM((2, nz, cores, rdown, D), bf16),
+            pltpu.VMEM((2, owners, rin, D), bf16),
+            pltpu.VMEM((2, owners, rdown, D), bf16),
             pltpu.VMEM((2, CHUNK, D), bf16),
             pltpu.VMEM((2, CHUNK, D), bf16),
             pltpu.VMEM((2, CHUNK, 128), f32),
@@ -685,7 +684,7 @@
             pltpu.VMEM((CHUNK, D), bf16),
             pltpu.VMEM((D, D), f32),
             pltpu.VMEM((FFE, D), f32),
-            pltpu.SemaphoreType.DMA((4, 2)),
+            pltpu.SemaphoreType.DMA((2, 2)),
             pltpu.SemaphoreType.DMA((3, 2)),
             pltpu.SemaphoreType.DMA((2, 3)),
         ],
@@ -945,15 +944,11 @@
     def cut(quarters):
         return quarters[0] * half // 4, quarters[1] * half // 4
 
-    def shard(a, b, *ready):
-        masters = lax.optimization_barrier((expert_in, expert_down, own, *ready))[:2]
-
-        def low(side):
-            return jnp.concatenate(
-                [lax.dynamic_slice_in_dim(w[0], side * half + a, b - a, 0).astype(bf16) for w in masters], axis=1
-            )
-
-        return jnp.stack([low(core), swap_core(low(1 - core))])
+    def shard(a, b):
+        low = [
+            jnp.concatenate([w[0, a:b], w[0, half + a : half + b]]).astype(bf16) for w in (expert_in, expert_down)
+        ]
+        return jnp.concatenate(low, axis=1)
 
     spans = [cut(quarters) for quarters in GATHERS]
     spans = [(a, b) for a, b in spans if a < b]
@@ -963,7 +958,7 @@
     column = lax.all_gather(own, "dp", axis=0, tiled=False, axis_index_groups=groups)
     held = {}
     for (a, b), part in zip(spans, shards):
-        whole = lax.all_gather(part, "dp", axis=0, tiled=False, axis_index_groups=groups)
+        whole = lax.all_gather(part, "dp", axis=0, tiled=False)
         held.update({i: (whole, i - a) for i in range(a, b)})
     dm_near = near(cotangent)
     pieces = spread_t(after(column[:, : 2 * wrows + 16], *dm_near))

time: 522 us -> 523 us (level)
  the two profiles are of different devices: /device:TPU:0 before, /device:TPU:16 now
where the time goes in v5:
time: 523 us; the launch traced here: 513 us
  Pallas kernels  253 us (48%)
  waiting for transfers between devices  97.7 us (19%)
  starting transfers between devices  44.9 us (9%)
  other arithmetic  42.4 us (8%)
  local copies, waits for them, and re-layouts  31.5 us (6%)
  blocking collectives  27.8 us (5%)
  between operations  15.2 us (3%)
    pallas_call x3, Pallas kernels, experts_step(): pl.pallas_call(functools.partial(experts_kernel, first, subs, sources, le...  96.3 us
    ppermute x30, waiting for transfers between devices, swap_t(): return lax.ppermute(x, 'tensor', [(i, i ^ k) for i in range(nt)])  72.4 us
    pallas_call x3, Pallas kernels, scatter(): pl.pallas_call(functools.partial(scatter_kernel, halves, sources, experts...  43.5 us
    pallas_call x2, Pallas kernels, gather(): pl.pallas_call(functools.partial(gather_kernel, tuple(starts), experts, w...  36.5 us
    ppermute x30, starting transfers between devices, swap_t(): return lax.ppermute(x, 'tensor', [(i, i ^ k) for i in range(nt)])  33.3 us
    pallas_call x1, Pallas kernels, attend_backward(): pl.pallas_call(functools.partial(attend_backward_kernel, nz, nt, whole),...  32.8 us
    all_gather x1, blocking collectives, on_device(): lax.all_gather(own, 'dp', axis=0, tiled=False, axis_index_groups=groups)  27.8 us
    pallas_call x2, Pallas kernels, adam_experts(): pl.pallas_call(functools.partial(adam_kernel, per), grid_spec=pltpu.Prefe...  19.9 us
  transfers between devices with their start and end apart: 67, of which 17 were waited for; matrix products, arithmetic and copies ran while one was open for 11% of the time, Pallas kernels for 49%

profile of v5, /device:TPU:16, one launch (start us, length us, event | category | flops | bytes accessed | tf_op | source)
XLA Modules:
  0.0 513.0 jit_solution(8808545104420356933)
XLA Ops:
  7.2 1.9 convert.53
  10.5 1.7 maximum_maximum_fusion
  13.4 1.6 collective-permute-start.1
  15.0 1.5 collective-permute-start.2
  18.2 27.8 %all-gather = bf16[1600,256]{1,0:T(8,128)(2,1)S(1)} all-gather(bf16[400,256]{1,0:T(8,128)(2,1)S(1)} %pad_maximum_fusion.2), channel_id=2, replica_groups={{0,8,16,24},{4,12,20,28},{1,9,17,25},{5,13,21,29},{2,10,18,26},{6,14,22..., dimensions={0}, use_global_device_ids=true | all-gather | bytes 1024000 | tf_op jit(solution)/shard_map/all_gather | solution.py:958
  47.2 2.5 collective-permute-start.5
  50.7 11.2 %collective-permute-done.3.rest_1_ = bf16[4,272,256]{2,1,0:T(8,128)(2,1)} collective-permute-done((bf16[4,272,256]{2,1,0:T(8,128)(2,1)S(1)}, bf16[4,272,256]{2,1,0:T(8,128)(2,1)}, u32[]{:S(2)}, u32[]{:S(2)}) %collective-permute-start.3) | collective-permute-done | bytes 557088 | tf_op jit(solution)/shard_map/ppermute | solution.py:909
  61.9 10.1 %collective-permute-done.4.rest_2_ = bf16[4,272,256]{2,1,0:T(8,128)(2,1)} collective-permute-done((bf16[4,272,256]{2,1,0:T(8,128)(2,1)S(1)}, bf16[4,272,256]{2,1,0:T(8,128)(2,1)}, u32[]{:S(2)}, u32[]{:S(2)}) %collective-permute-start.4) | collective-permute-done | bytes 557088 | tf_op jit(solution)/shard_map/ppermute | solution.py:909
  73.3 2.0 copy.67
  75.2 1.4 collective-permute-start.10
  78.1 1.5 collective-permute-start.12
  80.6 18.8 %attend_forward.1 = (bf16[512,1024]{1,0:T(8,128)(2,1)S(1)}, bf16[512,1024]{1,0:T(8,128)(2,1)S(1)}, bf16[512,1024]{1,0:T(8,128)(2,1)S(1)}, f32[512,128]{1,0:T(8,1...) custom-call(s32[4]{0:T(128)S(1)} %pad_add_fusion.place_ref, bf16[512,1024]{1,0:T(8,128)(2,1)S(1)} %copy-done.3, ...), custom_call_target="tpu_custom_call" | custom-call | flops 24999999488 | bytes 12582912 | tf_op jit(solution)/shard_map/attend_forward/pallas_call | solution.py:230
  102.3 1.5 slice.206
  105.5 1.4 collective-permute-start.20
  106.9 3.6 attend_out.1
  113.9 1.5 collective-permute-start.18
  115.4 3.3 collective-permute-done.19.rest_4_
  118.7 1.7 collective-permute-done.20.rest_5_
  120.4 21.2 %collective-permute-done.17.rest_1_ = bf16[512,1024]{1,0:T(8,128)(2,1)S(1)} collective-permute-done((bf16[512,1024]{1,0:T(8,128)(2,1)}, bf16[512,1024]{1,0:T(8,128)(2,1)S(1)}, u32[]{:S(2)}, u32[]{:S(2)}) %collective-permute-start.17) | collective-permute-done | bytes 1048608 | tf_op jit(solution)/shard_map/ppermute | solution.py:909
  143.0 1.9 slice.273
  145.9 1.4 collective-permute-start.27
  150.1 24.4 %gather_rows.2 = (bf16[4,2560,1024]{2,1,0:T(8,128)(2,1)}, f32[4,2560,128]{2,1,0:T(8,128)}) custom-call(s32[68]{0:T(128)} %reshape.129.offs_ref, f32[64,256]{1,0:T(8,128)} %copy-done.39, f32[64,256]{1,0:T(8,128)} %copy-done.44, bf16[512,1024]{1,0:T(8,128)(2,1)} %rest_1_.3, bf16[512,1024]{1,0:T(8,128)(2,1)} %collective-permute-done.1.rest_2_, ...), custom_call_target="tpu_custom_call" | custom-call | flops 1 | bytes 1 | tf_op jit(solution)/shard_map/gather_rows/pallas_call | solution.py:527
  174.6 3.1 collective-permute-start.31
  177.7 1.5 collective-permute-done.31.rest_8_
  180.9 12.1 %gather_rows.3.n2_ref = bf16[4,2560,1024]{2,1,0:T(8,128)(2,1)} custom-call(s32[68]{0:T(128)} %reshape.129.offs_ref, f32[64,256]{1,0:T(8,128)} %copy-done.39, bf16[512,1024]{1,0:T(8,128)(2,1)} %get-tuple-element.139.rest_0_, bf16[512,1024]{1,0:T(8,128)(2,1)} %copy-done.38, bf16[512,1024]{1,0:T(8,128)(2,1)} %collective-permute-done.18.rest_2_, ...), custom_call_target="tpu_custom_call" | custom-call | flops 1 | bytes 1 | tf_op jit(solution)/shard_map/gather_rows/pallas_call | solution.py:527
  193.1 46.4 %experts.3 = (bf16[2,3072,1024]{2,1,0:T(8,128)(2,1)}, bf16[2,3072,1024]{2,1,0:T(8,128)(2,1)}, bf16[4,2,2,192,1024]{4,3,2,1,0:T(8,128)(2,1)}) custom-call(s32[4]{0:T(128)} %copy-done.24, s32[68]{0:T(128)} %reshape.129.offs_ref, bf16[4,2560,1024]{2,1,0:T(8,128)(2,1)} %gather_rows.3.n2_ref, bf16[4,2560,1024]{2,1,0:T(8,128)(2,1)} %get-tuple-element.146.dm_ref, ...), custom_call_target="tpu_custom_call" | custom-call | flops 1 | bytes 1 | tf_op jit(solution)/shard_map/experts/pallas_call | solution.py:670
  239.5 26.5 %experts.4 = (bf16[1,3072,1024]{2,1,0:T(8,128)(2,1)}, bf16[1,3072,1024]{2,1,0:T(8,128)(2,1)}, bf16[4,2,2,192,1024]{4,3,2,1,0:T(8,128)(2,1)}) custom-call(s32[4]{0:T(128)} %copy-done.24, s32[68]{0:T(128)} %reshape.129.offs_ref, bf16[4,2560,1024]{2,1,0:T(8,128)(2,1)} %gather_rows.3.n2_ref, bf16[4,2560,1024]{2,1,0:T(8,128)(2,1)} %get-tuple-element.146.dm_ref, ...), custom_call_target="tpu_custom_call" | custom-call | flops 1 | bytes 1 | tf_op jit(solution)/shard_map/experts/pallas_call | solution.py:670
  266.1 23.4 %experts.5 = (bf16[1,3072,1024]{2,1,0:T(8,128)(2,1)}, bf16[1,3072,1024]{2,1,0:T(8,128)(2,1)}, bf16[4,2,2,192,1024]{4,3,2,1,0:T(8,128)(2,1)}) custom-call(s32[4]{0:T(128)} %copy-done.24, s32[68]{0:T(128)} %reshape.129.offs_ref, bf16[4,2560,1024]{2,1,0:T(8,128)(2,1)} %gather_rows.3.n2_ref, ...), custom_call_target="tpu_custom_call", output_to_operand_aliasing={{2}: (6, {})} | custom-call | flops 1 | bytes 1 | tf_op jit(solution)/shard_map/experts/pallas_call | solution.py:670
  289.5 12.1 %scatter_rows.4 = bf16[2048,1024]{1,0:T(8,128)(2,1)} custom-call(s32[68]{0:T(128)} %reshape.129.offs_ref, f32[4096,4]{1,0:T(8,128)} %bitcast.76, bf16[2,3072,1024]{2,1,0:T(8,128)(2,1)} %get-tuple-element.148.rest_0_, bf16[1,3072,1024]{2,1,0:T(8,128)(2,1)} %get-tuple-element.149.rest_1_, bf16[1,3072,1024]{2,1,0:T(8,128)(2,1)} %get-tuple-element.151.rest_2_), custom_call_target="tpu_custom_call" | custom-call | flops 1 | bytes 1 | tf_op jit(solution)/shard_map/scatter_rows/pallas_call | solution.py:767
  301.8 12.0 %scatter_rows.3 = bf16[2048,1024]{1,0:T(8,128)(2,1)} custom-call(s32[68]{0:T(128)} %reshape.129.offs_ref, f32[4096,4]{1,0:T(8,128)} %bitcast.77, bf16[2,3072,1024]{2,1,0:T(8,128)(2,1)} %get-tuple-element.148.rest_0_, bf16[1,3072,1024]{2,1,0:T(8,128)(2,1)} %get-tuple-element.149.rest_1_, bf16[1,3072,1024]{2,1,0:T(8,128)(2,1)} %get-tuple-element.151.rest_2_), custom_call_target="tpu_custom_call" | custom-call | flops 1 | bytes 1 | tf_op jit(solution)/shard_map/scatter_rows/pallas_call | solution.py:767
  313.8 4.4 add_convert_fusion.5
  318.4 1.3 copy-done.1
  321.5 2.0 collective-permute-start.34
  323.5 9.5 %collective-permute-done.35 = bf16[256,1024]{1,0:T(8,128)(2,1)S(1)} collective-permute-done((bf16[256,1024]{1,0:T(8,128)(2,1)S(1)}, bf16[256,1024]{1,0:T(8,128)(2,1)S(1)}, u32[]{:S(2)}, u32[]{:S(2)}) %collective-permute-start.35) | collective-permute-done | bytes 524320 | tf_op jit(solution)/shard_map/ppermute | solution.py:909
  333.4 2.1 collective-permute-start.38
  335.7 19.3 %scatter_rows.5 = (bf16[2048,1024]{1,0:T(8,128)(2,1)}, bf16[2048,1024]{1,0:T(8,128)(2,1)}) custom-call(s32[68]{0:T(128)} %reshape.129.offs_ref, f32[4096,4]{1,0:T(8,128)} %bitcast.78, bf16[2,3072,1024]{2,1,0:T(8,128)(2,1)} %get-tuple-element.155.rest_0_, bf16[1,3072,1024]{2,1,0:T(8,128)(2,1)} %get-tuple-element.156.rest_1_, ...), custom_call_target="tpu_custom_call" | custom-call | flops 1 | bytes 1 | tf_op jit(solution)/shard_map/scatter_rows/pallas_call | solution.py:767
  355.1 3.6 fusion.23
  359.3 1.5 convert_add_fusion.6
  360.8 1.4 convert_add_fusion.7
  362.2 2.7 multiply_reduce_fusion
  364.9 4.2 fusion.22
  369.2 1.6 add_convert_fusion
  372.0 1.5 collective-permute-start.44
  374.4 2.0 collective-permute-start.45
  377.6 32.8 %attend_backward.1 = (f32[512,1024]{1,0:T(8,128)}, bf16[4,4,400,256]{3,2,1,0:T(8,128)(2,1)}, bf16[4,400,256]{2,1,0:T(8,128)(2,1)}, bf16[4,400,256]{2,1,0:T(8,128...) custom-call(s32[4]{0:T(128)} %copy-done.24, bf16[512,1024]{1,0:T(8,128)(2,1)} %tokens_ref.2, ...), custom_call_target="tpu_custom_call" | custom-call | flops 1 | bytes 1 | tf_op jit(solution)/shard_map/attend_backward/pallas_call | solution.py:409
  411.6 2.2 add_convert_fusion.6
  415.4 1.5 collective-permute-start.54
  416.9 2.2 fusion.1
  420.3 1.5 collective-permute-start.49
  424.7 4.2 collective-permute-done.55
  428.9 1.4 convert_add_fusion.4
  431.7 3.5 maximum_add_fusion.1
  435.2 10.0 %adam_experts.2 = (f32[1,8,128,1024]{3,2,1,0:T(8,128)}, f32[1,8,128,1024]{3,2,1,0:T(8,128)}, f32[1,8,128,1024]{3,2,1,0:T(8,128)}, f32[1,8,64,1024]{3,2,1,0:T(8,1...) custom-call(s32[4]{0:T(128)} %copy-done.24, bf16[2,2,192,1024]{3,2,1,0:T(8,128)(2,1)} %bitcast.81, ...), custom_call_target="tpu_custom_call" | custom-call | flops 1 | bytes 1 | tf_op jit(solution)/shard_map/adam_experts/pallas_call | solution.py:808
  445.5 1.4 collective-permute-done.51
  448.0 1.4 collective-permute-start.58
  450.6 1.7 collective-permute-start.57
  452.3 6.1 %collective-permute-done.58 = bf16[2,400,256]{2,1,0:T(8,128)(2,1)S(1)} collective-permute-done((bf16[2,400,256]{2,1,0:T(8,128)(2,1)S(1)}, bf16[2,400,256]{2,1,0:T(8,128)(2,1)S(1)}, u32[]{:S(2)}, u32[]{:S(2)}) %collective-permute-start.58) | collective-permute-done | bytes 409632 | tf_op jit(solution)/shard_map/ppermute | solution.py:909
  459.5 3.0 collective-permute-done.57
  463.6 1.5 fusion.21
  465.9 15.2 %reduce-scatter.5.cloned.1.call-done = bf16[1,2,2,192,1024]{4,3,2,1,0:T(8,128)(2,1)} async-done(((bf16[4,2,2,192,1024]{4,3,2,1,0:T(8,128)(2,1)}), bf16[1,2,2,192,1024]{4,3,2,1,0:T(8,128)(2,1)}) %reduce-scatter.5.cloned.1.call-update) | async-done | bytes 1572880 | tf_op jit(solution)/shard_map/reduce_scatter | solution.py:1029
  483.9 2.0 collective-permute-start.61
  487.0 9.9 %adam_experts.3 = (f32[1,8,128,1024]{3,2,1,0:T(8,128)}, f32[1,8,128,1024]{3,2,1,0:T(8,128)}, f32[1,8,128,1024]{3,2,1,0:T(8,128)}, f32[1,8,64,1024]{3,2,1,0:T(8,1...) custom-call(s32[4]{0:T(128)} %copy-done.24, ...), custom_call_target="tpu_custom_call", output_to_operand_aliasing={{0}: (9, {}), {1}: (10, {}), {2}: (11, {}), {3}: (12, {}), ... | custom-call | flops 1 | bytes 1 | tf_op jit(solution)/shard_map/adam_experts/pallas_call | solution.py:808
  496.9 7.4 %collective-permute-done.61.rest_2_ = bf16[400,256]{1,0:T(8,128)(2,1)S(1)} collective-permute-done((bf16[400,256]{1,0:T(8,128)(2,1)S(1)}, bf16[400,256]{1,0:T(8,128)(2,1)S(1)}, u32[]{:S(2)}, u32[]{:S(2)}) %collective-permute-start.61) | collective-permute-done | bytes 204832 | tf_op jit(solution)/shard_map/ppermute | solution.py:906
  504.4 2.0 adam_rest.1
  (277 shorter events, 48.8 us)
Async XLA Ops:
  7.2 185.9 %all-gather.6.cloned.1.call-start = ((), (), s32[]{:S(2)}) async-start(), calls=%async_computation.4 | async-start | bytes 21233664 | tf_op jit(solution)/shard_map/all_gather | solution.py:961
  12.2 253.8 %all-gather.8.cloned.1.call-start = ((), (), s32[]{:S(2)}) async-start(), calls=%async_computation.5 | async-start | bytes 7077888 | tf_op jit(solution)/shard_map/all_gather | solution.py:961
  13.4 410.1 %reduce-scatter.3.cloned.1.call-start = ((), (), s32[]{:S(2)}) async-start(), calls=%async_computation.2 | async-start | bytes 7864320 | tf_op jit(solution)/shard_map/reduce_scatter | solution.py:1029
  13.4 32.7 %collective-permute-start.1 = (bf16[512,1024]{1,0:T(8,128)(2,1)}, bf16[512,1024]{1,0:T(8,128)(2,1)}, u32[]{:S(2)}, u32[]{:S(2)}) collective-permute-start(bf16[512,1024]{1,0:T(8,128)(2,1)} %rest_1_.3), channel_id=1, source_target_pairs={{0,1},{1,0},{2,3},{3,2},{4,5},{5,4},{6,7},{7,6},{8,9},{9,8},{10,11... | collective-permute-start | bytes 3145736 | tf_op jit(solution)/shard_map/ppermute | solution.py:909
  15.0 31.2 %collective-permute-start.2 = (bf16[512,1024]{1,0:T(8,128)(2,1)}, bf16[512,1024]{1,0:T(8,128)(2,1)}, u32[]{:S(2)}, u32[]{:S(2)}) collective-permute-start(bf16[512,1024]{1,0:T(8,128)(2,1)} %rest_1_.3), channel_id=1, source_target_pairs={{0,2},{1,3},{2,0},{3,1},{4,6},{5,7},{6,4},{7,5},{8,10},{9,11},{10,... | collective-permute-start | bytes 3145736 | tf_op jit(solution)/shard_map/ppermute | solution.py:909
  17.6 32.2 %collective-permute-start = (f32[4,2048]{1,0:T(4,128)S(1)}, f32[4,2048]{1,0:T(4,128)S(1)}, u32[]{:S(2)}, u32[]{:S(2)}) collective-permute-start(f32[4,2048]{1,0:T(4,128)S(1)} %get-tuple-element.263), channel_id=1, source_target_pairs={{0,4},{4,0},{8,12},{12,8},{16,20},{20,16},{24,28},{28,24},{1,5},{5... | collective-permute-start | bytes 98312 | tf_op jit(solution)/shard_map/ppermute | solution.py:903
  46.1 15.7 %collective-permute-start.3 = (bf16[4,272,256]{2,1,0:T(8,128)(2,1)S(1)}, bf16[4,272,256]{2,1,0:T(8,128)(2,1)}, u32[]{:S(2)}, u32[]{:S(2)}) collective-permute-start(bf16[4,272,256]{2,1,0:T(8,128)(2,1)S(1)} %slice.270.rest_0_), channel_id=1, source_target_pairs={{0,1},{1,0},{2,3},{3,2},{4,5},{5,4},{6,7},{7,6},{8,9},{9,8},{10,11... | collective-permute-start | bytes 1671176 | tf_op jit(solution)/shard_map/ppermute | solution.py:909
  46.4 25.5 %collective-permute-start.4 = (bf16[4,272,256]{2,1,0:T(8,128)(2,1)S(1)}, bf16[4,272,256]{2,1,0:T(8,128)(2,1)}, u32[]{:S(2)}, u32[]{:S(2)}) collective-permute-start(bf16[4,272,256]{2,1,0:T(8,128)(2,1)S(1)} %slice.270.rest_0_), channel_id=1, source_target_pairs={{0,2},{1,3},{2,0},{3,1},{4,6},{5,7},{6,4},{7,5},{8,10},{9,11},{10,... | collective-permute-start | bytes 1671176 | tf_op jit(solution)/shard_map/ppermute | solution.py:909
  47.2 24.8 %collective-permute-start.5 = (bf16[4,272,256]{2,1,0:T(8,128)(2,1)S(1)}, bf16[4,272,256]{2,1,0:T(8,128)(2,1)}, u32[]{:S(2)}, u32[]{:S(2)}) collective-permute-start(bf16[4,272,256]{2,1,0:T(8,128)(2,1)S(1)} %slice.270.rest_0_), channel_id=1, source_target_pairs={{0,3},{1,2},{2,1},{3,0},{4,7},{5,6},{6,5},{7,4},{8,11},{9,10},{10,... | collective-permute-start | bytes 1671176 | tf_op jit(solution)/shard_map/ppermute | solution.py:909
  50.6 26.0 %collective-permute-start.6 = (bf16[4,272,256]{2,1,0:T(8,128)(2,1)S(1)}, bf16[4,272,256]{2,1,0:T(8,128)(2,1)S(1)}, u32[]{:S(2)}, u32[]{:S(2)}) collective-permute-start(bf16[4,272,256]{2,1,0:T(8,128)(2,1)S(1)} %slice.270.rest_0_), channel_id=1, source_target_pairs={{0,4},{4,0},{8,12},{12,8},{16,20},{20,16},{24,28},{28,24},{1,5},{5... | collective-permute-start | bytes 1671176 | tf_op jit(solution)/shard_map/ppermute | solution.py:903
  61.9 16.2 %collective-permute-start.7 = (bf16[4,272,256]{2,1,0:T(8,128)(2,1)}, bf16[4,272,256]{2,1,0:T(8,128)(2,1)}, u32[]{:S(2)}, u32[]{:S(2)}) collective-permute-start(bf16[4,272,256]{2,1,0:T(8,128)(2,1)} %collective-permute-done.3.rest_1_), channel_id=1, source_target_pairs={{0,4},{4,0},{8,12},{12,8},{16,20},{20,16},{24,28},{28,24},{1,5},{5... | collective-permute-start | bytes 1671176 | tf_op jit(solution)/shard_map/ppermute | solution.py:903
  72.0 7.6 %collective-permute-start.8 = (bf16[4,272,256]{2,1,0:T(8,128)(2,1)}, bf16[4,272,256]{2,1,0:T(8,128)(2,1)}, u32[]{:S(2)}, u32[]{:S(2)}) collective-permute-start(bf16[4,272,256]{2,1,0:T(8,128)(2,1)} %collective-permute-done.4.rest_2_), channel_id=1, source_target_pairs={{0,4},{4,0},{8,12},{12,8},{16,20},{20,16},{24,28},{28,24},{1,5},{5... | collective-permute-start | bytes 1671176 | tf_op jit(solution)/shard_map/ppermute | solution.py:903
  72.0 7.6 %collective-permute-start.9 = (bf16[4,272,256]{2,1,0:T(8,128)(2,1)}, bf16[4,272,256]{2,1,0:T(8,128)(2,1)}, u32[]{:S(2)}, u32[]{:S(2)}) collective-permute-start(bf16[4,272,256]{2,1,0:T(8,128)(2,1)} %collective-permute-done.5.rest_3_), channel_id=1, source_target_pairs={{0,4},{4,0},{8,12},{12,8},{16,20},{20,16},{24,28},{28,24},{1,5},{5... | collective-permute-start | bytes 1671176 | tf_op jit(solution)/shard_map/ppermute | solution.py:903
  75.2 25.9 %collective-permute-start.10 = (bf16[4,128,256]{2,1,0:T(8,128)(2,1)S(1)}, bf16[4,128,256]{2,1,0:T(8,128)(2,1)S(1)}, u32[]{:S(2)}, u32[]{:S(2)}) collective-permute-start(bf16[4,128,256]{2,1,0:T(8,128)(2,1)S(1)} %slice.271.rest_0_), channel_id=1, source_target_pairs={{0,1},{1,0},{2,3},{3,2},{4,5},{5,4},{6,7},{7,6},{8,9},{9,8},{10,11... | collective-permute-start | bytes 786440 | tf_op jit(solution)/shard_map/ppermute | solution.py:909
  77.4 23.8 %collective-permute-start.11 = (bf16[4,128,256]{2,1,0:T(8,128)(2,1)S(1)}, bf16[4,128,256]{2,1,0:T(8,128)(2,1)S(1)}, u32[]{:S(2)}, u32[]{:S(2)}) collective-permute-start(bf16[4,128,256]{2,1,0:T(8,128)(2,1)S(1)} %slice.271.rest_0_), channel_id=1, source_target_pairs={{0,2},{1,3},{2,0},{3,1},{4,6},{5,7},{6,4},{7,5},{8,10},{9,11},{10,... | collective-permute-start | bytes 786440 | tf_op jit(solution)/shard_map/ppermute | solution.py:909
  78.1 23.2 %collective-permute-start.12 = (bf16[4,128,256]{2,1,0:T(8,128)(2,1)S(1)}, bf16[4,128,256]{2,1,0:T(8,128)(2,1)S(1)}, u32[]{:S(2)}, u32[]{:S(2)}) collective-permute-start(bf16[4,128,256]{2,1,0:T(8,128)(2,1)S(1)} %slice.271.rest_0_), channel_id=1, source_target_pairs={{0,3},{1,2},{2,1},{3,0},{4,7},{5,6},{6,5},{7,4},{8,11},{9,10},{10,... | collective-permute-start | bytes 786440 | tf_op jit(solution)/shard_map/ppermute | solution.py:909
  101.3 5.6 %collective-permute-start.14 = (bf16[4,128,256]{2,1,0:T(8,128)(2,1)S(1)}, bf16[4,128,256]{2,1,0:T(8,128)(2,1)S(1)}, u32[]{:S(2)}, u32[]{:S(2)}) collective-permute-start(bf16[4,128,256]{2,1,0:T(8,128)(2,1)S(1)} %collective-permute-done.10.rest_1_), channel_id=1, source_target_pairs={{0,4},{4,0},{8,12},{12,8},{16,20},{20,16},{24,28},{28,24},{1,5},{5... | collective-permute-start | bytes 786440 | tf_op jit(solution)/shard_map/ppermute | solution.py:903
  101.8 5.1 collective-permute-start.15
  101.9 5.0 collective-permute-start.16
  103.8 14.9 %collective-permute-start.19 = (bf16[256,1024]{1,0:T(8,128)(2,1)S(1)}, bf16[256,1024]{1,0:T(8,128)(2,1)S(1)}, u32[]{:S(2)}, u32[]{:S(2)}) collective-permute-start(bf16[256,1024]{1,0:T(8,128)(2,1)S(1)} %slice.206), channel_id=1, source_target_pairs={{0,2},{1,3},{2,0},{3,1},{4,6},{5,7},{6,4},{7,5},{8,10},{9,11},{10,... | collective-permute-start | bytes 1572872 | tf_op jit(solution)/shard_map/ppermute | solution.py:909
  105.5 14.9 %collective-permute-start.20 = (bf16[256,1024]{1,0:T(8,128)(2,1)S(1)}, bf16[256,1024]{1,0:T(8,128)(2,1)S(1)}, u32[]{:S(2)}, u32[]{:S(2)}) collective-permute-start(bf16[256,1024]{1,0:T(8,128)(2,1)S(1)} %slice.207), channel_id=1, source_target_pairs={{0,1},{1,0},{2,3},{3,2},{4,5},{5,4},{6,7},{7,6},{8,9},{9,8},{10,11... | collective-permute-start | bytes 1572872 | tf_op jit(solution)/shard_map/ppermute | solution.py:909
  113.2 28.4 %collective-permute-start.17 = (bf16[512,1024]{1,0:T(8,128)(2,1)}, bf16[512,1024]{1,0:T(8,128)(2,1)S(1)}, u32[]{:S(2)}, u32[]{:S(2)}) collective-permute-start(bf16[512,1024]{1,0:T(8,128)(2,1)} %get-tuple-element.139.rest_0_), channel_id=1, source_target_pairs={{0,1},{1,0},{2,3},{3,2},{4,5},{5,4},{6,7},{7,6},{8,9},{9,8},{10,11... | collective-permute-start | bytes 3145736 | tf_op jit(solution)/shard_map/ppermute | solution.py:909
  113.9 27.7 %collective-permute-start.18 = (bf16[512,1024]{1,0:T(8,128)(2,1)}, bf16[512,1024]{1,0:T(8,128)(2,1)}, u32[]{:S(2)}, u32[]{:S(2)}) collective-permute-start(bf16[512,1024]{1,0:T(8,128)(2,1)} %get-tuple-element.139.rest_0_), channel_id=1, source_target_pairs={{0,2},{1,3},{2,0},{3,1},{4,6},{5,7},{6,4},{7,5},{8,10},{9,11},{10,... | collective-permute-start | bytes 3145736 | tf_op jit(solution)/shard_map/ppermute | solution.py:909
  115.4 29.5 %collective-permute-start.21 = (bf16[512,1024]{1,0:T(8,128)(2,1)}, bf16[512,1024]{1,0:T(8,128)(2,1)S(1)}, u32[]{:S(2)}, u32[]{:S(2)}) collective-permute-start(bf16[512,1024]{1,0:T(8,128)(2,1)} %rest_1_.3), channel_id=1, source_target_pairs={{0,4},{4,0},{8,12},{12,8},{16,20},{20,16},{24,28},{28,24},{1,5},{5... | collective-permute-start | bytes 3145736 | tf_op jit(solution)/shard_map/ppermute | solution.py:903
  118.7 27.3 %collective-permute-start.22 = (bf16[512,1024]{1,0:T(8,128)(2,1)}, bf16[512,1024]{1,0:T(8,128)(2,1)S(1)}, u32[]{:S(2)}, u32[]{:S(2)}) collective-permute-start(bf16[512,1024]{1,0:T(8,128)(2,1)} %collective-permute-done.1.rest_2_), channel_id=1, source_target_pairs={{0,4},{4,0},{8,12},{12,8},{16,20},{20,16},{24,28},{28,24},{1,5},{5... | collective-permute-start | bytes 3145736 | tf_op jit(solution)/shard_map/ppermute | solution.py:903
  120.4 27.0 %collective-permute-start.23 = (bf16[512,1024]{1,0:T(8,128)(2,1)}, bf16[512,1024]{1,0:T(8,128)(2,1)S(1)}, u32[]{:S(2)}, u32[]{:S(2)}) collective-permute-start(bf16[512,1024]{1,0:T(8,128)(2,1)} %collective-permute-done.2.rest_3_), channel_id=1, source_target_pairs={{0,4},{4,0},{8,12},{12,8},{16,20},{20,16},{24,28},{28,24},{1,5},{5... | collective-permute-start | bytes 3145736 | tf_op jit(solution)/shard_map/ppermute | solution.py:903
  141.6 5.7 %collective-permute-start.24 = (bf16[256,1024]{1,0:T(8,128)(2,1)S(1)}, bf16[256,1024]{1,0:T(8,128)(2,1)S(1)}, u32[]{:S(2)}, u32[]{:S(2)}) collective-permute-start(bf16[256,1024]{1,0:T(8,128)(2,1)S(1)} %collective-permute-done.19.rest_4_), channel_id=1, source_target_pairs={{0,4},{4,0},{8,12},{12,8},{16,20},{20,16},{24,28},{28,24},{1,5},{5... | collective-permute-start | bytes 1572872 | tf_op jit(solution)/shard_map/ppermute | solution.py:903
  141.7 6.8 %collective-permute-start.25 = (bf16[256,1024]{1,0:T(8,128)(2,1)S(1)}, bf16[256,1024]{1,0:T(8,128)(2,1)S(1)}, u32[]{:S(2)}, u32[]{:S(2)}) collective-permute-start(bf16[256,1024]{1,0:T(8,128)(2,1)S(1)} %collective-permute-done.20.rest_5_), channel_id=1, source_target_pairs={{0,4},{4,0},{8,12},{12,8},{16,20},{20,16},{24,28},{28,24},{1,5},{5... | collective-permute-start | bytes 1572872 | tf_op jit(solution)/shard_map/ppermute | solution.py:903
  144.9 29.7 %collective-permute-start.26 = (bf16[256,1024]{1,0:T(8,128)(2,1)}, bf16[256,1024]{1,0:T(8,128)(2,1)S(1)}, u32[]{:S(2)}, u32[]{:S(2)}) collective-permute-start(bf16[256,1024]{1,0:T(8,128)(2,1)} %slice.272), channel_id=1, source_target_pairs={{0,2},{1,3},{2,0},{3,1},{4,6},{5,7},{6,4},{7,5},{8,10},{9,11},{10,... | collective-permute-start | bytes 1572872 | tf_op jit(solution)/shard_map/ppermute | solution.py:909
  145.9 28.6 %collective-permute-start.27 = (bf16[256,1024]{1,0:T(8,128)(2,1)}, bf16[256,1024]{1,0:T(8,128)(2,1)}, u32[]{:S(2)}, u32[]{:S(2)}) collective-permute-start(bf16[256,1024]{1,0:T(8,128)(2,1)} %slice.273), channel_id=1, source_target_pairs={{0,1},{1,0},{2,3},{3,2},{4,5},{5,4},{6,7},{7,6},{8,9},{9,8},{10,11... | collective-permute-start | bytes 1572872 | tf_op jit(solution)/shard_map/ppermute | solution.py:909
  147.4 30.3 %collective-permute-start.28 = (bf16[512,1024]{1,0:T(8,128)(2,1)}, bf16[512,1024]{1,0:T(8,128)(2,1)}, u32[]{:S(2)}, u32[]{:S(2)}) collective-permute-start(bf16[512,1024]{1,0:T(8,128)(2,1)} %get-tuple-element.139.rest_0_), channel_id=1, source_target_pairs={{0,4},{4,0},{8,12},{12,8},{16,20},{20,16},{24,28},{28,24},{1,5},{5... | collective-permute-start | bytes 3145736 | tf_op jit(solution)/shard_map/ppermute | solution.py:903
  147.4 32.7 %collective-permute-start.29 = (bf16[512,1024]{1,0:T(8,128)(2,1)S(1)}, bf16[512,1024]{1,0:T(8,128)(2,1)}, u32[]{:S(2)}, u32[]{:S(2)}) collective-permute-start(bf16[512,1024]{1,0:T(8,128)(2,1)S(1)} %collective-permute-done.17.rest_1_), channel_id=1, source_target_pairs={{0,4},{4,0},{8,12},{12,8},{16,20},{20,16},{24,28},{28,24},{1,5},{5... | collective-permute-start | bytes 3145736 | tf_op jit(solution)/shard_map/ppermute | solution.py:903
  149.3 31.6 %collective-permute-start.30 = (bf16[512,1024]{1,0:T(8,128)(2,1)}, bf16[512,1024]{1,0:T(8,128)(2,1)}, u32[]{:S(2)}, u32[]{:S(2)}) collective-permute-start(bf16[512,1024]{1,0:T(8,128)(2,1)} %collective-permute-done.18.rest_2_), channel_id=1, source_target_pairs={{0,4},{4,0},{8,12},{12,8},{16,20},{20,16},{24,28},{28,24},{1,5},{5... | collective-permute-start | bytes 3145736 | tf_op jit(solution)/shard_map/ppermute | solution.py:903
  174.6 4.6 collective-permute-start.31
  239.5 241.6 %reduce-scatter.5.cloned.1.call-start = ((), (), s32[]{:S(2)}) async-start(), calls=%async_computation.3 | async-start | bytes 7864320 | tf_op jit(solution)/shard_map/reduce_scatter | solution.py:1029
  301.7 12.1 %collective-permute-start.33 = (bf16[2048,1024]{1,0:T(8,128)(2,1)}, bf16[2048,1024]{1,0:T(8,128)(2,1)}, u32[]{:S(2)}, u32[]{:S(2)}) collective-permute-start(bf16[2048,1024]{1,0:T(8,128)(2,1)} %scatter_rows.4), channel_id=1, source_target_pairs={{0,4},{4,0},{8,12},{12,8},{16,20},{20,16},{24,28},{28,24},{1,5},{5... | collective-permute-start | bytes 12582920 | tf_op jit(solution)/shard_map/ppermute | solution.py:903
  318.2 14.8 %collective-permute-start.35 = (bf16[256,1024]{1,0:T(8,128)(2,1)S(1)}, bf16[256,1024]{1,0:T(8,128)(2,1)S(1)}, u32[]{:S(2)}, u32[]{:S(2)}) collective-permute-start(bf16[256,1024]{1,0:T(8,128)(2,1)S(1)} %get-tuple-element.252), channel_id=1, source_target_pairs={{0,1},{1,0},{2,3},{3,2},{4,5},{5,4},{6,7},{7,6},{8,9},{9,8},{10,11... | collective-permute-start | bytes 1572872 | tf_op jit(solution)/shard_map/ppermute | solution.py:909
  318.3 14.8 %collective-permute-start.36 = (bf16[256,1024]{1,0:T(8,128)(2,1)S(1)}, bf16[256,1024]{1,0:T(8,128)(2,1)S(1)}, u32[]{:S(2)}, u32[]{:S(2)}) collective-permute-start(bf16[256,1024]{1,0:T(8,128)(2,1)S(1)} %get-tuple-element.251), channel_id=1, source_target_pairs={{0,2},{1,3},{2,0},{3,1},{4,6},{5,7},{6,4},{7,5},{8,10},{9,11},{10,... | collective-permute-start | bytes 1572872 | tf_op jit(solution)/shard_map/ppermute | solution.py:909
  320.8 37.9 %collective-permute-start.39 = (bf16[256,1024]{1,0:T(8,128)(2,1)}, bf16[256,1024]{1,0:T(8,128)(2,1)}, u32[]{:S(2)}, u32[]{:S(2)}) collective-permute-start(bf16[256,1024]{1,0:T(8,128)(2,1)} %slice.295), channel_id=1, source_target_pairs={{0,2},{1,3},{2,0},{3,1},{4,6},{5,7},{6,4},{7,5},{8,10},{9,11},{10,... | collective-permute-start | bytes 1572872 | tf_op jit(solution)/shard_map/ppermute | solution.py:909
  321.5 39.3 %collective-permute-start.34 = (bf16[256,1024]{1,0:T(8,128)(2,1)S(1)}, bf16[256,1024]{1,0:T(8,128)(2,1)}, u32[]{:S(2)}, u32[]{:S(2)}) collective-permute-start(bf16[256,1024]{1,0:T(8,128)(2,1)S(1)} %slice.286), channel_id=1, source_target_pairs={{0,1},{1,0},{2,3},{3,2},{4,5},{5,4},{6,7},{7,6},{8,9},{9,8},{10,11... | collective-permute-start | bytes 1572872 | tf_op jit(solution)/shard_map/ppermute | solution.py:909
  333.4 25.8 %collective-permute-start.38 = (bf16[256,1024]{1,0:T(8,128)(2,1)S(1)}, bf16[256,1024]{1,0:T(8,128)(2,1)}, u32[]{:S(2)}, u32[]{:S(2)}) collective-permute-start(bf16[256,1024]{1,0:T(8,128)(2,1)S(1)} %add_convert_fusion.8), channel_id=1, source_target_pairs={{0,1},{1,0},{2,3},{3,2},{4,5},{5,4},{6,7},{7,6},{8,9},{9,8},{10,11... | collective-permute-start | bytes 1572872 | tf_op jit(solution)/shard_map/ppermute | solution.py:909
  335.6 25.2 %collective-permute-start.37 = (bf16[256,1024]{1,0:T(8,128)(2,1)S(1)}, bf16[256,1024]{1,0:T(8,128)(2,1)}, u32[]{:S(2)}, u32[]{:S(2)}) collective-permute-start(bf16[256,1024]{1,0:T(8,128)(2,1)S(1)} %add_convert_fusion.9), channel_id=1, source_target_pairs={{0,2},{1,3},{2,0},{3,1},{4,6},{5,7},{6,4},{7,5},{8,10},{9,11},{10,... | collective-permute-start | bytes 1572872 | tf_op jit(solution)/shard_map/ppermute | solution.py:909
  358.7 10.5 %collective-permute-start.42 = (bf16[512,1024]{1,0:T(8,128)(2,1)S(1)}, bf16[512,1024]{1,0:T(8,128)(2,1)S(1)}, u32[]{:S(2)}, u32[]{:S(2)}) collective-permute-start(bf16[512,1024]{1,0:T(8,128)(2,1)S(1)} %get-tuple-element.236), channel_id=1, source_target_pairs={{0,4},{4,0},{8,12},{12,8},{16,20},{20,16},{24,28},{28,24},{1,5},{5... | collective-permute-start | bytes 3145736 | tf_op jit(solution)/shard_map/ppermute | solution.py:903
  358.7 10.5 %collective-permute-start.41 = (bf16[512,1024]{1,0:T(8,128)(2,1)S(1)}, bf16[512,1024]{1,0:T(8,128)(2,1)S(1)}, u32[]{:S(2)}, u32[]{:S(2)}) collective-permute-start(bf16[512,1024]{1,0:T(8,128)(2,1)S(1)} %get-tuple-element.237), channel_id=1, source_target_pairs={{0,4},{4,0},{8,12},{12,8},{16,20},{20,16},{24,28},{28,24},{1,5},{5... | collective-permute-start | bytes 3145736 | tf_op jit(solution)/shard_map/ppermute | solution.py:903
  359.2 10.0 %collective-permute-start.40 = (bf16[512,1024]{1,0:T(8,128)(2,1)S(1)}, bf16[512,1024]{1,0:T(8,128)(2,1)S(1)}, u32[]{:S(2)}, u32[]{:S(2)}) collective-permute-start(bf16[512,1024]{1,0:T(8,128)(2,1)S(1)} %get-tuple-element.238), channel_id=1, source_target_pairs={{0,4},{4,0},{8,12},{12,8},{16,20},{20,16},{24,28},{28,24},{1,5},{5... | collective-permute-start | bytes 3145736 | tf_op jit(solution)/shard_map/ppermute | solution.py:903
  371.9 38.5 %collective-permute-start.43 = (bf16[256,1024]{1,0:T(8,128)(2,1)}, bf16[256,1024]{1,0:T(8,128)(2,1)S(1)}, u32[]{:S(2)}, u32[]{:S(2)}) collective-permute-start(bf16[256,1024]{1,0:T(8,128)(2,1)} %get-tuple-element.250), channel_id=1, source_target_pairs={{0,1},{1,0},{2,3},{3,2},{4,5},{5,4},{6,7},{7,6},{8,9},{9,8},{10,11... | collective-permute-start | bytes 1572872 | tf_op jit(solution)/shard_map/ppermute | solution.py:909
  372.0 38.4 %collective-permute-start.44 = (bf16[256,1024]{1,0:T(8,128)(2,1)}, bf16[256,1024]{1,0:T(8,128)(2,1)}, u32[]{:S(2)}, u32[]{:S(2)}) collective-permute-start(bf16[256,1024]{1,0:T(8,128)(2,1)} %get-tuple-element.249), channel_id=1, source_target_pairs={{0,2},{1,3},{2,0},{3,1},{4,6},{5,7},{6,4},{7,5},{8,10},{9,11},{10,... | collective-permute-start | bytes 1572872 | tf_op jit(solution)/shard_map/ppermute | solution.py:909
  374.4 36.1 %collective-permute-start.45 = (bf16[256,1024]{1,0:T(8,128)(2,1)}, bf16[256,1024]{1,0:T(8,128)(2,1)}, u32[]{:S(2)}, u32[]{:S(2)}) collective-permute-start(bf16[256,1024]{1,0:T(8,128)(2,1)} %slice.242), channel_id=1, source_target_pairs={{0,1},{1,0},{2,3},{3,2},{4,5},{5,4},{6,7},{7,6},{8,9},{9,8},{10,11... | collective-permute-start | bytes 1572872 | tf_op jit(solution)/shard_map/ppermute | solution.py:909
  377.3 33.2 %collective-permute-start.46 = (bf16[256,1024]{1,0:T(8,128)(2,1)}, bf16[256,1024]{1,0:T(8,128)(2,1)}, u32[]{:S(2)}, u32[]{:S(2)}) collective-permute-start(bf16[256,1024]{1,0:T(8,128)(2,1)} %slice.243), channel_id=1, source_target_pairs={{0,2},{1,3},{2,0},{3,1},{4,6},{5,7},{6,4},{7,5},{8,10},{9,11},{10,... | collective-permute-start | bytes 1572872 | tf_op jit(solution)/shard_map/ppermute | solution.py:909
  410.5 4.9 collective-permute-start.50
  410.6 6.3 %collective-permute-start.48 = (bf16[4,400,256]{2,1,0:T(8,128)(2,1)}, bf16[4,400,256]{2,1,0:T(8,128)(2,1)S(1)}, u32[]{:S(2)}, u32[]{:S(2)}) collective-permute-start(bf16[4,400,256]{2,1,0:T(8,128)(2,1)} %get-tuple-element.170), channel_id=1, source_target_pairs={{0,4},{4,0},{8,12},{12,8},{16,20},{20,16},{24,28},{28,24},{1,5},{5... | collective-permute-start | bytes 2457608 | tf_op jit(solution)/shard_map/ppermute | solution.py:903
  411.1 5.9 %collective-permute-start.47 = (bf16[4,400,256]{2,1,0:T(8,128)(2,1)}, bf16[4,400,256]{2,1,0:T(8,128)(2,1)S(1)}, u32[]{:S(2)}, u32[]{:S(2)}) collective-permute-start(bf16[4,400,256]{2,1,0:T(8,128)(2,1)} %get-tuple-element.169), channel_id=1, source_target_pairs={{0,4},{4,0},{8,12},{12,8},{16,20},{20,16},{24,28},{28,24},{1,5},{5... | collective-permute-start | bytes 2457608 | tf_op jit(solution)/shard_map/ppermute | solution.py:903
  411.1 20.5 %collective-permute-start.53 = (bf16[512,1024]{1,0:T(8,128)(2,1)}, bf16[512,1024]{1,0:T(8,128)(2,1)}, u32[]{:S(2)}, u32[]{:S(2)}) collective-permute-start(bf16[512,1024]{1,0:T(8,128)(2,1)} %get-tuple-element.235), channel_id=1, source_target_pairs={{0,4},{4,0},{8,12},{12,8},{16,20},{20,16},{24,28},{28,24},{1,5},{5... | collective-permute-start | bytes 3145736 | tf_op jit(solution)/shard_map/ppermute | solution.py:903
  413.8 15.1 %collective-permute-start.55 = (bf16[256,1024]{1,0:T(8,128)(2,1)}, bf16[256,1024]{1,0:T(8,128)(2,1)}, u32[]{:S(2)}, u32[]{:S(2)}) collective-permute-start(bf16[256,1024]{1,0:T(8,128)(2,1)} %add_convert_fusion.6), channel_id=1, source_target_pairs={{0,1},{1,0},{2,3},{3,2},{4,5},{5,4},{6,7},{7,6},{8,9},{9,8},{10,11... | collective-permute-start | bytes 1572872 | tf_op jit(solution)/shard_map/ppermute | solution.py:909
  415.4 15.0 %collective-permute-start.54 = (bf16[256,1024]{1,0:T(8,128)(2,1)}, bf16[256,1024]{1,0:T(8,128)(2,1)S(1)}, u32[]{:S(2)}, u32[]{:S(2)}) collective-permute-start(bf16[256,1024]{1,0:T(8,128)(2,1)} %add_convert_fusion.7), channel_id=1, source_target_pairs={{0,2},{1,3},{2,0},{3,1},{4,6},{5,7},{6,4},{7,5},{8,10},{9,11},{10,... | collective-permute-start | bytes 1572872 | tf_op jit(solution)/shard_map/ppermute | solution.py:909
  420.3 25.2 %collective-permute-start.49 = (bf16[4,400,256]{2,1,0:T(8,128)(2,1)}, bf16[4,400,256]{2,1,0:T(8,128)(2,1)}, u32[]{:S(2)}, u32[]{:S(2)}) collective-permute-start(bf16[4,400,256]{2,1,0:T(8,128)(2,1)} %pad_maximum_fusion), channel_id=1, source_target_pairs={{0,1},{1,0},{2,3},{3,2},{4,5},{5,4},{6,7},{7,6},{8,9},{9,8},{10,11... | collective-permute-start | bytes 2457608 | tf_op jit(solution)/shard_map/ppermute | solution.py:909
  422.8 24.1 %collective-permute-start.51 = (bf16[4,400,256]{2,1,0:T(8,128)(2,1)}, bf16[4,400,256]{2,1,0:T(8,128)(2,1)}, u32[]{:S(2)}, u32[]{:S(2)}) collective-permute-start(bf16[4,400,256]{2,1,0:T(8,128)(2,1)} %pad_maximum_fusion.1), channel_id=1, source_target_pairs={{0,2},{1,3},{2,0},{3,1},{4,6},{5,7},{6,4},{7,5},{8,10},{9,11},{10,... | collective-permute-start | bytes 2457608 | tf_op jit(solution)/shard_map/ppermute | solution.py:909
  428.9 6.3 %collective-permute-start.52 = (bf16[2,192,1024]{2,1,0:T(8,128)(2,1)S(1)}, bf16[2,192,1024]{2,1,0:T(8,128)(2,1)}, u32[]{:S(2)}, u32[]{:S(2)}) collective-permute-start(bf16[2,192,1024]{2,1,0:T(8,128)(2,1)S(1)} %slice_bitcast_fusion.3), channel_id=1, source_target_pairs={{0,4},{4,0},{8,12},{12,8},{16,20},{20,16},{24,28},{28,24},{1,5},{5... | collective-permute-start | bytes 2359304 | tf_op jit(solution)/shard_map/ppermute | solution.py:903
  448.0 10.4 %collective-permute-start.58 = (bf16[2,400,256]{2,1,0:T(8,128)(2,1)S(1)}, bf16[2,400,256]{2,1,0:T(8,128)(2,1)S(1)}, u32[]{:S(2)}, u32[]{:S(2)}) collective-permute-start(bf16[2,400,256]{2,1,0:T(8,128)(2,1)S(1)} %add_convert_fusion.10), channel_id=1, source_target_pairs={{0,1},{1,0},{2,3},{3,2},{4,5},{5,4},{6,7},{7,6},{8,9},{9,8},{10,11... | collective-permute-start | bytes 1228808 | tf_op jit(solution)/shard_map/ppermute | solution.py:909
  449.5 14.2 %collective-permute-start.56 = (bf16[4,400,256]{2,1,0:T(8,128)(2,1)S(1)}, bf16[4,400,256]{2,1,0:T(8,128)(2,1)S(1)}, u32[]{:S(2)}, u32[]{:S(2)}) collective-permute-start(bf16[4,400,256]{2,1,0:T(8,128)(2,1)S(1)} %copy-done.52), channel_id=1, source_target_pairs={{0,4},{4,0},{8,12},{12,8},{16,20},{20,16},{24,28},{28,24},{1,5},{5... | collective-permute-start | bytes 2457608 | tf_op jit(solution)/shard_map/ppermute | solution.py:903
  450.6 11.9 %collective-permute-start.57 = (bf16[2,400,256]{2,1,0:T(8,128)(2,1)S(1)}, bf16[2,400,256]{2,1,0:T(8,128)(2,1)S(1)}, u32[]{:S(2)}, u32[]{:S(2)}) collective-permute-start(bf16[2,400,256]{2,1,0:T(8,128)(2,1)S(1)} %add_convert_fusion.11), channel_id=1, source_target_pairs={{0,2},{1,3},{2,0},{3,1},{4,6},{5,7},{6,4},{7,5},{8,10},{9,11},{10,... | collective-permute-start | bytes 1228808 | tf_op jit(solution)/shard_map/ppermute | solution.py:909
  482.4 14.5 %collective-permute-start.59 = (bf16[400,256]{1,0:T(8,128)(2,1)}, bf16[400,256]{1,0:T(8,128)(2,1)S(1)}, u32[]{:S(2)}, u32[]{:S(2)}) collective-permute-start(bf16[400,256]{1,0:T(8,128)(2,1)} %get-tuple-element.259), channel_id=1, source_target_pairs={{0,8},{4,12},{8,0},{12,4},{16,24},{20,28},{24,16},{28,20},{1,9},{5... | collective-permute-start | bytes 614408 | tf_op jit(solution)/shard_map/ppermute | solution.py:906
  482.6 14.3 %collective-permute-start.60 = (bf16[400,256]{1,0:T(8,128)(2,1)S(1)}, bf16[400,256]{1,0:T(8,128)(2,1)S(1)}, u32[]{:S(2)}, u32[]{:S(2)}) collective-permute-start(bf16[400,256]{1,0:T(8,128)(2,1)S(1)} %get-tuple-element.258), channel_id=1, source_target_pairs={{0,16},{4,20},{8,24},{12,28},{16,0},{20,4},{24,8},{28,12},{1,17},{... | collective-permute-start | bytes 614408 | tf_op jit(solution)/shard_map/ppermute | solution.py:906
  483.9 20.4 %collective-permute-start.61 = (bf16[400,256]{1,0:T(8,128)(2,1)S(1)}, bf16[400,256]{1,0:T(8,128)(2,1)S(1)}, u32[]{:S(2)}, u32[]{:S(2)}) collective-permute-start(bf16[400,256]{1,0:T(8,128)(2,1)S(1)} %get-tuple-element.257), channel_id=1, source_target_pairs={{0,24},{4,28},{8,16},{12,20},{16,8},{20,12},{24,0},{28,4},{1,25},{... | collective-permute-start | bytes 614408 | tf_op jit(solution)/shard_map/ppermute | solution.py:906
  (56 other events, 909.3 us)
Sparse Core Ops, SparseCore 0:
  12.3 176.7 all-gather.5
  190.7 63.2 all-gather.7
  256.3 111.2 reduce-scatter.2
  369.8 111.2 reduce-scatter.4

commit v6 on v5

--- a/solution.py
+++ b/solution.py
@@ -1105,7 +1105,7 @@
     total = both[0].astype(f32) + received
     owned = total[0]
     sent = [total[j].astype(bf16) for j in range(1, nz)]
-    received = [swap_z(part, j + 1) for j, part in enumerate(sent)]
+    received = [swap_z(sent[j - 1], j) for j in range(nz - 1, 0, -1)]
     for start, got in expert_grads[-1:]:
         got = after(got, *sent, *experts_new)
         experts_new = adam_experts(place, start, got, swap_core(got[1]), states, experts_new)

time: 523 us -> 524 us (level)
  the two profiles are of different devices: /device:TPU:16 before, /device:TPU:0 now
where the time goes in v6:
time: 524 us; the launch traced here: 514 us
  Pallas kernels  229 us (44%)
  waiting for transfers between devices  110 us (21%)
  starting transfers between devices  55.3 us (11%)
  other arithmetic  42.4 us (8%)
  blocking collectives  32.3 us (6%)
  local copies, waits for them, and re-layouts  30.2 us (6%)
  between operations  15.2 us (3%)
    pallas_call x3, Pallas kernels, experts_step(): pl.pallas_call(functools.partial(experts_kernel, first, subs, sources, le...  72.9 us
    ppermute x30, waiting for transfers between devices, swap_t(): return lax.ppermute(x, 'tensor', [(i, i ^ k) for i in range(nt)])  72.1 us
    pallas_call x3, Pallas kernels, scatter(): pl.pallas_call(functools.partial(scatter_kernel, halves, sources, experts...  41.7 us
    ppermute x30, starting transfers between devices, swap_t(): return lax.ppermute(x, 'tensor', [(i, i ^ k) for i in range(nt)])  38.5 us
    pallas_call x2, Pallas kernels, gather(): pl.pallas_call(functools.partial(gather_kernel, tuple(starts), experts, w...  36.3 us
    pallas_call x1, Pallas kernels, attend_backward(): pl.pallas_call(functools.partial(attend_backward_kernel, nz, nt, whole),...  33.7 us
    all_gather x1, blocking collectives, on_device(): lax.all_gather(own, 'dp', axis=0, tiled=False, axis_index_groups=groups)  32.3 us
    pallas_call x2, Pallas kernels, adam_experts(): pl.pallas_call(functools.partial(adam_kernel, per), grid_spec=pltpu.Prefe...  19.9 us
  transfers between devices with their start and end apart: 67, of which 19 were waited for; matrix products, arithmetic and copies ran while one was open for 11% of the time, Pallas kernels for 44%

profile of v6, /device:TPU:0, one launch (start us, length us, event | category | flops | bytes accessed | tf_op | source)
XLA Modules:
  0.0 514.3 jit_solution(1482901429238965589)
XLA Ops:
  7.2 1.9 convert.53
  10.5 1.7 maximum_maximum_fusion
  13.4 3.0 collective-permute-start.1
  16.4 1.5 collective-permute-start.2
  19.6 32.3 %all-gather = bf16[1600,256]{1,0:T(8,128)(2,1)S(1)} all-gather(bf16[400,256]{1,0:T(8,128)(2,1)S(1)} %pad_maximum_fusion.2), channel_id=2, replica_groups={{0,8,16,24},{4,12,20,28},{1,9,17,25},{5,13,21,29},{2,10,18,26},{6,14,22..., dimensions={0}, use_global_device_ids=true | all-gather | bytes 1024000 | tf_op jit(solution)/shard_map/all_gather | solution.py:958
  52.3 3.4 collective-permute-start.5
  56.7 11.2 %collective-permute-done.3.rest_1_ = bf16[4,272,256]{2,1,0:T(8,128)(2,1)} collective-permute-done((bf16[4,272,256]{2,1,0:T(8,128)(2,1)S(1)}, bf16[4,272,256]{2,1,0:T(8,128)(2,1)}, u32[]{:S(2)}, u32[]{:S(2)}) %collective-permute-start.3) | collective-permute-done | bytes 557088 | tf_op jit(solution)/shard_map/ppermute | solution.py:909
  67.8 8.2 %collective-permute-done.4.rest_2_ = bf16[4,272,256]{2,1,0:T(8,128)(2,1)} collective-permute-done((bf16[4,272,256]{2,1,0:T(8,128)(2,1)S(1)}, bf16[4,272,256]{2,1,0:T(8,128)(2,1)}, u32[]{:S(2)}, u32[]{:S(2)}) %collective-permute-start.4) | collective-permute-done | bytes 557088 | tf_op jit(solution)/shard_map/ppermute | solution.py:909
  77.3 2.0 copy.67
  79.3 1.7 collective-permute-start.10
  82.1 1.5 collective-permute-start.12
  84.7 18.7 %attend_forward.1 = (bf16[512,1024]{1,0:T(8,128)(2,1)S(1)}, bf16[512,1024]{1,0:T(8,128)(2,1)S(1)}, bf16[512,1024]{1,0:T(8,128)(2,1)S(1)}, f32[512,128]{1,0:T(8,1...) custom-call(s32[4]{0:T(128)S(1)} %pad_add_fusion.place_ref, bf16[512,1024]{1,0:T(8,128)(2,1)S(1)} %copy-done.3, ...), custom_call_target="tpu_custom_call" | custom-call | flops 24999999488 | bytes 12582912 | tf_op jit(solution)/shard_map/attend_forward/pallas_call | solution.py:230
  106.2 1.5 slice.206
  110.9 3.6 attend_out.1
  119.3 3.2 collective-permute-done.19.rest_4_
  122.5 2.1 collective-permute-done.20.rest_5_
  124.6 21.3 %collective-permute-done.17.rest_1_ = bf16[512,1024]{1,0:T(8,128)(2,1)S(1)} collective-permute-done((bf16[512,1024]{1,0:T(8,128)(2,1)}, bf16[512,1024]{1,0:T(8,128)(2,1)S(1)}, u32[]{:S(2)}, u32[]{:S(2)}) %collective-permute-start.17) | collective-permute-done | bytes 1048608 | tf_op jit(solution)/shard_map/ppermute | solution.py:909
  147.2 1.9 slice.273
  150.0 1.6 collective-permute-start.27
  154.3 24.3 %gather_rows.2 = (bf16[4,2560,1024]{2,1,0:T(8,128)(2,1)}, f32[4,2560,128]{2,1,0:T(8,128)}) custom-call(s32[68]{0:T(128)} %reshape.129.offs_ref, f32[64,256]{1,0:T(8,128)} %copy-done.39, f32[64,256]{1,0:T(8,128)} %copy-done.44, bf16[512,1024]{1,0:T(8,128)(2,1)} %rest_1_.3, bf16[512,1024]{1,0:T(8,128)(2,1)} %collective-permute-done.1.rest_2_, ...), custom_call_target="tpu_custom_call" | custom-call | flops 1 | bytes 1 | tf_op jit(solution)/shard_map/gather_rows/pallas_call | solution.py:527
  178.6 2.8 collective-permute-start.31
  181.5 1.5 collective-permute-done.31.rest_8_
  184.8 12.0 %gather_rows.3.n2_ref = bf16[4,2560,1024]{2,1,0:T(8,128)(2,1)} custom-call(s32[68]{0:T(128)} %reshape.129.offs_ref, f32[64,256]{1,0:T(8,128)} %copy-done.39, bf16[512,1024]{1,0:T(8,128)(2,1)} %get-tuple-element.139.rest_0_, bf16[512,1024]{1,0:T(8,128)(2,1)} %copy-done.38, bf16[512,1024]{1,0:T(8,128)(2,1)} %collective-permute-done.18.rest_2_, ...), custom_call_target="tpu_custom_call" | custom-call | flops 1 | bytes 1 | tf_op jit(solution)/shard_map/gather_rows/pallas_call | solution.py:527
  196.8 34.8 %experts.3 = (bf16[2,3072,1024]{2,1,0:T(8,128)(2,1)}, bf16[2,3072,1024]{2,1,0:T(8,128)(2,1)}, bf16[4,2,2,192,1024]{4,3,2,1,0:T(8,128)(2,1)}) custom-call(s32[4]{0:T(128)} %copy-done.24, s32[68]{0:T(128)} %reshape.129.offs_ref, bf16[4,2560,1024]{2,1,0:T(8,128)(2,1)} %gather_rows.3.n2_ref, bf16[4,2560,1024]{2,1,0:T(8,128)(2,1)} %get-tuple-element.146.dm_ref, ...), custom_call_target="tpu_custom_call" | custom-call | flops 1 | bytes 1 | tf_op jit(solution)/shard_map/experts/pallas_call | solution.py:670
  231.6 14.7 %experts.4 = (bf16[1,3072,1024]{2,1,0:T(8,128)(2,1)}, bf16[1,3072,1024]{2,1,0:T(8,128)(2,1)}, bf16[4,2,2,192,1024]{4,3,2,1,0:T(8,128)(2,1)}) custom-call(s32[4]{0:T(128)} %copy-done.24, s32[68]{0:T(128)} %reshape.129.offs_ref, bf16[4,2560,1024]{2,1,0:T(8,128)(2,1)} %gather_rows.3.n2_ref, bf16[4,2560,1024]{2,1,0:T(8,128)(2,1)} %get-tuple-element.146.dm_ref, ...), custom_call_target="tpu_custom_call" | custom-call | flops 1 | bytes 1 | tf_op jit(solution)/shard_map/experts/pallas_call | solution.py:670
  246.3 10.7 %all-gather.8.cloned.1.call-done = bf16[16,192,1024]{2,1,0:T(8,128)(2,1)} async-done(((bf16[2,192,1024]{2,1,0:T(8,128)(2,1)}), bf16[16,192,1024]{2,1,0:T(8,128)(2,1)}) %all-gather.8.cloned.1.call-update) | async-done | bytes 6291472 | tf_op jit(solution)/shard_map/all_gather | solution.py:961
  257.0 23.4 %experts.5 = (bf16[1,3072,1024]{2,1,0:T(8,128)(2,1)}, bf16[1,3072,1024]{2,1,0:T(8,128)(2,1)}, bf16[4,2,2,192,1024]{4,3,2,1,0:T(8,128)(2,1)}) custom-call(s32[4]{0:T(128)} %copy-done.24, s32[68]{0:T(128)} %reshape.129.offs_ref, bf16[4,2560,1024]{2,1,0:T(8,128)(2,1)} %gather_rows.3.n2_ref, ...), custom_call_target="tpu_custom_call", output_to_operand_aliasing={{2}: (6, {})} | custom-call | flops 1 | bytes 1 | tf_op jit(solution)/shard_map/experts/pallas_call | solution.py:670
  280.4 11.5 %scatter_rows.4 = bf16[2048,1024]{1,0:T(8,128)(2,1)} custom-call(s32[68]{0:T(128)} %reshape.129.offs_ref, f32[4096,4]{1,0:T(8,128)} %bitcast.76, bf16[2,3072,1024]{2,1,0:T(8,128)(2,1)} %get-tuple-element.148.rest_0_, bf16[1,3072,1024]{2,1,0:T(8,128)(2,1)} %get-tuple-element.149.rest_1_, bf16[1,3072,1024]{2,1,0:T(8,128)(2,1)} %get-tuple-element.151.rest_2_), custom_call_target="tpu_custom_call" | custom-call | flops 1 | bytes 1 | tf_op jit(solution)/shard_map/scatter_rows/pallas_call | solution.py:767
  292.0 4.7 collective-permute-start.33
  296.7 11.3 %scatter_rows.3 = bf16[2048,1024]{1,0:T(8,128)(2,1)} custom-call(s32[68]{0:T(128)} %reshape.129.offs_ref, f32[4096,4]{1,0:T(8,128)} %bitcast.77, bf16[2,3072,1024]{2,1,0:T(8,128)(2,1)} %get-tuple-element.148.rest_0_, bf16[1,3072,1024]{2,1,0:T(8,128)(2,1)} %get-tuple-element.149.rest_1_, bf16[1,3072,1024]{2,1,0:T(8,128)(2,1)} %get-tuple-element.151.rest_2_), custom_call_target="tpu_custom_call" | custom-call | flops 1 | bytes 1 | tf_op jit(solution)/shard_map/scatter_rows/pallas_call | solution.py:767
  308.0 4.3 add_convert_fusion.5
  312.7 5.4 %collective-permute-start.36 = (bf16[256,1024]{1,0:T(8,128)(2,1)S(1)}, bf16[256,1024]{1,0:T(8,128)(2,1)S(1)}, u32[]{:S(2)}, u32[]{:S(2)}) collective-permute-start(bf16[256,1024]{1,0:T(8,128)(2,1)S(1)} %get-tuple-element.251), channel_id=1, source_target_pairs={{0,2},{1,3},{2,0},{3,1},{4,6},{5,7},{6,4},{7,5},{8,10},{9,11},{10,... | collective-permute-start | bytes 1572872 | tf_op jit(solution)/shard_map/ppermute | solution.py:909
  321.2 6.0 %collective-permute-done.35 = bf16[256,1024]{1,0:T(8,128)(2,1)S(1)} collective-permute-done((bf16[256,1024]{1,0:T(8,128)(2,1)S(1)}, bf16[256,1024]{1,0:T(8,128)(2,1)S(1)}, u32[]{:S(2)}, u32[]{:S(2)}) %collective-permute-start.35) | collective-permute-done | bytes 524320 | tf_op jit(solution)/shard_map/ppermute | solution.py:909
  327.3 3.5 collective-permute-done.36
  331.0 2.1 collective-permute-start.38
  333.3 2.0 collective-permute-start.37
  335.3 18.9 %scatter_rows.5 = (bf16[2048,1024]{1,0:T(8,128)(2,1)}, bf16[2048,1024]{1,0:T(8,128)(2,1)}) custom-call(s32[68]{0:T(128)} %reshape.129.offs_ref, f32[4096,4]{1,0:T(8,128)} %bitcast.78, bf16[2,3072,1024]{2,1,0:T(8,128)(2,1)} %get-tuple-element.155.rest_0_, bf16[1,3072,1024]{2,1,0:T(8,128)(2,1)} %get-tuple-element.156.rest_1_, ...), custom_call_target="tpu_custom_call" | custom-call | flops 1 | bytes 1 | tf_op jit(solution)/shard_map/scatter_rows/pallas_call | solution.py:767
  354.2 3.6 fusion.23
  358.4 1.5 convert_add_fusion.6
  359.9 1.4 convert_add_fusion.7
  361.4 2.7 multiply_reduce_fusion
  364.1 4.2 fusion.22
  368.3 1.6 add_convert_fusion
  372.2 1.7 collective-permute-start.45
  374.8 2.0 collective-permute-start.46
  376.8 33.7 %attend_backward.1 = (f32[512,1024]{1,0:T(8,128)}, bf16[4,4,400,256]{3,2,1,0:T(8,128)(2,1)}, bf16[4,400,256]{2,1,0:T(8,128)(2,1)}, bf16[4,400,256]{2,1,0:T(8,128...) custom-call(s32[4]{0:T(128)} %copy-done.24, bf16[512,1024]{1,0:T(8,128)(2,1)} %tokens_ref.2, ...), custom_call_target="tpu_custom_call" | custom-call | flops 1 | bytes 1 | tf_op jit(solution)/shard_map/attend_backward/pallas_call | solution.py:409
  411.7 2.2 add_convert_fusion.6
  415.5 1.5 collective-permute-done.47
  417.0 2.2 fusion.1
  421.9 1.4 collective-permute-start.51
  424.5 4.5 collective-permute-done.55
  429.0 1.4 convert_add_fusion.4
  431.6 3.5 maximum_add_fusion.1
  435.1 10.1 %adam_experts.2 = (f32[1,8,128,1024]{3,2,1,0:T(8,128)}, f32[1,8,128,1024]{3,2,1,0:T(8,128)}, f32[1,8,128,1024]{3,2,1,0:T(8,128)}, f32[1,8,64,1024]{3,2,1,0:T(8,1...) custom-call(s32[4]{0:T(128)} %copy-done.24, bf16[2,2,192,1024]{3,2,1,0:T(8,128)(2,1)} %bitcast.81, ...), custom_call_target="tpu_custom_call" | custom-call | flops 1 | bytes 1 | tf_op jit(solution)/shard_map/adam_experts/pallas_call | solution.py:808
  447.9 1.6 collective-permute-start.58
  451.0 7.3 %collective-permute-done.58 = bf16[2,400,256]{2,1,0:T(8,128)(2,1)S(1)} collective-permute-done((bf16[2,400,256]{2,1,0:T(8,128)(2,1)S(1)}, bf16[2,400,256]{2,1,0:T(8,128)(2,1)S(1)}, u32[]{:S(2)}, u32[]{:S(2)}) %collective-permute-start.58) | collective-permute-done | bytes 409632 | tf_op jit(solution)/shard_map/ppermute | solution.py:909
  459.4 3.2 collective-permute-done.57
  463.7 1.5 fusion.21
  465.9 16.3 %reduce-scatter.5.cloned.1.call-done = bf16[1,2,2,192,1024]{4,3,2,1,0:T(8,128)(2,1)} async-done(((bf16[4,2,2,192,1024]{4,3,2,1,0:T(8,128)(2,1)}), bf16[1,2,2,192,1024]{4,3,2,1,0:T(8,128)(2,1)}) %reduce-scatter.5.cloned.1.call-update) | async-done | bytes 1572880 | tf_op jit(solution)/shard_map/reduce_scatter | solution.py:1029
  483.5 2.7 collective-permute-start.59
  486.6 1.4 collective-permute-start.61
  489.0 9.9 %adam_experts.3 = (f32[1,8,128,1024]{3,2,1,0:T(8,128)}, f32[1,8,128,1024]{3,2,1,0:T(8,128)}, f32[1,8,128,1024]{3,2,1,0:T(8,128)}, f32[1,8,64,1024]{3,2,1,0:T(8,1...) custom-call(s32[4]{0:T(128)} %copy-done.24, ...), custom_call_target="tpu_custom_call", output_to_operand_aliasing={{0}: (9, {}), {1}: (10, {}), {2}: (11, {}), {3}: (12, {}), ... | custom-call | flops 1 | bytes 1 | tf_op jit(solution)/shard_map/adam_experts/pallas_call | solution.py:808
  498.9 6.6 %collective-permute-done.60.rest_1_ = bf16[400,256]{1,0:T(8,128)(2,1)S(1)} collective-permute-done((bf16[400,256]{1,0:T(8,128)(2,1)S(1)}, bf16[400,256]{1,0:T(8,128)(2,1)S(1)}, u32[]{:S(2)}, u32[]{:S(2)}) %collective-permute-start.60) | collective-permute-done | bytes 204832 | tf_op jit(solution)/shard_map/ppermute | solution.py:906
  505.7 2.0 adam_rest.1
  (277 shorter events, 51.5 us)
Async XLA Ops:
  7.2 189.6 %all-gather.6.cloned.1.call-start = ((), (), s32[]{:S(2)}) async-start(), calls=%async_computation.4 | async-start | bytes 21233664 | tf_op jit(solution)/shard_map/all_gather | solution.py:961
  12.2 244.7 %all-gather.8.cloned.1.call-start = ((), (), s32[]{:S(2)}) async-start(), calls=%async_computation.5 | async-start | bytes 7077888 | tf_op jit(solution)/shard_map/all_gather | solution.py:961
  13.4 410.0 %reduce-scatter.3.cloned.1.call-start = ((), (), s32[]{:S(2)}) async-start(), calls=%async_computation.2 | async-start | bytes 7864320 | tf_op jit(solution)/shard_map/reduce_scatter | solution.py:1029
  13.4 38.7 %collective-permute-start.1 = (bf16[512,1024]{1,0:T(8,128)(2,1)}, bf16[512,1024]{1,0:T(8,128)(2,1)}, u32[]{:S(2)}, u32[]{:S(2)}) collective-permute-start(bf16[512,1024]{1,0:T(8,128)(2,1)} %rest_1_.3), channel_id=1, source_target_pairs={{0,1},{1,0},{2,3},{3,2},{4,5},{5,4},{6,7},{7,6},{8,9},{9,8},{10,11... | collective-permute-start | bytes 3145736 | tf_op jit(solution)/shard_map/ppermute | solution.py:909
  16.4 35.7 %collective-permute-start.2 = (bf16[512,1024]{1,0:T(8,128)(2,1)}, bf16[512,1024]{1,0:T(8,128)(2,1)}, u32[]{:S(2)}, u32[]{:S(2)}) collective-permute-start(bf16[512,1024]{1,0:T(8,128)(2,1)} %rest_1_.3), channel_id=1, source_target_pairs={{0,2},{1,3},{2,0},{3,1},{4,6},{5,7},{6,4},{7,5},{8,10},{9,11},{10,... | collective-permute-start | bytes 3145736 | tf_op jit(solution)/shard_map/ppermute | solution.py:909
  19.1 36.7 %collective-permute-start = (f32[4,2048]{1,0:T(4,128)S(1)}, f32[4,2048]{1,0:T(4,128)S(1)}, u32[]{:S(2)}, u32[]{:S(2)}) collective-permute-start(f32[4,2048]{1,0:T(4,128)S(1)} %get-tuple-element.263), channel_id=1, source_target_pairs={{0,4},{4,0},{8,12},{12,8},{16,20},{20,16},{24,28},{28,24},{1,5},{5... | collective-permute-start | bytes 98312 | tf_op jit(solution)/shard_map/ppermute | solution.py:903
  52.1 15.7 %collective-permute-start.3 = (bf16[4,272,256]{2,1,0:T(8,128)(2,1)S(1)}, bf16[4,272,256]{2,1,0:T(8,128)(2,1)}, u32[]{:S(2)}, u32[]{:S(2)}) collective-permute-start(bf16[4,272,256]{2,1,0:T(8,128)(2,1)S(1)} %slice.270.rest_0_), channel_id=1, source_target_pairs={{0,1},{1,0},{2,3},{3,2},{4,5},{5,4},{6,7},{7,6},{8,9},{9,8},{10,11... | collective-permute-start | bytes 1671176 | tf_op jit(solution)/shard_map/ppermute | solution.py:909
  52.2 23.9 %collective-permute-start.4 = (bf16[4,272,256]{2,1,0:T(8,128)(2,1)S(1)}, bf16[4,272,256]{2,1,0:T(8,128)(2,1)}, u32[]{:S(2)}, u32[]{:S(2)}) collective-permute-start(bf16[4,272,256]{2,1,0:T(8,128)(2,1)S(1)} %slice.270.rest_0_), channel_id=1, source_target_pairs={{0,2},{1,3},{2,0},{3,1},{4,6},{5,7},{6,4},{7,5},{8,10},{9,11},{10,... | collective-permute-start | bytes 1671176 | tf_op jit(solution)/shard_map/ppermute | solution.py:909
  52.3 23.8 %collective-permute-start.5 = (bf16[4,272,256]{2,1,0:T(8,128)(2,1)S(1)}, bf16[4,272,256]{2,1,0:T(8,128)(2,1)}, u32[]{:S(2)}, u32[]{:S(2)}) collective-permute-start(bf16[4,272,256]{2,1,0:T(8,128)(2,1)S(1)} %slice.270.rest_0_), channel_id=1, source_target_pairs={{0,3},{1,2},{2,1},{3,0},{4,7},{5,6},{6,5},{7,4},{8,11},{9,10},{10,... | collective-permute-start | bytes 1671176 | tf_op jit(solution)/shard_map/ppermute | solution.py:909
  56.6 24.4 %collective-permute-start.6 = (bf16[4,272,256]{2,1,0:T(8,128)(2,1)S(1)}, bf16[4,272,256]{2,1,0:T(8,128)(2,1)S(1)}, u32[]{:S(2)}, u32[]{:S(2)}) collective-permute-start(bf16[4,272,256]{2,1,0:T(8,128)(2,1)S(1)} %slice.270.rest_0_), channel_id=1, source_target_pairs={{0,4},{4,0},{8,12},{12,8},{16,20},{20,16},{24,28},{28,24},{1,5},{5... | collective-permute-start | bytes 1671176 | tf_op jit(solution)/shard_map/ppermute | solution.py:903
  67.8 14.2 %collective-permute-start.7 = (bf16[4,272,256]{2,1,0:T(8,128)(2,1)}, bf16[4,272,256]{2,1,0:T(8,128)(2,1)}, u32[]{:S(2)}, u32[]{:S(2)}) collective-permute-start(bf16[4,272,256]{2,1,0:T(8,128)(2,1)} %collective-permute-done.3.rest_1_), channel_id=1, source_target_pairs={{0,4},{4,0},{8,12},{12,8},{16,20},{20,16},{24,28},{28,24},{1,5},{5... | collective-permute-start | bytes 1671176 | tf_op jit(solution)/shard_map/ppermute | solution.py:903
  76.0 7.6 %collective-permute-start.8 = (bf16[4,272,256]{2,1,0:T(8,128)(2,1)}, bf16[4,272,256]{2,1,0:T(8,128)(2,1)}, u32[]{:S(2)}, u32[]{:S(2)}) collective-permute-start(bf16[4,272,256]{2,1,0:T(8,128)(2,1)} %collective-permute-done.4.rest_2_), channel_id=1, source_target_pairs={{0,4},{4,0},{8,12},{12,8},{16,20},{20,16},{24,28},{28,24},{1,5},{5... | collective-permute-start | bytes 1671176 | tf_op jit(solution)/shard_map/ppermute | solution.py:903
  76.0 7.6 %collective-permute-start.9 = (bf16[4,272,256]{2,1,0:T(8,128)(2,1)}, bf16[4,272,256]{2,1,0:T(8,128)(2,1)}, u32[]{:S(2)}, u32[]{:S(2)}) collective-permute-start(bf16[4,272,256]{2,1,0:T(8,128)(2,1)} %collective-permute-done.5.rest_3_), channel_id=1, source_target_pairs={{0,4},{4,0},{8,12},{12,8},{16,20},{20,16},{24,28},{28,24},{1,5},{5... | collective-permute-start | bytes 1671176 | tf_op jit(solution)/shard_map/ppermute | solution.py:903
  79.3 25.8 %collective-permute-start.10 = (bf16[4,128,256]{2,1,0:T(8,128)(2,1)S(1)}, bf16[4,128,256]{2,1,0:T(8,128)(2,1)S(1)}, u32[]{:S(2)}, u32[]{:S(2)}) collective-permute-start(bf16[4,128,256]{2,1,0:T(8,128)(2,1)S(1)} %slice.271.rest_0_), channel_id=1, source_target_pairs={{0,1},{1,0},{2,3},{3,2},{4,5},{5,4},{6,7},{7,6},{8,9},{9,8},{10,11... | collective-permute-start | bytes 786440 | tf_op jit(solution)/shard_map/ppermute | solution.py:909
  81.8 23.3 %collective-permute-start.11 = (bf16[4,128,256]{2,1,0:T(8,128)(2,1)S(1)}, bf16[4,128,256]{2,1,0:T(8,128)(2,1)S(1)}, u32[]{:S(2)}, u32[]{:S(2)}) collective-permute-start(bf16[4,128,256]{2,1,0:T(8,128)(2,1)S(1)} %slice.271.rest_0_), channel_id=1, source_target_pairs={{0,2},{1,3},{2,0},{3,1},{4,6},{5,7},{6,4},{7,5},{8,10},{9,11},{10,... | collective-permute-start | bytes 786440 | tf_op jit(solution)/shard_map/ppermute | solution.py:909
  82.1 23.1 %collective-permute-start.12 = (bf16[4,128,256]{2,1,0:T(8,128)(2,1)S(1)}, bf16[4,128,256]{2,1,0:T(8,128)(2,1)S(1)}, u32[]{:S(2)}, u32[]{:S(2)}) collective-permute-start(bf16[4,128,256]{2,1,0:T(8,128)(2,1)S(1)} %slice.271.rest_0_), channel_id=1, source_target_pairs={{0,3},{1,2},{2,1},{3,0},{4,7},{5,6},{6,5},{7,4},{8,11},{9,10},{10,... | collective-permute-start | bytes 786440 | tf_op jit(solution)/shard_map/ppermute | solution.py:909
  105.2 5.7 %collective-permute-start.14 = (bf16[4,128,256]{2,1,0:T(8,128)(2,1)S(1)}, bf16[4,128,256]{2,1,0:T(8,128)(2,1)S(1)}, u32[]{:S(2)}, u32[]{:S(2)}) collective-permute-start(bf16[4,128,256]{2,1,0:T(8,128)(2,1)S(1)} %collective-permute-done.10.rest_1_), channel_id=1, source_target_pairs={{0,4},{4,0},{8,12},{12,8},{16,20},{20,16},{24,28},{28,24},{1,5},{5... | collective-permute-start | bytes 786440 | tf_op jit(solution)/shard_map/ppermute | solution.py:903
  105.7 5.2 %collective-permute-start.15 = (bf16[4,128,256]{2,1,0:T(8,128)(2,1)S(1)}, bf16[4,128,256]{2,1,0:T(8,128)(2,1)S(1)}, u32[]{:S(2)}, u32[]{:S(2)}) collective-permute-start(bf16[4,128,256]{2,1,0:T(8,128)(2,1)S(1)} %collective-permute-done.11.rest_2_), channel_id=1, source_target_pairs={{0,4},{4,0},{8,12},{12,8},{16,20},{20,16},{24,28},{28,24},{1,5},{5... | collective-permute-start | bytes 786440 | tf_op jit(solution)/shard_map/ppermute | solution.py:903
  105.8 5.1 collective-permute-start.16
  107.7 14.8 %collective-permute-start.19 = (bf16[256,1024]{1,0:T(8,128)(2,1)S(1)}, bf16[256,1024]{1,0:T(8,128)(2,1)S(1)}, u32[]{:S(2)}, u32[]{:S(2)}) collective-permute-start(bf16[256,1024]{1,0:T(8,128)(2,1)S(1)} %slice.206), channel_id=1, source_target_pairs={{0,2},{1,3},{2,0},{3,1},{4,6},{5,7},{6,4},{7,5},{8,10},{9,11},{10,... | collective-permute-start | bytes 1572872 | tf_op jit(solution)/shard_map/ppermute | solution.py:909
  109.7 14.9 %collective-permute-start.20 = (bf16[256,1024]{1,0:T(8,128)(2,1)S(1)}, bf16[256,1024]{1,0:T(8,128)(2,1)S(1)}, u32[]{:S(2)}, u32[]{:S(2)}) collective-permute-start(bf16[256,1024]{1,0:T(8,128)(2,1)S(1)} %slice.207), channel_id=1, source_target_pairs={{0,1},{1,0},{2,3},{3,2},{4,5},{5,4},{6,7},{7,6},{8,9},{9,8},{10,11... | collective-permute-start | bytes 1572872 | tf_op jit(solution)/shard_map/ppermute | solution.py:909
  117.2 28.6 %collective-permute-start.17 = (bf16[512,1024]{1,0:T(8,128)(2,1)}, bf16[512,1024]{1,0:T(8,128)(2,1)S(1)}, u32[]{:S(2)}, u32[]{:S(2)}) collective-permute-start(bf16[512,1024]{1,0:T(8,128)(2,1)} %get-tuple-element.139.rest_0_), channel_id=1, source_target_pairs={{0,1},{1,0},{2,3},{3,2},{4,5},{5,4},{6,7},{7,6},{8,9},{9,8},{10,11... | collective-permute-start | bytes 3145736 | tf_op jit(solution)/shard_map/ppermute | solution.py:909
  118.2 27.7 %collective-permute-start.18 = (bf16[512,1024]{1,0:T(8,128)(2,1)}, bf16[512,1024]{1,0:T(8,128)(2,1)}, u32[]{:S(2)}, u32[]{:S(2)}) collective-permute-start(bf16[512,1024]{1,0:T(8,128)(2,1)} %get-tuple-element.139.rest_0_), channel_id=1, source_target_pairs={{0,2},{1,3},{2,0},{3,1},{4,6},{5,7},{6,4},{7,5},{8,10},{9,11},{10,... | collective-permute-start | bytes 3145736 | tf_op jit(solution)/shard_map/ppermute | solution.py:909
  119.3 29.8 %collective-permute-start.21 = (bf16[512,1024]{1,0:T(8,128)(2,1)}, bf16[512,1024]{1,0:T(8,128)(2,1)S(1)}, u32[]{:S(2)}, u32[]{:S(2)}) collective-permute-start(bf16[512,1024]{1,0:T(8,128)(2,1)} %rest_1_.3), channel_id=1, source_target_pairs={{0,4},{4,0},{8,12},{12,8},{16,20},{20,16},{24,28},{28,24},{1,5},{5... | collective-permute-start | bytes 3145736 | tf_op jit(solution)/shard_map/ppermute | solution.py:903
  122.5 27.5 %collective-permute-start.22 = (bf16[512,1024]{1,0:T(8,128)(2,1)}, bf16[512,1024]{1,0:T(8,128)(2,1)S(1)}, u32[]{:S(2)}, u32[]{:S(2)}) collective-permute-start(bf16[512,1024]{1,0:T(8,128)(2,1)} %collective-permute-done.1.rest_2_), channel_id=1, source_target_pairs={{0,4},{4,0},{8,12},{12,8},{16,20},{20,16},{24,28},{28,24},{1,5},{5... | collective-permute-start | bytes 3145736 | tf_op jit(solution)/shard_map/ppermute | solution.py:903
  124.6 26.9 %collective-permute-start.23 = (bf16[512,1024]{1,0:T(8,128)(2,1)}, bf16[512,1024]{1,0:T(8,128)(2,1)S(1)}, u32[]{:S(2)}, u32[]{:S(2)}) collective-permute-start(bf16[512,1024]{1,0:T(8,128)(2,1)} %collective-permute-done.2.rest_3_), channel_id=1, source_target_pairs={{0,4},{4,0},{8,12},{12,8},{16,20},{20,16},{24,28},{28,24},{1,5},{5... | collective-permute-start | bytes 3145736 | tf_op jit(solution)/shard_map/ppermute | solution.py:903
  145.9 5.7 %collective-permute-start.24 = (bf16[256,1024]{1,0:T(8,128)(2,1)S(1)}, bf16[256,1024]{1,0:T(8,128)(2,1)S(1)}, u32[]{:S(2)}, u32[]{:S(2)}) collective-permute-start(bf16[256,1024]{1,0:T(8,128)(2,1)S(1)} %collective-permute-done.19.rest_4_), channel_id=1, source_target_pairs={{0,4},{4,0},{8,12},{12,8},{16,20},{20,16},{24,28},{28,24},{1,5},{5... | collective-permute-start | bytes 1572872 | tf_op jit(solution)/shard_map/ppermute | solution.py:903
  145.9 6.7 %collective-permute-start.25 = (bf16[256,1024]{1,0:T(8,128)(2,1)S(1)}, bf16[256,1024]{1,0:T(8,128)(2,1)S(1)}, u32[]{:S(2)}, u32[]{:S(2)}) collective-permute-start(bf16[256,1024]{1,0:T(8,128)(2,1)S(1)} %collective-permute-done.20.rest_5_), channel_id=1, source_target_pairs={{0,4},{4,0},{8,12},{12,8},{16,20},{20,16},{24,28},{28,24},{1,5},{5... | collective-permute-start | bytes 1572872 | tf_op jit(solution)/shard_map/ppermute | solution.py:903
  149.1 29.5 %collective-permute-start.26 = (bf16[256,1024]{1,0:T(8,128)(2,1)}, bf16[256,1024]{1,0:T(8,128)(2,1)S(1)}, u32[]{:S(2)}, u32[]{:S(2)}) collective-permute-start(bf16[256,1024]{1,0:T(8,128)(2,1)} %slice.272), channel_id=1, source_target_pairs={{0,2},{1,3},{2,0},{3,1},{4,6},{5,7},{6,4},{7,5},{8,10},{9,11},{10,... | collective-permute-start | bytes 1572872 | tf_op jit(solution)/shard_map/ppermute | solution.py:909
  150.0 28.6 %collective-permute-start.27 = (bf16[256,1024]{1,0:T(8,128)(2,1)}, bf16[256,1024]{1,0:T(8,128)(2,1)}, u32[]{:S(2)}, u32[]{:S(2)}) collective-permute-start(bf16[256,1024]{1,0:T(8,128)(2,1)} %slice.273), channel_id=1, source_target_pairs={{0,1},{1,0},{2,3},{3,2},{4,5},{5,4},{6,7},{7,6},{8,9},{9,8},{10,11... | collective-permute-start | bytes 1572872 | tf_op jit(solution)/shard_map/ppermute | solution.py:909
  151.5 30.0 %collective-permute-start.28 = (bf16[512,1024]{1,0:T(8,128)(2,1)}, bf16[512,1024]{1,0:T(8,128)(2,1)}, u32[]{:S(2)}, u32[]{:S(2)}) collective-permute-start(bf16[512,1024]{1,0:T(8,128)(2,1)} %get-tuple-element.139.rest_0_), channel_id=1, source_target_pairs={{0,4},{4,0},{8,12},{12,8},{16,20},{20,16},{24,28},{28,24},{1,5},{5... | collective-permute-start | bytes 3145736 | tf_op jit(solution)/shard_map/ppermute | solution.py:903
  151.6 32.3 %collective-permute-start.29 = (bf16[512,1024]{1,0:T(8,128)(2,1)S(1)}, bf16[512,1024]{1,0:T(8,128)(2,1)}, u32[]{:S(2)}, u32[]{:S(2)}) collective-permute-start(bf16[512,1024]{1,0:T(8,128)(2,1)S(1)} %collective-permute-done.17.rest_1_), channel_id=1, source_target_pairs={{0,4},{4,0},{8,12},{12,8},{16,20},{20,16},{24,28},{28,24},{1,5},{5... | collective-permute-start | bytes 3145736 | tf_op jit(solution)/shard_map/ppermute | solution.py:903
  153.5 31.2 %collective-permute-start.30 = (bf16[512,1024]{1,0:T(8,128)(2,1)}, bf16[512,1024]{1,0:T(8,128)(2,1)}, u32[]{:S(2)}, u32[]{:S(2)}) collective-permute-start(bf16[512,1024]{1,0:T(8,128)(2,1)} %collective-permute-done.18.rest_2_), channel_id=1, source_target_pairs={{0,4},{4,0},{8,12},{12,8},{16,20},{20,16},{24,28},{28,24},{1,5},{5... | collective-permute-start | bytes 3145736 | tf_op jit(solution)/shard_map/ppermute | solution.py:903
  231.6 250.7 %reduce-scatter.5.cloned.1.call-start = ((), (), s32[]{:S(2)}) async-start(), calls=%async_computation.3 | async-start | bytes 7864320 | tf_op jit(solution)/shard_map/reduce_scatter | solution.py:1029
  292.0 16.0 %collective-permute-start.33 = (bf16[2048,1024]{1,0:T(8,128)(2,1)}, bf16[2048,1024]{1,0:T(8,128)(2,1)}, u32[]{:S(2)}, u32[]{:S(2)}) collective-permute-start(bf16[2048,1024]{1,0:T(8,128)(2,1)} %scatter_rows.4), channel_id=1, source_target_pairs={{0,4},{4,0},{8,12},{12,8},{16,20},{20,16},{24,28},{28,24},{1,5},{5... | collective-permute-start | bytes 12582920 | tf_op jit(solution)/shard_map/ppermute | solution.py:903
  312.4 14.9 %collective-permute-start.35 = (bf16[256,1024]{1,0:T(8,128)(2,1)S(1)}, bf16[256,1024]{1,0:T(8,128)(2,1)S(1)}, u32[]{:S(2)}, u32[]{:S(2)}) collective-permute-start(bf16[256,1024]{1,0:T(8,128)(2,1)S(1)} %get-tuple-element.252), channel_id=1, source_target_pairs={{0,1},{1,0},{2,3},{3,2},{4,5},{5,4},{6,7},{7,6},{8,9},{9,8},{10,11... | collective-permute-start | bytes 1572872 | tf_op jit(solution)/shard_map/ppermute | solution.py:909
  312.7 18.1 %collective-permute-start.36 = (bf16[256,1024]{1,0:T(8,128)(2,1)S(1)}, bf16[256,1024]{1,0:T(8,128)(2,1)S(1)}, u32[]{:S(2)}, u32[]{:S(2)}) collective-permute-start(bf16[256,1024]{1,0:T(8,128)(2,1)S(1)} %get-tuple-element.251), channel_id=1, source_target_pairs={{0,2},{1,3},{2,0},{3,1},{4,6},{5,7},{6,4},{7,5},{8,10},{9,11},{10,... | collective-permute-start | bytes 1572872 | tf_op jit(solution)/shard_map/ppermute | solution.py:909
  319.2 38.6 %collective-permute-start.39 = (bf16[256,1024]{1,0:T(8,128)(2,1)}, bf16[256,1024]{1,0:T(8,128)(2,1)}, u32[]{:S(2)}, u32[]{:S(2)}) collective-permute-start(bf16[256,1024]{1,0:T(8,128)(2,1)} %slice.295), channel_id=1, source_target_pairs={{0,2},{1,3},{2,0},{3,1},{4,6},{5,7},{6,4},{7,5},{8,10},{9,11},{10,... | collective-permute-start | bytes 1572872 | tf_op jit(solution)/shard_map/ppermute | solution.py:909
  320.5 39.3 %collective-permute-start.34 = (bf16[256,1024]{1,0:T(8,128)(2,1)S(1)}, bf16[256,1024]{1,0:T(8,128)(2,1)}, u32[]{:S(2)}, u32[]{:S(2)}) collective-permute-start(bf16[256,1024]{1,0:T(8,128)(2,1)S(1)} %slice.286), channel_id=1, source_target_pairs={{0,1},{1,0},{2,3},{3,2},{4,5},{5,4},{6,7},{7,6},{8,9},{9,8},{10,11... | collective-permute-start | bytes 1572872 | tf_op jit(solution)/shard_map/ppermute | solution.py:909
  331.0 27.3 %collective-permute-start.38 = (bf16[256,1024]{1,0:T(8,128)(2,1)S(1)}, bf16[256,1024]{1,0:T(8,128)(2,1)}, u32[]{:S(2)}, u32[]{:S(2)}) collective-permute-start(bf16[256,1024]{1,0:T(8,128)(2,1)S(1)} %add_convert_fusion.8), channel_id=1, source_target_pairs={{0,1},{1,0},{2,3},{3,2},{4,5},{5,4},{6,7},{7,6},{8,9},{9,8},{10,11... | collective-permute-start | bytes 1572872 | tf_op jit(solution)/shard_map/ppermute | solution.py:909
  333.3 26.6 %collective-permute-start.37 = (bf16[256,1024]{1,0:T(8,128)(2,1)S(1)}, bf16[256,1024]{1,0:T(8,128)(2,1)}, u32[]{:S(2)}, u32[]{:S(2)}) collective-permute-start(bf16[256,1024]{1,0:T(8,128)(2,1)S(1)} %add_convert_fusion.9), channel_id=1, source_target_pairs={{0,2},{1,3},{2,0},{3,1},{4,6},{5,7},{6,4},{7,5},{8,10},{9,11},{10,... | collective-permute-start | bytes 1572872 | tf_op jit(solution)/shard_map/ppermute | solution.py:909
  357.8 10.6 %collective-permute-start.42 = (bf16[512,1024]{1,0:T(8,128)(2,1)S(1)}, bf16[512,1024]{1,0:T(8,128)(2,1)S(1)}, u32[]{:S(2)}, u32[]{:S(2)}) collective-permute-start(bf16[512,1024]{1,0:T(8,128)(2,1)S(1)} %get-tuple-element.236), channel_id=1, source_target_pairs={{0,4},{4,0},{8,12},{12,8},{16,20},{20,16},{24,28},{28,24},{1,5},{5... | collective-permute-start | bytes 3145736 | tf_op jit(solution)/shard_map/ppermute | solution.py:903
  357.8 10.6 %collective-permute-start.41 = (bf16[512,1024]{1,0:T(8,128)(2,1)S(1)}, bf16[512,1024]{1,0:T(8,128)(2,1)S(1)}, u32[]{:S(2)}, u32[]{:S(2)}) collective-permute-start(bf16[512,1024]{1,0:T(8,128)(2,1)S(1)} %get-tuple-element.237), channel_id=1, source_target_pairs={{0,4},{4,0},{8,12},{12,8},{16,20},{20,16},{24,28},{28,24},{1,5},{5... | collective-permute-start | bytes 3145736 | tf_op jit(solution)/shard_map/ppermute | solution.py:903
  358.3 10.0 %collective-permute-start.40 = (bf16[512,1024]{1,0:T(8,128)(2,1)S(1)}, bf16[512,1024]{1,0:T(8,128)(2,1)S(1)}, u32[]{:S(2)}, u32[]{:S(2)}) collective-permute-start(bf16[512,1024]{1,0:T(8,128)(2,1)S(1)} %get-tuple-element.238), channel_id=1, source_target_pairs={{0,4},{4,0},{8,12},{12,8},{16,20},{20,16},{24,28},{28,24},{1,5},{5... | collective-permute-start | bytes 3145736 | tf_op jit(solution)/shard_map/ppermute | solution.py:903
  371.1 39.5 %collective-permute-start.43 = (bf16[256,1024]{1,0:T(8,128)(2,1)}, bf16[256,1024]{1,0:T(8,128)(2,1)S(1)}, u32[]{:S(2)}, u32[]{:S(2)}) collective-permute-start(bf16[256,1024]{1,0:T(8,128)(2,1)} %get-tuple-element.250), channel_id=1, source_target_pairs={{0,1},{1,0},{2,3},{3,2},{4,5},{5,4},{6,7},{7,6},{8,9},{9,8},{10,11... | collective-permute-start | bytes 1572872 | tf_op jit(solution)/shard_map/ppermute | solution.py:909
  371.3 39.2 %collective-permute-start.44 = (bf16[256,1024]{1,0:T(8,128)(2,1)}, bf16[256,1024]{1,0:T(8,128)(2,1)}, u32[]{:S(2)}, u32[]{:S(2)}) collective-permute-start(bf16[256,1024]{1,0:T(8,128)(2,1)} %get-tuple-element.249), channel_id=1, source_target_pairs={{0,2},{1,3},{2,0},{3,1},{4,6},{5,7},{6,4},{7,5},{8,10},{9,11},{10,... | collective-permute-start | bytes 1572872 | tf_op jit(solution)/shard_map/ppermute | solution.py:909
  372.2 38.3 %collective-permute-start.45 = (bf16[256,1024]{1,0:T(8,128)(2,1)}, bf16[256,1024]{1,0:T(8,128)(2,1)}, u32[]{:S(2)}, u32[]{:S(2)}) collective-permute-start(bf16[256,1024]{1,0:T(8,128)(2,1)} %slice.242), channel_id=1, source_target_pairs={{0,1},{1,0},{2,3},{3,2},{4,5},{5,4},{6,7},{7,6},{8,9},{9,8},{10,11... | collective-permute-start | bytes 1572872 | tf_op jit(solution)/shard_map/ppermute | solution.py:909
  374.8 35.8 %collective-permute-start.46 = (bf16[256,1024]{1,0:T(8,128)(2,1)}, bf16[256,1024]{1,0:T(8,128)(2,1)}, u32[]{:S(2)}, u32[]{:S(2)}) collective-permute-start(bf16[256,1024]{1,0:T(8,128)(2,1)} %slice.243), channel_id=1, source_target_pairs={{0,2},{1,3},{2,0},{3,1},{4,6},{5,7},{6,4},{7,5},{8,10},{9,11},{10,... | collective-permute-start | bytes 1572872 | tf_op jit(solution)/shard_map/ppermute | solution.py:909
  410.6 4.7 collective-permute-start.50
  410.7 4.9 collective-permute-start.48
  411.2 5.9 %collective-permute-start.47 = (bf16[4,400,256]{2,1,0:T(8,128)(2,1)}, bf16[4,400,256]{2,1,0:T(8,128)(2,1)S(1)}, u32[]{:S(2)}, u32[]{:S(2)}) collective-permute-start(bf16[4,400,256]{2,1,0:T(8,128)(2,1)} %get-tuple-element.169), channel_id=1, source_target_pairs={{0,4},{4,0},{8,12},{12,8},{16,20},{20,16},{24,28},{28,24},{1,5},{5... | collective-permute-start | bytes 2457608 | tf_op jit(solution)/shard_map/ppermute | solution.py:903
  411.2 20.4 %collective-permute-start.53 = (bf16[512,1024]{1,0:T(8,128)(2,1)}, bf16[512,1024]{1,0:T(8,128)(2,1)}, u32[]{:S(2)}, u32[]{:S(2)}) collective-permute-start(bf16[512,1024]{1,0:T(8,128)(2,1)} %get-tuple-element.235), channel_id=1, source_target_pairs={{0,4},{4,0},{8,12},{12,8},{16,20},{20,16},{24,28},{28,24},{1,5},{5... | collective-permute-start | bytes 3145736 | tf_op jit(solution)/shard_map/ppermute | solution.py:903
  413.9 15.1 %collective-permute-start.55 = (bf16[256,1024]{1,0:T(8,128)(2,1)}, bf16[256,1024]{1,0:T(8,128)(2,1)}, u32[]{:S(2)}, u32[]{:S(2)}) collective-permute-start(bf16[256,1024]{1,0:T(8,128)(2,1)} %add_convert_fusion.6), channel_id=1, source_target_pairs={{0,1},{1,0},{2,3},{3,2},{4,5},{5,4},{6,7},{7,6},{8,9},{9,8},{10,11... | collective-permute-start | bytes 1572872 | tf_op jit(solution)/shard_map/ppermute | solution.py:909
  415.3 15.0 %collective-permute-start.54 = (bf16[256,1024]{1,0:T(8,128)(2,1)}, bf16[256,1024]{1,0:T(8,128)(2,1)S(1)}, u32[]{:S(2)}, u32[]{:S(2)}) collective-permute-start(bf16[256,1024]{1,0:T(8,128)(2,1)} %add_convert_fusion.7), channel_id=1, source_target_pairs={{0,2},{1,3},{2,0},{3,1},{4,6},{5,7},{6,4},{7,5},{8,10},{9,11},{10,... | collective-permute-start | bytes 1572872 | tf_op jit(solution)/shard_map/ppermute | solution.py:909
  420.4 25.2 %collective-permute-start.49 = (bf16[4,400,256]{2,1,0:T(8,128)(2,1)}, bf16[4,400,256]{2,1,0:T(8,128)(2,1)}, u32[]{:S(2)}, u32[]{:S(2)}) collective-permute-start(bf16[4,400,256]{2,1,0:T(8,128)(2,1)} %pad_maximum_fusion), channel_id=1, source_target_pairs={{0,1},{1,0},{2,3},{3,2},{4,5},{5,4},{6,7},{7,6},{8,9},{9,8},{10,11... | collective-permute-start | bytes 2457608 | tf_op jit(solution)/shard_map/ppermute | solution.py:909
  421.9 24.9 %collective-permute-start.51 = (bf16[4,400,256]{2,1,0:T(8,128)(2,1)}, bf16[4,400,256]{2,1,0:T(8,128)(2,1)}, u32[]{:S(2)}, u32[]{:S(2)}) collective-permute-start(bf16[4,400,256]{2,1,0:T(8,128)(2,1)} %pad_maximum_fusion.1), channel_id=1, source_target_pairs={{0,2},{1,3},{2,0},{3,1},{4,6},{5,7},{6,4},{7,5},{8,10},{9,11},{10,... | collective-permute-start | bytes 2457608 | tf_op jit(solution)/shard_map/ppermute | solution.py:909
  429.0 6.2 %collective-permute-start.52 = (bf16[2,192,1024]{2,1,0:T(8,128)(2,1)S(1)}, bf16[2,192,1024]{2,1,0:T(8,128)(2,1)}, u32[]{:S(2)}, u32[]{:S(2)}) collective-permute-start(bf16[2,192,1024]{2,1,0:T(8,128)(2,1)S(1)} %slice_bitcast_fusion.3), channel_id=1, source_target_pairs={{0,4},{4,0},{8,12},{12,8},{16,20},{20,16},{24,28},{28,24},{1,5},{5... | collective-permute-start | bytes 2359304 | tf_op jit(solution)/shard_map/ppermute | solution.py:903
  447.9 10.4 %collective-permute-start.58 = (bf16[2,400,256]{2,1,0:T(8,128)(2,1)S(1)}, bf16[2,400,256]{2,1,0:T(8,128)(2,1)S(1)}, u32[]{:S(2)}, u32[]{:S(2)}) collective-permute-start(bf16[2,400,256]{2,1,0:T(8,128)(2,1)S(1)} %add_convert_fusion.10), channel_id=1, source_target_pairs={{0,1},{1,0},{2,3},{3,2},{4,5},{5,4},{6,7},{7,6},{8,9},{9,8},{10,11... | collective-permute-start | bytes 1228808 | tf_op jit(solution)/shard_map/ppermute | solution.py:909
  449.6 14.2 %collective-permute-start.56 = (bf16[4,400,256]{2,1,0:T(8,128)(2,1)S(1)}, bf16[4,400,256]{2,1,0:T(8,128)(2,1)S(1)}, u32[]{:S(2)}, u32[]{:S(2)}) collective-permute-start(bf16[4,400,256]{2,1,0:T(8,128)(2,1)S(1)} %copy-done.52), channel_id=1, source_target_pairs={{0,4},{4,0},{8,12},{12,8},{16,20},{20,16},{24,28},{28,24},{1,5},{5... | collective-permute-start | bytes 2457608 | tf_op jit(solution)/shard_map/ppermute | solution.py:903
  450.7 11.9 %collective-permute-start.57 = (bf16[2,400,256]{2,1,0:T(8,128)(2,1)S(1)}, bf16[2,400,256]{2,1,0:T(8,128)(2,1)S(1)}, u32[]{:S(2)}, u32[]{:S(2)}) collective-permute-start(bf16[2,400,256]{2,1,0:T(8,128)(2,1)S(1)} %add_convert_fusion.11), channel_id=1, source_target_pairs={{0,2},{1,3},{2,0},{3,1},{4,6},{5,7},{6,4},{7,5},{8,10},{9,11},{10,... | collective-permute-start | bytes 1228808 | tf_op jit(solution)/shard_map/ppermute | solution.py:909
  483.4 4.7 collective-permute-start.62
  483.5 15.4 %collective-permute-start.59 = (bf16[400,256]{1,0:T(8,128)(2,1)}, bf16[400,256]{1,0:T(8,128)(2,1)S(1)}, u32[]{:S(2)}, u32[]{:S(2)}) collective-permute-start(bf16[400,256]{1,0:T(8,128)(2,1)} %get-tuple-element.259), channel_id=1, source_target_pairs={{0,24},{4,28},{8,16},{12,20},{16,8},{20,12},{24,0},{28,4},{1,25},{... | collective-permute-start | bytes 614408 | tf_op jit(solution)/shard_map/ppermute | solution.py:906
  486.1 19.4 %collective-permute-start.60 = (bf16[400,256]{1,0:T(8,128)(2,1)S(1)}, bf16[400,256]{1,0:T(8,128)(2,1)S(1)}, u32[]{:S(2)}, u32[]{:S(2)}) collective-permute-start(bf16[400,256]{1,0:T(8,128)(2,1)S(1)} %get-tuple-element.258), channel_id=1, source_target_pairs={{0,16},{4,20},{8,24},{12,28},{16,0},{20,4},{24,8},{28,12},{1,17},{... | collective-permute-start | bytes 614408 | tf_op jit(solution)/shard_map/ppermute | solution.py:906
  486.6 19.0 %collective-permute-start.61 = (bf16[400,256]{1,0:T(8,128)(2,1)S(1)}, bf16[400,256]{1,0:T(8,128)(2,1)S(1)}, u32[]{:S(2)}, u32[]{:S(2)}) collective-permute-start(bf16[400,256]{1,0:T(8,128)(2,1)S(1)} %get-tuple-element.257), channel_id=1, source_target_pairs={{0,8},{4,12},{8,0},{12,4},{16,24},{20,28},{24,16},{28,20},{1,9},{5... | collective-permute-start | bytes 614408 | tf_op jit(solution)/shard_map/ppermute | solution.py:906
  (56 other events, 894.5 us)
Sparse Core Ops, SparseCore 0:
  12.3 180.1 all-gather.5
  194.2 62.7 all-gather.7
  259.3 109.4 reduce-scatter.2
  370.9 111.2 reduce-scatter.4
